TPU v7x, 32 devices: a whole 2x2x4 slice. The times are simulated.
32 devices in a mesh: dp: 4 (over x, core), expert: 4 (over z), head: 2 (over y).
Axes of the slice: x: 2, y: 2, z: 4, core: 2. Of those that a mesh axis runs over, the one named last changes fastest.
Arguments:
- block_input: bfloat16 [16384, 768], P(('dp', 'expert', 'head')), may hold values from -6 to 6
- output_cotangent: bfloat16 [16384, 768], P(('dp', 'expert', 'head')), may hold values from -6 to 6
- token_ids: int32 [16384], P(('dp', 'expert', 'head')), may hold values from 0 to 8007, as said below
- positions: int32 [16384], P(('dp', 'expert', 'head')), may hold values from 0 to 1023, as said below
- hash_table: int32 [8008], replicated, may hold values from 0 to 3, as said below
- first_gain: float32 [768], replicated, may hold values from 0.5 to 1.5
- second_gain: float32 [768], replicated, may hold values from 0.5 to 1.5
- project_weight: bfloat16 [3, 768, 768], P(None, None, 'head'), may hold values from -0.21875 to 0.21875
- output_weight: bfloat16 [768, 768], P('head'), may hold values from -0.875 to 0.875
- expert_inner: bfloat16 [4, 768, 3072], P('expert'), may hold values from -0.21875 to 0.21875
- expert_outer: bfloat16 [4, 3072, 768], P('expert'), may hold values from -0.109375 to 0.109375
Outputs:
- block_output: bfloat16 [16384, 768], P(('dp', 'expert', 'head'))
- input_grad: float32 [16384, 768], P(('dp', 'expert', 'head'))
- first_gain_grad: float32 [768], replicated
- second_gain_grad: float32 [768], replicated
- project_grad: float32 [3, 768, 768], P(None, None, 'head')
- output_weight_grad: float32 [768, 768], P('head')
- expert_inner_grad: float32 [4, 768, 3072], P('expert')
- expert_outer_grad: float32 [4, 3072, 768], P('expert')
Inputs may be any that keep to these rules, and one draw needn't show every extreme that they name: `token_ids`: on every device, exactly 256 of its 512 tokens have ids that hash_table maps to one expert, and at most 256 map to any other expert; within a group of devices along the expert axis this busiest expert is the same for all devices. `hash_table`: every expert is named by 2002 ids. `positions`: documents lie inside sequences of 1024 tokens; the first starts at a sequence's first token; a token's value is its index in the sequence minus that of its document's first token. In every sequence, tokens 1024 // 2 - 1 and 512 share a document. Some sequence is a single document.
All inputs are finite; a program needn't handle non-finite values.
Results may differ from a plain program's by a relative error of at most 0.012.
Values may be sent and summed in bfloat16 or wider, within the bound.
No kernel may reach another device: no remote copies, remote signals or barrier semaphores. Data moves between devices by JAX's collectives and lax.ppermute only.
A program may use at most 256 MiB of HBM per device.

v0:
```python
import functools

import jax
import jax.numpy as jnp
from jax import lax
from jax.experimental import pallas as pl
from jax.experimental.pallas import tpu as pltpu
from jax.sharding import Mesh
from jax.sharding import PartitionSpec as P

HEAD_DIM = 64
BF = jnp.bfloat16
F32 = jnp.float32


def swap(values, axis, bit, name):
    size = lax.axis_size(axis)
    with jax.named_scope(name):
        return lax.ppermute(values, axis, [(i, i ^ bit) for i in range(size)])


def bits_of(axis, low=1):
    size = lax.axis_size(axis)
    found = []
    while low < size:
        found.append((axis, low))
        low *= 2
    return found


def side(axis, bit):
    return (lax.axis_index(axis) // bit) % 2


PAIR = 2 * HEAD_DIM
ATTEND_FLOPS = 20 * 10**9
BACK_FLOPS = 300 * 10**9
HIDE = -1000000000.0
VMEM_LIMIT = 64 * 1024 * 1024


def dot(left, right):
    return jnp.dot(left, right, preferred_element_type=F32)


def dot_nt(left, right):
    return lax.dot_general(left, right, (((1,), (1,)), ((), ())), preferred_element_type=F32)


def norm_parts(values):
    center = values - jnp.mean(values, axis=-1, keepdims=True)
    scale = lax.rsqrt(jnp.mean(center * center, axis=-1, keepdims=True) + 1e-05)
    return center * scale, scale


def norm_back(grad, normed, scale):
    along = jnp.mean(grad * normed, axis=-1, keepdims=True)
    return scale * (grad - jnp.mean(grad, axis=-1, keepdims=True) - normed * along)


def shaped(shape, dtype):
    return jax.ShapeDtypeStruct(shape, dtype)


def call(kernel, operands, after=(), alias=(), prefetch=(), flops=1, **options):
    extra = [*alias, *after]
    anywhere = pl.BlockSpec(memory_space=pl.ANY)
    options["in_specs"] = [*options["in_specs"], *[anywhere] * len(extra)]
    first = len(prefetch) + len(operands)
    fixed, skip = len(operands), len(extra)

    def body(*refs):
        cut = len(prefetch) + fixed
        kernel(*refs[:cut], *refs[cut + skip :])

    if prefetch:
        specs = {name: options.pop(name) for name in ("grid", "in_specs", "out_specs")}
        specs["scratch_shapes"] = options.pop("scratch_shapes", ())
        options["grid_spec"] = pltpu.PrefetchScalarGridSpec(
            num_scalar_prefetch=len(prefetch), **specs
        )
    return pl.pallas_call(
        body,
        input_output_aliases={first + i: i for i in range(len(alias))},
        compiler_params=pltpu.CompilerParams(vmem_limit_bytes=VMEM_LIMIT),
        cost_estimate=pl.CostEstimate(flops=flops, bytes_accessed=1, transcendentals=0),
        **options,
    )(*prefetch, *operands, *extra)


def whole(shape):
    return pl.BlockSpec(shape, lambda *_: (0,) * len(shape))


def plain(kernel, operands, out_shape, name, after=(), scratch=(), flops=1):
    return call(
        kernel,
        operands,
        after=after,
        flops=flops,
        grid=(1,),
        in_specs=[whole(x.shape) for x in operands],
        out_specs=jax.tree.map(lambda s: whole(s.shape), out_shape),
        out_shape=out_shape,
        scratch_shapes=scratch,
        name=name,
    )


def project_kernel(which_ref, x_ref, gain_ref, weight_ref, first_ref, out_ref):
    @pl.when(pl.program_id(0) == 0)
    def _():
        normed, _ = norm_parts(x_ref[...].astype(F32))
        first_ref[0] = (normed * gain_ref[...]).astype(BF)

    out_ref[0, 0] = dot(first_ref[0], weight_ref[0]).astype(BF)


def project(which, rows, gain, weight, earlier, after=()):
    count, width = rows.shape
    cols = weight.shape[2]
    return call(
        project_kernel,
        [rows, gain, weight],
        after=after,
        alias=earlier,
        prefetch=[which],
        grid=(3,),
        in_specs=[
            whole((count, width)),
            whole((1, width)),
            pl.BlockSpec((1, width, cols), lambda c, w: (c, 0, 0)),
        ],
        out_specs=[
            pl.BlockSpec((1, count, width), lambda c, w: (w[0], 0, 0)),
            pl.BlockSpec((1, 1, count, cols), lambda c, w: (c, w[0], 0, 0)),
        ],
        out_shape=[shaped((2, count, width), BF), shaped((3, 2, count, cols), BF)],
        name="project",
    )


def attend_kernel(
    which_ref, q_ref, kd_ref, vd_ref, kc_ref, vc_ref, pos_ref,
    pd_ref, pc_ref, rl_ref, context_ref, bias_d, bias_c,
):
    count = q_ref.shape[2]
    step = count // 2

    @pl.when(pl.program_id(0) == 0)
    def _():
        row = lax.broadcasted_iota(jnp.int32, (count, count), 0)
        col = lax.broadcasted_iota(jnp.int32, (count, count), 1)
        start = row - pos_ref[0]
        bias_d[...] = jnp.where((col <= row) & (col >= start), 0.0, HIDE)
        bias_c[...] = jnp.where(col >= start + count, 0.0, HIDE)

    lane = lax.broadcasted_iota(jnp.int32, (1, PAIR), 1) // HEAD_DIM

    def half(late):
        for at in (0, step):
            rows = pl.ds(at, step)
            keys = at + step
            q = q_ref[0, 0, rows, :] * 0.125
            mixed, scale = 0.0, []
            for a in (0, 1):
                mine = jnp.where(lane == a, q, 0.0).astype(BF)
                s_d = dot_nt(mine, kd_ref[0, 0, :keys, :]) + bias_d[rows, :keys]
                top = jnp.max(s_d, axis=-1, keepdims=True)
                if late:
                    s_c = dot_nt(mine, kc_ref[0, 0]) + bias_c[rows, :]
                    top = jnp.maximum(top, jnp.max(s_c, axis=-1, keepdims=True))
                p_d = jnp.exp(s_d - top)
                total = jnp.sum(p_d, axis=-1, keepdims=True)
                p_d = p_d.astype(BF)
                pd_ref[0, a, rows, :keys] = p_d
                value = jnp.where(lane == a, vd_ref[0, 0, :keys, :], 0.0).astype(BF)
                mixed = mixed + dot(p_d, value)
                if late:
                    p_c = jnp.exp(s_c - top)
                    total = total + jnp.sum(p_c, axis=-1, keepdims=True)
                    p_c = p_c.astype(BF)
                    pc_ref[0, a, rows, :] = p_c
                    value = jnp.where(lane == a, vc_ref[0, 0], 0.0).astype(BF)
                    mixed = mixed + dot(p_c, value)
                scale.append(1.0 / total)
            scale = jnp.where(lane == 0, scale[0], scale[1])
            rl_ref[0, rows, :] = scale
            context_ref[rows, :] = (mixed * scale).astype(BF)

    pl.when(which_ref[0] == 0)(lambda: half(False))
    pl.when(which_ref[0] == 1)(lambda: half(True))


def attend(which, projected, positions, earlier, after=(), flops=1):
    _, _, count, cols = projected.shape
    heads = cols // HEAD_DIM

    def block(part, other):
        if other:
            return pl.BlockSpec((1, 1, count, PAIR), lambda g, w: (part, 0, 0, g))
        return pl.BlockSpec((1, 1, count, PAIR), lambda g, w: (part, w[0], 0, g))

    score_spec = pl.BlockSpec((1, 2, count, count), lambda g, w: (w[0], g, 0, 0))
    return call(
        attend_kernel,
        [*[projected] * 5, positions],
        after=after,
        alias=earlier,
        prefetch=[which],
        flops=flops,
        grid=(cols // PAIR,),
        in_specs=[
            block(0, False),
            block(1, False),
            block(2, False),
            block(1, True),
            block(2, True),
            pl.BlockSpec((1, count, 1), lambda g, w: (w[0], 0, 0)),
        ],
        out_specs=[
            score_spec,
            score_spec,
            pl.BlockSpec((1, count, PAIR), lambda g, w: (w[0], 0, g)),
            pl.BlockSpec((count, PAIR), lambda g, w: (0, g)),
        ],
        scratch_shapes=[pltpu.VMEM((count, count), F32)] * 2,
        out_shape=[
            shaped((2, heads, count, count), BF),
            shaped((2, heads, count, count), BF),
            shaped((2, count, cols), F32),
            shaped((count, cols), BF),
        ],
        name="attend",
    )


def hidden_kernel(
    x_ref, own_ref, got_ref, own_weight_ref, got_weight_ref, gain_ref, slot_ref, hidden_ref, *out_refs
):
    attended = dot(own_ref[...], own_weight_ref[...]) + dot(got_ref[...], got_weight_ref[...])
    hidden = x_ref[...].astype(F32) + attended
    hidden_ref[...] = hidden
    normed, _ = norm_parts(hidden)
    second = (normed * gain_ref[...]).astype(BF)
    send_rows(second, slot_ref, out_refs)


def send_rows(rows, slot_ref, out_refs):
    capacity = out_refs[0].shape[0]
    for k, ref in enumerate(out_refs):
        slot = lax.broadcasted_iota(jnp.int32, (capacity, rows.shape[0]), 0) + k * capacity
        place = jnp.where(slot_ref[...] == slot, 1.0, 0.0).astype(BF)
        ref[...] = dot(place, rows).astype(BF)


def hidden_rows(x, own, got, own_weight, got_weight, gain, slot_row, experts, after=()):
    count, width = x.shape
    out = [shaped((count, width), F32)] + [shaped((count // 2, width), BF)] * experts
    return plain(
        hidden_kernel,
        [x, own, got, own_weight, got_weight, gain, slot_row],
        out,
        "hidden_rows",
        after,
    )


def send_kernel(rows_ref, slot_ref, out_ref):
    send_rows(rows_ref[...], slot_ref, [out_ref.at[k] for k in range(out_ref.shape[0])])


def sent_rows(rows, slot_row, experts):
    count, width = rows.shape
    out = shaped((experts, count // 2, width), BF)
    return plain(send_kernel, [rows, slot_row], out, "sent_rows")


def taken_rows(slot_ref, block_refs):
    count, capacity = slot_ref.shape[0], block_refs[0].shape[0]
    total = 0.0
    for k, ref in enumerate(block_refs):
        slot = lax.broadcasted_iota(jnp.int32, (count, capacity), 1) + k * capacity
        place = jnp.where(slot_ref[...] == slot, 1.0, 0.0).astype(BF)
        total = total + dot(place, ref[...])
    return total


def output_kernel(hidden_ref, slot_ref, *refs):
    blocks = [refs[0].at[k] for k in range(refs[0].shape[0])]
    refs[-1][...] = (hidden_ref[...] + taken_rows(slot_ref, blocks)).astype(BF)


def output_rows(hidden, slot_col, blocks, after=()):
    return plain(
        output_kernel,
        [hidden, slot_col, blocks],
        shaped(hidden.shape, BF),
        "output_rows",
        after,
    )


def second_kernel(cot_ref, hidden_ref, gain_ref, slot_ref, own_weight_ref, got_weight_ref, *refs):
    grad_ref, low_ref, gain_grad_ref, own_ref, send_ref = refs[-5:]
    second_grad = taken_rows(slot_ref, refs[:-5])
    normed, scale = norm_parts(hidden_ref[...])
    gain_grad_ref[...] = jnp.sum(second_grad * normed, axis=0, keepdims=True)
    grad = cot_ref[...].astype(F32) + norm_back(second_grad * gain_ref[...], normed, scale)
    grad_ref[...] = grad
    low = grad.astype(BF)
    low_ref[...] = low
    send_ref[...] = dot_nt(low, got_weight_ref[...]).astype(BF)
    own_ref[...] = dot_nt(low, own_weight_ref[...]).astype(BF)


def second_back(cot, hidden, gain, slot_col, own_weight, got_weight, blocks, after=()):
    count, width = hidden.shape
    part = shaped((count, own_weight.shape[0]), BF)
    out = [
        shaped((count, width), F32),
        shaped((count, width), BF),
        shaped((1, width), F32),
        part,
        part,
    ]
    return plain(
        second_kernel,
        [cot, hidden, gain, slot_col, own_weight, got_weight, *blocks],
        out,
        "second_back",
        after,
        flops=BACK_FLOPS,
    )


def output_weight_kernel(
    core_ref, own_ref, got_ref, low_ref, own_out, kept_out, sent_out, scratch
):
    def part(ref):
        return lax.dot_general(
            ref[...], low_ref[...], (((0,), (0,)), ((), ())), preferred_element_type=F32
        ).astype(BF)

    scratch[...] = part(got_ref)
    rows = kept_out.shape[0]
    for ref, half in ((kept_out, core_ref[0]), (sent_out, 1 - core_ref[0])):
        ref[...] = scratch[pl.ds(pl.multiple_of(half * rows, rows), rows), :]
    own_out[...] = part(own_ref)


def output_weight_parts(core, own, got, low, after=()):
    cols, width = own.shape[1], low.shape[1]
    part = shaped((cols // 2, width), BF)
    out = [shaped((cols, width), BF), part, part]
    return call(
        output_weight_kernel,
        [own, got, low],
        after=after,
        prefetch=[core.reshape(1).astype(jnp.int32)],
        grid=(1,),
        in_specs=[whole(x.shape) for x in (own, got, low)],
        out_specs=[whole(o.shape) for o in out],
        out_shape=out,
        scratch_shapes=[pltpu.VMEM((cols, width), BF)],
        name="output_weight_parts",
    )


def first_kernel(x_ref, gain_ref, hidden_grad_ref, own_ref, theirs_ref, out_ref):
    grad = (own_ref[...] + theirs_ref[...].astype(F32)) * gain_ref[...]
    normed, scale = norm_parts(x_ref[...].astype(F32))
    out_ref[...] = hidden_grad_ref[...] + norm_back(grad, normed, scale)


def first_back(x, gain, hidden_grad, own, theirs, after=()):
    return plain(
        first_kernel, [x, gain, hidden_grad, own, theirs], shaped(x.shape, F32), "first_back", after
    )


def fill(target, refs):
    rows = refs[0].shape[0]
    for i, ref in enumerate(refs):
        target[i * rows : (i + 1) * rows] = ref[...]


def expert_kernel(count, sub, place_ref, *refs):
    x_refs, cot_refs, refs = refs[:count], refs[count : 2 * count], refs[2 * count :]
    inner_ref, outer_ref, act_ref, pre_ref, out_ref, *grad_refs, x, cot, grad_acc, out_acc = refs
    at = pl.program_id(0)
    last = pl.num_programs(0) - count
    size = out_ref.shape[1]

    @pl.when(at > last)
    def _():
        rows = pl.ds(pl.multiple_of((at - last) * size, size), size)
        out_ref[0] = out_acc[rows, :].astype(BF)

    pl.when(at <= last)(
        lambda: expert_step(
            count, sub, x_refs, cot_refs, inner_ref, outer_ref, act_ref, pre_ref, out_ref,
            grad_refs, x, cot, grad_acc, out_acc, at, last,
        )
    )


def expert_step(
    count, sub, x_refs, cot_refs, inner_ref, outer_ref, act_ref, pre_ref, out_ref, grad_refs,
    x, cot, grad_acc, out_acc, at, last,
):

    @pl.when(at == 0)
    def _():
        fill(x, x_refs)
        fill(cot, [ref.at[0] for ref in cot_refs])
        grad_acc[...] = jnp.zeros_like(grad_acc)
        out_acc[...] = jnp.zeros_like(out_acc)

    def front(i):
        cols = slice(i * sub, (i + 1) * sub)
        return dot(x[...], inner_ref[:, cols]), dot_nt(cot[...], outer_ref[cols, :])

    parts = inner_ref.shape[1] // sub
    now = front(0)
    for i in range(parts):
        later = front(i + 1) if i + 1 < parts else None
        value, grad = now
        square = value * value
        half = 0.5 + 0.5 * jnp.tanh(
            value * (0.7978845608028654 + 0.035677408136300125 * square)
        )
        act = value * half
        slope = half + act * (1.0 - half) * (1.5957691216057308 + 0.21406444881780074 * square)
        cols = slice(i * sub, (i + 1) * sub)
        act_ref[:, cols] = act.astype(BF)
        pre_ref[:, cols] = (grad * slope).astype(BF)
        now = later
    grad_acc[...] += dot_nt(pre_ref[...], inner_ref[...])
    out_acc[...] += dot(act_ref[...], outer_ref[...])

    @pl.when(at == last)
    def _():
        size = out_ref.shape[1]
        out_ref[0] = out_acc[:size].astype(BF)
        for i, ref in enumerate(grad_refs):
            ref[...] = grad_acc[i * size : (i + 1) * size].astype(BF)


def expert(index, blocks, cot, places, inner, outer, earlier, after=(), tile=768, sub=256):
    count, width = blocks[0].shape
    size, units = len(blocks), inner.shape[1]
    total = count * cot.shape[0]
    tiles = units // tile

    def held(j):
        return jnp.minimum(j, tiles - 1)

    wide = pl.BlockSpec((count * size, tile), lambda j, p: (index // size, held(j)))
    out = pl.BlockSpec(
        (1, count, width), lambda j, p: (p[jnp.maximum(j - tiles + 1, 0)], 0, 0)
    )

    def placed(i):
        return pl.BlockSpec((1, count, width), lambda j, p: (p[i], 0, 0))

    return call(
        functools.partial(expert_kernel, size, sub),
        [*blocks, *[cot] * size, inner, outer],
        after=after,
        alias=earlier,
        prefetch=[jnp.stack(places).astype(jnp.int32)],
        grid=(tiles + size - 1,),
        in_specs=[whole((count, width))] * size
        + [placed(i) for i in range(size)]
        + [
            pl.BlockSpec((width, tile), lambda j, p: (0, held(j))),
            pl.BlockSpec((tile, width), lambda j, p: (held(j), 0)),
        ],
        out_specs=[wide, wide, out] + [whole((count, width))] * size,
        out_shape=[shaped((total, units), BF)] * 2
        + [shaped(cot.shape, BF)]
        + [shaped((count, width), BF)] * size,
        scratch_shapes=[pltpu.VMEM((count * size, width), BF)] * 2
        + [pltpu.VMEM((count * size, width), F32)] * 2,
        name="expert",
    )


def weight_kernel(is_outer, count, which_ref, place_ref, wide_ref, *refs):
    *row_refs, out_ref, rows = refs
    if is_outer:
        row_refs = [row_refs[0].at[place_ref[i]] for i in range(count)]
    pl.when(pl.program_id(0) == 0)(lambda: fill(rows, row_refs))
    sides = (wide_ref[...], rows[...]) if is_outer else (rows[...], wide_ref[...])
    out_ref[...] = lax.dot_general(
        *sides, (((0,), (0,)), ((), ())), preferred_element_type=F32
    ).astype(BF)


def weight_part(is_outer, half, blocks, places, wide, after=(), tiles=4):
    count, width = blocks[0].shape
    total, units = wide.shape
    tile = units // 2 // tiles
    if is_outer:
        row_specs, blocks = [whole(blocks.shape)], [blocks]
        shape, spec = (units // 2, width), pl.BlockSpec((tile, width), lambda j, w, p: (j, 0))
    else:
        row_specs = [whole((count, width))] * len(blocks)
        shape, spec = (width, units // 2), pl.BlockSpec((width, tile), lambda j, w, p: (0, j))
    return call(
        functools.partial(weight_kernel, is_outer, len(places)),
        [wide, *blocks],
        after=after,
        prefetch=[half.reshape(1).astype(jnp.int32), jnp.stack(places).astype(jnp.int32)],
        grid=(tiles,),
        in_specs=[pl.BlockSpec((total, tile), lambda j, w, p: (0, w[0] * tiles + j))] + row_specs,
        out_specs=spec,
        out_shape=shaped(shape, BF),
        scratch_shapes=[pltpu.VMEM((total, width), BF)],
        name="weight_part",
    )


def split_kernel(place_ref, kept_ref, got_ref, sent_out, kept_out):
    total = (kept_ref[...].astype(F32) + got_ref[...].astype(F32)).astype(BF)
    half = pl.num_programs(0) // 2

    @pl.when(pl.program_id(0) < half)
    def _():
        sent_out[...] = total

    @pl.when(pl.program_id(0) >= half)
    def _():
        kept_out[...] = total


def split_sum(kept, got, turn, by_rows, after=(), tiles=4):
    rows, cols = kept.shape
    if by_rows:
        tile, out = (rows // tiles, cols), (rows // 2, cols)
    else:
        tile, out = (rows, cols // tiles), (rows, cols // 2)

    def at(j):
        return (j, 0) if by_rows else (0, j)

    def place(j, w):
        return at((w[0] * (tiles // 2) + j) % tiles)

    return call(
        split_kernel,
        [kept, got],
        after=after,
        prefetch=[turn.reshape(1).astype(jnp.int32)],
        grid=(tiles,),
        in_specs=[pl.BlockSpec(tile, place)] * 2,
        out_specs=[
            pl.BlockSpec(tile, lambda j, w: at(jnp.minimum(j, tiles // 2 - 1))),
            pl.BlockSpec(tile, lambda j, w: at(jnp.maximum(j - tiles // 2, 0))),
        ],
        out_shape=[shaped(out, BF)] * 2,
        name="split_sum",
    )


def assemble_kernel(place_ref, *refs):
    *piece_refs, out_ref = refs
    for i, ref in enumerate(piece_refs):

        @pl.when(pl.program_id(0) == i)
        def _(ref=ref):
            out_ref[...] = ref[...].astype(F32)


def assemble(pieces, places, shape, earlier, after=()):
    size = pieces[0].shape
    table = jnp.stack([jnp.stack(place) for place in places]).astype(jnp.int32)
    return call(
        assemble_kernel,
        pieces,
        after=after,
        alias=earlier,
        prefetch=[table],
        grid=(len(pieces),),
        in_specs=[whole(size)] * len(pieces),
        out_specs=[pl.BlockSpec(size, lambda i, t: (t[i, 0], t[i, 1]))],
        out_shape=[shaped(shape, F32)],
        name="assemble",
    )


def add_kernel(more_at, place_ref, kept_ref, got_ref, *refs):
    out_refs, more_refs = (refs, ()) if more_at is None else (refs[1:-1], refs[:1])
    rows = out_refs[0].shape[0]
    if more_refs:
        kept_ref, scratch = refs[-1], kept_ref
        kept_ref[...] = scratch[...].astype(F32)
        span = pl.ds(more_at, more_refs[0].shape[0])
        for ref in more_refs:
            kept_ref[span, :] += ref[...].astype(F32)
    for i, ref in enumerate(out_refs):
        cut = pl.ds(pl.multiple_of(place_ref[i] * rows, rows), rows)
        ref[...] = (kept_ref[cut, :].astype(F32) + got_ref[cut, :].astype(F32)).astype(BF)


def add(kept, got, places, after=(), more=(), more_at=None):
    shape = kept.shape
    out = [shaped((shape[0] // len(places), *shape[1:]), BF)] * len(places)
    return call(
        functools.partial(add_kernel, more_at),
        [kept, got, *more],
        after=after,
        prefetch=[jnp.stack(places).astype(jnp.int32)],
        grid=(1,),
        in_specs=[whole(shape)] * 2 + [whole(x.shape) for x in more],
        out_specs=[whole(o.shape) for o in out],
        scratch_shapes=[pltpu.VMEM(shape, F32)] if more else [],
        out_shape=out,
        name="add",
    )


def adds_kernel(count, cuts, place_ref, *refs):
    in_refs, out_refs = refs[: 2 * count], refs[2 * count :]
    for i in range(count):
        kept_ref, got_ref = in_refs[2 * i : 2 * i + 2]
        for j in range(cuts):
            ref = out_refs[cuts * i + j]
            rows = ref.shape[0]
            cut = pl.ds(pl.multiple_of(place_ref[cuts * i + j] * rows, rows), rows)
            ref[...] = (kept_ref[cut, :].astype(F32) + got_ref[cut, :].astype(F32)).astype(BF)


def adds(pairs, places, after=()):
    cuts = len(places[0])
    out = [
        shaped((kept.shape[0] // cuts, kept.shape[1]), BF) for kept, _ in pairs for _ in range(cuts)
    ]
    operands = [x for pair in pairs for x in pair]
    parts = call(
        functools.partial(adds_kernel, len(pairs), cuts),
        operands,
        after=after,
        prefetch=[jnp.stack([p for at in places for p in at]).astype(jnp.int32)],
        grid=(1,),
        in_specs=[whole(x.shape) for x in operands],
        out_specs=[whole(o.shape) for o in out],
        out_shape=out,
        name="adds",
    )
    return [parts[cuts * i : cuts * (i + 1)] for i in range(len(pairs))]


def gather_pieces(own, steps, order):
    weights = {step: 1 << (len(steps) - 1 - i) for i, step in enumerate(steps)}
    place = sum(side(*step) * weight for step, weight in weights.items())
    pieces = [(place, own)]
    for step in order:
        change = weights[step] * (1 - 2 * side(*step))
        pieces += [(at + change, swap(piece, *step, "piece")) for at, piece in pieces]
    return pieces


def total_kernel(in_ref, out_ref):
    count = in_ref.shape[0]
    value = sum(in_ref[i].astype(F32) for i in range(count)).astype(BF)
    for i in range(count):
        out_ref[i] = value


def total(blocks, after=()):
    return plain(total_kernel, [blocks], shaped(blocks.shape, BF), "total", after)


def halves(step):
    mine = side(*step)
    return [1 - mine, mine]


def touch_kernel(*out_refs):
    pass


def touch(values, after, flops=1):
    return call(
        touch_kernel,
        [],
        after=after,
        alias=values,
        flops=flops,
        in_specs=[],
        out_specs=[pl.BlockSpec(memory_space=pl.ANY)] * len(values),
        out_shape=[shaped(x.shape, x.dtype) for x in values],
        name="touch",
    )


def back_kernel(
    at_ref, own_ref, other_ref, q_ref, k_ref, v_ref, pd_ref, pc_ref, own_context_ref,
    other_context_ref, rl_ref, first_ref, wp_ref, gain_ref, second_ref, own_output_ref,
    sent_ref, kept_ref, mine_ref, theirs_ref,
    acc, scaled, through, key_acc, value_acc, queries, weights,
):
    group = pl.program_id(0)
    count = own_ref.shape[0]
    step = count // 2
    me, core = at_ref[0], at_ref[1]
    lane = lax.broadcasted_iota(jnp.int32, (1, PAIR), 1) // HEAD_DIM

    for ref, context, at in (
        (own_ref, own_context_ref, me),
        (other_ref, other_context_ref, 1 - me),
    ):
        grad = ref[...].astype(F32) * rl_ref[at]
        scaled[at] = grad
        through[at] = grad.astype(BF).astype(F32) * context[...].astype(F32)
    key_acc[...] = jnp.zeros_like(key_acc)
    value_acc[...] = jnp.zeros_like(value_acc)

    for h in (0, 1):
        for at in (0, step):
            rows = pl.ds(at, step)
            grads = scaled[h, rows, :]
            low = grads.astype(BF)
            low_t = jnp.transpose(grads).astype(BF)
            q_t = jnp.transpose(q_ref[0, h, rows, :].astype(F32)).astype(BF)
            query = 0.0
            for a in (0, 1):
                line = pl.ds(a * HEAD_DIM, HEAD_DIM)
                mine = jnp.where(lane == a, low, 0.0).astype(BF)
                along = jnp.sum(
                    jnp.where(lane == a, through[h, rows, :], 0.0), axis=-1, keepdims=True
                )
                parts = [(pd_ref, h, h * count, at + step)]
                if h:
                    parts.append((pc_ref, 0, 0, count))
                for p_ref, p_at, key_at, keys in parts:
                    source = key_at // count
                    p = p_ref[p_at, a, rows, :keys]
                    prob_grad = dot_nt(mine, v_ref[0, source, :keys, :])
                    score = (p.astype(F32) * (prob_grad - along)).astype(BF)
                    k = jnp.where(lane == a, k_ref[0, source, :keys, :], 0.0).astype(BF)
                    query = query + dot(score, k)
                    cols = pl.ds(key_at, keys)
                    key_acc[line, cols] += dot(q_t[a * HEAD_DIM : (a + 1) * HEAD_DIM], score)
                    value_acc[line, cols] += dot(low_t[a * HEAD_DIM : (a + 1) * HEAD_DIM], p)
            queries[pl.ds(h * count + at, step), :] = query * 0.125

    query = queries[...]
    key_t = key_acc[...] * 0.125
    value_t = value_acc[...]
    both = jnp.concatenate(
        [query.astype(BF), jnp.transpose(key_t).astype(BF), jnp.transpose(value_t).astype(BF)],
        axis=1,
    )
    both_t = jnp.concatenate(
        [jnp.transpose(query).astype(BF), key_t.astype(BF), value_t.astype(BF)], axis=0
    )
    first = jnp.concatenate([first_ref[0], first_ref[1]], axis=0)
    weights[...] = dot(both_t, first)
    size = 3 * PAIR // 2
    groups = pl.num_programs(0)
    here = pl.ds(pl.multiple_of(group * size, size), size)
    for ref, half in ((sent_ref, 1 - core), (kept_ref, core)):
        ref[here, :] = weights[pl.ds(pl.multiple_of(half * size, size), size), :].astype(BF)
    weight = jnp.concatenate([wp_ref[0], wp_ref[1], wp_ref[2]], axis=1)
    added = dot_nt(both, weight)

    @pl.when(group == 0)
    def _():
        for h in (0, 1):
            acc[h] = added[h * count : (h + 1) * count]

    @pl.when(group > 0)
    def _():
        for h in (0, 1):
            acc[h] += added[h * count : (h + 1) * count]

    @pl.when(group == groups - 1)
    def _():
        mine_ref[...] = acc[me]
        theirs_ref[...] = acc[1 - me].astype(BF)
        gain = 0.0
        for h in (0, 1):
            gain = gain + jnp.sum(acc[h] * first_ref[h].astype(F32), axis=0, keepdims=True)
        gain = gain / gain_ref[...]
        part = own_output_ref.shape[0] // 2
        at = groups * size
        end = at + part
        for ref, half in ((sent_ref, 1 - core), (kept_ref, core)):
            cut = pl.ds(pl.multiple_of(half * part, part), part)
            ref[at:end, :] = own_output_ref[cut, :]
            value = jnp.where(half == 0, gain, second_ref[...])
            high = value.astype(BF).astype(F32)
            line = lax.broadcasted_iota(jnp.int32, (ref.shape[0] - end, value.shape[1]), 0)
            tail = jnp.where(line == 0, high, jnp.where(line == 1, value - high, 0.0))
            ref[end:, :] = tail.astype(BF)


def attend_back(
    at, own, other, projected, p_diag, p_cross, own_context, other_context, inverse, first, weight,
    gain, second, own_output, lines, after=(),
):
    _, _, count, cols = projected.shape
    width = first.shape[2]
    rows = whole((count, width))
    pair = pl.BlockSpec((count, PAIR), lambda g, w: (0, g))

    def block(part):
        return pl.BlockSpec((1, 2, count, PAIR), lambda g, w: (part, 0, 0, g))

    sent = shaped((lines, width), BF)
    out = [sent, sent, shaped((count, width), F32), shaped((count, width), BF)]
    return call(
        back_kernel,
        [
            own, other, projected, projected, projected, p_diag, p_cross, own_context,
            other_context, inverse, first, weight, gain, second, own_output,
        ],
        after=after,
        prefetch=[at],
        grid=(cols // PAIR,),
        in_specs=[
            pair,
            pair,
            block(0),
            block(1),
            block(2),
            pl.BlockSpec((2, 2, count, count), lambda g, w: (0, g, 0, 0)),
            pl.BlockSpec((1, 2, count, count), lambda g, w: (1, g, 0, 0)),
            pair,
            pair,
            pl.BlockSpec((2, count, PAIR), lambda g, w: (0, 0, g)),
            whole((2, count, width)),
            pl.BlockSpec((3, width, PAIR), lambda g, w: (0, 0, g)),
            whole((1, width)),
            whole((1, width)),
            whole((cols, width)),
        ],
        out_specs=[whole(o.shape) for o in out],
        scratch_shapes=[
            pltpu.VMEM((2, count, width), F32),
            pltpu.VMEM((2, count, PAIR), F32),
            pltpu.VMEM((2, count, PAIR), F32),
            pltpu.VMEM((PAIR, 2 * count), F32),
            pltpu.VMEM((PAIR, 2 * count), F32),
            pltpu.VMEM((2 * count, PAIR), F32),
            pltpu.VMEM((3 * PAIR, width), F32),
        ],
        out_shape=out,
        name="attend_back",
    )


def project_grad_kernel(low_ref, high_ref, out_ref):
    both = jnp.concatenate([low_ref[...], high_ref[...]], axis=0).astype(F32)
    flat = jnp.transpose(both)
    for c in range(3):
        out_ref[c] = flat[:, c * PAIR : (c + 1) * PAIR]


def project_grads(low, high, cols):
    width = low.shape[1]
    part = pl.BlockSpec((3 * PAIR // 2, width), lambda g: (g, 0))
    return call(
        project_grad_kernel,
        [low, high],
        grid=(cols // PAIR,),
        in_specs=[part, part],
        out_specs=pl.BlockSpec((3, width, PAIR), lambda g: (0, 0, g)),
        out_shape=shaped((3, width, cols), F32),
        name="project_grads",
    )


def on_device(
    block_input,
    output_cotangent,
    token_ids,
    positions,
    hash_table,
    first_gain,
    second_gain,
    project_weight,
    output_weight,
    expert_inner,
    expert_outer,
):
    tok_rows, model_width = block_input.shape
    local_cols = output_weight.shape[0]
    expert_count = lax.axis_size("expert")
    capacity = tok_rows // 2
    inner_weight = expert_inner[0]
    outer_weight = expert_outer[0]
    my_head = lax.axis_index("head")
    my_expert = lax.axis_index("expert")
    own_at = my_head.reshape(1).astype(jnp.int32)
    other_at = 1 - own_at
    first_gain = first_gain.reshape(1, model_width)
    second_gain = second_gain.reshape(1, model_width)

    other_input = swap(block_input, "head", 1, "rows")
    other_pos = swap(positions, "head", 1, "positions")
    seq_pos = jnp.where(
        my_head == 0, jnp.stack([positions, other_pos]), jnp.stack([other_pos, positions])
    )[:, :, None]

    chosen = jnp.take(hash_table, token_ids)
    relative = chosen ^ my_expert
    one_hot = relative[:, None] == jnp.arange(expert_count, dtype=jnp.int32)[None, :]
    rank_table = jnp.cumsum(one_hot.astype(jnp.int32), axis=0) - 1
    slot_index = relative * capacity + jnp.sum(jnp.where(one_hot, rank_table, 0), axis=1)
    slot_row, slot_col = slot_index[None, :], slot_index[:, None]
    absolute = slot_index + (chosen - relative) * capacity
    order = [my_expert ^ k for k in range(expert_count)]

    def exchange(blocks, name, first=0):
        return [
            swap(block, "expert", k, f"{name}{k}") if k else block
            for k, block in enumerate(blocks, first)
        ]

    def exchange_all(blocks):
        return lax.all_to_all(blocks, "expert", split_axis=0, concat_axis=0, tiled=True)

    sent = sent_rows(output_cotangent, absolute[None, :], expert_count)
    grad_blocks = exchange_all(sent)

    done = project(
        own_at, block_input, first_gain, project_weight, [], after=[sent, other_pos]
    )
    first_low, projected = project(other_at, other_input, first_gain, project_weight, done)
    other_weight = swap(touch([output_weight], [done[0]])[0], "head", 1, "output_weight")
    *done, other_context = attend(other_at, projected, seq_pos, [])
    got_context = swap(other_context, "head", 1, "context")
    p_diag, p_cross, inverse, own_context = attend(
        own_at,
        projected,
        seq_pos,
        done,
        after=[other_weight],
        flops=ATTEND_FLOPS,
    )
    hidden, *outgoing = hidden_rows(
        block_input,
        own_context,
        got_context,
        output_weight,
        other_weight,
        second_gain,
        slot_row,
        expert_count,
    )

    row_blocks = exchange(outgoing, "dispatch")
    done, returned, at = [], [], 0
    while at < expert_count:
        size = max(at, 1)
        parts = expert(
            at, row_blocks[at : at + size], grad_blocks, order[at : at + size], inner_weight,
            outer_weight, done,
        )
        done, grads = parts[:3], parts[3:]
        returned += exchange(grads, "return", at)
        at += size
    activated, pre_grad, produced = done

    core = lax.axis_index("core")
    turns = bits_of("x") + bits_of("head")
    outer_steps, inner_steps = turns, turns[::-1]
    outer_sent = weight_part(True, 1 - core, grad_blocks, order, activated, after=grads)
    outer_got = swap(outer_sent, "core", 1, "outer_core")
    inner_sent = weight_part(False, 1 - core, row_blocks, order, pre_grad, after=[outer_sent])
    inner_got = swap(inner_sent, "core", 1, "inner_core")
    outer_kept = weight_part(True, core, grad_blocks, order, activated, after=[inner_sent])
    inner_kept = weight_part(False, core, row_blocks, order, pre_grad, after=[outer_kept])

    hidden_grad, hidden_low, second_gain_part, own_grad, grad_sent = second_back(
        output_cotangent,
        hidden,
        second_gain,
        slot_col,
        output_weight,
        other_weight,
        returned,
        after=[inner_kept],
    )
    other_grad = swap(grad_sent, "head", 1, "context_grad")
    def pairs_of(outer, inner, i):
        return [
            (outer[1], swap(outer[0], *outer_steps[i], f"outer{i}")),
            (inner[1], swap(inner[0], *inner_steps[i], f"inner{i}")),
        ]

    outer_parts = split_sum(
        outer_kept, outer_got, 1 - side(*outer_steps[0]), True, after=[grad_sent]
    )
    inner_parts = split_sum(
        inner_kept, inner_got, 1 - side(*inner_steps[0]), False, after=[outer_parts[0]]
    )

    combined = exchange_all(produced)
    own_output, output_kept, output_sent = output_weight_parts(
        core, own_context, got_context, hidden_low, after=[grad_sent]
    )
    (output_sent,) = add(output_kept, swap(output_sent, "core", 1, "output_core"), [0 * core])
    output_sent, outer_sent, inner_sent = touch(
        [output_sent, outer_parts[0], inner_parts[0]], [other_grad]
    )
    got_output = swap(output_sent, "head", 1, "output_grad")
    outer_parts, inner_parts = [outer_sent, outer_parts[1]], [inner_sent, inner_parts[1]]

    groups = local_cols // PAIR
    end = 2 * local_cols
    grain = 16 * expert_count * lax.axis_size("x")
    lines = -(-(end + 16) // grain) * grain
    sent, kept, mine, theirs = attend_back(
        jnp.stack([my_head, core]).astype(jnp.int32), own_grad, other_grad, projected, p_diag,
        p_cross, own_context, other_context, inverse, first_low, project_weight, first_gain,
        second_gain_part, own_output, lines, after=[inner_parts[0]],
    )
    theirs = swap(theirs, "head", 1, "theirs")

    at = 3 * local_cols // 2
    for i in range(len(turns) - 1):
        outer_parts, inner_parts = adds(
            pairs_of(outer_parts, inner_parts, i),
            [halves(outer_steps[i + 1]), halves(inner_steps[i + 1])],
            after=[kept],
        )
    more = touch([got_output], [*outer_parts, combined], flops=BACK_FLOPS)
    got = swap(sent, "core", 1, "weight")
    (summed,) = add(kept, got, [0 * core], more=more, more_at=at)
    crowd = ("x", "expert")
    summed = summed.reshape(-1, lines // lax.axis_size(crowd), model_width)
    arrived = lax.all_to_all(summed, crowd, split_axis=0, concat_axis=0, tiled=True)
    block_output = output_rows(hidden, absolute[:, None], combined, after=[summed])
    input_grad = first_back(
        block_input, first_gain, hidden_grad, mine, theirs, after=[block_output]
    )
    (outer_own,), (inner_own,) = adds(
        pairs_of(outer_parts, inner_parts, -1), [[0 * core]] * 2, after=[input_grad]
    )
    outer_pieces = gather_pieces(outer_own, outer_steps, outer_steps[::-1])
    inner_pieces = gather_pieces(inner_own, inner_steps, inner_steps[::-1])
    summed = lax.all_to_all(
        total(arrived, after=[outer_own, inner_own]), crowd, split_axis=0, concat_axis=0, tiled=True
    )

    def whole_sum(pieces, is_outer, shape, which, earlier, after):
        half = 1 << (len(turns) - 1)

        def placed(place):
            if is_outer:
                return which * 2 * half + place, 0 * place
            return place % half, which * 2 + place // half

        return assemble(
            [piece for _, piece in pieces],
            [placed(at) for at, _ in pieces],
            shape,
            earlier,
            after=after,
        )

    outer_total = whole_sum(outer_pieces, True, outer_weight.shape, core, [], [])
    inner_total = whole_sum(inner_pieces, False, inner_weight.shape, core, [], outer_total)
    kept = summed.reshape(lines, model_width)
    got = swap(kept, "core", 1, "weight_back")
    outer_pieces, inner_pieces = [
        [(at, swap(piece, "core", 1, "piece_core")) for at, piece in pieces]
        for pieces in (outer_pieces, inner_pieces)
    ]
    (outer_total,) = whole_sum(
        outer_pieces, True, outer_weight.shape, 1 - core, outer_total, inner_total
    )
    (inner_total,) = whole_sum(
        inner_pieces, False, inner_weight.shape, 1 - core, inner_total, [outer_total]
    )
    low, high = jnp.where(core == 0, kept, got), jnp.where(core == 0, got, kept)

    project_grad = project_grads(low, high, local_cols)
    output_weight_grad = jnp.concatenate([low[at:end], high[at:end]]).astype(F32)
    gains = jnp.stack([x[end : end + 2].astype(F32).sum(axis=0) for x in (low, high)])
    gains = gains + swap(gains, "head", 1, "gains")
    return (
        block_output,
        input_grad,
        gains[0],
        gains[1],
        project_grad,
        output_weight_grad,
        inner_total[None],
        outer_total[None],
    )


def solution(mesh):
    devices = mesh.devices
    mesh = Mesh(
        devices.reshape(devices.shape[0] // 2, 2, *devices.shape[1:]), ("x", "core", "expert", "head")
    )
    in_specs = (
        P(("x", "core", "expert", "head"), None),
        P(("x", "core", "expert", "head"), None),
        P(("x", "core", "expert", "head")),
        P(("x", "core", "expert", "head")),
        P(),
        P(),
        P(),
        P(None, None, "head"),
        P("head", None),
        P("expert", None, None),
        P("expert", None, None),
    )
    out_specs = (
        P(("x", "core", "expert", "head"), None),
        P(("x", "core", "expert", "head"), None),
        P(),
        P(),
        P(None, None, "head"),
        P("head", None),
        P("expert", None, None),
        P("expert", None, None),
    )
    return jax.shard_map(
        on_device, mesh=mesh, in_specs=in_specs, out_specs=out_specs, check_vma=False
    )
```

profile of v0, /device:TPU:0, one launch (start us, length us, event | category | flops | bytes accessed | tf_op | source)
XLA Modules:
  0.0 366.6 jit_solution(8228667983761758412)
XLA Ops:
  16.7 4.9 %project.2 = (bf16[2,512,768]{2,1,0:T(8,128)(2,1)}, bf16[3,2,512,384]{3,2,1,0:T(8,128)(2,1)}) custom-call(s32[1]{0:T(128)} %bitcast.refs_0_, bf16[512,768]{1,0:T(8,128)(2,1)} %refs_0_.8, f32[1,768]{1,0:T(1,128)} %reshape.155.refs_2_.refs_13_.refs_1_, bf16[3,768,384]{2,1,0:T(8,128)(2,1)} %refs_12_.1, bf16[4,256,768]{2,1,0:T(8,128)(2,1)} %sent_rows.1.refs_4_, ...), custom_call_target="tpu_custom_call" | custom-call | flops 1 | bytes 1 | tf_op jit(solution)/shard_map/project/pallas_call | solution.py:82
  23.7 5.4 %all-to-all-start = ((bf16[4,256,768]{2,1,0:T(8,128)(2,1)}), bf16[4,256,768]{2,1,0:T(8,128)(2,1)}, u32[]{:S(2)}, u32[]{:S(2)}) async-start(bf16[4,256,768]{2,1,0:T(8,128)(2,1)} %sent_rows.1.refs_4_), calls=%async_computation | async-start | bytes 3145728 | tf_op jit(solution)/shard_map/all_to_all | solution.py:925
  31.5 4.9 %project.3 = (bf16[2,512,768]{2,1,0:T(8,128)(2,1)}, bf16[3,2,512,384]{3,2,1,0:T(8,128)(2,1)}) custom-call(s32[1]{0:T(128)S(6)} %sub.69.refs_0_, bf16[512,768]{1,0:T(8,128)(2,1)} %collective-permute-done.refs_1_, f32[1,768]{1,0:T(1,128)} %reshape.155.refs_2_.refs_13_.refs_1_, ...), custom_call_target="tpu_custom_call", output_to_operand_aliasing={{0}: (4, {}), {1}: (5, {})} | custom-call | flops 1 | bytes 1 | tf_op jit(solution)/shard_map/project/pallas_call | solution.py:82
  36.4 9.5 %attend.2 = (bf16[2,6,512,512]{3,2,1,0:T(8,128)(2,1)}, bf16[2,6,512,512]{3,2,1,0:T(8,128)(2,1)}, f32[2,512,384]{2,1,0:T(8,128)}, bf16[512,384]{1,0:T(8,128)(2,1)}) custom-call(s32[1]{0:T(128)S(6)} %sub.69.refs_0_, bf16[3,2,512,384]{3,2,1,0:T(8,128)(2,1)} %get-tuple-element.65.refs_1_.refs_2_.refs_3_.refs_4_.refs_5_, ...), custom_call_target="tpu_custom_call" | custom-call | flops 1 | bytes 1 | tf_op jit(solution)/shard_map/attend/pallas_call | solution.py:82
  46.0 7.0 %attend.3 = (bf16[2,6,512,512]{3,2,1,0:T(8,128)(2,1)}, bf16[2,6,512,512]{3,2,1,0:T(8,128)(2,1)}, f32[2,512,384]{2,1,0:T(8,128)}, bf16[512,384]{1,0:T(8,128)(2,1)}) custom-call(s32[1]{0:T(128)} %bitcast.refs_0_, ...), custom_call_target="tpu_custom_call", output_to_operand_aliasing={{0}: (7, {}), {1}: (8, {}), {2}: (9, {})} | custom-call | flops 20000000000 | bytes 1 | tf_op jit(solution)/shard_map/attend/pallas_call | solution.py:82
  56.0 5.2 %hidden_rows.1 = (f32[512,768]{1,0:T(8,128)}, bf16[256,768]{1,0:T(8,128)(2,1)}, bf16[256,768]{1,0:T(8,128)(2,1)}, bf16[256,768]{1,0:T(8,128)(2,1)}, bf16[256,768]{1,0:T(8,128)(2,1)}) custom-call(bf16[512,768]{1,0:T(8,128)(2,1)} %refs_0_.8, bf16[512,384]{1,0:T(8,128)(2,1)} %get-tuple-element.69.refs_1_.refs_8_, ...), custom_call_target="tpu_custom_call" | custom-call | flops 1 | bytes 1 | tf_op jit(solution)/shard_map/hidden_rows/pallas_call | solution.py:82
  66.4 9.7 %expert.3 = (bf16[1024,3072]{1,0:T(8,128)(2,1)}, bf16[1024,3072]{1,0:T(8,128)(2,1)}, bf16[4,256,768]{2,1,0:T(8,128)(2,1)}, bf16[256,768]{1,0:T(8,128)(2,1)}) custom-call(s32[1]{0:T(128)} %bitcast.13.refs_0_, bf16[256,768]{1,0:T(8,128)(2,1)} %get-tuple-element.75.refs_1_.refs_3_, bf16[4,256,768]{2,1,0:T(8,128)(2,1)} %all-to-all-done.refs_2_.refs_3_.refs_4_, ...), custom_call_target="tpu_custom_call" | custom-call | flops 1 | bytes 1 | tf_op jit(solution)/shard_map/expert/pallas_call | solution.py:82
  76.1 7.0 %collective-permute-done.6.refs_1_.refs_4_ = bf16[256,768]{1,0:T(8,128)(2,1)} collective-permute-done((bf16[256,768]{1,0:T(8,128)(2,1)}, bf16[256,768]{1,0:T(8,128)(2,1)}, u32[]{:S(2)}, u32[]{:S(2)}) %collective-permute-start.6) | collective-permute-done | bytes 393248 | tf_op jit(solution)/shard_map/dispatch1/ppermute | solution.py:19
  83.1 9.9 %expert.4 = (bf16[1024,3072]{1,0:T(8,128)(2,1)}, bf16[1024,3072]{1,0:T(8,128)(2,1)}, bf16[4,256,768]{2,1,0:T(8,128)(2,1)}, bf16[256,768]{1,0:T(8,128)(2,1)}) custom-call(s32[1]{0:T(128)} %bitcast.12.refs_0_, bf16[256,768]{1,0:T(8,128)(2,1)} %collective-permute-done.6.refs_1_.refs_4_, ...), custom_call_target="tpu_custom_call", output_to_operand_aliasing={{0}: (5, {}), {1}: (6, {}), {2}: (7, {})} | custom-call | flops 1 | bytes 1 | tf_op jit(solution)/shard_map/expert/pallas_call | solution.py:82
  93.1 16.3 %expert.5 = (bf16[1024,3072]{1,0:T(8,128)(2,1)}, bf16[1024,3072]{1,0:T(8,128)(2,1)}, bf16[4,256,768]{2,1,0:T(8,128)(2,1)}, bf16[256,768]{1,0:T(8,128)(2,1)}, bf16[256,768]{1,0:T(8,128)(2,1)}) custom-call(s32[2]{0:T(128)} %pad_add_fusion.12.refs_0_, ...), custom_call_target="tpu_custom_call", output_to_operand_aliasing={{0}: (7, {}), {1}: (8, {}), {2}: (9, {})} | custom-call | flops 1 | bytes 1 | tf_op jit(solution)/shard_map/expert/pallas_call | solution.py:82
  109.4 6.5 %collective-permute-start.8 = (bf16[256,768]{1,0:T(8,128)(2,1)}, bf16[256,768]{1,0:T(8,128)(2,1)}, u32[]{:S(2)}, u32[]{:S(2)}) collective-permute-start(bf16[256,768]{1,0:T(8,128)(2,1)} %get-tuple-element.85.refs_4_), channel_id=1, source_target_pairs={{0,4},{2,6},{4,0},{6,2},{1,5},{3,7},{5,1},{7,3},{8,12},{10,14},{12... | collective-permute-start | bytes 1179656 | tf_op jit(solution)/shard_map/return2/ppermute | solution.py:19
  120.4 7.2 %weight_part.4.refs_7_ = bf16[1536,768]{1,0:T(8,128)(2,1)} custom-call(s32[1]{0:T(128)} %bitcast.16.refs_0_, s32[4]{0:T(128)} %pad_add_fusion.14.refs_1_, bf16[1024,3072]{1,0:T(8,128)(2,1)} %get-tuple-element.88.refs_2_, bf16[4,256,768]{2,1,0:T(8,128)(2,1)} %all-to-all-done.refs_2_.refs_3_.refs_4_, bf16[256,768]{1,0:T(8,128)(2,1)} %get-tuple-element.85.refs_4_, ...), custom_call_target="tpu_custom_call" | custom-call | flops 1 | bytes 1 | tf_op jit(solution)/shard_map/weight_part/pallas_call | solution.py:82
  127.7 7.8 %weight_part.5.refs_4_ = bf16[768,1536]{1,0:T(8,128)(2,1)} custom-call(s32[1]{0:T(128)} %bitcast.16.refs_0_, s32[4]{0:T(128)} %pad_add_fusion.14.refs_1_, bf16[1024,3072]{1,0:T(8,128)(2,1)} %get-tuple-element.87.refs_2_, bf16[256,768]{1,0:T(8,128)(2,1)} %get-tuple-element.75.refs_1_.refs_3_, bf16[256,768]{1,0:T(8,128)(2,1)} %collective-permute-done.6.refs_1_.refs_4_, ...), custom_call_target="tpu_custom_call" | custom-call | flops 1 | bytes 1 | tf_op jit(solution)/shard_map/weight_part/pallas_call | solution.py:82
  136.0 7.3 %weight_part.6.refs_7_.refs_1_ = bf16[1536,768]{1,0:T(8,128)(2,1)} custom-call(s32[1]{0:T(128)} %bitcast.14.refs_0_, s32[4]{0:T(128)} %pad_add_fusion.14.refs_1_, bf16[1024,3072]{1,0:T(8,128)(2,1)} %get-tuple-element.88.refs_2_, bf16[4,256,768]{2,1,0:T(8,128)(2,1)} %all-to-all-done.refs_2_.refs_3_.refs_4_, bf16[768,1536]{1,0:T(8,128)(2,1)} %weight_part.5.refs_4_), custom_call_target="tpu_custom_call" | custom-call | flops 1 | bytes 1 | tf_op jit(solution)/shard_map/weight_part/pallas_call | solution.py:82
  147.8 7.8 %weight_part.7.refs_10_.refs_1_ = bf16[768,1536]{1,0:T(8,128)(2,1)} custom-call(s32[1]{0:T(128)} %bitcast.14.refs_0_, s32[4]{0:T(128)} %pad_add_fusion.14.refs_1_, bf16[1024,3072]{1,0:T(8,128)(2,1)} %get-tuple-element.87.refs_2_, bf16[256,768]{1,0:T(8,128)(2,1)} %get-tuple-element.75.refs_1_.refs_3_, ...), custom_call_target="tpu_custom_call" | custom-call | flops 1 | bytes 1 | tf_op jit(solution)/shard_map/weight_part/pallas_call | solution.py:82
  155.6 6.5 %second_back.1 = (f32[512,768]{1,0:T(8,128)}, bf16[512,768]{1,0:T(8,128)(2,1)}, f32[1,768]{1,0:T(1,128)}, bf16[512,384]{1,0:T(8,128)(2,1)}, bf16[512,384]{1,0:T(8,128)(2,1)}) custom-call(bf16[512,768]{1,0:T(8,128)(2,1)} %refs_0_.7, f32[512,768]{1,0:T(8,128)} %get-tuple-element.71.refs_1_.refs_0_, f32[1,768]{1,0:T(1,128)} %reshape.157.refs_5_.refs_2_, ...), custom_call_target="tpu_custom_call" | custom-call | flops 299999985664 | bytes 1 | tf_op jit(solution)/shard_map/second_back/pallas_call | solution.py:82
  170.1 5.0 %split_sum.2 = (bf16[768,768]{1,0:T(8,128)(2,1)}, bf16[768,768]{1,0:T(8,128)(2,1)}) custom-call(s32[1]{0:T(128)} %bitcast.17.refs_0_, bf16[1536,768]{1,0:T(8,128)(2,1)} %weight_part.6.refs_7_.refs_1_, bf16[1536,768]{1,0:T(8,128)(2,1)} %collective-permute-done.12.refs_2_, bf16[512,384]{1,0:T(8,128)(2,1)} %get-tuple-element.90.refs_4_.refs_3_), custom_call_target="tpu_custom_call" | custom-call | flops 1 | bytes 1 | tf_op jit(solution)/shard_map/split_sum/pallas_call | solution.py:82
  175.1 5.1 %split_sum.3 = (bf16[768,768]{1,0:T(8,128)(2,1)}, bf16[768,768]{1,0:T(8,128)(2,1)}) custom-call(s32[1]{0:T(128)} %bitcast.18.refs_0_, bf16[768,1536]{1,0:T(8,128)(2,1)} %weight_part.7.refs_10_.refs_1_, bf16[768,1536]{1,0:T(8,128)(2,1)} %collective-permute-done.13.refs_2_, bf16[768,768]{1,0:T(8,128)(2,1)} %get-tuple-element.100.refs_3_.refs_1_), custom_call_target="tpu_custom_call" | custom-call | flops 1 | bytes 1 | tf_op jit(solution)/shard_map/split_sum/pallas_call | solution.py:82
  185.0 23.4 %attend_back.1 = (bf16[896,768]{1,0:T(8,128)(2,1)}, bf16[896,768]{1,0:T(8,128)(2,1)}, f32[512,768]{1,0:T(8,128)}, bf16[512,768]{1,0:T(8,128)(2,1)}) custom-call(s32[2]{0:T(128)} %pad_add_fusion.13.refs_0_, bf16[512,384]{1,0:T(8,128)(2,1)} %get-tuple-element.89.refs_1_, bf16[512,384]{1,0:T(8,128)(2,1)} %collective-permute-done.10.refs_3_.refs_2_, ...), custom_call_target="tpu_custom_call" | custom-call | flops 1 | bytes 1 | tf_op jit(solution)/shard_map/attend_back/pallas_call | solution.py:82
  210.9 4.9 %adds.2 = (bf16[384,768]{1,0:T(8,128)(2,1)}, bf16[384,768]{1,0:T(8,128)(2,1)}, bf16[384,768]{1,0:T(8,128)(2,1)}, bf16[384,768]{1,0:T(8,128)(2,1)}) custom-call(s32[4]{0:T(128)} %pad_add_fusion.15.refs_0_, bf16[768,768]{1,0:T(8,128)(2,1)} %get-tuple-element.106.refs_1_, bf16[768,768]{1,0:T(8,128)(2,1)} %collective-permute-done.16.refs_2_, ...), custom_call_target="tpu_custom_call" | custom-call | flops 1 | bytes 1 | tf_op jit(solution)/shard_map/adds/pallas_call | solution.py:82
  219.7 5.2 %all-to-all-start.2 = ((bf16[8,112,768]{2,1,0:T(8,128)(2,1)}), bf16[8,112,768]{2,1,0:T(8,128)(2,1)}, u32[]{:S(2)}, u32[]{:S(2)}) async-start(bf16[8,112,768]{2,1,0:T(8,128)(2,1)} %bitcast.101), calls=%async_computation.2 | async-start | bytes 2752512 | tf_op jit(solution)/shard_map/all_to_all | solution.py:1037
  233.7 12.0 %collective-permute-done.18.refs_4_ = bf16[512,768]{1,0:T(8,128)(2,1)} collective-permute-done((bf16[512,768]{1,0:T(8,128)(2,1)}, bf16[512,768]{1,0:T(8,128)(2,1)}, u32[]{:S(2)}, u32[]{:S(2)}) %collective-permute-start.18) | collective-permute-done | bytes 786464 | tf_op jit(solution)/shard_map/theirs/ppermute | solution.py:19
  250.3 5.8 %collective-permute-done.19.refs_2_ = bf16[384,768]{1,0:T(8,128)(2,1)} collective-permute-done((bf16[384,768]{1,0:T(8,128)(2,1)}, bf16[384,768]{1,0:T(8,128)(2,1)}, u32[]{:S(2)}, u32[]{:S(2)}) %collective-permute-start.19) | collective-permute-done | bytes 589856 | tf_op jit(solution)/shard_map/outer-1/ppermute | solution.py:19
  262.6 5.8 %all-to-all-start.3 = ((bf16[8,112,768]{2,1,0:T(8,128)(2,1)}), bf16[8,112,768]{2,1,0:T(8,128)(2,1)}, u32[]{:S(2)}, u32[]{:S(2)}) async-start(bf16[8,112,768]{2,1,0:T(8,128)(2,1)} %total.1), calls=%async_computation.3 | async-start | bytes 2752512 | tf_op jit(solution)/shard_map/all_to_all | solution.py:1047
  272.6 12.2 %collective-permute-done.30.refs_2_ = bf16[384,768]{1,0:T(8,128)(2,1)S(1)} collective-permute-done((bf16[384,768]{1,0:T(8,128)(2,1)S(1)}, bf16[384,768]{1,0:T(8,128)(2,1)S(1)}, u32[]{:S(2)}, u32[]{:S(2)}) %collective-permute-start.30) | collective-permute-done | bytes 589856 | tf_op jit(solution)/shard_map/piece/ppermute | solution.py:19
  286.8 10.2 %collective-permute-done.31.refs_3_ = bf16[384,768]{1,0:T(8,128)(2,1)S(1)} collective-permute-done((bf16[384,768]{1,0:T(8,128)(2,1)S(1)}, bf16[384,768]{1,0:T(8,128)(2,1)S(1)}, u32[]{:S(2)}, u32[]{:S(2)}) %collective-permute-start.31) | collective-permute-done | bytes 589856 | tf_op jit(solution)/shard_map/piece/ppermute | solution.py:19
  300.0 11.5 %collective-permute-done.24.refs_2_ = bf16[384,768]{1,0:T(8,128)(2,1)} collective-permute-done((bf16[384,768]{1,0:T(8,128)(2,1)}, bf16[384,768]{1,0:T(8,128)(2,1)}, u32[]{:S(2)}, u32[]{:S(2)}) %collective-permute-start.24) | collective-permute-done | bytes 589856 | tf_op jit(solution)/shard_map/piece/ppermute | solution.py:19
  312.7 8.5 %collective-permute-done.32.refs_4_ = bf16[384,768]{1,0:T(8,128)(2,1)S(1)} collective-permute-done((bf16[384,768]{1,0:T(8,128)(2,1)S(1)}, bf16[384,768]{1,0:T(8,128)(2,1)S(1)}, u32[]{:S(2)}, u32[]{:S(2)}) %collective-permute-start.32) | collective-permute-done | bytes 589856 | tf_op jit(solution)/shard_map/piece/ppermute | solution.py:19
  333.4 4.9 %assemble.4.refs_5_ = f32[3072,768]{1,0:T(8,128)} custom-call(s32[4,2]{1,0:T(4,128)} %pad_add_fusion.2.refs_0_, bf16[384,768]{1,0:T(8,128)(2,1)} %get-tuple-element.116.refs_1_, bf16[384,768]{1,0:T(8,128)(2,1)} %copy-done.3, bf16[384,768]{1,0:T(8,128)(2,1)} %copy-done.4, bf16[384,768]{1,0:T(8,128)(2,1)} %copy-done.5), custom_call_target="tpu_custom_call" | custom-call | flops 1 | bytes 1 | tf_op jit(solution)/shard_map/assemble/pallas_call | solution.py:82
  339.6 4.9 %assemble.5.refs_6_.refs_5_ = f32[768,3072]{1,0:T(8,128)} custom-call(s32[4,2]{1,0:T(4,128)} %pad_add_fusion.1.refs_0_, bf16[384,768]{1,0:T(8,128)(2,1)} %get-tuple-element.117.refs_2_.refs_1_, bf16[384,768]{1,0:T(8,128)(2,1)} %collective-permute-done.24.refs_2_, bf16[384,768]{1,0:T(8,128)(2,1)} %collective-permute-done.26.refs_3_, ...), custom_call_target="tpu_custom_call" | custom-call | flops 1 | bytes 1 | tf_op jit(solution)/shard_map/assemble/pallas_call | solution.py:82
  344.5 4.9 %assemble.6.refs_6_ = f32[3072,768]{1,0:T(8,128)} custom-call(s32[4,2]{1,0:T(4,128)} %pad_add_fusion.3.refs_0_, bf16[384,768]{1,0:T(8,128)(2,1)} %copy-done.6, bf16[384,768]{1,0:T(8,128)(2,1)} %copy-done.7, bf16[384,768]{1,0:T(8,128)(2,1)} %copy-done.8, bf16[384,768]{1,0:T(8,128)(2,1)} %collective-permute-done.36.refs_4_, ...), custom_call_target="tpu_custom_call", output_to_operand_aliasing={{}: (5, {})} | custom-call | flops 1 | bytes 1 | tf_op jit(solution)/shard_map/assemble/pallas_call | solution.py:82
  349.4 4.9 %assemble.7 = f32[768,3072]{1,0:T(8,128)} custom-call(s32[4,2]{1,0:T(4,128)} %pad_add_fusion.refs_0_, bf16[384,768]{1,0:T(8,128)(2,1)} %collective-permute-done.23.refs_1_, bf16[384,768]{1,0:T(8,128)(2,1)} %collective-permute-done.25.refs_2_, bf16[384,768]{1,0:T(8,128)(2,1)} %collective-permute-done.27.refs_3_, ...), custom_call_target="tpu_custom_call", output_to_operand_aliasing={{}: (5, {})} | custom-call | flops 1 | bytes 1 | tf_op jit(solution)/shard_map/assemble/pallas_call | solution.py:82
  (159 shorter events, 113.4 us)
Async XLA Ops:
  3.7 27.8 %collective-permute-start = (bf16[512,768]{1,0:T(8,128)(2,1)}, bf16[512,768]{1,0:T(8,128)(2,1)}, u32[]{:S(2)}, u32[]{:S(2)}) collective-permute-start(bf16[512,768]{1,0:T(8,128)(2,1)} %refs_0_.8), channel_id=1, source_target_pairs={{0,1},{1,0},{2,3},{3,2},{4,5},{5,4},{6,7},{7,6},{8,9},{9,8},{10,11... | collective-permute-start | bytes 2359304 | tf_op jit(solution)/shard_map/rows/ppermute | solution.py:19
  21.7 24.3 %collective-permute-start.2 = (bf16[384,768]{1,0:T(8,128)(2,1)}, bf16[384,768]{1,0:T(8,128)(2,1)}, u32[]{:S(2)}, u32[]{:S(2)}) collective-permute-start(bf16[384,768]{1,0:T(8,128)(2,1)} %touch.3), channel_id=1, source_target_pairs={{0,1},{1,0},{2,3},{3,2},{4,5},{5,4},{6,7},{7,6},{8,9},{9,8},{10,11... | collective-permute-start | bytes 1769480 | tf_op jit(solution)/shard_map/output_weight/ppermute | solution.py:19
  23.7 42.8 %all-to-all-start = ((bf16[4,256,768]{2,1,0:T(8,128)(2,1)}), bf16[4,256,768]{2,1,0:T(8,128)(2,1)}, u32[]{:S(2)}, u32[]{:S(2)}) async-start(bf16[4,256,768]{2,1,0:T(8,128)(2,1)} %sent_rows.1.refs_4_), calls=%async_computation | async-start | bytes 3145728 | tf_op jit(solution)/shard_map/all_to_all | solution.py:925
  61.3 21.8 %collective-permute-start.6 = (bf16[256,768]{1,0:T(8,128)(2,1)}, bf16[256,768]{1,0:T(8,128)(2,1)}, u32[]{:S(2)}, u32[]{:S(2)}) collective-permute-start(bf16[256,768]{1,0:T(8,128)(2,1)} %get-tuple-element.74), channel_id=1, source_target_pairs={{0,2},{2,0},{4,6},{6,4},{1,3},{3,1},{5,7},{7,5},{8,10},{10,8},{12,... | collective-permute-start | bytes 1179656 | tf_op jit(solution)/shard_map/dispatch1/ppermute | solution.py:19
  63.0 30.1 %collective-permute-start.4 = (bf16[256,768]{1,0:T(8,128)(2,1)}, bf16[256,768]{1,0:T(8,128)(2,1)}, u32[]{:S(2)}, u32[]{:S(2)}) collective-permute-start(bf16[256,768]{1,0:T(8,128)(2,1)} %get-tuple-element.72), channel_id=1, source_target_pairs={{0,4},{2,6},{4,0},{6,2},{1,5},{3,7},{5,1},{7,3},{8,12},{10,14},{12... | collective-permute-start | bytes 1179656 | tf_op jit(solution)/shard_map/dispatch2/ppermute | solution.py:19
  65.4 27.8 %collective-permute-start.5 = (bf16[256,768]{1,0:T(8,128)(2,1)}, bf16[256,768]{1,0:T(8,128)(2,1)}, u32[]{:S(2)}, u32[]{:S(2)}) collective-permute-start(bf16[256,768]{1,0:T(8,128)(2,1)} %get-tuple-element.73), channel_id=1, source_target_pairs={{0,6},{2,4},{4,2},{6,0},{1,7},{3,5},{5,3},{7,1},{8,14},{10,12},{12... | collective-permute-start | bytes 1179656 | tf_op jit(solution)/shard_map/dispatch3/ppermute | solution.py:19
  109.4 46.1 %collective-permute-start.8 = (bf16[256,768]{1,0:T(8,128)(2,1)}, bf16[256,768]{1,0:T(8,128)(2,1)}, u32[]{:S(2)}, u32[]{:S(2)}) collective-permute-start(bf16[256,768]{1,0:T(8,128)(2,1)} %get-tuple-element.85.refs_4_), channel_id=1, source_target_pairs={{0,4},{2,6},{4,0},{6,2},{1,5},{3,7},{5,1},{7,3},{8,12},{10,14},{12... | collective-permute-start | bytes 1179656 | tf_op jit(solution)/shard_map/return2/ppermute | solution.py:19
  115.9 39.7 %collective-permute-start.9 = (bf16[256,768]{1,0:T(8,128)(2,1)}, bf16[256,768]{1,0:T(8,128)(2,1)}, u32[]{:S(2)}, u32[]{:S(2)}) collective-permute-start(bf16[256,768]{1,0:T(8,128)(2,1)} %get-tuple-element.86.refs_5_), channel_id=1, source_target_pairs={{0,6},{2,4},{4,2},{6,0},{1,7},{3,5},{5,3},{7,1},{8,14},{10,12},{12... | collective-permute-start | bytes 1179656 | tf_op jit(solution)/shard_map/return3/ppermute | solution.py:19
  118.3 37.3 %collective-permute-start.7 = (bf16[256,768]{1,0:T(8,128)(2,1)}, bf16[256,768]{1,0:T(8,128)(2,1)}, u32[]{:S(2)}, u32[]{:S(2)}) collective-permute-start(bf16[256,768]{1,0:T(8,128)(2,1)} %get-tuple-element.84), channel_id=1, source_target_pairs={{0,2},{2,0},{4,6},{6,4},{1,3},{3,1},{5,7},{7,5},{8,10},{10,8},{12,... | collective-permute-start | bytes 1179656 | tf_op jit(solution)/shard_map/return1/ppermute | solution.py:19
  127.6 42.4 %collective-permute-start.12 = (bf16[1536,768]{1,0:T(8,128)(2,1)}, bf16[1536,768]{1,0:T(8,128)(2,1)}, u32[]{:S(2)}, u32[]{:S(2)}) collective-permute-start(bf16[1536,768]{1,0:T(8,128)(2,1)} %weight_part.4.refs_7_), channel_id=1, source_target_pairs={{0,8},{8,0},{1,9},{9,1},{2,10},{10,2},{3,11},{11,3},{4,12},{12,4},... | collective-permute-start | bytes 7077896 | tf_op jit(solution)/shard_map/outer_core/ppermute | solution.py:19
  135.5 39.7 %collective-permute-start.13 = (bf16[768,1536]{1,0:T(8,128)(2,1)}, bf16[768,1536]{1,0:T(8,128)(2,1)}, u32[]{:S(2)}, u32[]{:S(2)}) collective-permute-start(bf16[768,1536]{1,0:T(8,128)(2,1)} %weight_part.5.refs_4_), channel_id=1, source_target_pairs={{0,8},{8,0},{1,9},{9,1},{2,10},{10,2},{3,11},{11,3},{4,12},{12,4},... | collective-permute-start | bytes 7077896 | tf_op jit(solution)/shard_map/inner_core/ppermute | solution.py:19
  143.2 72.5 %all-to-all-start.1 = ((bf16[4,256,768]{2,1,0:T(8,128)(2,1)}), bf16[4,256,768]{2,1,0:T(8,128)(2,1)}, u32[]{:S(2)}, u32[]{:S(2)}) async-start(bf16[4,256,768]{2,1,0:T(8,128)(2,1)} %get-tuple-element.82), calls=%async_computation.1 | async-start | bytes 3145728 | tf_op jit(solution)/shard_map/all_to_all | solution.py:925
  162.1 18.1 %collective-permute-start.10 = (bf16[512,384]{1,0:T(8,128)(2,1)}, bf16[512,384]{1,0:T(8,128)(2,1)}, u32[]{:S(2)}, u32[]{:S(2)}) collective-permute-start(bf16[512,384]{1,0:T(8,128)(2,1)} %get-tuple-element.90.refs_4_.refs_3_), channel_id=1, source_target_pairs={{0,1},{1,0},{2,3},{3,2},{4,5},{5,4},{6,7},{7,6},{8,9},{9,8},{10,11... | collective-permute-start | bytes 1179656 | tf_op jit(solution)/shard_map/context_grad/ppermute | solution.py:19
  180.2 28.4 %collective-permute-start.16 = (bf16[768,768]{1,0:T(8,128)(2,1)}, bf16[768,768]{1,0:T(8,128)(2,1)}, u32[]{:S(2)}, u32[]{:S(2)}) collective-permute-start(bf16[768,768]{1,0:T(8,128)(2,1)} %get-tuple-element.107), channel_id=1, source_target_pairs={{0,16},{16,0},{1,17},{17,1},{2,18},{18,2},{3,19},{19,3},{4,20},{20... | collective-permute-start | bytes 3538952 | tf_op jit(solution)/shard_map/outer0/ppermute | solution.py:19
  181.7 29.2 %collective-permute-start.17 = (bf16[768,768]{1,0:T(8,128)(2,1)}, bf16[768,768]{1,0:T(8,128)(2,1)}, u32[]{:S(2)}, u32[]{:S(2)}) collective-permute-start(bf16[768,768]{1,0:T(8,128)(2,1)} %get-tuple-element.102.refs_16_), channel_id=1, source_target_pairs={{0,1},{1,0},{2,3},{3,2},{4,5},{5,4},{6,7},{7,6},{8,9},{9,8},{10,11... | collective-permute-start | bytes 3538952 | tf_op jit(solution)/shard_map/inner0/ppermute | solution.py:19
  182.6 33.5 %collective-permute-start.15 = (bf16[192,768]{1,0:T(8,128)(2,1)}, bf16[192,768]{1,0:T(8,128)(2,1)}, u32[]{:S(2)}, u32[]{:S(2)}) collective-permute-start(bf16[192,768]{1,0:T(8,128)(2,1)} %get-tuple-element.105), channel_id=1, source_target_pairs={{0,1},{1,0},{2,3},{3,2},{4,5},{5,4},{6,7},{7,6},{8,9},{9,8},{10,11... | collective-permute-start | bytes 884744 | tf_op jit(solution)/shard_map/output_grad/ppermute | solution.py:19
  219.7 40.3 %all-to-all-start.2 = ((bf16[8,112,768]{2,1,0:T(8,128)(2,1)}), bf16[8,112,768]{2,1,0:T(8,128)(2,1)}, u32[]{:S(2)}, u32[]{:S(2)}) async-start(bf16[8,112,768]{2,1,0:T(8,128)(2,1)} %bitcast.101), calls=%async_computation.2 | async-start | bytes 2752512 | tf_op jit(solution)/shard_map/all_to_all | solution.py:1037
  224.9 20.8 %collective-permute-start.18 = (bf16[512,768]{1,0:T(8,128)(2,1)}, bf16[512,768]{1,0:T(8,128)(2,1)}, u32[]{:S(2)}, u32[]{:S(2)}) collective-permute-start(bf16[512,768]{1,0:T(8,128)(2,1)} %get-tuple-element.113), channel_id=1, source_target_pairs={{0,1},{1,0},{2,3},{3,2},{4,5},{5,4},{6,7},{7,6},{8,9},{9,8},{10,11... | collective-permute-start | bytes 2359304 | tf_op jit(solution)/shard_map/theirs/ppermute | solution.py:19
  225.8 30.3 %collective-permute-start.19 = (bf16[384,768]{1,0:T(8,128)(2,1)}, bf16[384,768]{1,0:T(8,128)(2,1)}, u32[]{:S(2)}, u32[]{:S(2)}) collective-permute-start(bf16[384,768]{1,0:T(8,128)(2,1)} %get-tuple-element.109.refs_1_), channel_id=1, source_target_pairs={{0,1},{1,0},{2,3},{3,2},{4,5},{5,4},{6,7},{7,6},{8,9},{9,8},{10,11... | collective-permute-start | bytes 1769480 | tf_op jit(solution)/shard_map/outer-1/ppermute | solution.py:19
  227.0 29.1 %collective-permute-start.20 = (bf16[384,768]{1,0:T(8,128)(2,1)}, bf16[384,768]{1,0:T(8,128)(2,1)}, u32[]{:S(2)}, u32[]{:S(2)}) collective-permute-start(bf16[384,768]{1,0:T(8,128)(2,1)} %get-tuple-element.115), channel_id=1, source_target_pairs={{0,16},{16,0},{1,17},{17,1},{2,18},{18,2},{3,19},{19,3},{4,20},{20... | collective-permute-start | bytes 1769480 | tf_op jit(solution)/shard_map/inner-1/ppermute | solution.py:19
  262.6 37.4 %all-to-all-start.3 = ((bf16[8,112,768]{2,1,0:T(8,128)(2,1)}), bf16[8,112,768]{2,1,0:T(8,128)(2,1)}, u32[]{:S(2)}, u32[]{:S(2)}) async-start(bf16[8,112,768]{2,1,0:T(8,128)(2,1)} %total.1), calls=%async_computation.3 | async-start | bytes 2752512 | tf_op jit(solution)/shard_map/all_to_all | solution.py:1047
  268.5 16.3 %collective-permute-start.30 = (bf16[384,768]{1,0:T(8,128)(2,1)S(1)}, bf16[384,768]{1,0:T(8,128)(2,1)S(1)}, u32[]{:S(2)}, u32[]{:S(2)}) collective-permute-start(bf16[384,768]{1,0:T(8,128)(2,1)S(1)} %copy-done.2), channel_id=1, source_target_pairs={{0,1},{1,0},{2,3},{3,2},{4,5},{5,4},{6,7},{7,6},{8,9},{9,8},{10,11... | collective-permute-start | bytes 1769480 | tf_op jit(solution)/shard_map/piece/ppermute | solution.py:19
  269.4 27.6 %collective-permute-start.31 = (bf16[384,768]{1,0:T(8,128)(2,1)S(1)}, bf16[384,768]{1,0:T(8,128)(2,1)S(1)}, u32[]{:S(2)}, u32[]{:S(2)}) collective-permute-start(bf16[384,768]{1,0:T(8,128)(2,1)S(1)} %copy-done.2), channel_id=1, source_target_pairs={{0,16},{16,0},{1,17},{17,1},{2,18},{18,2},{3,19},{19,3},{4,20},{20... | collective-permute-start | bytes 1769480 | tf_op jit(solution)/shard_map/piece/ppermute | solution.py:19
  271.3 40.2 %collective-permute-start.24 = (bf16[384,768]{1,0:T(8,128)(2,1)}, bf16[384,768]{1,0:T(8,128)(2,1)}, u32[]{:S(2)}, u32[]{:S(2)}) collective-permute-start(bf16[384,768]{1,0:T(8,128)(2,1)} %get-tuple-element.117.refs_2_.refs_1_), channel_id=1, source_target_pairs={{0,16},{16,0},{1,17},{17,1},{2,18},{18,2},{3,19},{19,3},{4,20},{20... | collective-permute-start | bytes 1769480 | tf_op jit(solution)/shard_map/piece/ppermute | solution.py:19
  271.4 40.1 %collective-permute-start.26 = (bf16[384,768]{1,0:T(8,128)(2,1)}, bf16[384,768]{1,0:T(8,128)(2,1)}, u32[]{:S(2)}, u32[]{:S(2)}) collective-permute-start(bf16[384,768]{1,0:T(8,128)(2,1)} %get-tuple-element.117.refs_2_.refs_1_), channel_id=1, source_target_pairs={{0,1},{1,0},{2,3},{3,2},{4,5},{5,4},{6,7},{7,6},{8,9},{9,8},{10,11... | collective-permute-start | bytes 1769480 | tf_op jit(solution)/shard_map/piece/ppermute | solution.py:19
  272.6 39.8 %collective-permute-start.33 = (bf16[384,768]{1,0:T(8,128)(2,1)S(1)}, bf16[384,768]{1,0:T(8,128)(2,1)S(1)}, u32[]{:S(2)}, u32[]{:S(2)}) collective-permute-start(bf16[384,768]{1,0:T(8,128)(2,1)S(1)} %copy-done.2), channel_id=1, source_target_pairs={{0,8},{8,0},{1,9},{9,1},{2,10},{10,2},{3,11},{11,3},{4,12},{12,4},... | collective-permute-start | bytes 1769480 | tf_op jit(solution)/shard_map/piece_core/ppermute | solution.py:19
  284.8 36.4 %collective-permute-start.32 = (bf16[384,768]{1,0:T(8,128)(2,1)S(1)}, bf16[384,768]{1,0:T(8,128)(2,1)S(1)}, u32[]{:S(2)}, u32[]{:S(2)}) collective-permute-start(bf16[384,768]{1,0:T(8,128)(2,1)S(1)} %collective-permute-done.30.refs_2_), channel_id=1, source_target_pairs={{0,16},{16,0},{1,17},{17,1},{2,18},{18,2},{3,19},{19,3},{4,20},{20... | collective-permute-start | bytes 1769480 | tf_op jit(solution)/shard_map/piece/ppermute | solution.py:19
  300.0 54.3 %collective-permute-start.21 = (bf16[896,768]{1,0:T(8,128)(2,1)}, bf16[896,768]{1,0:T(8,128)(2,1)}, u32[]{:S(2)}, u32[]{:S(2)}) collective-permute-start(bf16[896,768]{1,0:T(8,128)(2,1)} %bitcast.22), channel_id=1, source_target_pairs={{0,8},{8,0},{1,9},{9,1},{2,10},{10,2},{3,11},{11,3},{4,12},{12,4},... | collective-permute-start | bytes 4128776 | tf_op jit(solution)/shard_map/weight_back/ppermute | solution.py:19
  327.6 21.8 %collective-permute-start.23 = (bf16[384,768]{1,0:T(8,128)(2,1)}, bf16[384,768]{1,0:T(8,128)(2,1)}, u32[]{:S(2)}, u32[]{:S(2)}) collective-permute-start(bf16[384,768]{1,0:T(8,128)(2,1)} %get-tuple-element.117.refs_2_.refs_1_), channel_id=1, source_target_pairs={{0,8},{8,0},{1,9},{9,1},{2,10},{10,2},{3,11},{11,3},{4,12},{12,4},... | collective-permute-start | bytes 1769480 | tf_op jit(solution)/shard_map/piece_core/ppermute | solution.py:19
  327.6 21.8 %collective-permute-start.25 = (bf16[384,768]{1,0:T(8,128)(2,1)}, bf16[384,768]{1,0:T(8,128)(2,1)}, u32[]{:S(2)}, u32[]{:S(2)}) collective-permute-start(bf16[384,768]{1,0:T(8,128)(2,1)} %collective-permute-done.24.refs_2_), channel_id=1, source_target_pairs={{0,8},{8,0},{1,9},{9,1},{2,10},{10,2},{3,11},{11,3},{4,12},{12,4},... | collective-permute-start | bytes 1769480 | tf_op jit(solution)/shard_map/piece_core/ppermute | solution.py:19
  328.2 21.3 %collective-permute-start.27 = (bf16[384,768]{1,0:T(8,128)(2,1)}, bf16[384,768]{1,0:T(8,128)(2,1)}, u32[]{:S(2)}, u32[]{:S(2)}) collective-permute-start(bf16[384,768]{1,0:T(8,128)(2,1)} %collective-permute-done.26.refs_3_), channel_id=1, source_target_pairs={{0,8},{8,0},{1,9},{9,1},{2,10},{10,2},{3,11},{11,3},{4,12},{12,4},... | collective-permute-start | bytes 1769480 | tf_op jit(solution)/shard_map/piece_core/ppermute | solution.py:19
  328.3 21.2 %collective-permute-start.29 = (bf16[384,768]{1,0:T(8,128)(2,1)}, bf16[384,768]{1,0:T(8,128)(2,1)}, u32[]{:S(2)}, u32[]{:S(2)}) collective-permute-start(bf16[384,768]{1,0:T(8,128)(2,1)} %collective-permute-done.28.refs_4_), channel_id=1, source_target_pairs={{0,8},{8,0},{1,9},{9,1},{2,10},{10,2},{3,11},{11,3},{4,12},{12,4},... | collective-permute-start | bytes 1769480 | tf_op jit(solution)/shard_map/piece_core/ppermute | solution.py:19
  (24 other events, 221.2 us)
where the time goes:
time: 372 us; the launch traced here: 367 us
  Pallas kernels  192 us (52%)
  waiting for transfers between devices  82.1 us (22%)
  starting transfers between devices  58 us (16%)
  other arithmetic  18.8 us (5%)
  local copies, waits for them, and re-layouts  14.2 us (4%)
    pallas_call x33, Pallas kernels, call(): pl.pallas_call(body, input_output_aliases={first + i: i for i in range(le...  192 us
    ppermute x37, waiting for transfers between devices, swap(): return lax.ppermute(values, axis, [(i, i ^ bit) for i in range(size)])  78.8 us
    ppermute x37, starting transfers between devices, swap(): return lax.ppermute(values, axis, [(i, i ^ bit) for i in range(size)])  36.9 us
    all_to_all x2, starting transfers between devices, exchange_all(): lax.all_to_all(blocks, 'expert', split_axis=0, concat_axis=0, tiled=True)  9.97 us
    another operation x12, other arithmetic, assemble(): table = jnp.stack([jnp.stack(place) for place in places]).astype(jnp.int32)  8.31 us
  transfers between devices with their start and end apart: 41, of which 16 were waited for; matrix products, arithmetic and copies ran while one was open for 7% of the time, Pallas kernels for 46%

commit v1 on v0

--- a/solution.py
+++ b/solution.py
@@ -35,6 +35,7 @@
 PAIR = 2 * HEAD_DIM
 ATTEND_FLOPS = 20 * 10**9
 BACK_FLOPS = 300 * 10**9
+FIRST_FLOPS = 300 * 10**9
 HIDE = -1000000000.0
 VMEM_LIMIT = 64 * 1024 * 1024
 
@@ -375,7 +376,12 @@
 
 def first_back(x, gain, hidden_grad, own, theirs, after=()):
     return plain(
-        first_kernel, [x, gain, hidden_grad, own, theirs], shaped(x.shape, F32), "first_back", after
+        first_kernel,
+        [x, gain, hidden_grad, own, theirs],
+        shaped(x.shape, F32),
+        "first_back",
+        after,
+        flops=FIRST_FLOPS,
     )
 
 
@@ -487,81 +493,103 @@
     )
 
 
-def weight_kernel(is_outer, count, which_ref, place_ref, wide_ref, *refs):
-    *row_refs, out_ref, rows = refs
-    if is_outer:
-        row_refs = [row_refs[0].at[place_ref[i]] for i in range(count)]
-    pl.when(pl.program_id(0) == 0)(lambda: fill(rows, row_refs))
-    sides = (wide_ref[...], rows[...]) if is_outer else (rows[...], wide_ref[...])
-    out_ref[...] = lax.dot_general(
-        *sides, (((0,), (0,)), ((), ())), preferred_element_type=F32
-    ).astype(BF)
-
-
-def weight_part(is_outer, half, blocks, places, wide, after=(), tiles=4):
-    count, width = blocks[0].shape
-    total, units = wide.shape
+def weight_kernel(count, which_ref, place_ref, act_ref, pre_ref, *refs):
+    x_refs, (cot_ref, outer_out, inner_out, x, cot) = refs[:count], refs[count:]
+    at = pl.program_id(0)
+    half = pl.num_programs(0) // 2
+
+    @pl.when(at == 0)
+    def _():
+        fill(cot, [cot_ref.at[place_ref[i]] for i in range(count)])
+        fill(x, x_refs)
+
+    def put(ref, left, right):
+        ref[...] = lax.dot_general(
+            left, right, (((0,), (0,)), ((), ())), preferred_element_type=F32
+        ).astype(BF)
+
+    pl.when(at < half)(lambda: put(outer_out, act_ref[...], cot[...]))
+    pl.when(at >= half)(lambda: put(inner_out, x[...], pre_ref[...]))
+
+
+def weight_parts(half, x_blocks, cot_blocks, places, act, pre, after=(), tiles=4):
+    count, width = x_blocks[0].shape
+    total, units = act.shape
     tile = units // 2 // tiles
-    if is_outer:
-        row_specs, blocks = [whole(blocks.shape)], [blocks]
-        shape, spec = (units // 2, width), pl.BlockSpec((tile, width), lambda j, w, p: (j, 0))
-    else:
-        row_specs = [whole((count, width))] * len(blocks)
-        shape, spec = (width, units // 2), pl.BlockSpec((width, tile), lambda j, w, p: (0, j))
+
+    def early(j):
+        return jnp.minimum(j, tiles - 1)
+
+    def late(j):
+        return jnp.maximum(j - tiles, 0)
+
     return call(
-        functools.partial(weight_kernel, is_outer, len(places)),
-        [wide, *blocks],
+        functools.partial(weight_kernel, len(x_blocks)),
+        [act, pre, *x_blocks, cot_blocks],
         after=after,
         prefetch=[half.reshape(1).astype(jnp.int32), jnp.stack(places).astype(jnp.int32)],
-        grid=(tiles,),
-        in_specs=[pl.BlockSpec((total, tile), lambda j, w, p: (0, w[0] * tiles + j))] + row_specs,
-        out_specs=spec,
-        out_shape=shaped(shape, BF),
-        scratch_shapes=[pltpu.VMEM((total, width), BF)],
-        name="weight_part",
-    )
-
-
-def split_kernel(place_ref, kept_ref, got_ref, sent_out, kept_out):
-    total = (kept_ref[...].astype(F32) + got_ref[...].astype(F32)).astype(BF)
-    half = pl.num_programs(0) // 2
-
-    @pl.when(pl.program_id(0) < half)
-    def _():
-        sent_out[...] = total
-
-    @pl.when(pl.program_id(0) >= half)
-    def _():
-        kept_out[...] = total
-
-
-def split_sum(kept, got, turn, by_rows, after=(), tiles=4):
-    rows, cols = kept.shape
-    if by_rows:
-        tile, out = (rows // tiles, cols), (rows // 2, cols)
-    else:
-        tile, out = (rows, cols // tiles), (rows, cols // 2)
-
-    def at(j):
-        return (j, 0) if by_rows else (0, j)
-
-    def place(j, w):
-        return at((w[0] * (tiles // 2) + j) % tiles)
-
-    return call(
+        grid=(2 * tiles,),
+        in_specs=[
+            pl.BlockSpec((total, tile), lambda j, w, p: (0, w[0] * tiles + early(j))),
+            pl.BlockSpec((total, tile), lambda j, w, p: (0, w[0] * tiles + late(j))),
+        ]
+        + [whole((count, width))] * len(x_blocks)
+        + [whole(cot_blocks.shape)],
+        out_specs=[
+            pl.BlockSpec((tile, width), lambda j, w, p: (early(j), 0)),
+            pl.BlockSpec((width, tile), lambda j, w, p: (0, late(j))),
+        ],
+        out_shape=[shaped((units // 2, width), BF), shaped((width, units // 2), BF)],
+        scratch_shapes=[pltpu.VMEM((total, width), BF)] * 2,
+        name="weight_parts",
+    )
+
+
+def split_kernel(place_ref, outer_kept, outer_got, inner_kept, inner_got, *out_refs):
+    at = pl.program_id(0)
+    quarter = pl.num_programs(0) // 4
+    for i, out_ref in enumerate(out_refs):
+        kept_ref, got_ref = ((outer_kept, outer_got), (inner_kept, inner_got))[i // 2]
+
+        @pl.when(at // quarter == i)
+        def _(kept_ref=kept_ref, got_ref=got_ref, out_ref=out_ref):
+            out_ref[...] = (kept_ref[...].astype(F32) + got_ref[...].astype(F32)).astype(BF)
+
+
+def split_sums(outer, inner, outer_turn, inner_turn, after=(), tiles=4):
+    rows, cols = outer[0].shape
+    outer_tile, inner_tile = (rows // tiles, cols), (cols, rows // tiles)
+
+    def held(j, i):
+        return jnp.clip(j - i * (tiles // 2), 0, tiles // 2 - 1)
+
+    def source(i):
+        def at(j, w):
+            step = jnp.clip(j - i * tiles, 0, tiles - 1)
+            return (w[i] * (tiles // 2) + step) % tiles
+
+        return at
+
+    outer_at, inner_at = source(0), source(1)
+    outer_in = pl.BlockSpec(outer_tile, lambda j, w: (outer_at(j, w), 0))
+    inner_in = pl.BlockSpec(inner_tile, lambda j, w: (0, inner_at(j, w)))
+    parts = call(
         split_kernel,
-        [kept, got],
-        after=after,
-        prefetch=[turn.reshape(1).astype(jnp.int32)],
-        grid=(tiles,),
-        in_specs=[pl.BlockSpec(tile, place)] * 2,
+        [*outer, *inner],
+        after=after,
+        prefetch=[jnp.stack([outer_turn, inner_turn]).astype(jnp.int32)],
+        grid=(2 * tiles,),
+        in_specs=[outer_in, outer_in, inner_in, inner_in],
         out_specs=[
-            pl.BlockSpec(tile, lambda j, w: at(jnp.minimum(j, tiles // 2 - 1))),
-            pl.BlockSpec(tile, lambda j, w: at(jnp.maximum(j - tiles // 2, 0))),
+            pl.BlockSpec(outer_tile, lambda j, w: (held(j, 0), 0)),
+            pl.BlockSpec(outer_tile, lambda j, w: (held(j, 1), 0)),
+            pl.BlockSpec(inner_tile, lambda j, w: (0, held(j, 2))),
+            pl.BlockSpec(inner_tile, lambda j, w: (0, held(j, 3))),
         ],
-        out_shape=[shaped(out, BF)] * 2,
-        name="split_sum",
-    )
+        out_shape=[shaped((rows // 2, cols), BF)] * 2 + [shaped((cols, rows // 2), BF)] * 2,
+        name="split_sums",
+    )
+    return parts[:2], parts[2:]
 
 
 def assemble_kernel(place_ref, *refs):
@@ -573,12 +601,13 @@
             out_ref[...] = ref[...].astype(F32)
 
 
-def assemble(pieces, places, shape, earlier, after=()):
+def assemble(pieces, places, shape, earlier, after=(), flops=1):
     size = pieces[0].shape
     table = jnp.stack([jnp.stack(place) for place in places]).astype(jnp.int32)
     return call(
         assemble_kernel,
         pieces,
+        flops=flops,
         after=after,
         alias=earlier,
         prefetch=[table],
@@ -655,11 +684,14 @@
 def gather_pieces(own, steps, order):
     weights = {step: 1 << (len(steps) - 1 - i) for i, step in enumerate(steps)}
     place = sum(side(*step) * weight for step, weight in weights.items())
-    pieces = [(place, own)]
+    pieces = [(0, place, own)]
     for step in order:
         change = weights[step] * (1 - 2 * side(*step))
-        pieces += [(at + change, swap(piece, *step, "piece")) for at, piece in pieces]
-    return pieces
+        pieces += [
+            (hops + 1, at + change, swap(piece, *step, "piece")) for hops, at, piece in pieces
+        ]
+    pieces.sort(key=lambda piece: piece[0])
+    return [piece[1:] for piece in pieces]
 
 
 def total_kernel(in_ref, out_ref):
@@ -853,24 +885,45 @@
     )
 
 
-def project_grad_kernel(low_ref, high_ref, out_ref):
-    both = jnp.concatenate([low_ref[...], high_ref[...]], axis=0).astype(F32)
-    flat = jnp.transpose(both)
+def weight_outputs_kernel(core_ref, kept_ref, got_ref, project_ref, output_ref, gains_ref):
+    group, groups = pl.program_id(0), pl.num_programs(0)
+    size = 3 * PAIR // 2
+
+    def halves_of(start, rows):
+        cut = pl.ds(start, rows)
+        kept, got = kept_ref[cut, :].astype(F32), got_ref[cut, :].astype(F32)
+        low = jnp.where(core_ref[0] == 0, kept, got)
+        return low, jnp.where(core_ref[0] == 0, got, kept)
+
+    low, high = halves_of(pl.multiple_of(group * size, size), size)
+    flat = jnp.transpose(jnp.concatenate([low, high], axis=0))
     for c in range(3):
-        out_ref[c] = flat[:, c * PAIR : (c + 1) * PAIR]
-
-
-def project_grads(low, high, cols):
-    width = low.shape[1]
-    part = pl.BlockSpec((3 * PAIR // 2, width), lambda g: (g, 0))
+        project_ref[c] = flat[:, c * PAIR : (c + 1) * PAIR]
+
+    @pl.when(group == groups - 1)
+    def _():
+        part = output_ref.shape[0] // 2
+        output_ref[:part], output_ref[part:] = halves_of(groups * size, part)
+        for i, rows in enumerate(halves_of(groups * size + part, 16)):
+            gains_ref[i : i + 1] = rows[0:1] + rows[1:2]
+
+
+def weight_outputs(core, kept, got, cols, after=()):
+    lines, width = kept.shape
     return call(
-        project_grad_kernel,
-        [low, high],
+        weight_outputs_kernel,
+        [kept, got],
+        after=after,
+        prefetch=[core.reshape(1).astype(jnp.int32)],
         grid=(cols // PAIR,),
-        in_specs=[part, part],
-        out_specs=pl.BlockSpec((3, width, PAIR), lambda g: (0, 0, g)),
-        out_shape=shaped((3, width, cols), F32),
-        name="project_grads",
+        in_specs=[whole((lines, width))] * 2,
+        out_specs=[
+            pl.BlockSpec((3, width, PAIR), lambda g, w: (0, 0, g)),
+            whole((cols, width)),
+            whole((2, width)),
+        ],
+        out_shape=[shaped((3, width, cols), F32), shaped((cols, width), F32), shaped((2, width), F32)],
+        name="weight_outputs",
     )
 
 
@@ -969,12 +1022,14 @@
     core = lax.axis_index("core")
     turns = bits_of("x") + bits_of("head")
     outer_steps, inner_steps = turns, turns[::-1]
-    outer_sent = weight_part(True, 1 - core, grad_blocks, order, activated, after=grads)
+    outer_sent, inner_sent = weight_parts(
+        1 - core, row_blocks, grad_blocks, order, activated, pre_grad, after=grads
+    )
     outer_got = swap(outer_sent, "core", 1, "outer_core")
-    inner_sent = weight_part(False, 1 - core, row_blocks, order, pre_grad, after=[outer_sent])
     inner_got = swap(inner_sent, "core", 1, "inner_core")
-    outer_kept = weight_part(True, core, grad_blocks, order, activated, after=[inner_sent])
-    inner_kept = weight_part(False, core, row_blocks, order, pre_grad, after=[outer_kept])
+    outer_kept, inner_kept = weight_parts(
+        core, row_blocks, grad_blocks, order, activated, pre_grad, after=[inner_sent]
+    )
 
     hidden_grad, hidden_low, second_gain_part, own_grad, grad_sent = second_back(
         output_cotangent,
@@ -993,14 +1048,15 @@
             (inner[1], swap(inner[0], *inner_steps[i], f"inner{i}")),
         ]
 
-    outer_parts = split_sum(
-        outer_kept, outer_got, 1 - side(*outer_steps[0]), True, after=[grad_sent]
-    )
-    inner_parts = split_sum(
-        inner_kept, inner_got, 1 - side(*inner_steps[0]), False, after=[outer_parts[0]]
-    )
-
-    combined = exchange_all(produced)
+    outer_parts, inner_parts = split_sums(
+        (outer_kept, outer_got),
+        (inner_kept, inner_got),
+        1 - side(*outer_steps[0]),
+        1 - side(*inner_steps[0]),
+        after=[grad_sent],
+    )
+
+    combined = exchange_all(touch([produced], [grad_sent])[0])
     own_output, output_kept, output_sent = output_weight_parts(
         core, own_context, got_context, hidden_low, after=[grad_sent]
     )
@@ -1020,8 +1076,6 @@
         p_cross, own_context, other_context, inverse, first_low, project_weight, first_gain,
         second_gain_part, own_output, lines, after=[inner_parts[0]],
     )
-    theirs = swap(theirs, "head", 1, "theirs")
-
     at = 3 * local_cols // 2
     for i in range(len(turns) - 1):
         outer_parts, inner_parts = adds(
@@ -1035,6 +1089,7 @@
     crowd = ("x", "expert")
     summed = summed.reshape(-1, lines // lax.axis_size(crowd), model_width)
     arrived = lax.all_to_all(summed, crowd, split_axis=0, concat_axis=0, tiled=True)
+    theirs = swap(theirs, "head", 1, "theirs")
     block_output = output_rows(hidden, absolute[:, None], combined, after=[summed])
     input_grad = first_back(
         block_input, first_gain, hidden_grad, mine, theirs, after=[block_output]
@@ -1044,46 +1099,60 @@
     )
     outer_pieces = gather_pieces(outer_own, outer_steps, outer_steps[::-1])
     inner_pieces = gather_pieces(inner_own, inner_steps, inner_steps[::-1])
-    summed = lax.all_to_all(
-        total(arrived, after=[outer_own, inner_own]), crowd, split_axis=0, concat_axis=0, tiled=True
-    )
-
-    def whole_sum(pieces, is_outer, shape, which, earlier, after):
+    arrived = total(arrived, after=[outer_own, inner_own])
+    summed = lax.all_to_all(arrived, crowd, split_axis=0, concat_axis=0, tiled=True)
+
+    def whole_sum(own_core, other_core, is_outer, earlier, after):
         half = 1 << (len(turns) - 1)
 
-        def placed(place):
+        def placed(place, which):
             if is_outer:
                 return which * 2 * half + place, 0 * place
             return place % half, which * 2 + place // half
 
+        chosen = [
+            (piece, placed(at, which))
+            for pieces, which in ((own_core, core), (other_core, 1 - core))
+            for at, piece in pieces
+        ]
         return assemble(
-            [piece for _, piece in pieces],
-            [placed(at) for at, _ in pieces],
-            shape,
+            [piece for piece, _ in chosen],
+            [place for _, place in chosen],
+            (outer_weight if is_outer else inner_weight).shape,
             earlier,
             after=after,
+            flops=1,
+        )[0]
+
+    early = len(turns) + 1
+
+    def core_swaps(pieces):
+        return [(at, swap(piece, "core", 1, "piece_core")) for at, piece in pieces]
+
+    others = []
+    for pieces in (outer_pieces, inner_pieces):
+        (held,) = touch([pieces[0][1]], [arrived])
+        others.append(core_swaps([(pieces[0][0], held), *pieces[1:early]]))
+    totals = []
+    for is_outer, own_core, other_core in zip(
+        (True, False), (outer_pieces, inner_pieces), others
+    ):
+        totals.append(
+            whole_sum(own_core[:early], other_core, is_outer, [], [arrived] + totals[-1:])
         )
-
-    outer_total = whole_sum(outer_pieces, True, outer_weight.shape, core, [], [])
-    inner_total = whole_sum(inner_pieces, False, inner_weight.shape, core, [], outer_total)
-    kept = summed.reshape(lines, model_width)
+    late = []
+    for pieces in (outer_pieces, inner_pieces):
+        held = touch([piece for _, piece in pieces[early:]], totals)
+        late.append([(at, piece) for (at, _), piece in zip(pieces[early:], held)])
+    late_others = [core_swaps(pieces) for pieces in late]
+    kept = touch([summed], [pieces[0][1] for pieces in late])[0].reshape(lines, model_width)
     got = swap(kept, "core", 1, "weight_back")
-    outer_pieces, inner_pieces = [
-        [(at, swap(piece, "core", 1, "piece_core")) for at, piece in pieces]
-        for pieces in (outer_pieces, inner_pieces)
-    ]
-    (outer_total,) = whole_sum(
-        outer_pieces, True, outer_weight.shape, 1 - core, outer_total, inner_total
-    )
-    (inner_total,) = whole_sum(
-        inner_pieces, False, inner_weight.shape, 1 - core, inner_total, [outer_total]
-    )
-    low, high = jnp.where(core == 0, kept, got), jnp.where(core == 0, got, kept)
-
-    project_grad = project_grads(low, high, local_cols)
-    output_weight_grad = jnp.concatenate([low[at:end], high[at:end]]).astype(F32)
-    gains = jnp.stack([x[end : end + 2].astype(F32).sum(axis=0) for x in (low, high)])
+    project_grad, output_weight_grad, gains = weight_outputs(
+        core, kept, got, local_cols
+    )
     gains = gains + swap(gains, "head", 1, "gains")
+    outer_total = whole_sum(late[0], late_others[0], True, totals[:1], [project_grad])
+    inner_total = whole_sum(late[1], late_others[1], False, totals[1:], [outer_total])
     return (
         block_output,
         input_grad,

time: 372 us -> 344 us (0.925)
  waiting for transfers between devices: 82.1 us -> 68 us
  other arithmetic: 18.8 us -> 10.3 us
  Pallas kernels: 192 us -> 188 us
    ppermute x37, waiting for transfers between devices: 78.8 us -> 56.8 us  [swap(): return lax.ppermute(values, axis, [(i, i ^ bit) for i in range(size)])]
    all_to_all x1, waiting for transfers between devices: 0.01 us -> 10.9 us  [on_device(): lax.all_to_all(summed, crowd, split_axis=0, concat_axis=0, tiled=True)]
    another operation x12 -> x10, other arithmetic: 8.31 us -> 2.98 us  [assemble(): table = jnp.stack([jnp.stack(place) for place in places]).astype(jnp.int32)]
    pallas_call x33 -> x36, Pallas kernels: 192 us -> 188 us  [call(): pl.pallas_call(body, input_output_aliases={first + i: i for i in range(le...]
  transfers between devices with their start and end apart: 41 -> 41, of which waited for: 16 -> 12; matrix products, arithmetic and copies ran while one was open for 7% -> 7% of each run, Pallas kernels for 46% -> 50%
where the time goes in v1:
time: 344 us; the launch traced here: 340 us
  Pallas kernels  188 us (55%)
  waiting for transfers between devices  68 us (20%)
  starting transfers between devices  55.3 us (16%)
  local copies, waits for them, and re-layouts  16.3 us (5%)
  other arithmetic  10.3 us (3%)
    pallas_call x36, Pallas kernels, call(): pl.pallas_call(body, input_output_aliases={first + i: i for i in range(le...  188 us
    ppermute x37, waiting for transfers between devices, swap(): return lax.ppermute(values, axis, [(i, i ^ bit) for i in range(size)])  56.8 us
    ppermute x37, starting transfers between devices, swap(): return lax.ppermute(values, axis, [(i, i ^ bit) for i in range(size)])  34.7 us
    all_to_all x1, waiting for transfers between devices, on_device(): lax.all_to_all(summed, crowd, split_axis=0, concat_axis=0, tiled=True)  10.9 us
    all_to_all x2, starting transfers between devices, exchange_all(): lax.all_to_all(blocks, 'expert', split_axis=0, concat_axis=0, tiled=True)  9.95 us
  transfers between devices with their start and end apart: 41, of which 12 were waited for; matrix products, arithmetic and copies ran while one was open for 7% of the time, Pallas kernels for 50%

profile of v1, /device:TPU:0, one launch (start us, length us, event | category | flops | bytes accessed | tf_op | source)
XLA Modules:
  0.0 339.5 jit_solution(17569001526380316004)
XLA Ops:
  16.6 4.9 %project.2 = (bf16[2,512,768]{2,1,0:T(8,128)(2,1)}, bf16[3,2,512,384]{3,2,1,0:T(8,128)(2,1)}) custom-call(s32[1]{0:T(128)} %bitcast.refs_0_, bf16[512,768]{1,0:T(8,128)(2,1)} %refs_0_.8, f32[1,768]{1,0:T(1,128)} %reshape.150.refs_2_.refs_13_.refs_1_, bf16[3,768,384]{2,1,0:T(8,128)(2,1)} %refs_12_.1, bf16[4,256,768]{2,1,0:T(8,128)(2,1)} %sent_rows.1.refs_4_, ...), custom_call_target="tpu_custom_call" | custom-call | flops 1 | bytes 1 | tf_op jit(solution)/shard_map/project/pallas_call | solution.py:83
  23.6 5.4 %all-to-all-start = ((bf16[4,256,768]{2,1,0:T(8,128)(2,1)}), bf16[4,256,768]{2,1,0:T(8,128)(2,1)}, u32[]{:S(2)}, u32[]{:S(2)}) async-start(bf16[4,256,768]{2,1,0:T(8,128)(2,1)} %sent_rows.1.refs_4_), calls=%async_computation | async-start | bytes 3145728 | tf_op jit(solution)/shard_map/all_to_all | solution.py:978
  31.4 4.9 %project.3 = (bf16[2,512,768]{2,1,0:T(8,128)(2,1)}, bf16[3,2,512,384]{3,2,1,0:T(8,128)(2,1)}) custom-call(s32[1]{0:T(128)S(6)} %sub.70.refs_0_, bf16[512,768]{1,0:T(8,128)(2,1)} %collective-permute-done.refs_1_, f32[1,768]{1,0:T(1,128)} %reshape.150.refs_2_.refs_13_.refs_1_, ...), custom_call_target="tpu_custom_call", output_to_operand_aliasing={{0}: (4, {}), {1}: (5, {})} | custom-call | flops 1 | bytes 1 | tf_op jit(solution)/shard_map/project/pallas_call | solution.py:83
  36.3 9.5 %attend.2 = (bf16[2,6,512,512]{3,2,1,0:T(8,128)(2,1)}, bf16[2,6,512,512]{3,2,1,0:T(8,128)(2,1)}, f32[2,512,384]{2,1,0:T(8,128)}, bf16[512,384]{1,0:T(8,128)(2,1)}) custom-call(s32[1]{0:T(128)S(6)} %sub.70.refs_0_, bf16[3,2,512,384]{3,2,1,0:T(8,128)(2,1)} %get-tuple-element.72.refs_1_.refs_2_.refs_3_.refs_4_.refs_5_, ...), custom_call_target="tpu_custom_call" | custom-call | flops 1 | bytes 1 | tf_op jit(solution)/shard_map/attend/pallas_call | solution.py:83
  45.9 7.0 %attend.3 = (bf16[2,6,512,512]{3,2,1,0:T(8,128)(2,1)}, bf16[2,6,512,512]{3,2,1,0:T(8,128)(2,1)}, f32[2,512,384]{2,1,0:T(8,128)}, bf16[512,384]{1,0:T(8,128)(2,1)}) custom-call(s32[1]{0:T(128)} %bitcast.refs_0_, ...), custom_call_target="tpu_custom_call", output_to_operand_aliasing={{0}: (7, {}), {1}: (8, {}), {2}: (9, {})} | custom-call | flops 20000000000 | bytes 1 | tf_op jit(solution)/shard_map/attend/pallas_call | solution.py:83
  55.9 5.2 %hidden_rows.1 = (f32[512,768]{1,0:T(8,128)}, bf16[256,768]{1,0:T(8,128)(2,1)}, bf16[256,768]{1,0:T(8,128)(2,1)}, bf16[256,768]{1,0:T(8,128)(2,1)}, bf16[256,768]{1,0:T(8,128)(2,1)}) custom-call(bf16[512,768]{1,0:T(8,128)(2,1)} %refs_0_.8, bf16[512,384]{1,0:T(8,128)(2,1)} %get-tuple-element.76.refs_1_.refs_8_, ...), custom_call_target="tpu_custom_call" | custom-call | flops 1 | bytes 1 | tf_op jit(solution)/shard_map/hidden_rows/pallas_call | solution.py:83
  66.4 9.7 %expert.3 = (bf16[1024,3072]{1,0:T(8,128)(2,1)}, bf16[1024,3072]{1,0:T(8,128)(2,1)}, bf16[4,256,768]{2,1,0:T(8,128)(2,1)}, bf16[256,768]{1,0:T(8,128)(2,1)}) custom-call(s32[1]{0:T(128)} %bitcast.13.refs_0_, bf16[256,768]{1,0:T(8,128)(2,1)} %get-tuple-element.82.refs_1_.refs_4_, bf16[4,256,768]{2,1,0:T(8,128)(2,1)} %all-to-all-done.refs_2_.refs_3_.refs_4_.refs_8_, ...), custom_call_target="tpu_custom_call" | custom-call | flops 1 | bytes 1 | tf_op jit(solution)/shard_map/expert/pallas_call | solution.py:83
  76.1 7.0 %collective-permute-done.6.refs_1_.refs_5_ = bf16[256,768]{1,0:T(8,128)(2,1)} collective-permute-done((bf16[256,768]{1,0:T(8,128)(2,1)}, bf16[256,768]{1,0:T(8,128)(2,1)}, u32[]{:S(2)}, u32[]{:S(2)}) %collective-permute-start.6) | collective-permute-done | bytes 393248 | tf_op jit(solution)/shard_map/dispatch1/ppermute | solution.py:19
  83.1 9.9 %expert.4 = (bf16[1024,3072]{1,0:T(8,128)(2,1)}, bf16[1024,3072]{1,0:T(8,128)(2,1)}, bf16[4,256,768]{2,1,0:T(8,128)(2,1)}, bf16[256,768]{1,0:T(8,128)(2,1)}) custom-call(s32[1]{0:T(128)} %bitcast.12.refs_0_, bf16[256,768]{1,0:T(8,128)(2,1)} %collective-permute-done.6.refs_1_.refs_5_, ...), custom_call_target="tpu_custom_call", output_to_operand_aliasing={{0}: (5, {}), {1}: (6, {}), {2}: (7, {})} | custom-call | flops 1 | bytes 1 | tf_op jit(solution)/shard_map/expert/pallas_call | solution.py:83
  93.0 16.3 %expert.5 = (bf16[1024,3072]{1,0:T(8,128)(2,1)}, bf16[1024,3072]{1,0:T(8,128)(2,1)}, bf16[4,256,768]{2,1,0:T(8,128)(2,1)}, bf16[256,768]{1,0:T(8,128)(2,1)}, bf16[256,768]{1,0:T(8,128)(2,1)}) custom-call(s32[2]{0:T(128)} %pad_add_fusion.10.refs_0_, ...), custom_call_target="tpu_custom_call", output_to_operand_aliasing={{0}: (7, {}), {1}: (8, {}), {2}: (9, {})} | custom-call | flops 1 | bytes 1 | tf_op jit(solution)/shard_map/expert/pallas_call | solution.py:83
  109.3 6.5 %collective-permute-start.8 = (bf16[256,768]{1,0:T(8,128)(2,1)}, bf16[256,768]{1,0:T(8,128)(2,1)}, u32[]{:S(2)}, u32[]{:S(2)}) collective-permute-start(bf16[256,768]{1,0:T(8,128)(2,1)} %get-tuple-element.92.refs_9_), channel_id=1, source_target_pairs={{0,4},{2,6},{4,0},{6,2},{1,5},{3,7},{5,1},{7,3},{8,12},{10,14},{12... | collective-permute-start | bytes 1179656 | tf_op jit(solution)/shard_map/return2/ppermute | solution.py:19
  120.3 13.1 %weight_parts.2 = (bf16[1536,768]{1,0:T(8,128)(2,1)}, bf16[768,1536]{1,0:T(8,128)(2,1)}) custom-call(s32[1]{0:T(128)} %bitcast.16.refs_0_, s32[4]{0:T(128)} %pad_add_fusion.11.refs_1_, bf16[1024,3072]{1,0:T(8,128)(2,1)} %get-tuple-element.94.refs_2_, bf16[1024,3072]{1,0:T(8,128)(2,1)} %get-tuple-element.95.refs_3_, ...), custom_call_target="tpu_custom_call" | custom-call | flops 1 | bytes 1 | tf_op jit(solution)/shard_map/weight_parts/pallas_call | solution.py:83
  133.8 12.9 %weight_parts.3 = (bf16[1536,768]{1,0:T(8,128)(2,1)}, bf16[768,1536]{1,0:T(8,128)(2,1)}) custom-call(s32[1]{0:T(128)} %bitcast.15.refs_0_, s32[4]{0:T(128)} %pad_add_fusion.11.refs_1_, bf16[1024,3072]{1,0:T(8,128)(2,1)} %get-tuple-element.94.refs_2_, bf16[1024,3072]{1,0:T(8,128)(2,1)} %get-tuple-element.95.refs_3_, ...), custom_call_target="tpu_custom_call" | custom-call | flops 1 | bytes 1 | tf_op jit(solution)/shard_map/weight_parts/pallas_call | solution.py:83
  146.8 6.5 %second_back.1 = (f32[512,768]{1,0:T(8,128)}, bf16[512,768]{1,0:T(8,128)(2,1)}, f32[1,768]{1,0:T(1,128)}, bf16[512,384]{1,0:T(8,128)(2,1)}, bf16[512,384]{1,0:T(8,128)(2,1)}) custom-call(bf16[512,768]{1,0:T(8,128)(2,1)} %refs_0_.7, f32[512,768]{1,0:T(8,128)} %get-tuple-element.78.refs_1_.refs_0_, f32[1,768]{1,0:T(1,128)} %reshape.152.refs_5_.refs_2_, ...), custom_call_target="tpu_custom_call" | custom-call | flops 299999985664 | bytes 1 | tf_op jit(solution)/shard_map/second_back/pallas_call | solution.py:83
  153.3 4.6 %all-to-all-start.1 = ((bf16[4,256,768]{2,1,0:T(8,128)(2,1)}), bf16[4,256,768]{2,1,0:T(8,128)(2,1)}, u32[]{:S(2)}, u32[]{:S(2)}) async-start(bf16[4,256,768]{2,1,0:T(8,128)(2,1)} %touch.10), calls=%async_computation.1 | async-start | bytes 3145728 | tf_op jit(solution)/shard_map/all_to_all | solution.py:978
  165.8 9.7 %split_sums.1 = (bf16[768,768]{1,0:T(8,128)(2,1)}, bf16[768,768]{1,0:T(8,128)(2,1)}, bf16[768,768]{1,0:T(8,128)(2,1)}, bf16[768,768]{1,0:T(8,128)(2,1)}) custom-call(s32[2]{0:T(128)} %pad_add_fusion.13.refs_0_, bf16[1536,768]{1,0:T(8,128)(2,1)} %get-tuple-element.109.refs_1_, bf16[1536,768]{1,0:T(8,128)(2,1)} %collective-permute-done.12.refs_2_, ...), custom_call_target="tpu_custom_call" | custom-call | flops 1 | bytes 1 | tf_op jit(solution)/shard_map/split_sums/pallas_call | solution.py:83
  181.8 23.1 %attend_back.1 = (bf16[896,768]{1,0:T(8,128)(2,1)}, bf16[896,768]{1,0:T(8,128)(2,1)}, f32[512,768]{1,0:T(8,128)}, bf16[512,768]{1,0:T(8,128)(2,1)}) custom-call(s32[2]{0:T(128)} %pad_add_fusion.12.refs_0_, bf16[512,384]{1,0:T(8,128)(2,1)} %get-tuple-element.99.refs_1_, bf16[512,384]{1,0:T(8,128)(2,1)} %collective-permute-done.10.refs_3_.refs_2_, ...), custom_call_target="tpu_custom_call" | custom-call | flops 1 | bytes 1 | tf_op jit(solution)/shard_map/attend_back/pallas_call | solution.py:83
  206.3 4.9 %adds.2 = (bf16[384,768]{1,0:T(8,128)(2,1)}, bf16[384,768]{1,0:T(8,128)(2,1)}, bf16[384,768]{1,0:T(8,128)(2,1)}, bf16[384,768]{1,0:T(8,128)(2,1)}) custom-call(s32[4]{0:T(128)} %pad_add_fusion.14.refs_0_, bf16[768,768]{1,0:T(8,128)(2,1)} %get-tuple-element.117.refs_1_, bf16[768,768]{1,0:T(8,128)(2,1)} %collective-permute-done.16.refs_2_, ...), custom_call_target="tpu_custom_call" | custom-call | flops 1 | bytes 1 | tf_op jit(solution)/shard_map/adds/pallas_call | solution.py:83
  212.6 3.6 %add.282 = bf16[896,768]{1,0:T(8,128)(2,1)} custom-call(s32[1]{0:T(128)} %constant.182.clone.1.refs_0_, bf16[896,768]{1,0:T(8,128)(2,1)} %get-tuple-element.114.refs_5_.refs_1_, bf16[896,768]{1,0:T(8,128)(2,1)} %collective-permute-done.14.refs_2_, bf16[192,768]{1,0:T(8,128)(2,1)} %touch.12.refs_3_), custom_call_target="tpu_custom_call" | custom-call | flops 1 | bytes 1 | tf_op jit(solution)/shard_map/add/pallas_call | solution.py:83
  216.2 6.3 %all-to-all-start.2 = ((bf16[8,112,768]{2,1,0:T(8,128)(2,1)}), bf16[8,112,768]{2,1,0:T(8,128)(2,1)}, u32[]{:S(2)}, u32[]{:S(2)}) async-start(bf16[8,112,768]{2,1,0:T(8,128)(2,1)} %bitcast.99), calls=%async_computation.2 | async-start | bytes 2752512 | tf_op jit(solution)/shard_map/all_to_all | solution.py:1091
  222.6 3.9 %output_rows.1.refs_5_ = bf16[512,768]{1,0:T(8,128)(2,1)} custom-call(f32[512,768]{1,0:T(8,128)} %get-tuple-element.78.refs_1_.refs_0_, s32[512,1]{1,0:T(8,128)} %copy.76.refs_1_, bf16[4,256,768]{2,1,0:T(8,128)(2,1)} %all-to-all-done.1.refs_3_.refs_2_, bf16[8,112,768]{2,1,0:T(8,128)(2,1)} %bitcast.100), custom_call_target="tpu_custom_call" | custom-call | flops 1 | bytes 1 | tf_op jit(solution)/shard_map/output_rows/pallas_call | solution.py:83
  229.4 4.5 %first_back.1.refs_5_ = f32[512,768]{1,0:T(8,128)} custom-call(bf16[512,768]{1,0:T(8,128)(2,1)} %refs_0_.8, f32[1,768]{1,0:T(1,128)} %reshape.150.refs_2_.refs_13_.refs_1_, f32[512,768]{1,0:T(8,128)} %get-tuple-element.122.refs_2_, f32[512,768]{1,0:T(8,128)} %get-tuple-element.123.refs_3_, bf16[512,768]{1,0:T(8,128)(2,1)} %collective-permute-done.18.refs_4_, ...), custom_call_target="tpu_custom_call" | custom-call | flops 299999985664 | bytes 1 | tf_op jit(solution)/shard_map/first_back/pallas_call | solution.py:83
  234.0 7.0 %collective-permute-done.19.refs_2_ = bf16[384,768]{1,0:T(8,128)(2,1)} collective-permute-done((bf16[384,768]{1,0:T(8,128)(2,1)}, bf16[384,768]{1,0:T(8,128)(2,1)}, u32[]{:S(2)}, u32[]{:S(2)}) %collective-permute-start.19) | collective-permute-done | bytes 589856 | tf_op jit(solution)/shard_map/outer-1/ppermute | solution.py:19
  241.5 3.5 %adds.3 = (bf16[384,768]{1,0:T(8,128)(2,1)}, bf16[384,768]{1,0:T(8,128)(2,1)}) custom-call(s32[2]{0:T(128)} %broadcast_2_refs_0_.2.refs_0_, bf16[384,768]{1,0:T(8,128)(2,1)} %get-tuple-element.121.refs_2_.refs_1_, bf16[384,768]{1,0:T(8,128)(2,1)} %collective-permute-done.19.refs_2_, bf16[384,768]{1,0:T(8,128)(2,1)} %get-tuple-element.125.refs_3_, ...), custom_call_target="tpu_custom_call" | custom-call | flops 1 | bytes 1 | tf_op jit(solution)/shard_map/adds/pallas_call | solution.py:83
  244.9 10.9 %all-to-all-done.2.refs_0_ = bf16[8,112,768]{2,1,0:T(8,128)(2,1)} async-done(((bf16[8,112,768]{2,1,0:T(8,128)(2,1)}), bf16[8,112,768]{2,1,0:T(8,128)(2,1)}, u32[]{:S(2)}, u32[]{:S(2)}) %all-to-all-start.2) | async-done | bytes 1376288 | tf_op jit(solution)/shard_map/all_to_all | solution.py:1091
  258.5 4.4 %all-to-all-start.3 = ((bf16[8,112,768]{2,1,0:T(8,128)(2,1)}), bf16[8,112,768]{2,1,0:T(8,128)(2,1)}, u32[]{:S(2)}, u32[]{:S(2)}) async-start(bf16[8,112,768]{2,1,0:T(8,128)(2,1)} %total.1.refs_1_.refs_7_), calls=%async_computation.3 | async-start | bytes 2752512 | tf_op jit(solution)/shard_map/all_to_all | solution.py:1103
  267.8 11.5 %collective-permute-done.21.refs_2_ = bf16[384,768]{1,0:T(8,128)(2,1)} collective-permute-done((bf16[384,768]{1,0:T(8,128)(2,1)S(1)}, bf16[384,768]{1,0:T(8,128)(2,1)}, u32[]{:S(2)}, u32[]{:S(2)}) %collective-permute-start.21) | collective-permute-done | bytes 589856 | tf_op jit(solution)/shard_map/piece/ppermute | solution.py:19
  279.3 12.8 %collective-permute-done.23.refs_3_ = bf16[384,768]{1,0:T(8,128)(2,1)} collective-permute-done((bf16[384,768]{1,0:T(8,128)(2,1)S(1)}, bf16[384,768]{1,0:T(8,128)(2,1)}, u32[]{:S(2)}, u32[]{:S(2)}) %collective-permute-start.23) | collective-permute-done | bytes 589856 | tf_op jit(solution)/shard_map/piece/ppermute | solution.py:19
  294.5 9.2 %collective-permute-done.27.refs_2_ = bf16[384,768]{1,0:T(8,128)(2,1)} collective-permute-done((bf16[384,768]{1,0:T(8,128)(2,1)}, bf16[384,768]{1,0:T(8,128)(2,1)}, u32[]{:S(2)}, u32[]{:S(2)}) %collective-permute-start.27) | collective-permute-done | bytes 589856 | tf_op jit(solution)/shard_map/piece/ppermute | solution.py:19
  307.4 6.4 %assemble.4.refs_8_.refs_1_.refs_3_ = f32[3072,768]{1,0:T(8,128)} custom-call(s32[6,2]{1,0:T(8,128)} %stack.273.refs_0_, bf16[384,768]{1,0:T(8,128)(2,1)} %get-tuple-element.127.refs_1_, bf16[384,768]{1,0:T(8,128)(2,1)} %collective-permute-done.21.refs_2_, bf16[384,768]{1,0:T(8,128)(2,1)} %collective-permute-done.23.refs_3_, ...), custom_call_target="tpu_custom_call" | custom-call | flops 1 | bytes 1 | tf_op jit(solution)/shard_map/assemble/pallas_call | solution.py:83
  313.8 6.4 %assemble.5.refs_2_.refs_3_ = f32[768,3072]{1,0:T(8,128)} custom-call(s32[6,2]{1,0:T(8,128)} %stack.295.refs_0_, bf16[384,768]{1,0:T(8,128)(2,1)} %get-tuple-element.128.refs_2_.refs_1_, bf16[384,768]{1,0:T(8,128)(2,1)} %collective-permute-done.27.refs_2_, bf16[384,768]{1,0:T(8,128)(2,1)} %collective-permute-done.28.refs_3_, ...), custom_call_target="tpu_custom_call" | custom-call | flops 1 | bytes 1 | tf_op jit(solution)/shard_map/assemble/pallas_call | solution.py:83
  323.8 4.8 %weight_outputs.1 = (f32[3,768,384]{2,1,0:T(8,128)}, f32[384,768]{1,0:T(8,128)}, f32[2,768]{1,0:T(2,128)}) custom-call(s32[1]{0:T(128)} %bitcast.15.refs_0_, bf16[896,768]{1,0:T(8,128)(2,1)} %bitcast.49.refs_1_, bf16[896,768]{1,0:T(8,128)(2,1)} %collective-permute-done.33.refs_2_), custom_call_target="tpu_custom_call" | custom-call | flops 1 | bytes 1 | tf_op jit(solution)/shard_map/weight_outputs/pallas_call | solution.py:83
  (135 shorter events, 82.0 us)
Async XLA Ops:
  0.6 16.0 %collective-permute-start.1 = (s32[512]{0:T(512)}, s32[512]{0:T(512)}, u32[]{:S(2)}, u32[]{:S(2)}) collective-permute-start(s32[512]{0:T(512)} %param.14), channel_id=1, source_target_pairs={{0,1},{1,0},{2,3},{3,2},{4,5},{5,4},{6,7},{7,6},{8,9},{9,8},{10,11... | collective-permute-start | bytes 6152 | tf_op jit(solution)/shard_map/positions/ppermute | solution.py:19
  3.7 27.7 %collective-permute-start = (bf16[512,768]{1,0:T(8,128)(2,1)}, bf16[512,768]{1,0:T(8,128)(2,1)}, u32[]{:S(2)}, u32[]{:S(2)}) collective-permute-start(bf16[512,768]{1,0:T(8,128)(2,1)} %refs_0_.8), channel_id=1, source_target_pairs={{0,1},{1,0},{2,3},{3,2},{4,5},{5,4},{6,7},{7,6},{8,9},{9,8},{10,11... | collective-permute-start | bytes 2359304 | tf_op jit(solution)/shard_map/rows/ppermute | solution.py:19
  21.6 24.3 %collective-permute-start.2 = (bf16[384,768]{1,0:T(8,128)(2,1)}, bf16[384,768]{1,0:T(8,128)(2,1)}, u32[]{:S(2)}, u32[]{:S(2)}) collective-permute-start(bf16[384,768]{1,0:T(8,128)(2,1)} %touch.9), channel_id=1, source_target_pairs={{0,1},{1,0},{2,3},{3,2},{4,5},{5,4},{6,7},{7,6},{8,9},{9,8},{10,11... | collective-permute-start | bytes 1769480 | tf_op jit(solution)/shard_map/output_weight/ppermute | solution.py:19
  23.6 42.8 %all-to-all-start = ((bf16[4,256,768]{2,1,0:T(8,128)(2,1)}), bf16[4,256,768]{2,1,0:T(8,128)(2,1)}, u32[]{:S(2)}, u32[]{:S(2)}) async-start(bf16[4,256,768]{2,1,0:T(8,128)(2,1)} %sent_rows.1.refs_4_), calls=%async_computation | async-start | bytes 3145728 | tf_op jit(solution)/shard_map/all_to_all | solution.py:978
  61.1 22.0 %collective-permute-start.6 = (bf16[256,768]{1,0:T(8,128)(2,1)}, bf16[256,768]{1,0:T(8,128)(2,1)}, u32[]{:S(2)}, u32[]{:S(2)}) collective-permute-start(bf16[256,768]{1,0:T(8,128)(2,1)} %get-tuple-element.81), channel_id=1, source_target_pairs={{0,2},{2,0},{4,6},{6,4},{1,3},{3,1},{5,7},{7,5},{8,10},{10,8},{12,... | collective-permute-start | bytes 1179656 | tf_op jit(solution)/shard_map/dispatch1/ppermute | solution.py:19
  62.9 30.1 %collective-permute-start.4 = (bf16[256,768]{1,0:T(8,128)(2,1)}, bf16[256,768]{1,0:T(8,128)(2,1)}, u32[]{:S(2)}, u32[]{:S(2)}) collective-permute-start(bf16[256,768]{1,0:T(8,128)(2,1)} %get-tuple-element.79), channel_id=1, source_target_pairs={{0,4},{2,6},{4,0},{6,2},{1,5},{3,7},{5,1},{7,3},{8,12},{10,14},{12... | collective-permute-start | bytes 1179656 | tf_op jit(solution)/shard_map/dispatch2/ppermute | solution.py:19
  65.2 27.8 %collective-permute-start.5 = (bf16[256,768]{1,0:T(8,128)(2,1)}, bf16[256,768]{1,0:T(8,128)(2,1)}, u32[]{:S(2)}, u32[]{:S(2)}) collective-permute-start(bf16[256,768]{1,0:T(8,128)(2,1)} %get-tuple-element.80), channel_id=1, source_target_pairs={{0,6},{2,4},{4,2},{6,0},{1,7},{3,5},{5,3},{7,1},{8,14},{10,12},{12... | collective-permute-start | bytes 1179656 | tf_op jit(solution)/shard_map/dispatch3/ppermute | solution.py:19
  109.3 37.5 %collective-permute-start.8 = (bf16[256,768]{1,0:T(8,128)(2,1)}, bf16[256,768]{1,0:T(8,128)(2,1)}, u32[]{:S(2)}, u32[]{:S(2)}) collective-permute-start(bf16[256,768]{1,0:T(8,128)(2,1)} %get-tuple-element.92.refs_9_), channel_id=1, source_target_pairs={{0,4},{2,6},{4,0},{6,2},{1,5},{3,7},{5,1},{7,3},{8,12},{10,14},{12... | collective-permute-start | bytes 1179656 | tf_op jit(solution)/shard_map/return2/ppermute | solution.py:19
  115.8 30.9 %collective-permute-start.9 = (bf16[256,768]{1,0:T(8,128)(2,1)}, bf16[256,768]{1,0:T(8,128)(2,1)}, u32[]{:S(2)}, u32[]{:S(2)}) collective-permute-start(bf16[256,768]{1,0:T(8,128)(2,1)} %get-tuple-element.93.refs_10_), channel_id=1, source_target_pairs={{0,6},{2,4},{4,2},{6,0},{1,7},{3,5},{5,3},{7,1},{8,14},{10,12},{12... | collective-permute-start | bytes 1179656 | tf_op jit(solution)/shard_map/return3/ppermute | solution.py:19
  118.2 28.6 %collective-permute-start.7 = (bf16[256,768]{1,0:T(8,128)(2,1)}, bf16[256,768]{1,0:T(8,128)(2,1)}, u32[]{:S(2)}, u32[]{:S(2)}) collective-permute-start(bf16[256,768]{1,0:T(8,128)(2,1)} %get-tuple-element.91), channel_id=1, source_target_pairs={{0,2},{2,0},{4,6},{6,4},{1,3},{3,1},{5,7},{7,5},{8,10},{10,8},{12,... | collective-permute-start | bytes 1179656 | tf_op jit(solution)/shard_map/return1/ppermute | solution.py:19
  133.3 32.5 %collective-permute-start.12 = (bf16[1536,768]{1,0:T(8,128)(2,1)}, bf16[1536,768]{1,0:T(8,128)(2,1)}, u32[]{:S(2)}, u32[]{:S(2)}) collective-permute-start(bf16[1536,768]{1,0:T(8,128)(2,1)} %get-tuple-element.110), channel_id=1, source_target_pairs={{0,8},{8,0},{1,9},{9,1},{2,10},{10,2},{3,11},{11,3},{4,12},{12,4},... | collective-permute-start | bytes 7077896 | tf_op jit(solution)/shard_map/outer_core/ppermute | solution.py:19
  133.3 32.5 %collective-permute-start.13 = (bf16[768,1536]{1,0:T(8,128)(2,1)}, bf16[768,1536]{1,0:T(8,128)(2,1)}, u32[]{:S(2)}, u32[]{:S(2)}) collective-permute-start(bf16[768,1536]{1,0:T(8,128)(2,1)} %get-tuple-element.96.refs_9_), channel_id=1, source_target_pairs={{0,8},{8,0},{1,9},{9,1},{2,10},{10,2},{3,11},{11,3},{4,12},{12,4},... | collective-permute-start | bytes 7077896 | tf_op jit(solution)/shard_map/inner_core/ppermute | solution.py:19
  153.3 59.3 %all-to-all-start.1 = ((bf16[4,256,768]{2,1,0:T(8,128)(2,1)}), bf16[4,256,768]{2,1,0:T(8,128)(2,1)}, u32[]{:S(2)}, u32[]{:S(2)}) async-start(bf16[4,256,768]{2,1,0:T(8,128)(2,1)} %touch.10), calls=%async_computation.1 | async-start | bytes 3145728 | tf_op jit(solution)/shard_map/all_to_all | solution.py:978
  157.8 17.6 %collective-permute-start.10 = (bf16[512,384]{1,0:T(8,128)(2,1)}, bf16[512,384]{1,0:T(8,128)(2,1)}, u32[]{:S(2)}, u32[]{:S(2)}) collective-permute-start(bf16[512,384]{1,0:T(8,128)(2,1)} %get-tuple-element.98.refs_1_.refs_4_.refs_5_), channel_id=1, source_target_pairs={{0,1},{1,0},{2,3},{3,2},{4,5},{5,4},{6,7},{7,6},{8,9},{9,8},{10,11... | collective-permute-start | bytes 1179656 | tf_op jit(solution)/shard_map/context_grad/ppermute | solution.py:19
  175.5 30.4 %collective-permute-start.16 = (bf16[768,768]{1,0:T(8,128)(2,1)}, bf16[768,768]{1,0:T(8,128)(2,1)}, u32[]{:S(2)}, u32[]{:S(2)}) collective-permute-start(bf16[768,768]{1,0:T(8,128)(2,1)} %get-tuple-element.118), channel_id=1, source_target_pairs={{0,16},{16,0},{1,17},{17,1},{2,18},{18,2},{3,19},{19,3},{4,20},{20... | collective-permute-start | bytes 3538952 | tf_op jit(solution)/shard_map/outer0/ppermute | solution.py:19
  177.1 29.2 %collective-permute-start.17 = (bf16[768,768]{1,0:T(8,128)(2,1)}, bf16[768,768]{1,0:T(8,128)(2,1)}, u32[]{:S(2)}, u32[]{:S(2)}) collective-permute-start(bf16[768,768]{1,0:T(8,128)(2,1)} %get-tuple-element.113.refs_16_), channel_id=1, source_target_pairs={{0,1},{1,0},{2,3},{3,2},{4,5},{5,4},{6,7},{7,6},{8,9},{9,8},{10,11... | collective-permute-start | bytes 3538952 | tf_op jit(solution)/shard_map/inner0/ppermute | solution.py:19
  178.0 34.6 %collective-permute-start.15 = (bf16[192,768]{1,0:T(8,128)(2,1)}, bf16[192,768]{1,0:T(8,128)(2,1)}, u32[]{:S(2)}, u32[]{:S(2)}) collective-permute-start(bf16[192,768]{1,0:T(8,128)(2,1)} %get-tuple-element.116), channel_id=1, source_target_pairs={{0,1},{1,0},{2,3},{3,2},{4,5},{5,4},{6,7},{7,6},{8,9},{9,8},{10,11... | collective-permute-start | bytes 884744 | tf_op jit(solution)/shard_map/output_grad/ppermute | solution.py:19
  204.9 24.5 %collective-permute-start.18 = (bf16[512,768]{1,0:T(8,128)(2,1)}, bf16[512,768]{1,0:T(8,128)(2,1)}, u32[]{:S(2)}, u32[]{:S(2)}) collective-permute-start(bf16[512,768]{1,0:T(8,128)(2,1)} %get-tuple-element.124), channel_id=1, source_target_pairs={{0,1},{1,0},{2,3},{3,2},{4,5},{5,4},{6,7},{7,6},{8,9},{9,8},{10,11... | collective-permute-start | bytes 2359304 | tf_op jit(solution)/shard_map/theirs/ppermute | solution.py:19
  211.2 29.8 %collective-permute-start.19 = (bf16[384,768]{1,0:T(8,128)(2,1)}, bf16[384,768]{1,0:T(8,128)(2,1)}, u32[]{:S(2)}, u32[]{:S(2)}) collective-permute-start(bf16[384,768]{1,0:T(8,128)(2,1)} %get-tuple-element.120.refs_1_), channel_id=1, source_target_pairs={{0,1},{1,0},{2,3},{3,2},{4,5},{5,4},{6,7},{7,6},{8,9},{9,8},{10,11... | collective-permute-start | bytes 1769480 | tf_op jit(solution)/shard_map/outer-1/ppermute | solution.py:19
  212.1 28.9 %collective-permute-start.20 = (bf16[384,768]{1,0:T(8,128)(2,1)}, bf16[384,768]{1,0:T(8,128)(2,1)}, u32[]{:S(2)}, u32[]{:S(2)}) collective-permute-start(bf16[384,768]{1,0:T(8,128)(2,1)} %get-tuple-element.126), channel_id=1, source_target_pairs={{0,16},{16,0},{1,17},{17,1},{2,18},{18,2},{3,19},{19,3},{4,20},{20... | collective-permute-start | bytes 1769480 | tf_op jit(solution)/shard_map/inner-1/ppermute | solution.py:19
  216.2 39.6 %all-to-all-start.2 = ((bf16[8,112,768]{2,1,0:T(8,128)(2,1)}), bf16[8,112,768]{2,1,0:T(8,128)(2,1)}, u32[]{:S(2)}, u32[]{:S(2)}) async-start(bf16[8,112,768]{2,1,0:T(8,128)(2,1)} %bitcast.99), calls=%async_computation.2 | async-start | bytes 2752512 | tf_op jit(solution)/shard_map/all_to_all | solution.py:1091
  258.5 61.8 %all-to-all-start.3 = ((bf16[8,112,768]{2,1,0:T(8,128)(2,1)}), bf16[8,112,768]{2,1,0:T(8,128)(2,1)}, u32[]{:S(2)}, u32[]{:S(2)}) async-start(bf16[8,112,768]{2,1,0:T(8,128)(2,1)} %total.1.refs_1_.refs_7_), calls=%async_computation.3 | async-start | bytes 2752512 | tf_op jit(solution)/shard_map/all_to_all | solution.py:1103
  262.9 16.4 %collective-permute-start.21 = (bf16[384,768]{1,0:T(8,128)(2,1)S(1)}, bf16[384,768]{1,0:T(8,128)(2,1)}, u32[]{:S(2)}, u32[]{:S(2)}) collective-permute-start(bf16[384,768]{1,0:T(8,128)(2,1)S(1)} %copy-done), channel_id=1, source_target_pairs={{0,1},{1,0},{2,3},{3,2},{4,5},{5,4},{6,7},{7,6},{8,9},{9,8},{10,11... | collective-permute-start | bytes 1769480 | tf_op jit(solution)/shard_map/piece/ppermute | solution.py:19
  263.9 28.2 %collective-permute-start.23 = (bf16[384,768]{1,0:T(8,128)(2,1)S(1)}, bf16[384,768]{1,0:T(8,128)(2,1)}, u32[]{:S(2)}, u32[]{:S(2)}) collective-permute-start(bf16[384,768]{1,0:T(8,128)(2,1)S(1)} %copy-done), channel_id=1, source_target_pairs={{0,16},{16,0},{1,17},{17,1},{2,18},{18,2},{3,19},{19,3},{4,20},{20... | collective-permute-start | bytes 1769480 | tf_op jit(solution)/shard_map/piece/ppermute | solution.py:19
  265.7 37.9 %collective-permute-start.27 = (bf16[384,768]{1,0:T(8,128)(2,1)}, bf16[384,768]{1,0:T(8,128)(2,1)}, u32[]{:S(2)}, u32[]{:S(2)}) collective-permute-start(bf16[384,768]{1,0:T(8,128)(2,1)} %get-tuple-element.128.refs_2_.refs_1_), channel_id=1, source_target_pairs={{0,16},{16,0},{1,17},{17,1},{2,18},{18,2},{3,19},{19,3},{4,20},{20... | collective-permute-start | bytes 1769480 | tf_op jit(solution)/shard_map/piece/ppermute | solution.py:19
  266.7 36.9 %collective-permute-start.28 = (bf16[384,768]{1,0:T(8,128)(2,1)}, bf16[384,768]{1,0:T(8,128)(2,1)}, u32[]{:S(2)}, u32[]{:S(2)}) collective-permute-start(bf16[384,768]{1,0:T(8,128)(2,1)} %get-tuple-element.128.refs_2_.refs_1_), channel_id=1, source_target_pairs={{0,1},{1,0},{2,3},{3,2},{4,5},{5,4},{6,7},{7,6},{8,9},{9,8},{10,11... | collective-permute-start | bytes 1769480 | tf_op jit(solution)/shard_map/piece/ppermute | solution.py:19
  279.3 25.1 %collective-permute-start.25 = (bf16[384,768]{1,0:T(8,128)(2,1)}, bf16[384,768]{1,0:T(8,128)(2,1)}, u32[]{:S(2)}, u32[]{:S(2)}) collective-permute-start(bf16[384,768]{1,0:T(8,128)(2,1)} %collective-permute-done.21.refs_2_), channel_id=1, source_target_pairs={{0,8},{8,0},{1,9},{9,1},{2,10},{10,2},{3,11},{11,3},{4,12},{12,4},... | collective-permute-start | bytes 1769480 | tf_op jit(solution)/shard_map/piece_core/ppermute | solution.py:19
  292.1 13.1 %collective-permute-start.26 = (bf16[384,768]{1,0:T(8,128)(2,1)}, bf16[384,768]{1,0:T(8,128)(2,1)}, u32[]{:S(2)}, u32[]{:S(2)}) collective-permute-start(bf16[384,768]{1,0:T(8,128)(2,1)} %collective-permute-done.23.refs_3_), channel_id=1, source_target_pairs={{0,8},{8,0},{1,9},{9,1},{2,10},{10,2},{3,11},{11,3},{4,12},{12,4},... | collective-permute-start | bytes 1769480 | tf_op jit(solution)/shard_map/piece_core/ppermute | solution.py:19
  292.1 13.1 %collective-permute-start.24 = (bf16[384,768]{1,0:T(8,128)(2,1)}, bf16[384,768]{1,0:T(8,128)(2,1)}, u32[]{:S(2)}, u32[]{:S(2)}) collective-permute-start(bf16[384,768]{1,0:T(8,128)(2,1)} %touch.13), channel_id=1, source_target_pairs={{0,8},{8,0},{1,9},{9,1},{2,10},{10,2},{3,11},{11,3},{4,12},{12,4},... | collective-permute-start | bytes 1769480 | tf_op jit(solution)/shard_map/piece_core/ppermute | solution.py:19
  303.7 16.6 %collective-permute-start.32 = (bf16[384,768]{1,0:T(8,128)(2,1)}, bf16[384,768]{1,0:T(8,128)(2,1)}, u32[]{:S(2)}, u32[]{:S(2)}) collective-permute-start(bf16[384,768]{1,0:T(8,128)(2,1)} %collective-permute-done.27.refs_2_), channel_id=1, source_target_pairs={{0,1},{1,0},{2,3},{3,2},{4,5},{5,4},{6,7},{7,6},{8,9},{9,8},{10,11... | collective-permute-start | bytes 1769480 | tf_op jit(solution)/shard_map/piece/ppermute | solution.py:19
  304.5 15.8 %collective-permute-start.22 = (bf16[384,768]{1,0:T(8,128)(2,1)}, bf16[384,768]{1,0:T(8,128)(2,1)}, u32[]{:S(2)}, u32[]{:S(2)}) collective-permute-start(bf16[384,768]{1,0:T(8,128)(2,1)} %collective-permute-done.21.refs_2_), channel_id=1, source_target_pairs={{0,16},{16,0},{1,17},{17,1},{2,18},{18,2},{3,19},{19,3},{4,20},{20... | collective-permute-start | bytes 1769480 | tf_op jit(solution)/shard_map/piece/ppermute | solution.py:19
  320.9 13.6 %collective-permute-start.35 = (bf16[384,768]{1,0:T(8,128)(2,1)}, bf16[384,768]{1,0:T(8,128)(2,1)}, u32[]{:S(2)}, u32[]{:S(2)}) collective-permute-start(bf16[384,768]{1,0:T(8,128)(2,1)} %touch.16.refs_2_.refs_1_), channel_id=1, source_target_pairs={{0,8},{8,0},{1,9},{9,1},{2,10},{10,2},{3,11},{11,3},{4,12},{12,4},... | collective-permute-start | bytes 1769480 | tf_op jit(solution)/shard_map/piece_core/ppermute | solution.py:19
  (13 other events, 97.2 us)

commit v2 on v1

--- a/solution.py
+++ b/solution.py
@@ -35,6 +35,7 @@
 PAIR = 2 * HEAD_DIM
 ATTEND_FLOPS = 20 * 10**9
 BACK_FLOPS = 300 * 10**9
+ATTBACK_FLOPS = 50 * 10**9
 FIRST_FLOPS = 300 * 10**9
 HIDE = -1000000000.0
 VMEM_LIMIT = 64 * 1024 * 1024
@@ -109,32 +110,32 @@
 
 
 def project_kernel(which_ref, x_ref, gain_ref, weight_ref, first_ref, out_ref):
-    @pl.when(pl.program_id(0) == 0)
-    def _():
-        normed, _ = norm_parts(x_ref[...].astype(F32))
-        first_ref[0] = (normed * gain_ref[...]).astype(BF)
-
-    out_ref[0, 0] = dot(first_ref[0], weight_ref[0]).astype(BF)
-
-
-def project(which, rows, gain, weight, earlier, after=()):
+    normed, _ = norm_parts(x_ref[...].astype(F32))
+    first = (normed * gain_ref[...]).astype(BF)
+    first_ref[0] = first
+    for c in range(3):
+        out_ref[c, 0] = dot(first, weight_ref[c]).astype(BF)
+
+
+def project(which, rows, gain, weight, earlier, after=(), tiles=1):
     count, width = rows.shape
     cols = weight.shape[2]
+    size = count // tiles
     return call(
         project_kernel,
         [rows, gain, weight],
         after=after,
         alias=earlier,
         prefetch=[which],
-        grid=(3,),
+        grid=(tiles,),
         in_specs=[
-            whole((count, width)),
+            pl.BlockSpec((size, width), lambda i, w: (i, 0)),
             whole((1, width)),
-            pl.BlockSpec((1, width, cols), lambda c, w: (c, 0, 0)),
+            whole((3, width, cols)),
         ],
         out_specs=[
-            pl.BlockSpec((1, count, width), lambda c, w: (w[0], 0, 0)),
-            pl.BlockSpec((1, 1, count, cols), lambda c, w: (c, w[0], 0, 0)),
+            pl.BlockSpec((1, size, width), lambda i, w: (w[0], i, 0)),
+            pl.BlockSpec((3, 1, size, cols), lambda i, w: (0, w[0], i, 0)),
         ],
         out_shape=[shaped((2, count, width), BF), shaped((3, 2, count, cols), BF)],
         name="project",
@@ -159,35 +160,41 @@
     lane = lax.broadcasted_iota(jnp.int32, (1, PAIR), 1) // HEAD_DIM
 
     def half(late):
+        blocks = [(at, a) for at in (0, step) for a in (0, 1)]
+        for a in (0, 1):
+            pd_ref[0, a, :step, step:] = jnp.zeros((step, step), BF)
+        scores = []
+        for at, a in blocks:
+            rows, keys = pl.ds(at, step), at + step
+            mine = jnp.where(lane == a, q_ref[0, 0, rows, :] * 0.125, 0.0).astype(BF)
+            s_d = dot_nt(mine, kd_ref[0, 0, :keys, :]) + bias_d[rows, :keys]
+            s_c = dot_nt(mine, kc_ref[0, 0]) + bias_c[rows, :] if late else None
+            scores.append((s_d, s_c))
+        mixed, scale = {}, {}
+        for (at, a), (s_d, s_c) in zip(blocks, scores):
+            rows, keys = pl.ds(at, step), at + step
+            top = jnp.max(s_d, axis=-1, keepdims=True)
+            if late:
+                top = jnp.maximum(top, jnp.max(s_c, axis=-1, keepdims=True))
+            p_d = jnp.exp(s_d - top)
+            total = jnp.sum(p_d, axis=-1, keepdims=True)
+            p_d = p_d.astype(BF)
+            pd_ref[0, a, rows, :keys] = p_d
+            value = jnp.where(lane == a, vd_ref[0, 0, :keys, :], 0.0).astype(BF)
+            mix = dot(p_d, value)
+            if late:
+                p_c = jnp.exp(s_c - top)
+                total = total + jnp.sum(p_c, axis=-1, keepdims=True)
+                p_c = p_c.astype(BF)
+                pc_ref[0, a, rows, :] = p_c
+                value = jnp.where(lane == a, vc_ref[0, 0], 0.0).astype(BF)
+                mix = mix + dot(p_c, value)
+            mixed[at, a], scale[at, a] = mix, 1.0 / total
         for at in (0, step):
             rows = pl.ds(at, step)
-            keys = at + step
-            q = q_ref[0, 0, rows, :] * 0.125
-            mixed, scale = 0.0, []
-            for a in (0, 1):
-                mine = jnp.where(lane == a, q, 0.0).astype(BF)
-                s_d = dot_nt(mine, kd_ref[0, 0, :keys, :]) + bias_d[rows, :keys]
-                top = jnp.max(s_d, axis=-1, keepdims=True)
-                if late:
-                    s_c = dot_nt(mine, kc_ref[0, 0]) + bias_c[rows, :]
-                    top = jnp.maximum(top, jnp.max(s_c, axis=-1, keepdims=True))
-                p_d = jnp.exp(s_d - top)
-                total = jnp.sum(p_d, axis=-1, keepdims=True)
-                p_d = p_d.astype(BF)
-                pd_ref[0, a, rows, :keys] = p_d
-                value = jnp.where(lane == a, vd_ref[0, 0, :keys, :], 0.0).astype(BF)
-                mixed = mixed + dot(p_d, value)
-                if late:
-                    p_c = jnp.exp(s_c - top)
-                    total = total + jnp.sum(p_c, axis=-1, keepdims=True)
-                    p_c = p_c.astype(BF)
-                    pc_ref[0, a, rows, :] = p_c
-                    value = jnp.where(lane == a, vc_ref[0, 0], 0.0).astype(BF)
-                    mixed = mixed + dot(p_c, value)
-                scale.append(1.0 / total)
-            scale = jnp.where(lane == 0, scale[0], scale[1])
-            rl_ref[0, rows, :] = scale
-            context_ref[rows, :] = (mixed * scale).astype(BF)
+            inverse = jnp.where(lane == 0, scale[at, 0], scale[at, 1])
+            rl_ref[0, rows, :] = inverse
+            context_ref[rows, :] = ((mixed[at, 0] + mixed[at, 1]) * inverse).astype(BF)
 
     pl.when(which_ref[0] == 0)(lambda: half(False))
     pl.when(which_ref[0] == 1)(lambda: half(True))
@@ -278,12 +285,14 @@
 
 
 def taken_rows(slot_ref, block_refs):
-    count, capacity = slot_ref.shape[0], block_refs[0].shape[0]
+    count, capacity = slot_ref.shape[1], block_refs[0].shape[0]
     total = 0.0
     for k, ref in enumerate(block_refs):
-        slot = lax.broadcasted_iota(jnp.int32, (count, capacity), 1) + k * capacity
+        slot = lax.broadcasted_iota(jnp.int32, (capacity, count), 0) + k * capacity
         place = jnp.where(slot_ref[...] == slot, 1.0, 0.0).astype(BF)
-        total = total + dot(place, ref[...])
+        total = total + lax.dot_general(
+            place, ref[...], (((0,), (0,)), ((), ())), preferred_element_type=F32
+        )
     return total
 
 
@@ -292,10 +301,10 @@
     refs[-1][...] = (hidden_ref[...] + taken_rows(slot_ref, blocks)).astype(BF)
 
 
-def output_rows(hidden, slot_col, blocks, after=()):
+def output_rows(hidden, slot_row, blocks, after=()):
     return plain(
         output_kernel,
-        [hidden, slot_col, blocks],
+        [hidden, slot_row, blocks],
         shaped(hidden.shape, BF),
         "output_rows",
         after,
@@ -315,7 +324,7 @@
     own_ref[...] = dot_nt(low, own_weight_ref[...]).astype(BF)
 
 
-def second_back(cot, hidden, gain, slot_col, own_weight, got_weight, blocks, after=()):
+def second_back(cot, hidden, gain, slot_row, own_weight, got_weight, blocks, after=()):
     count, width = hidden.shape
     part = shaped((count, own_weight.shape[0]), BF)
     out = [
@@ -327,7 +336,7 @@
     ]
     return plain(
         second_kernel,
-        [cot, hidden, gain, slot_col, own_weight, got_weight, *blocks],
+        [cot, hidden, gain, slot_row, own_weight, got_weight, *blocks],
         out,
         "second_back",
         after,
@@ -512,7 +521,7 @@
     pl.when(at >= half)(lambda: put(inner_out, x[...], pre_ref[...]))
 
 
-def weight_parts(half, x_blocks, cot_blocks, places, act, pre, after=(), tiles=4):
+def weight_parts(half, x_blocks, cot_blocks, places, act, pre, after=(), tiles=2):
     count, width = x_blocks[0].shape
     total, units = act.shape
     tile = units // 2 // tiles
@@ -545,49 +554,68 @@
     )
 
 
-def split_kernel(place_ref, outer_kept, outer_got, inner_kept, inner_got, *out_refs):
+def weight_sum_kernel(count, which_ref, place_ref, act_ref, pre_ref, *refs):
+    x_refs, (cot_ref, outer_got, inner_got, *out_refs, x, cot) = refs[:count], refs[count:]
     at = pl.program_id(0)
-    quarter = pl.num_programs(0) // 4
+
+    @pl.when(at == 0)
+    def _():
+        fill(cot, [cot_ref.at[place_ref[i]] for i in range(count)])
+        fill(x, x_refs)
+
+    def put(out_ref, got_ref, left, right):
+        part = lax.dot_general(
+            left, right, (((0,), (0,)), ((), ())), preferred_element_type=F32
+        )
+        out_ref[...] = (part + got_ref[...].astype(F32)).astype(BF)
+
     for i, out_ref in enumerate(out_refs):
-        kept_ref, got_ref = ((outer_kept, outer_got), (inner_kept, inner_got))[i // 2]
-
-        @pl.when(at // quarter == i)
-        def _(kept_ref=kept_ref, got_ref=got_ref, out_ref=out_ref):
-            out_ref[...] = (kept_ref[...].astype(F32) + got_ref[...].astype(F32)).astype(BF)
-
-
-def split_sums(outer, inner, outer_turn, inner_turn, after=(), tiles=4):
-    rows, cols = outer[0].shape
-    outer_tile, inner_tile = (rows // tiles, cols), (cols, rows // tiles)
-
-    def held(j, i):
-        return jnp.clip(j - i * (tiles // 2), 0, tiles // 2 - 1)
-
-    def source(i):
-        def at(j, w):
-            step = jnp.clip(j - i * tiles, 0, tiles - 1)
-            return (w[i] * (tiles // 2) + step) % tiles
-
-        return at
-
-    outer_at, inner_at = source(0), source(1)
-    outer_in = pl.BlockSpec(outer_tile, lambda j, w: (outer_at(j, w), 0))
-    inner_in = pl.BlockSpec(inner_tile, lambda j, w: (0, inner_at(j, w)))
+
+        @pl.when(at == i)
+        def _(i=i, out_ref=out_ref):
+            if i < 2:
+                put(out_ref, outer_got, act_ref[...], cot[...])
+            else:
+                put(out_ref, inner_got, x[...], pre_ref[...])
+
+
+def weight_sums(
+    half, outer_turn, inner_turn, x_blocks, cot_blocks, places, act, pre, outer_got, inner_got, after=()
+):
+    count, width = x_blocks[0].shape
+    total, units = act.shape
+    tile = units // 4
+
+    def outer_at(j, w):
+        return (w[1] + jnp.minimum(j, 1)) % 2
+
+    def inner_at(j, w):
+        return (w[2] + jnp.maximum(j - 2, 0)) % 2
+
+    out = [shaped((tile, width), BF)] * 2 + [shaped((width, tile), BF)] * 2
     parts = call(
-        split_kernel,
-        [*outer, *inner],
+        functools.partial(weight_sum_kernel, len(x_blocks)),
+        [act, pre, *x_blocks, cot_blocks, outer_got, inner_got],
         after=after,
-        prefetch=[jnp.stack([outer_turn, inner_turn]).astype(jnp.int32)],
-        grid=(2 * tiles,),
-        in_specs=[outer_in, outer_in, inner_in, inner_in],
-        out_specs=[
-            pl.BlockSpec(outer_tile, lambda j, w: (held(j, 0), 0)),
-            pl.BlockSpec(outer_tile, lambda j, w: (held(j, 1), 0)),
-            pl.BlockSpec(inner_tile, lambda j, w: (0, held(j, 2))),
-            pl.BlockSpec(inner_tile, lambda j, w: (0, held(j, 3))),
+        prefetch=[
+            jnp.stack([half, outer_turn, inner_turn]).astype(jnp.int32),
+            jnp.stack(places).astype(jnp.int32),
         ],
-        out_shape=[shaped((rows // 2, cols), BF)] * 2 + [shaped((cols, rows // 2), BF)] * 2,
-        name="split_sums",
+        grid=(4,),
+        in_specs=[
+            pl.BlockSpec((total, tile), lambda j, w, p: (0, w[0] * 2 + outer_at(j, w))),
+            pl.BlockSpec((total, tile), lambda j, w, p: (0, w[0] * 2 + inner_at(j, w))),
+        ]
+        + [whole((count, width))] * len(x_blocks)
+        + [
+            whole(cot_blocks.shape),
+            pl.BlockSpec((tile, width), lambda j, w, p: (outer_at(j, w), 0)),
+            pl.BlockSpec((width, tile), lambda j, w, p: (0, inner_at(j, w))),
+        ],
+        out_specs=[whole(o.shape) for o in out],
+        out_shape=out,
+        scratch_shapes=[pltpu.VMEM((total, width), BF)] * 2,
+        name="weight_sums",
     )
     return parts[:2], parts[2:]
 
@@ -599,6 +627,41 @@
         @pl.when(pl.program_id(0) == i)
         def _(ref=ref):
             out_ref[...] = ref[...].astype(F32)
+
+
+def assemble_two_kernel(count, place_ref, *refs):
+    *piece_refs, outer_ref, inner_ref = refs
+    for i, ref in enumerate(piece_refs):
+
+        @pl.when(pl.program_id(0) == i)
+        def _(ref=ref, out_ref=outer_ref if i < count else inner_ref):
+            out_ref[...] = ref[...].astype(F32)
+
+
+def assemble_two(outer, inner, places, earlier, after=()):
+    size, count = outer[0].shape, len(outer)
+    table = jnp.stack([jnp.stack(place) for place in places]).astype(jnp.int32)
+
+    def outer_at(i, t):
+        held = jnp.minimum(i, count - 1)
+        return t[held, 0], t[held, 1]
+
+    def inner_at(i, t):
+        held = jnp.maximum(i, count)
+        return t[held, 0], t[held, 1]
+
+    return call(
+        functools.partial(assemble_two_kernel, count),
+        [*outer, *inner],
+        after=after,
+        alias=earlier,
+        prefetch=[table],
+        grid=(2 * count,),
+        in_specs=[whole(size)] * (2 * count),
+        out_specs=[pl.BlockSpec(size, outer_at), pl.BlockSpec(size, inner_at)],
+        out_shape=[shaped(x.shape, F32) for x in earlier],
+        name="assemble_two",
+    )
 
 
 def assemble(pieces, places, shape, earlier, after=(), flops=1):
@@ -619,35 +682,27 @@
     )
 
 
-def add_kernel(more_at, place_ref, kept_ref, got_ref, *refs):
-    out_refs, more_refs = (refs, ()) if more_at is None else (refs[1:-1], refs[:1])
-    rows = out_refs[0].shape[0]
-    if more_refs:
-        kept_ref, scratch = refs[-1], kept_ref
-        kept_ref[...] = scratch[...].astype(F32)
-        span = pl.ds(more_at, more_refs[0].shape[0])
-        for ref in more_refs:
-            kept_ref[span, :] += ref[...].astype(F32)
-    for i, ref in enumerate(out_refs):
-        cut = pl.ds(pl.multiple_of(place_ref[i] * rows, rows), rows)
-        ref[...] = (kept_ref[cut, :].astype(F32) + got_ref[cut, :].astype(F32)).astype(BF)
-
-
-def add(kept, got, places, after=(), more=(), more_at=None):
-    shape = kept.shape
-    out = [shaped((shape[0] // len(places), *shape[1:]), BF)] * len(places)
-    return call(
-        functools.partial(add_kernel, more_at),
-        [kept, got, *more],
-        after=after,
-        prefetch=[jnp.stack(places).astype(jnp.int32)],
-        grid=(1,),
-        in_specs=[whole(shape)] * 2 + [whole(x.shape) for x in more],
-        out_specs=[whole(o.shape) for o in out],
-        scratch_shapes=[pltpu.VMEM(shape, F32)] if more else [],
-        out_shape=out,
-        name="add",
-    )
+def add_kernel(kept_ref, got_ref, out_ref):
+    out_ref[...] = (kept_ref[...].astype(F32) + got_ref[...].astype(F32)).astype(BF)
+
+
+def add(kept, got):
+    return plain(add_kernel, [kept, got], shaped(kept.shape, BF), "add")
+
+
+def gather_sum_kernel(kept_ref, got_ref, more_ref, out_ref, tail_ref):
+    rows, more = out_ref.shape[0], more_ref.shape[0]
+    first = rows - more
+    out_ref[:first] = (kept_ref[:first].astype(F32) + got_ref[:first].astype(F32)).astype(BF)
+    last = kept_ref[first:rows].astype(F32) + got_ref[first:rows].astype(F32)
+    out_ref[first:] = (last + more_ref[...].astype(F32)).astype(BF)
+    tail_ref[...] = (kept_ref[rows:].astype(F32) + got_ref[rows:].astype(F32)).astype(BF)
+
+
+def gather_sum(kept, got, more, rows, after=()):
+    lines, width = kept.shape
+    out = [shaped((rows, width), BF), shaped((lines - rows, width), BF)]
+    return plain(gather_sum_kernel, [kept, got, more], out, "gather_sum", after)
 
 
 def adds_kernel(count, cuts, place_ref, *refs):
@@ -681,28 +736,36 @@
     return [parts[cuts * i : cuts * (i + 1)] for i in range(len(pairs))]
 
 
-def gather_pieces(own, steps, order):
+def gather_pieces(own, steps, order, flops):
     weights = {step: 1 << (len(steps) - 1 - i) for i, step in enumerate(steps)}
     place = sum(side(*step) * weight for step, weight in weights.items())
-    pieces = [(0, place, own)]
-    for step in order:
-        change = weights[step] * (1 - 2 * side(*step))
-        pieces += [
-            (hops + 1, at + change, swap(piece, *step, "piece")) for hops, at, piece in pieces
-        ]
-    pieces.sort(key=lambda piece: piece[0])
-    return [piece[1:] for piece in pieces]
-
-
-def total_kernel(in_ref, out_ref):
-    count = in_ref.shape[0]
+    pieces, newest = [(place, own)], [(0, place, own)]
+    while newest:
+        found = []
+        for first, at, piece in newest:
+            for i in range(first, len(order)):
+                change = weights[order[i]] * (1 - 2 * side(*order[i]))
+                found.append((i + 1, at + change, swap(piece, *order[i], "piece")))
+        if len(pieces) == 1:
+            held = touch([piece for _, _, piece in found], [], flops=flops)
+            found = [(first, at, piece) for (first, at, _), piece in zip(found, held)]
+        pieces += [(at, piece) for _, at, piece in found]
+        newest = found
+    return pieces
+
+
+def total_kernel(in_ref, tail_ref, out_ref):
+    count, rows = in_ref.shape[:2]
     value = sum(in_ref[i].astype(F32) for i in range(count)).astype(BF)
     for i in range(count):
-        out_ref[i] = value
-
-
-def total(blocks, after=()):
-    return plain(total_kernel, [blocks], shaped(blocks.shape, BF), "total", after)
+        out_ref[i, :rows] = value
+        out_ref[i, rows:] = tail_ref[...]
+
+
+def total(blocks, tail, after=()):
+    count, rows, width = blocks.shape
+    out = shaped((count, rows + tail.shape[0], width), BF)
+    return plain(total_kernel, [blocks, tail], out, "total", after)
 
 
 def halves(step):
@@ -732,7 +795,7 @@
     at_ref, own_ref, other_ref, q_ref, k_ref, v_ref, pd_ref, pc_ref, own_context_ref,
     other_context_ref, rl_ref, first_ref, wp_ref, gain_ref, second_ref, own_output_ref,
     sent_ref, kept_ref, mine_ref, theirs_ref,
-    acc, scaled, through, key_acc, value_acc, queries, weights,
+    acc, scaled, through, key_acc, value_acc, queries, weights, scores,
 ):
     group = pl.program_id(0)
     count = own_ref.shape[0]
@@ -747,37 +810,44 @@
         grad = ref[...].astype(F32) * rl_ref[at]
         scaled[at] = grad
         through[at] = grad.astype(BF).astype(F32) * context[...].astype(F32)
-    key_acc[...] = jnp.zeros_like(key_acc)
-    value_acc[...] = jnp.zeros_like(value_acc)
+    @pl.when(group == 0)
+    def _():
+        for h in (0, 1):
+            for a in (0, 1):
+                scores[h, a, :step, step:] = jnp.zeros((step, step), BF)
 
     for h in (0, 1):
         for at in (0, step):
             rows = pl.ds(at, step)
-            grads = scaled[h, rows, :]
-            low = grads.astype(BF)
-            low_t = jnp.transpose(grads).astype(BF)
-            q_t = jnp.transpose(q_ref[0, h, rows, :].astype(F32)).astype(BF)
+            low = scaled[h, rows, :].astype(BF)
             query = 0.0
             for a in (0, 1):
-                line = pl.ds(a * HEAD_DIM, HEAD_DIM)
                 mine = jnp.where(lane == a, low, 0.0).astype(BF)
                 along = jnp.sum(
                     jnp.where(lane == a, through[h, rows, :], 0.0), axis=-1, keepdims=True
                 )
-                parts = [(pd_ref, h, h * count, at + step)]
+                parts = [(pd_ref, h, h, at + step)]
                 if h:
-                    parts.append((pc_ref, 0, 0, count))
-                for p_ref, p_at, key_at, keys in parts:
-                    source = key_at // count
+                    parts.append((pc_ref, 0, 2, count))
+                for p_ref, p_at, to, keys in parts:
+                    source = 0 if to == 2 else h
+                    prob_grad = dot_nt(mine, v_ref[0, source, :keys, :])
                     p = p_ref[p_at, a, rows, :keys]
-                    prob_grad = dot_nt(mine, v_ref[0, source, :keys, :])
                     score = (p.astype(F32) * (prob_grad - along)).astype(BF)
+                    scores[to, a, rows, :keys] = score
                     k = jnp.where(lane == a, k_ref[0, source, :keys, :], 0.0).astype(BF)
                     query = query + dot(score, k)
-                    cols = pl.ds(key_at, keys)
-                    key_acc[line, cols] += dot(q_t[a * HEAD_DIM : (a + 1) * HEAD_DIM], score)
-                    value_acc[line, cols] += dot(low_t[a * HEAD_DIM : (a + 1) * HEAD_DIM], p)
             queries[pl.ds(h * count + at, step), :] = query * 0.125
+    low_t = [jnp.transpose(scaled[h]).astype(BF) for h in (0, 1)]
+    q_t = [jnp.transpose(q_ref[0, h].astype(F32)).astype(BF) for h in (0, 1)]
+    for a in (0, 1):
+        line = slice(a * HEAD_DIM, (a + 1) * HEAD_DIM)
+        key_acc[line, :count] = dot(q_t[0][line], scores[0, a]) + dot(q_t[1][line], scores[2, a])
+        key_acc[line, count:] = dot(q_t[1][line], scores[1, a])
+        value_acc[line, :count] = dot(low_t[0][line], pd_ref[0, a]) + dot(
+            low_t[1][line], pc_ref[0, a]
+        )
+        value_acc[line, count:] = dot(low_t[1][line], pd_ref[1, a])
 
     query = queries[...]
     key_t = key_acc[...] * 0.125
@@ -851,6 +921,7 @@
             other_context, inverse, first, weight, gain, second, own_output,
         ],
         after=after,
+        flops=ATTBACK_FLOPS,
         prefetch=[at],
         grid=(cols // PAIR,),
         in_specs=[
@@ -879,44 +950,52 @@
             pltpu.VMEM((PAIR, 2 * count), F32),
             pltpu.VMEM((2 * count, PAIR), F32),
             pltpu.VMEM((3 * PAIR, width), F32),
+            pltpu.VMEM((3, 2, count, count), BF),
         ],
         out_shape=out,
         name="attend_back",
     )
 
 
-def weight_outputs_kernel(core_ref, kept_ref, got_ref, project_ref, output_ref, gains_ref):
+def weight_outputs_kernel(rows, core_ref, kept_ref, got_ref, project_ref, output_ref, gains_ref):
     group, groups = pl.program_id(0), pl.num_programs(0)
     size = 3 * PAIR // 2
 
-    def halves_of(start, rows):
-        cut = pl.ds(start, rows)
-        kept, got = kept_ref[cut, :].astype(F32), got_ref[cut, :].astype(F32)
+    def halves_of(cut, which):
+        kept, got = [
+            jnp.concatenate([ref[block, cut, :] for block in which], axis=0).astype(F32)
+            for ref in (kept_ref, got_ref)
+        ]
         low = jnp.where(core_ref[0] == 0, kept, got)
         return low, jnp.where(core_ref[0] == 0, got, kept)
 
-    low, high = halves_of(pl.multiple_of(group * size, size), size)
+    body, blocks = slice(0, rows), size // rows
+    low, high = halves_of(body, [group * blocks + i for i in range(blocks)])
     flat = jnp.transpose(jnp.concatenate([low, high], axis=0))
     for c in range(3):
         project_ref[c] = flat[:, c * PAIR : (c + 1) * PAIR]
 
     @pl.when(group == groups - 1)
     def _():
-        part = output_ref.shape[0] // 2
-        output_ref[:part], output_ref[part:] = halves_of(groups * size, part)
-        for i, rows in enumerate(halves_of(groups * size + part, 16)):
-            gains_ref[i : i + 1] = rows[0:1] + rows[1:2]
+        part, count = output_ref.shape[0] // 2, kept_ref.shape[0]
+        first = groups * size // rows
+        output_ref[:part], output_ref[part:] = halves_of(body, range(first, count))
+        tails = halves_of(slice(rows, rows + 16), range(count))
+        for i, tail in enumerate(tails):
+            gains_ref[i : i + 1] = sum(
+                tail[16 * b : 16 * b + 1] + tail[16 * b + 1 : 16 * b + 2] for b in range(count)
+            )
 
 
 def weight_outputs(core, kept, got, cols, after=()):
-    lines, width = kept.shape
+    _, rows, width = kept.shape
     return call(
-        weight_outputs_kernel,
+        functools.partial(weight_outputs_kernel, rows - 16),
         [kept, got],
         after=after,
         prefetch=[core.reshape(1).astype(jnp.int32)],
         grid=(cols // PAIR,),
-        in_specs=[whole((lines, width))] * 2,
+        in_specs=[whole(kept.shape)] * 2,
         out_specs=[
             pl.BlockSpec((3, width, PAIR), lambda g, w: (0, 0, g)),
             whole((cols, width)),
@@ -964,7 +1043,7 @@
     one_hot = relative[:, None] == jnp.arange(expert_count, dtype=jnp.int32)[None, :]
     rank_table = jnp.cumsum(one_hot.astype(jnp.int32), axis=0) - 1
     slot_index = relative * capacity + jnp.sum(jnp.where(one_hot, rank_table, 0), axis=1)
-    slot_row, slot_col = slot_index[None, :], slot_index[:, None]
+    slot_row = slot_index[None, :]
     absolute = slot_index + (chosen - relative) * capacity
     order = [my_expert ^ k for k in range(expert_count)]
 
@@ -1027,19 +1106,21 @@
     )
     outer_got = swap(outer_sent, "core", 1, "outer_core")
     inner_got = swap(inner_sent, "core", 1, "inner_core")
-    outer_kept, inner_kept = weight_parts(
-        core, row_blocks, grad_blocks, order, activated, pre_grad, after=[inner_sent]
+    token = touch([jnp.zeros((8, 128), F32)], [inner_sent], flops=BACK_FLOPS)
+    outer_parts, inner_parts = weight_sums(
+        core, 1 - side(*outer_steps[0]), 1 - side(*inner_steps[0]), row_blocks, grad_blocks, order,
+        activated, pre_grad, outer_got, inner_got, after=token,
     )
 
     hidden_grad, hidden_low, second_gain_part, own_grad, grad_sent = second_back(
         output_cotangent,
         hidden,
         second_gain,
-        slot_col,
+        slot_row,
         output_weight,
         other_weight,
         returned,
-        after=[inner_kept],
+        after=[inner_parts[0]],
     )
     other_grad = swap(grad_sent, "head", 1, "context_grad")
     def pairs_of(outer, inner, i):
@@ -1048,29 +1129,16 @@
             (inner[1], swap(inner[0], *inner_steps[i], f"inner{i}")),
         ]
 
-    outer_parts, inner_parts = split_sums(
-        (outer_kept, outer_got),
-        (inner_kept, inner_got),
-        1 - side(*outer_steps[0]),
-        1 - side(*inner_steps[0]),
-        after=[grad_sent],
-    )
-
-    combined = exchange_all(touch([produced], [grad_sent])[0])
     own_output, output_kept, output_sent = output_weight_parts(
         core, own_context, got_context, hidden_low, after=[grad_sent]
     )
-    (output_sent,) = add(output_kept, swap(output_sent, "core", 1, "output_core"), [0 * core])
-    output_sent, outer_sent, inner_sent = touch(
-        [output_sent, outer_parts[0], inner_parts[0]], [other_grad]
-    )
+    output_sent = add(output_kept, swap(output_sent, "core", 1, "output_core"))
+    combined = exchange_all(touch([produced], [output_sent])[0])
     got_output = swap(output_sent, "head", 1, "output_grad")
-    outer_parts, inner_parts = [outer_sent, outer_parts[1]], [inner_sent, inner_parts[1]]
 
     groups = local_cols // PAIR
     end = 2 * local_cols
-    grain = 16 * expert_count * lax.axis_size("x")
-    lines = -(-(end + 16) // grain) * grain
+    lines = end + 16
     sent, kept, mine, theirs = attend_back(
         jnp.stack([my_head, core]).astype(jnp.int32), own_grad, other_grad, projected, p_diag,
         p_cross, own_context, other_context, inverse, first_low, project_weight, first_gain,
@@ -1083,26 +1151,26 @@
             [halves(outer_steps[i + 1]), halves(inner_steps[i + 1])],
             after=[kept],
         )
-    more = touch([got_output], [*outer_parts, combined], flops=BACK_FLOPS)
+    more = touch([got_output], outer_parts, flops=BACK_FLOPS)
     got = swap(sent, "core", 1, "weight")
-    (summed,) = add(kept, got, [0 * core], more=more, more_at=at)
+    summed, tail = gather_sum(kept, got, more[0], end, after=more)
     crowd = ("x", "expert")
-    summed = summed.reshape(-1, lines // lax.axis_size(crowd), model_width)
+    summed = summed.reshape(-1, end // lax.axis_size(crowd), model_width)
     arrived = lax.all_to_all(summed, crowd, split_axis=0, concat_axis=0, tiled=True)
     theirs = swap(theirs, "head", 1, "theirs")
-    block_output = output_rows(hidden, absolute[:, None], combined, after=[summed])
+    block_output = output_rows(hidden, absolute[None, :], combined, after=[summed])
     input_grad = first_back(
         block_input, first_gain, hidden_grad, mine, theirs, after=[block_output]
     )
     (outer_own,), (inner_own,) = adds(
         pairs_of(outer_parts, inner_parts, -1), [[0 * core]] * 2, after=[input_grad]
     )
-    outer_pieces = gather_pieces(outer_own, outer_steps, outer_steps[::-1])
-    inner_pieces = gather_pieces(inner_own, inner_steps, inner_steps[::-1])
-    arrived = total(arrived, after=[outer_own, inner_own])
+    outer_pieces = gather_pieces(outer_own, outer_steps, outer_steps[::-1], BACK_FLOPS)
+    inner_pieces = gather_pieces(inner_own, inner_steps, inner_steps[::-1], 1)
+    arrived = total(arrived, tail, after=[outer_own, inner_own])
     summed = lax.all_to_all(arrived, crowd, split_axis=0, concat_axis=0, tiled=True)
 
-    def whole_sum(own_core, other_core, is_outer, earlier, after):
+    def chosen_pieces(own_core, other_core, is_outer):
         half = 1 << (len(turns) - 1)
 
         def placed(place, which):
@@ -1110,19 +1178,11 @@
                 return which * 2 * half + place, 0 * place
             return place % half, which * 2 + place // half
 
-        chosen = [
+        return [
             (piece, placed(at, which))
             for pieces, which in ((own_core, core), (other_core, 1 - core))
             for at, piece in pieces
         ]
-        return assemble(
-            [piece for piece, _ in chosen],
-            [place for _, place in chosen],
-            (outer_weight if is_outer else inner_weight).shape,
-            earlier,
-            after=after,
-            flops=1,
-        )[0]
 
     early = len(turns) + 1
 
@@ -1137,22 +1197,36 @@
     for is_outer, own_core, other_core in zip(
         (True, False), (outer_pieces, inner_pieces), others
     ):
-        totals.append(
-            whole_sum(own_core[:early], other_core, is_outer, [], [arrived] + totals[-1:])
+        chosen = chosen_pieces(own_core[:early], other_core, is_outer)
+        totals += assemble(
+            [piece for piece, _ in chosen],
+            [place for _, place in chosen],
+            (outer_weight if is_outer else inner_weight).shape,
+            [],
+            after=[arrived] + totals[-1:],
         )
     late = []
     for pieces in (outer_pieces, inner_pieces):
         held = touch([piece for _, piece in pieces[early:]], totals)
         late.append([(at, piece) for (at, _), piece in zip(pieces[early:], held)])
     late_others = [core_swaps(pieces) for pieces in late]
-    kept = touch([summed], [pieces[0][1] for pieces in late])[0].reshape(lines, model_width)
+    (kept,) = touch([summed], [pieces[0][1] for pieces in late])
     got = swap(kept, "core", 1, "weight_back")
     project_grad, output_weight_grad, gains = weight_outputs(
         core, kept, got, local_cols
     )
     gains = gains + swap(gains, "head", 1, "gains")
-    outer_total = whole_sum(late[0], late_others[0], True, totals[:1], [project_grad])
-    inner_total = whole_sum(late[1], late_others[1], False, totals[1:], [outer_total])
+    outer_late, inner_late = [
+        chosen_pieces(own_core, other_core, is_outer)
+        for own_core, other_core, is_outer in zip(late, late_others, (True, False))
+    ]
+    outer_total, inner_total = assemble_two(
+        [piece for piece, _ in outer_late],
+        [piece for piece, _ in inner_late],
+        [place for _, place in outer_late + inner_late],
+        totals,
+        after=[project_grad],
+    )
     return (
         block_output,
         input_grad,

time: 344 us -> 315 us (0.916)
  Pallas kernels: 188 us -> 171 us
  waiting for transfers between devices: 68 us -> 57.2 us
    pallas_call x36, Pallas kernels: 188 us -> 171 us  [call(): pl.pallas_call(body, input_output_aliases={first + i: i for i in range(le...]
    ppermute x37, waiting for transfers between devices: 56.8 us -> 48.4 us  [swap(): return lax.ppermute(values, axis, [(i, i ^ bit) for i in range(size)])]
    all_to_all x1, waiting for transfers between devices: 10.9 us -> 4.32 us  [on_device(): lax.all_to_all(summed, crowd, split_axis=0, concat_axis=0, tiled=True)]
    all_to_all x2, waiting for transfers between devices: 0.24 us -> 4.46 us  [exchange_all(): lax.all_to_all(blocks, 'expert', split_axis=0, concat_axis=0, tiled=True)]
  transfers between devices with their start and end apart: 41 -> 41, of which waited for: 12 -> 14; matrix products, arithmetic and copies ran while one was open for 7% -> 8% of each run, Pallas kernels for 50% -> 53%
where the time goes in v2:
time: 315 us; the launch traced here: 310 us
  Pallas kernels  171 us (54%)
  waiting for transfers between devices  57.2 us (18%)
  starting transfers between devices  54.9 us (17%)
  local copies, waits for them, and re-layouts  15.2 us (5%)
  other arithmetic  10.4 us (3%)
    pallas_call x36, Pallas kernels, call(): pl.pallas_call(body, input_output_aliases={first + i: i for i in range(le...  171 us
    ppermute x37, waiting for transfers between devices, swap(): return lax.ppermute(values, axis, [(i, i ^ bit) for i in range(size)])  48.4 us
    ppermute x37, starting transfers between devices, swap(): return lax.ppermute(values, axis, [(i, i ^ bit) for i in range(size)])  36.6 us
    all_to_all x2, starting transfers between devices, exchange_all(): lax.all_to_all(blocks, 'expert', split_axis=0, concat_axis=0, tiled=True)  9.56 us
  transfers between devices with their start and end apart: 41, of which 14 were waited for; matrix products, arithmetic and copies ran while one was open for 8% of the time, Pallas kernels for 53%

profile of v2, /device:TPU:0, one launch (start us, length us, event | category | flops | bytes accessed | tf_op | source)
XLA Modules:
  0.0 309.9 jit_solution(9512649100910844783)
XLA Ops:
  16.7 4.5 %project.2 = (bf16[2,512,768]{2,1,0:T(8,128)(2,1)}, bf16[3,2,512,384]{3,2,1,0:T(8,128)(2,1)}) custom-call(s32[1]{0:T(128)} %bitcast.refs_0_, bf16[512,768]{1,0:T(8,128)(2,1)} %refs_0_.8, f32[1,768]{1,0:T(1,128)} %reshape.137.refs_2_.refs_13_.refs_1_, bf16[3,768,384]{2,1,0:T(8,128)(2,1)} %refs_12_.1, bf16[4,256,768]{2,1,0:T(8,128)(2,1)} %sent_rows.1.refs_4_, ...), custom_call_target="tpu_custom_call" | custom-call | flops 1 | bytes 1 | tf_op jit(solution)/shard_map/project/pallas_call | solution.py:84
  23.1 5.1 %all-to-all-start = ((bf16[4,256,768]{2,1,0:T(8,128)(2,1)}), bf16[4,256,768]{2,1,0:T(8,128)(2,1)}, u32[]{:S(2)}, u32[]{:S(2)}) async-start(bf16[4,256,768]{2,1,0:T(8,128)(2,1)} %sent_rows.1.refs_4_), calls=%async_computation | async-start | bytes 3145728 | tf_op jit(solution)/shard_map/all_to_all | solution.py:1057
  30.6 4.5 %project.3 = (bf16[2,512,768]{2,1,0:T(8,128)(2,1)}, bf16[3,2,512,384]{3,2,1,0:T(8,128)(2,1)}) custom-call(s32[1]{0:T(128)S(6)} %sub.72.refs_0_, bf16[512,768]{1,0:T(8,128)(2,1)} %collective-permute-done.refs_1_, f32[1,768]{1,0:T(1,128)} %reshape.137.refs_2_.refs_13_.refs_1_, ...), custom_call_target="tpu_custom_call", output_to_operand_aliasing={{0}: (4, {}), {1}: (5, {})} | custom-call | flops 1 | bytes 1 | tf_op jit(solution)/shard_map/project/pallas_call | solution.py:84
  35.1 8.6 %attend.2 = (bf16[2,6,512,512]{3,2,1,0:T(8,128)(2,1)}, bf16[2,6,512,512]{3,2,1,0:T(8,128)(2,1)}, f32[2,512,384]{2,1,0:T(8,128)}, bf16[512,384]{1,0:T(8,128)(2,1)}) custom-call(s32[1]{0:T(128)S(6)} %sub.72.refs_0_, bf16[3,2,512,384]{3,2,1,0:T(8,128)(2,1)} %get-tuple-element.75.refs_1_.refs_2_.refs_3_.refs_4_.refs_5_, ...), custom_call_target="tpu_custom_call" | custom-call | flops 1 | bytes 1 | tf_op jit(solution)/shard_map/attend/pallas_call | solution.py:84
  43.7 6.8 %attend.3 = (bf16[2,6,512,512]{3,2,1,0:T(8,128)(2,1)}, bf16[2,6,512,512]{3,2,1,0:T(8,128)(2,1)}, f32[2,512,384]{2,1,0:T(8,128)}, bf16[512,384]{1,0:T(8,128)(2,1)}) custom-call(s32[1]{0:T(128)} %bitcast.refs_0_, ...), custom_call_target="tpu_custom_call", output_to_operand_aliasing={{0}: (7, {}), {1}: (8, {}), {2}: (9, {})} | custom-call | flops 20000000000 | bytes 1 | tf_op jit(solution)/shard_map/attend/pallas_call | solution.py:84
  53.8 5.2 %hidden_rows.1 = (f32[512,768]{1,0:T(8,128)}, bf16[256,768]{1,0:T(8,128)(2,1)}, bf16[256,768]{1,0:T(8,128)(2,1)}, bf16[256,768]{1,0:T(8,128)(2,1)}, bf16[256,768]{1,0:T(8,128)(2,1)}) custom-call(bf16[512,768]{1,0:T(8,128)(2,1)} %refs_0_.8, bf16[512,384]{1,0:T(8,128)(2,1)} %get-tuple-element.79.refs_1_.refs_8_, ...), custom_call_target="tpu_custom_call" | custom-call | flops 1 | bytes 1 | tf_op jit(solution)/shard_map/hidden_rows/pallas_call | solution.py:84
  65.5 9.7 %expert.3 = (bf16[1024,3072]{1,0:T(8,128)(2,1)}, bf16[1024,3072]{1,0:T(8,128)(2,1)}, bf16[4,256,768]{2,1,0:T(8,128)(2,1)}, bf16[256,768]{1,0:T(8,128)(2,1)}) custom-call(s32[1]{0:T(128)} %bitcast.12.refs_0_, bf16[256,768]{1,0:T(8,128)(2,1)} %get-tuple-element.85.refs_1_.refs_4_, bf16[4,256,768]{2,1,0:T(8,128)(2,1)} %all-to-all-done.refs_2_.refs_3_.refs_4_.refs_8_, ...), custom_call_target="tpu_custom_call" | custom-call | flops 1 | bytes 1 | tf_op jit(solution)/shard_map/expert/pallas_call | solution.py:84
  75.2 6.7 %collective-permute-done.6.refs_1_.refs_5_ = bf16[256,768]{1,0:T(8,128)(2,1)} collective-permute-done((bf16[256,768]{1,0:T(8,128)(2,1)}, bf16[256,768]{1,0:T(8,128)(2,1)}, u32[]{:S(2)}, u32[]{:S(2)}) %collective-permute-start.6) | collective-permute-done | bytes 393248 | tf_op jit(solution)/shard_map/dispatch1/ppermute | solution.py:19
  81.9 9.9 %expert.4 = (bf16[1024,3072]{1,0:T(8,128)(2,1)}, bf16[1024,3072]{1,0:T(8,128)(2,1)}, bf16[4,256,768]{2,1,0:T(8,128)(2,1)}, bf16[256,768]{1,0:T(8,128)(2,1)}) custom-call(s32[1]{0:T(128)} %bitcast.11.refs_0_, bf16[256,768]{1,0:T(8,128)(2,1)} %collective-permute-done.6.refs_1_.refs_5_, ...), custom_call_target="tpu_custom_call", output_to_operand_aliasing={{0}: (5, {}), {1}: (6, {}), {2}: (7, {})} | custom-call | flops 1 | bytes 1 | tf_op jit(solution)/shard_map/expert/pallas_call | solution.py:84
  91.8 16.3 %expert.5 = (bf16[1024,3072]{1,0:T(8,128)(2,1)}, bf16[1024,3072]{1,0:T(8,128)(2,1)}, bf16[4,256,768]{2,1,0:T(8,128)(2,1)}, bf16[256,768]{1,0:T(8,128)(2,1)}, bf16[256,768]{1,0:T(8,128)(2,1)}) custom-call(s32[2]{0:T(128)} %pad_add_fusion.9.refs_0_, ...), custom_call_target="tpu_custom_call", output_to_operand_aliasing={{0}: (7, {}), {1}: (8, {}), {2}: (9, {})} | custom-call | flops 1 | bytes 1 | tf_op jit(solution)/shard_map/expert/pallas_call | solution.py:84
  108.1 6.9 %collective-permute-start.8 = (bf16[256,768]{1,0:T(8,128)(2,1)}, bf16[256,768]{1,0:T(8,128)(2,1)}, u32[]{:S(2)}, u32[]{:S(2)}) collective-permute-start(bf16[256,768]{1,0:T(8,128)(2,1)} %get-tuple-element.95.refs_9_), channel_id=1, source_target_pairs={{0,4},{2,6},{4,0},{6,2},{1,5},{3,7},{5,1},{7,3},{8,12},{10,14},{12... | collective-permute-start | bytes 1179656 | tf_op jit(solution)/shard_map/return2/ppermute | solution.py:19
  117.4 11.2 %weight_parts.1 = (bf16[1536,768]{1,0:T(8,128)(2,1)}, bf16[768,1536]{1,0:T(8,128)(2,1)}) custom-call(s32[1]{0:T(128)} %bitcast.16.refs_0_, s32[4]{0:T(128)} %pad_add_fusion.11.refs_1_, bf16[1024,3072]{1,0:T(8,128)(2,1)} %get-tuple-element.97.refs_2_, bf16[1024,3072]{1,0:T(8,128)(2,1)} %get-tuple-element.98.refs_3_, ...), custom_call_target="tpu_custom_call" | custom-call | flops 1 | bytes 1 | tf_op jit(solution)/shard_map/weight_parts/pallas_call | solution.py:84
  129.7 3.8 %collective-permute-done.10.refs_9_ = bf16[1536,768]{1,0:T(8,128)(2,1)} collective-permute-done((bf16[1536,768]{1,0:T(8,128)(2,1)}, bf16[1536,768]{1,0:T(8,128)(2,1)}, u32[]{:S(2)}, u32[]{:S(2)}) %collective-permute-start.10) | collective-permute-done | bytes 2359328 | tf_op jit(solution)/shard_map/outer_core/ppermute | solution.py:19
  136.8 13.2 %weight_sums.1 = (bf16[768,768]{1,0:T(8,128)(2,1)}, bf16[768,768]{1,0:T(8,128)(2,1)}, bf16[768,768]{1,0:T(8,128)(2,1)}, bf16[768,768]{1,0:T(8,128)(2,1)}) custom-call(s32[3]{0:T(128)} %pad_add_fusion.10.refs_0_, s32[4]{0:T(128)} %pad_add_fusion.11.refs_1_, bf16[1024,3072]{1,0:T(8,128)(2,1)} %get-tuple-element.97.refs_2_, ...), custom_call_target="tpu_custom_call" | custom-call | flops 1 | bytes 1 | tf_op jit(solution)/shard_map/weight_sums/pallas_call | solution.py:84
  150.0 6.3 %second_back.1 = (f32[512,768]{1,0:T(8,128)}, bf16[512,768]{1,0:T(8,128)(2,1)}, f32[1,768]{1,0:T(1,128)}, bf16[512,384]{1,0:T(8,128)(2,1)}, bf16[512,384]{1,0:T(8,128)(2,1)}) custom-call(bf16[512,768]{1,0:T(8,128)(2,1)} %refs_0_.7, f32[512,768]{1,0:T(8,128)} %get-tuple-element.81.refs_1_.refs_0_, f32[1,768]{1,0:T(1,128)} %reshape.139.refs_5_.refs_2_, ...), custom_call_target="tpu_custom_call" | custom-call | flops 299999985664 | bytes 1 | tf_op jit(solution)/shard_map/second_back/pallas_call | solution.py:84
  166.4 4.5 %all-to-all-start.1 = ((bf16[4,256,768]{2,1,0:T(8,128)(2,1)}), bf16[4,256,768]{2,1,0:T(8,128)(2,1)}, u32[]{:S(2)}, u32[]{:S(2)}) async-start(bf16[4,256,768]{2,1,0:T(8,128)(2,1)} %touch.13), calls=%async_computation.1 | async-start | bytes 3145728 | tf_op jit(solution)/shard_map/all_to_all | solution.py:1057
  170.9 21.4 %attend_back.1 = (bf16[784,768]{1,0:T(8,128)(2,1)}, bf16[784,768]{1,0:T(8,128)(2,1)}, f32[512,768]{1,0:T(8,128)}, bf16[512,768]{1,0:T(8,128)(2,1)}) custom-call(s32[2]{0:T(128)} %pad_add_fusion.12.refs_0_, bf16[512,384]{1,0:T(8,128)(2,1)} %get-tuple-element.106.refs_1_, bf16[512,384]{1,0:T(8,128)(2,1)} %collective-permute-done.13.refs_2_, ...), custom_call_target="tpu_custom_call" | custom-call | flops 49999998976 | bytes 1 | tf_op jit(solution)/shard_map/attend_back/pallas_call | solution.py:84
  194.0 4.9 %adds.2 = (bf16[384,768]{1,0:T(8,128)(2,1)}, bf16[384,768]{1,0:T(8,128)(2,1)}, bf16[384,768]{1,0:T(8,128)(2,1)}, bf16[384,768]{1,0:T(8,128)(2,1)}) custom-call(s32[4]{0:T(128)} %pad_add_fusion.13.refs_0_, bf16[768,768]{1,0:T(8,128)(2,1)} %get-tuple-element.115.refs_1_, bf16[768,768]{1,0:T(8,128)(2,1)} %collective-permute-done.16.refs_2_, ...), custom_call_target="tpu_custom_call" | custom-call | flops 1 | bytes 1 | tf_op jit(solution)/shard_map/adds/pallas_call | solution.py:84
  203.8 4.2 %all-to-all-done.1.refs_2_ = bf16[4,256,768]{2,1,0:T(8,128)(2,1)} async-done(((bf16[4,256,768]{2,1,0:T(8,128)(2,1)}), bf16[4,256,768]{2,1,0:T(8,128)(2,1)}, u32[]{:S(2)}, u32[]{:S(2)}) %all-to-all-start.1) | async-done | bytes 1572896 | tf_op jit(solution)/shard_map/all_to_all | solution.py:1057
  208.0 4.3 %all-to-all-start.2 = ((bf16[8,96,768]{2,1,0:T(8,128)(2,1)}), bf16[8,96,768]{2,1,0:T(8,128)(2,1)}, u32[]{:S(2)}, u32[]{:S(2)}) async-start(bf16[8,96,768]{2,1,0:T(8,128)(2,1)} %bitcast.96), calls=%async_computation.2 | async-start | bytes 2359296 | tf_op jit(solution)/shard_map/all_to_all | solution.py:1159
  212.3 3.8 %output_rows.1.refs_5_ = bf16[512,768]{1,0:T(8,128)(2,1)} custom-call(f32[512,768]{1,0:T(8,128)} %get-tuple-element.81.refs_1_.refs_0_, s32[1,512]{1,0:T(1,128)} %bitcast.100, bf16[4,256,768]{2,1,0:T(8,128)(2,1)} %all-to-all-done.1.refs_2_, bf16[8,96,768]{2,1,0:T(8,128)(2,1)} %bitcast.97), custom_call_target="tpu_custom_call" | custom-call | flops 1 | bytes 1 | tf_op jit(solution)/shard_map/output_rows/pallas_call | solution.py:84
  217.0 4.5 %first_back.1.refs_5_ = f32[512,768]{1,0:T(8,128)} custom-call(bf16[512,768]{1,0:T(8,128)(2,1)} %refs_0_.8, f32[1,768]{1,0:T(1,128)} %reshape.137.refs_2_.refs_13_.refs_1_, f32[512,768]{1,0:T(8,128)} %get-tuple-element.121.refs_2_, f32[512,768]{1,0:T(8,128)} %get-tuple-element.122.refs_3_, bf16[512,768]{1,0:T(8,128)(2,1)} %collective-permute-done.18.refs_4_, ...), custom_call_target="tpu_custom_call" | custom-call | flops 299999985664 | bytes 1 | tf_op jit(solution)/shard_map/first_back/pallas_call | solution.py:84
  221.6 7.4 %collective-permute-done.19.refs_2_ = bf16[384,768]{1,0:T(8,128)(2,1)} collective-permute-done((bf16[384,768]{1,0:T(8,128)(2,1)}, bf16[384,768]{1,0:T(8,128)(2,1)}, u32[]{:S(2)}, u32[]{:S(2)}) %collective-permute-start.19) | collective-permute-done | bytes 589856 | tf_op jit(solution)/shard_map/outer-1/ppermute | solution.py:19
  229.5 3.5 %adds.3 = (bf16[384,768]{1,0:T(8,128)(2,1)}, bf16[384,768]{1,0:T(8,128)(2,1)}) custom-call(s32[2]{0:T(128)} %broadcast_2_refs_0_.2.refs_0_, bf16[384,768]{1,0:T(8,128)(2,1)} %get-tuple-element.119.refs_2_.refs_1_, bf16[384,768]{1,0:T(8,128)(2,1)} %collective-permute-done.19.refs_2_, bf16[384,768]{1,0:T(8,128)(2,1)} %get-tuple-element.125.refs_3_, ...), custom_call_target="tpu_custom_call" | custom-call | flops 1 | bytes 1 | tf_op jit(solution)/shard_map/adds/pallas_call | solution.py:84
  237.0 4.3 %all-to-all-done.2.refs_0_ = bf16[8,96,768]{2,1,0:T(8,128)(2,1)} async-done(((bf16[8,96,768]{2,1,0:T(8,128)(2,1)}), bf16[8,96,768]{2,1,0:T(8,128)(2,1)}, u32[]{:S(2)}, u32[]{:S(2)}) %all-to-all-start.2) | async-done | bytes 1179680 | tf_op jit(solution)/shard_map/all_to_all | solution.py:1159
  243.8 4.5 %all-to-all-start.3 = ((bf16[8,112,768]{2,1,0:T(8,128)(2,1)}), bf16[8,112,768]{2,1,0:T(8,128)(2,1)}, u32[]{:S(2)}, u32[]{:S(2)}) async-start(bf16[8,112,768]{2,1,0:T(8,128)(2,1)} %total.1.refs_1_.refs_7_), calls=%async_computation.3 | async-start | bytes 2752512 | tf_op jit(solution)/shard_map/all_to_all | solution.py:1171
  249.5 4.9 %collective-permute-done.22.refs_1_ = bf16[384,768]{1,0:T(8,128)(2,1)} collective-permute-done((bf16[384,768]{1,0:T(8,128)(2,1)}, bf16[384,768]{1,0:T(8,128)(2,1)}, u32[]{:S(2)}, u32[]{:S(2)}) %collective-permute-start.22) | collective-permute-done | bytes 589856 | tf_op jit(solution)/shard_map/piece/ppermute | solution.py:19
  258.8 12.2 %collective-permute-done.27.refs_0_ = bf16[384,768]{1,0:T(8,128)(2,1)} collective-permute-done((bf16[384,768]{1,0:T(8,128)(2,1)}, bf16[384,768]{1,0:T(8,128)(2,1)}, u32[]{:S(2)}, u32[]{:S(2)}) %collective-permute-start.27) | collective-permute-done | bytes 589856 | tf_op jit(solution)/shard_map/piece/ppermute | solution.py:19
  275.8 6.4 %assemble.2.refs_8_.refs_1_.refs_5_ = f32[3072,768]{1,0:T(8,128)} custom-call(s32[6,2]{1,0:T(8,128)} %stack.271.refs_0_, bf16[384,768]{1,0:T(8,128)(2,1)} %get-tuple-element.127.refs_2_.refs_1_, bf16[384,768]{1,0:T(8,128)(2,1)} %get-tuple-element.129.refs_2_, bf16[384,768]{1,0:T(8,128)(2,1)} %get-tuple-element.130.refs_3_, ...), custom_call_target="tpu_custom_call" | custom-call | flops 1 | bytes 1 | tf_op jit(solution)/shard_map/assemble/pallas_call | solution.py:84
  282.2 6.4 %assemble.3.refs_2_.refs_6_ = f32[768,3072]{1,0:T(8,128)} custom-call(s32[6,2]{1,0:T(8,128)} %stack.293.refs_0_, bf16[384,768]{1,0:T(8,128)(2,1)} %get-tuple-element.128.refs_3_.refs_1_, bf16[384,768]{1,0:T(8,128)(2,1)} %get-tuple-element.131.refs_2_, bf16[384,768]{1,0:T(8,128)(2,1)} %get-tuple-element.132.refs_3_, ...), custom_call_target="tpu_custom_call" | custom-call | flops 1 | bytes 1 | tf_op jit(solution)/shard_map/assemble/pallas_call | solution.py:84
  295.3 4.9 %weight_outputs.1 = (f32[3,768,384]{2,1,0:T(8,128)}, f32[384,768]{1,0:T(8,128)}, f32[2,768]{1,0:T(2,128)}) custom-call(s32[1]{0:T(128)} %bitcast.13.refs_0_, bf16[8,112,768]{2,1,0:T(8,128)(2,1)} %touch.21.refs_1_, bf16[8,112,768]{2,1,0:T(8,128)(2,1)} %collective-permute-done.33.refs_2_), custom_call_target="tpu_custom_call" | custom-call | flops 1 | bytes 1 | tf_op jit(solution)/shard_map/weight_outputs/pallas_call | solution.py:84
  303.0 5.3 %assemble_two.1 = (f32[3072,768]{1,0:T(8,128)}, f32[768,3072]{1,0:T(8,128)}) custom-call(s32[4,2]{1,0:T(4,128)} %pad_add_fusion.refs_0_, bf16[384,768]{1,0:T(8,128)(2,1)} %touch.19.refs_1_, bf16[384,768]{1,0:T(8,128)(2,1)} %collective-permute-done.35.refs_2_, bf16[384,768]{1,0:T(8,128)(2,1)} %touch.20.refs_2_.refs_3_, ...), custom_call_target="tpu_custom_call", output_to_operand_aliasing={{0}: (5, {}), {1}: (6, {})} | custom-call | flops 1 | bytes 1 | tf_op jit(solution)/shard_map/assemble_two/pallas_call | solution.py:84
  (131 shorter events, 82.8 us)
Async XLA Ops:
  0.6 16.1 %collective-permute-start.1 = (s32[512]{0:T(512)}, s32[512]{0:T(512)}, u32[]{:S(2)}, u32[]{:S(2)}) collective-permute-start(s32[512]{0:T(512)} %param.14), channel_id=1, source_target_pairs={{0,1},{1,0},{2,3},{3,2},{4,5},{5,4},{6,7},{7,6},{8,9},{9,8},{10,11... | collective-permute-start | bytes 6152 | tf_op jit(solution)/shard_map/positions/ppermute | solution.py:19
  3.7 26.9 %collective-permute-start = (bf16[512,768]{1,0:T(8,128)(2,1)}, bf16[512,768]{1,0:T(8,128)(2,1)}, u32[]{:S(2)}, u32[]{:S(2)}) collective-permute-start(bf16[512,768]{1,0:T(8,128)(2,1)} %refs_0_.8), channel_id=1, source_target_pairs={{0,1},{1,0},{2,3},{3,2},{4,5},{5,4},{6,7},{7,6},{8,9},{9,8},{10,11... | collective-permute-start | bytes 2359304 | tf_op jit(solution)/shard_map/rows/ppermute | solution.py:19
  21.2 22.6 %collective-permute-start.2 = (bf16[384,768]{1,0:T(8,128)(2,1)}, bf16[384,768]{1,0:T(8,128)(2,1)}, u32[]{:S(2)}, u32[]{:S(2)}) collective-permute-start(bf16[384,768]{1,0:T(8,128)(2,1)} %touch.11), channel_id=1, source_target_pairs={{0,1},{1,0},{2,3},{3,2},{4,5},{5,4},{6,7},{7,6},{8,9},{9,8},{10,11... | collective-permute-start | bytes 1769480 | tf_op jit(solution)/shard_map/output_weight/ppermute | solution.py:19
  23.1 42.4 %all-to-all-start = ((bf16[4,256,768]{2,1,0:T(8,128)(2,1)}), bf16[4,256,768]{2,1,0:T(8,128)(2,1)}, u32[]{:S(2)}, u32[]{:S(2)}) async-start(bf16[4,256,768]{2,1,0:T(8,128)(2,1)} %sent_rows.1.refs_4_), calls=%async_computation | async-start | bytes 3145728 | tf_op jit(solution)/shard_map/all_to_all | solution.py:1057
  59.0 22.9 %collective-permute-start.6 = (bf16[256,768]{1,0:T(8,128)(2,1)}, bf16[256,768]{1,0:T(8,128)(2,1)}, u32[]{:S(2)}, u32[]{:S(2)}) collective-permute-start(bf16[256,768]{1,0:T(8,128)(2,1)} %get-tuple-element.84), channel_id=1, source_target_pairs={{0,2},{2,0},{4,6},{6,4},{1,3},{3,1},{5,7},{7,5},{8,10},{10,8},{12,... | collective-permute-start | bytes 1179656 | tf_op jit(solution)/shard_map/dispatch1/ppermute | solution.py:19
  60.7 31.1 %collective-permute-start.4 = (bf16[256,768]{1,0:T(8,128)(2,1)}, bf16[256,768]{1,0:T(8,128)(2,1)}, u32[]{:S(2)}, u32[]{:S(2)}) collective-permute-start(bf16[256,768]{1,0:T(8,128)(2,1)} %get-tuple-element.82), channel_id=1, source_target_pairs={{0,4},{2,6},{4,0},{6,2},{1,5},{3,7},{5,1},{7,3},{8,12},{10,14},{12... | collective-permute-start | bytes 1179656 | tf_op jit(solution)/shard_map/dispatch2/ppermute | solution.py:19
  63.1 28.7 %collective-permute-start.5 = (bf16[256,768]{1,0:T(8,128)(2,1)}, bf16[256,768]{1,0:T(8,128)(2,1)}, u32[]{:S(2)}, u32[]{:S(2)}) collective-permute-start(bf16[256,768]{1,0:T(8,128)(2,1)} %get-tuple-element.83), channel_id=1, source_target_pairs={{0,6},{2,4},{4,2},{6,0},{1,7},{3,5},{5,3},{7,1},{8,14},{10,12},{12... | collective-permute-start | bytes 1179656 | tf_op jit(solution)/shard_map/dispatch3/ppermute | solution.py:19
  91.8 58.2 %collective-permute-start.7 = (bf16[256,768]{1,0:T(8,128)(2,1)}, bf16[256,768]{1,0:T(8,128)(2,1)}, u32[]{:S(2)}, u32[]{:S(2)}) collective-permute-start(bf16[256,768]{1,0:T(8,128)(2,1)} %get-tuple-element.94), channel_id=1, source_target_pairs={{0,2},{2,0},{4,6},{6,4},{1,3},{3,1},{5,7},{7,5},{8,10},{10,8},{12,... | collective-permute-start | bytes 1179656 | tf_op jit(solution)/shard_map/return1/ppermute | solution.py:19
  108.1 41.9 %collective-permute-start.8 = (bf16[256,768]{1,0:T(8,128)(2,1)}, bf16[256,768]{1,0:T(8,128)(2,1)}, u32[]{:S(2)}, u32[]{:S(2)}) collective-permute-start(bf16[256,768]{1,0:T(8,128)(2,1)} %get-tuple-element.95.refs_9_), channel_id=1, source_target_pairs={{0,4},{2,6},{4,0},{6,2},{1,5},{3,7},{5,1},{7,3},{8,12},{10,14},{12... | collective-permute-start | bytes 1179656 | tf_op jit(solution)/shard_map/return2/ppermute | solution.py:19
  115.0 35.0 %collective-permute-start.9 = (bf16[256,768]{1,0:T(8,128)(2,1)}, bf16[256,768]{1,0:T(8,128)(2,1)}, u32[]{:S(2)}, u32[]{:S(2)}) collective-permute-start(bf16[256,768]{1,0:T(8,128)(2,1)} %get-tuple-element.96.refs_10_), channel_id=1, source_target_pairs={{0,6},{2,4},{4,2},{6,0},{1,7},{3,5},{5,3},{7,1},{8,14},{10,12},{12... | collective-permute-start | bytes 1179656 | tf_op jit(solution)/shard_map/return3/ppermute | solution.py:19
  156.3 14.6 %collective-permute-start.13 = (bf16[512,384]{1,0:T(8,128)(2,1)}, bf16[512,384]{1,0:T(8,128)(2,1)}, u32[]{:S(2)}, u32[]{:S(2)}) collective-permute-start(bf16[512,384]{1,0:T(8,128)(2,1)} %get-tuple-element.103.refs_4_), channel_id=1, source_target_pairs={{0,1},{1,0},{2,3},{3,2},{4,5},{5,4},{6,7},{7,6},{8,9},{9,8},{10,11... | collective-permute-start | bytes 1179656 | tf_op jit(solution)/shard_map/context_grad/ppermute | solution.py:19
  161.0 33.0 %collective-permute-start.17 = (bf16[768,768]{1,0:T(8,128)(2,1)}, bf16[768,768]{1,0:T(8,128)(2,1)}, u32[]{:S(2)}, u32[]{:S(2)}) collective-permute-start(bf16[768,768]{1,0:T(8,128)(2,1)} %get-tuple-element.101.refs_10_.refs_16_), channel_id=1, source_target_pairs={{0,1},{1,0},{2,3},{3,2},{4,5},{5,4},{6,7},{7,6},{8,9},{9,8},{10,11... | collective-permute-start | bytes 3538952 | tf_op jit(solution)/shard_map/inner0/ppermute | solution.py:19
  162.5 31.5 %collective-permute-start.16 = (bf16[768,768]{1,0:T(8,128)(2,1)}, bf16[768,768]{1,0:T(8,128)(2,1)}, u32[]{:S(2)}, u32[]{:S(2)}) collective-permute-start(bf16[768,768]{1,0:T(8,128)(2,1)} %get-tuple-element.116), channel_id=1, source_target_pairs={{0,16},{16,0},{1,17},{17,1},{2,18},{18,2},{3,19},{19,3},{4,20},{20... | collective-permute-start | bytes 3538952 | tf_op jit(solution)/shard_map/outer0/ppermute | solution.py:19
  165.8 34.9 %collective-permute-start.15 = (bf16[192,768]{1,0:T(8,128)(2,1)}, bf16[192,768]{1,0:T(8,128)(2,1)}, u32[]{:S(2)}, u32[]{:S(2)}) collective-permute-start(bf16[192,768]{1,0:T(8,128)(2,1)} %add.275.refs_1_), channel_id=1, source_target_pairs={{0,1},{1,0},{2,3},{3,2},{4,5},{5,4},{6,7},{7,6},{8,9},{9,8},{10,11... | collective-permute-start | bytes 884744 | tf_op jit(solution)/shard_map/output_grad/ppermute | solution.py:19
  166.4 41.6 %all-to-all-start.1 = ((bf16[4,256,768]{2,1,0:T(8,128)(2,1)}), bf16[4,256,768]{2,1,0:T(8,128)(2,1)}, u32[]{:S(2)}, u32[]{:S(2)}) async-start(bf16[4,256,768]{2,1,0:T(8,128)(2,1)} %touch.13), calls=%async_computation.1 | async-start | bytes 3145728 | tf_op jit(solution)/shard_map/all_to_all | solution.py:1057
  192.4 24.6 %collective-permute-start.18 = (bf16[512,768]{1,0:T(8,128)(2,1)}, bf16[512,768]{1,0:T(8,128)(2,1)}, u32[]{:S(2)}, u32[]{:S(2)}) collective-permute-start(bf16[512,768]{1,0:T(8,128)(2,1)} %get-tuple-element.123), channel_id=1, source_target_pairs={{0,1},{1,0},{2,3},{3,2},{4,5},{5,4},{6,7},{7,6},{8,9},{9,8},{10,11... | collective-permute-start | bytes 2359304 | tf_op jit(solution)/shard_map/theirs/ppermute | solution.py:19
  198.9 30.1 %collective-permute-start.19 = (bf16[384,768]{1,0:T(8,128)(2,1)}, bf16[384,768]{1,0:T(8,128)(2,1)}, u32[]{:S(2)}, u32[]{:S(2)}) collective-permute-start(bf16[384,768]{1,0:T(8,128)(2,1)} %get-tuple-element.118.refs_1_), channel_id=1, source_target_pairs={{0,1},{1,0},{2,3},{3,2},{4,5},{5,4},{6,7},{7,6},{8,9},{9,8},{10,11... | collective-permute-start | bytes 1769480 | tf_op jit(solution)/shard_map/outer-1/ppermute | solution.py:19
  199.4 29.6 %collective-permute-start.20 = (bf16[384,768]{1,0:T(8,128)(2,1)}, bf16[384,768]{1,0:T(8,128)(2,1)}, u32[]{:S(2)}, u32[]{:S(2)}) collective-permute-start(bf16[384,768]{1,0:T(8,128)(2,1)} %get-tuple-element.126), channel_id=1, source_target_pairs={{0,16},{16,0},{1,17},{17,1},{2,18},{18,2},{3,19},{19,3},{4,20},{20... | collective-permute-start | bytes 1769480 | tf_op jit(solution)/shard_map/inner-1/ppermute | solution.py:19
  208.0 33.3 %all-to-all-start.2 = ((bf16[8,96,768]{2,1,0:T(8,128)(2,1)}), bf16[8,96,768]{2,1,0:T(8,128)(2,1)}, u32[]{:S(2)}, u32[]{:S(2)}) async-start(bf16[8,96,768]{2,1,0:T(8,128)(2,1)} %bitcast.96), calls=%async_computation.2 | async-start | bytes 2359296 | tf_op jit(solution)/shard_map/all_to_all | solution.py:1159
  232.9 16.6 %collective-permute-start.21 = (bf16[384,768]{1,0:T(8,128)(2,1)}, bf16[384,768]{1,0:T(8,128)(2,1)}, u32[]{:S(2)}, u32[]{:S(2)}) collective-permute-start(bf16[384,768]{1,0:T(8,128)(2,1)} %get-tuple-element.127.refs_2_.refs_1_), channel_id=1, source_target_pairs={{0,1},{1,0},{2,3},{3,2},{4,5},{5,4},{6,7},{7,6},{8,9},{9,8},{10,11... | collective-permute-start | bytes 1769480 | tf_op jit(solution)/shard_map/piece/ppermute | solution.py:19
  233.4 21.0 %collective-permute-start.22 = (bf16[384,768]{1,0:T(8,128)(2,1)}, bf16[384,768]{1,0:T(8,128)(2,1)}, u32[]{:S(2)}, u32[]{:S(2)}) collective-permute-start(bf16[384,768]{1,0:T(8,128)(2,1)} %get-tuple-element.127.refs_2_.refs_1_), channel_id=1, source_target_pairs={{0,16},{16,0},{1,17},{17,1},{2,18},{18,2},{3,19},{19,3},{4,20},{20... | collective-permute-start | bytes 1769480 | tf_op jit(solution)/shard_map/piece/ppermute | solution.py:19
  234.9 36.1 %collective-permute-start.27 = (bf16[384,768]{1,0:T(8,128)(2,1)}, bf16[384,768]{1,0:T(8,128)(2,1)}, u32[]{:S(2)}, u32[]{:S(2)}) collective-permute-start(bf16[384,768]{1,0:T(8,128)(2,1)} %get-tuple-element.128.refs_3_.refs_1_), channel_id=1, source_target_pairs={{0,16},{16,0},{1,17},{17,1},{2,18},{18,2},{3,19},{19,3},{4,20},{20... | collective-permute-start | bytes 1769480 | tf_op jit(solution)/shard_map/piece/ppermute | solution.py:19
  235.4 36.6 %collective-permute-start.28 = (bf16[384,768]{1,0:T(8,128)(2,1)}, bf16[384,768]{1,0:T(8,128)(2,1)}, u32[]{:S(2)}, u32[]{:S(2)}) collective-permute-start(bf16[384,768]{1,0:T(8,128)(2,1)} %get-tuple-element.128.refs_3_.refs_1_), channel_id=1, source_target_pairs={{0,1},{1,0},{2,3},{3,2},{4,5},{5,4},{6,7},{7,6},{8,9},{9,8},{10,11... | collective-permute-start | bytes 1769480 | tf_op jit(solution)/shard_map/piece/ppermute | solution.py:19
  243.8 48.0 %all-to-all-start.3 = ((bf16[8,112,768]{2,1,0:T(8,128)(2,1)}), bf16[8,112,768]{2,1,0:T(8,128)(2,1)}, u32[]{:S(2)}, u32[]{:S(2)}) async-start(bf16[8,112,768]{2,1,0:T(8,128)(2,1)} %total.1.refs_1_.refs_7_), calls=%async_computation.3 | async-start | bytes 2752512 | tf_op jit(solution)/shard_map/all_to_all | solution.py:1171
  254.4 17.6 %collective-permute-start.25 = (bf16[384,768]{1,0:T(8,128)(2,1)}, bf16[384,768]{1,0:T(8,128)(2,1)}, u32[]{:S(2)}, u32[]{:S(2)}) collective-permute-start(bf16[384,768]{1,0:T(8,128)(2,1)} %get-tuple-element.129.refs_2_), channel_id=1, source_target_pairs={{0,8},{8,0},{1,9},{9,1},{2,10},{10,2},{3,11},{11,3},{4,12},{12,4},... | collective-permute-start | bytes 1769480 | tf_op jit(solution)/shard_map/piece_core/ppermute | solution.py:19
  254.4 19.2 %collective-permute-start.26 = (bf16[384,768]{1,0:T(8,128)(2,1)}, bf16[384,768]{1,0:T(8,128)(2,1)}, u32[]{:S(2)}, u32[]{:S(2)}) collective-permute-start(bf16[384,768]{1,0:T(8,128)(2,1)} %get-tuple-element.130.refs_3_), channel_id=1, source_target_pairs={{0,8},{8,0},{1,9},{9,1},{2,10},{10,2},{3,11},{11,3},{4,12},{12,4},... | collective-permute-start | bytes 1769480 | tf_op jit(solution)/shard_map/piece_core/ppermute | solution.py:19
  256.8 16.9 %collective-permute-start.24 = (bf16[384,768]{1,0:T(8,128)(2,1)}, bf16[384,768]{1,0:T(8,128)(2,1)}, u32[]{:S(2)}, u32[]{:S(2)}) collective-permute-start(bf16[384,768]{1,0:T(8,128)(2,1)} %touch.16), channel_id=1, source_target_pairs={{0,8},{8,0},{1,9},{9,1},{2,10},{10,2},{3,11},{11,3},{4,12},{12,4},... | collective-permute-start | bytes 1769480 | tf_op jit(solution)/shard_map/piece_core/ppermute | solution.py:19
  271.0 20.8 %collective-permute-start.23 = (bf16[384,768]{1,0:T(8,128)(2,1)}, bf16[384,768]{1,0:T(8,128)(2,1)}, u32[]{:S(2)}, u32[]{:S(2)}) collective-permute-start(bf16[384,768]{1,0:T(8,128)(2,1)} %get-tuple-element.129.refs_2_), channel_id=1, source_target_pairs={{0,16},{16,0},{1,17},{17,1},{2,18},{18,2},{3,19},{19,3},{4,20},{20... | collective-permute-start | bytes 1769480 | tf_op jit(solution)/shard_map/piece/ppermute | solution.py:19
  272.0 10.2 %collective-permute-start.30 = (bf16[384,768]{1,0:T(8,128)(2,1)}, bf16[384,768]{1,0:T(8,128)(2,1)}, u32[]{:S(2)}, u32[]{:S(2)}) collective-permute-start(bf16[384,768]{1,0:T(8,128)(2,1)} %get-tuple-element.131.refs_2_), channel_id=1, source_target_pairs={{0,8},{8,0},{1,9},{9,1},{2,10},{10,2},{3,11},{11,3},{4,12},{12,4},... | collective-permute-start | bytes 1769480 | tf_op jit(solution)/shard_map/piece_core/ppermute | solution.py:19
  272.0 19.8 %collective-permute-start.32 = (bf16[384,768]{1,0:T(8,128)(2,1)}, bf16[384,768]{1,0:T(8,128)(2,1)}, u32[]{:S(2)}, u32[]{:S(2)}) collective-permute-start(bf16[384,768]{1,0:T(8,128)(2,1)} %get-tuple-element.131.refs_2_), channel_id=1, source_target_pairs={{0,1},{1,0},{2,3},{3,2},{4,5},{5,4},{6,7},{7,6},{8,9},{9,8},{10,11... | collective-permute-start | bytes 1769480 | tf_op jit(solution)/shard_map/piece/ppermute | solution.py:19
  291.9 11.2 %collective-permute-start.35 = (bf16[384,768]{1,0:T(8,128)(2,1)}, bf16[384,768]{1,0:T(8,128)(2,1)}, u32[]{:S(2)}, u32[]{:S(2)}) collective-permute-start(bf16[384,768]{1,0:T(8,128)(2,1)} %touch.19.refs_1_), channel_id=1, source_target_pairs={{0,8},{8,0},{1,9},{9,1},{2,10},{10,2},{3,11},{11,3},{4,12},{12,4},... | collective-permute-start | bytes 1769480 | tf_op jit(solution)/shard_map/piece_core/ppermute | solution.py:19
  292.4 10.7 %collective-permute-start.36 = (bf16[384,768]{1,0:T(8,128)(2,1)}, bf16[384,768]{1,0:T(8,128)(2,1)}, u32[]{:S(2)}, u32[]{:S(2)}) collective-permute-start(bf16[384,768]{1,0:T(8,128)(2,1)} %touch.20.refs_2_.refs_3_), channel_id=1, source_target_pairs={{0,8},{8,0},{1,9},{9,1},{2,10},{10,2},{3,11},{11,3},{4,12},{12,4},... | collective-permute-start | bytes 1769480 | tf_op jit(solution)/shard_map/piece_core/ppermute | solution.py:19
  (12 other events, 86.0 us)

commit v3 on v2

--- a/solution.py
+++ b/solution.py
@@ -33,6 +33,8 @@
 
 
 PAIR = 2 * HEAD_DIM
+CORE, OTHER_CORE, NONE, OUTER_TURN, INNER_TURN, ORDER = 2, 3, 4, 5, 6, 7
+EXPERT_FLOPS = 2 * 10**9
 ATTEND_FLOPS = 20 * 10**9
 BACK_FLOPS = 300 * 10**9
 ATTBACK_FLOPS = 50 * 10**9
@@ -153,7 +155,8 @@
     def _():
         row = lax.broadcasted_iota(jnp.int32, (count, count), 0)
         col = lax.broadcasted_iota(jnp.int32, (count, count), 1)
-        start = row - pos_ref[0]
+        spread = jnp.broadcast_to(pos_ref[...].astype(F32), (8, count))
+        start = row - jnp.transpose(spread)[:, :1].astype(jnp.int32)
         bias_d[...] = jnp.where((col <= row) & (col >= start), 0.0, HIDE)
         bias_c[...] = jnp.where(col >= start + count, 0.0, HIDE)
 
@@ -224,7 +227,7 @@
             block(2, False),
             block(1, True),
             block(2, True),
-            pl.BlockSpec((1, count, 1), lambda g, w: (w[0], 0, 0)),
+            whole((1, count)),
         ],
         out_specs=[
             score_spec,
@@ -274,14 +277,15 @@
     )
 
 
-def send_kernel(rows_ref, slot_ref, out_ref):
+def send_kernel(rows_ref, slot_ref, weight_ref, out_ref, weight_out):
     send_rows(rows_ref[...], slot_ref, [out_ref.at[k] for k in range(out_ref.shape[0])])
-
-
-def sent_rows(rows, slot_row, experts):
+    weight_out[...] = weight_ref[...]
+
+
+def sent_rows(rows, slot_row, weight, experts, after=()):
     count, width = rows.shape
-    out = shaped((experts, count // 2, width), BF)
-    return plain(send_kernel, [rows, slot_row], out, "sent_rows")
+    out = [shaped((experts, count // 2, width), BF), shaped(weight.shape, BF)]
+    return plain(send_kernel, [rows, slot_row, weight], out, "sent_rows", after)
 
 
 def taken_rows(slot_ref, block_refs):
@@ -367,7 +371,7 @@
         output_weight_kernel,
         [own, got, low],
         after=after,
-        prefetch=[core.reshape(1).astype(jnp.int32)],
+        prefetch=[core],
         grid=(1,),
         in_specs=[whole(x.shape) for x in (own, got, low)],
         out_specs=[whole(o.shape) for o in out],
@@ -462,7 +466,7 @@
             ref[...] = grad_acc[i * size : (i + 1) * size].astype(BF)
 
 
-def expert(index, blocks, cot, places, inner, outer, earlier, after=(), tile=768, sub=256):
+def expert(place, index, blocks, cot, inner, outer, earlier, after=(), tile=768, sub=256):
     count, width = blocks[0].shape
     size, units = len(blocks), inner.shape[1]
     total = count * cot.shape[0]
@@ -483,8 +487,9 @@
         functools.partial(expert_kernel, size, sub),
         [*blocks, *[cot] * size, inner, outer],
         after=after,
+        flops=EXPERT_FLOPS,
         alias=earlier,
-        prefetch=[jnp.stack(places).astype(jnp.int32)],
+        prefetch=[place],
         grid=(tiles + size - 1,),
         in_specs=[whole((count, width))] * size
         + [placed(i) for i in range(size)]
@@ -502,182 +507,102 @@
     )
 
 
-def weight_kernel(count, which_ref, place_ref, act_ref, pre_ref, *refs):
-    x_refs, (cot_ref, outer_out, inner_out, x, cot) = refs[:count], refs[count:]
+def weight_kernel(is_outer, count, added, info_ref, wide_ref, *refs):
+    row_count = 1 if is_outer else count
+    row_refs, refs = refs[:row_count], refs[row_count:]
+    if is_outer:
+        row_refs = [row_refs[0].at[info_ref[ORDER + i]] for i in range(count)]
+    got_ref = refs[0] if added else None
+    *out_refs, rows = refs[1:] if added else refs
     at = pl.program_id(0)
-    half = pl.num_programs(0) // 2
-
-    @pl.when(at == 0)
-    def _():
-        fill(cot, [cot_ref.at[place_ref[i]] for i in range(count)])
-        fill(x, x_refs)
-
-    def put(ref, left, right):
-        ref[...] = lax.dot_general(
-            left, right, (((0,), (0,)), ((), ())), preferred_element_type=F32
-        ).astype(BF)
-
-    pl.when(at < half)(lambda: put(outer_out, act_ref[...], cot[...]))
-    pl.when(at >= half)(lambda: put(inner_out, x[...], pre_ref[...]))
-
-
-def weight_parts(half, x_blocks, cot_blocks, places, act, pre, after=(), tiles=2):
-    count, width = x_blocks[0].shape
-    total, units = act.shape
-    tile = units // 2 // tiles
-
-    def early(j):
-        return jnp.minimum(j, tiles - 1)
-
-    def late(j):
-        return jnp.maximum(j - tiles, 0)
-
+    pl.when(at == 0)(lambda: fill(rows, row_refs))
+
+    def put(out_ref):
+        sides = (wide_ref[...], rows[...]) if is_outer else (rows[...], wide_ref[...])
+        part = lax.dot_general(*sides, (((0,), (0,)), ((), ())), preferred_element_type=F32)
+        if added:
+            part = part + got_ref[...].astype(F32)
+        out_ref[...] = part.astype(BF)
+
+    if added:
+        for i, out_ref in enumerate(out_refs):
+            pl.when(at == i)(functools.partial(put, out_ref))
+    else:
+        put(out_refs[0])
+
+
+def weight_part(info, is_outer, half, turn, blocks, wide, got=None, after=()):
+    total, units = wide.shape
+    width, added, tile = blocks[0].shape[1], got is not None, units // 4
+    count = len(blocks) if not is_outer else blocks.shape[0]
+    if is_outer:
+        row_specs, blocks = [whole(blocks.shape)], [blocks]
+    else:
+        row_specs = [whole(block.shape) for block in blocks]
+
+    def at(j):
+        return (j, 0) if is_outer else (0, j)
+
+    def place(j, w):
+        return (w[turn] + j) % 2
+
+    def shape(units):
+        return (units, width) if is_outer else (width, units)
+
+    block = pl.BlockSpec(shape(tile), lambda j, w: at(place(j, w)))
+    if added:
+        out, out_specs = [shaped(shape(tile), BF)] * 2, [whole(shape(tile))] * 2
+    else:
+        out, out_specs = [shaped(shape(2 * tile), BF)], [block]
     return call(
-        functools.partial(weight_kernel, len(x_blocks)),
-        [act, pre, *x_blocks, cot_blocks],
+        functools.partial(weight_kernel, is_outer, count, added),
+        [wide, *blocks] + ([got] if added else []),
         after=after,
-        prefetch=[half.reshape(1).astype(jnp.int32), jnp.stack(places).astype(jnp.int32)],
-        grid=(2 * tiles,),
-        in_specs=[
-            pl.BlockSpec((total, tile), lambda j, w, p: (0, w[0] * tiles + early(j))),
-            pl.BlockSpec((total, tile), lambda j, w, p: (0, w[0] * tiles + late(j))),
-        ]
-        + [whole((count, width))] * len(x_blocks)
-        + [whole(cot_blocks.shape)],
-        out_specs=[
-            pl.BlockSpec((tile, width), lambda j, w, p: (early(j), 0)),
-            pl.BlockSpec((width, tile), lambda j, w, p: (0, late(j))),
-        ],
-        out_shape=[shaped((units // 2, width), BF), shaped((width, units // 2), BF)],
-        scratch_shapes=[pltpu.VMEM((total, width), BF)] * 2,
-        name="weight_parts",
-    )
-
-
-def weight_sum_kernel(count, which_ref, place_ref, act_ref, pre_ref, *refs):
-    x_refs, (cot_ref, outer_got, inner_got, *out_refs, x, cot) = refs[:count], refs[count:]
-    at = pl.program_id(0)
-
-    @pl.when(at == 0)
-    def _():
-        fill(cot, [cot_ref.at[place_ref[i]] for i in range(count)])
-        fill(x, x_refs)
-
-    def put(out_ref, got_ref, left, right):
-        part = lax.dot_general(
-            left, right, (((0,), (0,)), ((), ())), preferred_element_type=F32
-        )
-        out_ref[...] = (part + got_ref[...].astype(F32)).astype(BF)
-
-    for i, out_ref in enumerate(out_refs):
-
-        @pl.when(at == i)
-        def _(i=i, out_ref=out_ref):
-            if i < 2:
-                put(out_ref, outer_got, act_ref[...], cot[...])
-            else:
-                put(out_ref, inner_got, x[...], pre_ref[...])
-
-
-def weight_sums(
-    half, outer_turn, inner_turn, x_blocks, cot_blocks, places, act, pre, outer_got, inner_got, after=()
-):
-    count, width = x_blocks[0].shape
-    total, units = act.shape
-    tile = units // 4
-
-    def outer_at(j, w):
-        return (w[1] + jnp.minimum(j, 1)) % 2
-
-    def inner_at(j, w):
-        return (w[2] + jnp.maximum(j - 2, 0)) % 2
-
-    out = [shaped((tile, width), BF)] * 2 + [shaped((width, tile), BF)] * 2
-    parts = call(
-        functools.partial(weight_sum_kernel, len(x_blocks)),
-        [act, pre, *x_blocks, cot_blocks, outer_got, inner_got],
-        after=after,
-        prefetch=[
-            jnp.stack([half, outer_turn, inner_turn]).astype(jnp.int32),
-            jnp.stack(places).astype(jnp.int32),
-        ],
-        grid=(4,),
-        in_specs=[
-            pl.BlockSpec((total, tile), lambda j, w, p: (0, w[0] * 2 + outer_at(j, w))),
-            pl.BlockSpec((total, tile), lambda j, w, p: (0, w[0] * 2 + inner_at(j, w))),
-        ]
-        + [whole((count, width))] * len(x_blocks)
-        + [
-            whole(cot_blocks.shape),
-            pl.BlockSpec((tile, width), lambda j, w, p: (outer_at(j, w), 0)),
-            pl.BlockSpec((width, tile), lambda j, w, p: (0, inner_at(j, w))),
-        ],
-        out_specs=[whole(o.shape) for o in out],
+        prefetch=[info],
+        grid=(2,),
+        in_specs=[pl.BlockSpec((total, tile), lambda j, w: (0, w[half] * 2 + place(j, w)))]
+        + row_specs
+        + ([block] if added else []),
+        out_specs=out_specs,
         out_shape=out,
-        scratch_shapes=[pltpu.VMEM((total, width), BF)] * 2,
-        name="weight_sums",
-    )
-    return parts[:2], parts[2:]
-
-
-def assemble_kernel(place_ref, *refs):
-    *piece_refs, out_ref = refs
-    for i, ref in enumerate(piece_refs):
+        scratch_shapes=[pltpu.VMEM((total, width), BF)],
+        name="weight_part",
+    )
+
+
+def assemble_kernel(counts, info_ref, *refs):
+    piece_refs, out_refs = refs[: sum(counts)], refs[sum(counts) :]
+    targets = [out for out, count in zip(out_refs, counts) for _ in range(count)]
+    for i, (ref, out_ref) in enumerate(zip(piece_refs, targets)):
 
         @pl.when(pl.program_id(0) == i)
-        def _(ref=ref):
+        def _(ref=ref, out_ref=out_ref):
             out_ref[...] = ref[...].astype(F32)
 
 
-def assemble_two_kernel(count, place_ref, *refs):
-    *piece_refs, outer_ref, inner_ref = refs
-    for i, ref in enumerate(piece_refs):
-
-        @pl.when(pl.program_id(0) == i)
-        def _(ref=ref, out_ref=outer_ref if i < count else inner_ref):
-            out_ref[...] = ref[...].astype(F32)
-
-
-def assemble_two(outer, inner, places, earlier, after=()):
-    size, count = outer[0].shape, len(outer)
-    table = jnp.stack([jnp.stack(place) for place in places]).astype(jnp.int32)
-
-    def outer_at(i, t):
-        held = jnp.minimum(i, count - 1)
-        return t[held, 0], t[held, 1]
-
-    def inner_at(i, t):
-        held = jnp.maximum(i, count)
-        return t[held, 0], t[held, 1]
-
+def assemble(info, start, groups, shapes, earlier, after=()):
+    counts = [len(pieces) for pieces in groups]
+    pieces = [piece for group in groups for piece in group]
+    size = pieces[0].shape
+
+    def spec(first, count):
+        def at(i, t):
+            held = start + 2 * jnp.clip(i, first, first + count - 1)
+            return t[held], t[held + 1]
+
+        return pl.BlockSpec(size, at)
+
+    firsts = [sum(counts[:i]) for i in range(len(counts))]
     return call(
-        functools.partial(assemble_two_kernel, count),
-        [*outer, *inner],
+        functools.partial(assemble_kernel, counts),
+        pieces,
         after=after,
         alias=earlier,
-        prefetch=[table],
-        grid=(2 * count,),
-        in_specs=[whole(size)] * (2 * count),
-        out_specs=[pl.BlockSpec(size, outer_at), pl.BlockSpec(size, inner_at)],
-        out_shape=[shaped(x.shape, F32) for x in earlier],
-        name="assemble_two",
-    )
-
-
-def assemble(pieces, places, shape, earlier, after=(), flops=1):
-    size = pieces[0].shape
-    table = jnp.stack([jnp.stack(place) for place in places]).astype(jnp.int32)
-    return call(
-        assemble_kernel,
-        pieces,
-        flops=flops,
-        after=after,
-        alias=earlier,
-        prefetch=[table],
+        prefetch=[info],
         grid=(len(pieces),),
         in_specs=[whole(size)] * len(pieces),
-        out_specs=[pl.BlockSpec(size, lambda i, t: (t[i, 0], t[i, 1]))],
-        out_shape=[shaped(shape, F32)],
+        out_specs=[spec(first, count) for first, count in zip(firsts, counts)],
+        out_shape=[shaped(shape, F32) for shape in shapes],
         name="assemble",
     )
 
@@ -705,28 +630,28 @@
     return plain(gather_sum_kernel, [kept, got, more], out, "gather_sum", after)
 
 
-def adds_kernel(count, cuts, place_ref, *refs):
+def adds_kernel(start, count, cuts, info_ref, *refs):
     in_refs, out_refs = refs[: 2 * count], refs[2 * count :]
     for i in range(count):
         kept_ref, got_ref = in_refs[2 * i : 2 * i + 2]
         for j in range(cuts):
             ref = out_refs[cuts * i + j]
             rows = ref.shape[0]
-            cut = pl.ds(pl.multiple_of(place_ref[cuts * i + j] * rows, rows), rows)
+            at = info_ref[start + cuts * i + j] if cuts > 1 else 0
+            cut = pl.ds(pl.multiple_of(at * rows, rows), rows)
             ref[...] = (kept_ref[cut, :].astype(F32) + got_ref[cut, :].astype(F32)).astype(BF)
 
 
-def adds(pairs, places, after=()):
-    cuts = len(places[0])
+def adds(info, start, pairs, cuts, after=()):
     out = [
         shaped((kept.shape[0] // cuts, kept.shape[1]), BF) for kept, _ in pairs for _ in range(cuts)
     ]
     operands = [x for pair in pairs for x in pair]
     parts = call(
-        functools.partial(adds_kernel, len(pairs), cuts),
+        functools.partial(adds_kernel, start, len(pairs), cuts),
         operands,
         after=after,
-        prefetch=[jnp.stack([p for at in places for p in at]).astype(jnp.int32)],
+        prefetch=[info],
         grid=(1,),
         in_specs=[whole(x.shape) for x in operands],
         out_specs=[whole(o.shape) for o in out],
@@ -736,36 +661,52 @@
     return [parts[cuts * i : cuts * (i + 1)] for i in range(len(pairs))]
 
 
-def gather_pieces(own, steps, order, flops):
+def piece_places(steps, order):
     weights = {step: 1 << (len(steps) - 1 - i) for i, step in enumerate(steps)}
     place = sum(side(*step) * weight for step, weight in weights.items())
-    pieces, newest = [(place, own)], [(0, place, own)]
+    places, newest = [place], [(0, place)]
     while newest:
-        found = []
-        for first, at, piece in newest:
-            for i in range(first, len(order)):
-                change = weights[order[i]] * (1 - 2 * side(*order[i]))
-                found.append((i + 1, at + change, swap(piece, *order[i], "piece")))
+        newest = [
+            (i + 1, at + weights[order[i]] * (1 - 2 * side(*order[i])))
+            for first, at in newest
+            for i in range(first, len(order))
+        ]
+        places += [at for _, at in newest]
+    return places
+
+
+def gather_pieces(own, steps, order, flops):
+    pieces, newest = [own], [(0, own)]
+    while newest:
+        found = [
+            (i + 1, swap(piece, *order[i], "piece"))
+            for first, piece in newest
+            for i in range(first, len(order))
+        ]
         if len(pieces) == 1:
-            held = touch([piece for _, _, piece in found], [], flops=flops)
-            found = [(first, at, piece) for (first, at, _), piece in zip(found, held)]
-        pieces += [(at, piece) for _, at, piece in found]
+            held = touch([piece for _, piece in found], [], flops=flops)
+            found = [(first, piece) for (first, _), piece in zip(found, held)]
+        pieces += [piece for _, piece in found]
         newest = found
-    return pieces
-
-
-def total_kernel(in_ref, tail_ref, out_ref):
+    return list(zip(piece_places(steps, order), pieces))
+
+
+def total_kernel(in_ref, tail_ref, got_ref, out_ref):
     count, rows = in_ref.shape[:2]
     value = sum(in_ref[i].astype(F32) for i in range(count)).astype(BF)
+    tail = sum(ref[i : i + 1].astype(F32) for ref in (tail_ref, got_ref) for i in (0, 1))
+    high = tail.astype(BF).astype(F32)
+    line = lax.broadcasted_iota(jnp.int32, tail_ref.shape, 0)
+    tail = jnp.where(line == 0, high, jnp.where(line == 1, tail - high, 0.0)).astype(BF)
     for i in range(count):
         out_ref[i, :rows] = value
-        out_ref[i, rows:] = tail_ref[...]
-
-
-def total(blocks, tail, after=()):
+        out_ref[i, rows:] = tail
+
+
+def total(blocks, tail, got, after=()):
     count, rows, width = blocks.shape
     out = shaped((count, rows + tail.shape[0], width), BF)
-    return plain(total_kernel, [blocks, tail], out, "total", after)
+    return plain(total_kernel, [blocks, tail, got], out, "total", after)
 
 
 def halves(step):
@@ -800,7 +741,7 @@
     group = pl.program_id(0)
     count = own_ref.shape[0]
     step = count // 2
-    me, core = at_ref[0], at_ref[1]
+    me, core = at_ref[0], at_ref[CORE]
     lane = lax.broadcasted_iota(jnp.int32, (1, PAIR), 1) // HEAD_DIM
 
     for ref, context, at in (
@@ -993,7 +934,7 @@
         functools.partial(weight_outputs_kernel, rows - 16),
         [kept, got],
         after=after,
-        prefetch=[core.reshape(1).astype(jnp.int32)],
+        prefetch=[core],
         grid=(cols // PAIR,),
         in_specs=[whole(kept.shape)] * 2,
         out_specs=[
@@ -1027,16 +968,41 @@
     outer_weight = expert_outer[0]
     my_head = lax.axis_index("head")
     my_expert = lax.axis_index("expert")
-    own_at = my_head.reshape(1).astype(jnp.int32)
+    core = lax.axis_index("core")
+    turns = bits_of("x") + bits_of("head")
+    outer_steps, inner_steps = turns, turns[::-1]
+    order = [my_expert ^ k for k in range(expert_count)]
+
+    early = len(turns) + 1
+    entries = [
+        my_head, 1 - my_head, core, 1 - core, 0 * core,
+        1 - side(*outer_steps[0]), 1 - side(*inner_steps[0]), *order,
+    ]
+    adds_at = [len(entries) + 4 * i for i in range(len(turns) - 1)]
+    for i in range(1, len(turns)):
+        entries += [*halves(outer_steps[i]), *halves(inner_steps[i])]
+    half = 1 << (len(turns) - 1)
+
+    def placed(place, which, is_outer):
+        if is_outer:
+            return [which * 2 * half + place, 0 * place]
+        return [place % half, which * 2 + place // half]
+
+    piece_at = []
+    for chosen in (slice(early), slice(early, None)):
+        for steps, is_outer in ((outer_steps, True), (inner_steps, False)):
+            piece_at.append(len(entries))
+            for which in (core, 1 - core):
+                for place in piece_places(steps, steps[::-1])[chosen]:
+                    entries += placed(place, which, is_outer)
+    info = jnp.stack(entries).astype(jnp.int32)
+    own_at, core_at = my_head.reshape(1).astype(jnp.int32), core.reshape(1).astype(jnp.int32)
     other_at = 1 - own_at
     first_gain = first_gain.reshape(1, model_width)
     second_gain = second_gain.reshape(1, model_width)
 
     other_input = swap(block_input, "head", 1, "rows")
     other_pos = swap(positions, "head", 1, "positions")
-    seq_pos = jnp.where(
-        my_head == 0, jnp.stack([positions, other_pos]), jnp.stack([other_pos, positions])
-    )[:, :, None]
 
     chosen = jnp.take(hash_table, token_ids)
     relative = chosen ^ my_expert
@@ -1045,7 +1011,6 @@
     slot_index = relative * capacity + jnp.sum(jnp.where(one_hot, rank_table, 0), axis=1)
     slot_row = slot_index[None, :]
     absolute = slot_index + (chosen - relative) * capacity
-    order = [my_expert ^ k for k in range(expert_count)]
 
     def exchange(blocks, name, first=0):
         return [
@@ -1056,20 +1021,19 @@
     def exchange_all(blocks):
         return lax.all_to_all(blocks, "expert", split_axis=0, concat_axis=0, tiled=True)
 
-    sent = sent_rows(output_cotangent, absolute[None, :], expert_count)
+    done = project(own_at, block_input, first_gain, project_weight, [])
+    sent, weight_sent = sent_rows(
+        output_cotangent, absolute[None, :], output_weight, expert_count, after=[done[0], other_pos]
+    )
     grad_blocks = exchange_all(sent)
-
-    done = project(
-        own_at, block_input, first_gain, project_weight, [], after=[sent, other_pos]
-    )
     first_low, projected = project(other_at, other_input, first_gain, project_weight, done)
-    other_weight = swap(touch([output_weight], [done[0]])[0], "head", 1, "output_weight")
-    *done, other_context = attend(other_at, projected, seq_pos, [])
+    other_weight = swap(weight_sent, "head", 1, "output_weight")
+    *done, other_context = attend(other_at, projected, other_pos[None, :], [])
     got_context = swap(other_context, "head", 1, "context")
     p_diag, p_cross, inverse, own_context = attend(
         own_at,
         projected,
-        seq_pos,
+        positions[None, :],
         done,
         after=[other_weight],
         flops=ATTEND_FLOPS,
@@ -1088,9 +1052,9 @@
     row_blocks = exchange(outgoing, "dispatch")
     done, returned, at = [], [], 0
     while at < expert_count:
-        size = max(at, 1)
+        size = 1
         parts = expert(
-            at, row_blocks[at : at + size], grad_blocks, order[at : at + size], inner_weight,
+            order[at].reshape(1).astype(jnp.int32), at, row_blocks[at : at + size], grad_blocks if at else sent, inner_weight,
             outer_weight, done,
         )
         done, grads = parts[:3], parts[3:]
@@ -1098,18 +1062,18 @@
         at += size
     activated, pre_grad, produced = done
 
-    core = lax.axis_index("core")
-    turns = bits_of("x") + bits_of("head")
-    outer_steps, inner_steps = turns, turns[::-1]
-    outer_sent, inner_sent = weight_parts(
-        1 - core, row_blocks, grad_blocks, order, activated, pre_grad, after=grads
-    )
+    (outer_sent,) = weight_part(info, True, OTHER_CORE, NONE, grad_blocks, activated, after=grads)
     outer_got = swap(outer_sent, "core", 1, "outer_core")
+    (inner_sent,) = weight_part(
+        info, False, OTHER_CORE, NONE, row_blocks, pre_grad, after=[outer_sent]
+    )
     inner_got = swap(inner_sent, "core", 1, "inner_core")
     token = touch([jnp.zeros((8, 128), F32)], [inner_sent], flops=BACK_FLOPS)
-    outer_parts, inner_parts = weight_sums(
-        core, 1 - side(*outer_steps[0]), 1 - side(*inner_steps[0]), row_blocks, grad_blocks, order,
-        activated, pre_grad, outer_got, inner_got, after=token,
+    outer_parts = weight_part(
+        info, True, CORE, OUTER_TURN, grad_blocks, activated, outer_got, after=token
+    )
+    inner_parts = weight_part(
+        info, False, CORE, INNER_TURN, row_blocks, pre_grad, inner_got, after=[outer_parts[0]]
     )
 
     hidden_grad, hidden_low, second_gain_part, own_grad, grad_sent = second_back(
@@ -1130,7 +1094,7 @@
         ]
 
     own_output, output_kept, output_sent = output_weight_parts(
-        core, own_context, got_context, hidden_low, after=[grad_sent]
+        core_at, own_context, got_context, hidden_low, after=[grad_sent]
     )
     output_sent = add(output_kept, swap(output_sent, "core", 1, "output_core"))
     combined = exchange_all(touch([produced], [output_sent])[0])
@@ -1140,16 +1104,14 @@
     end = 2 * local_cols
     lines = end + 16
     sent, kept, mine, theirs = attend_back(
-        jnp.stack([my_head, core]).astype(jnp.int32), own_grad, other_grad, projected, p_diag,
+        info, own_grad, other_grad, projected, p_diag,
         p_cross, own_context, other_context, inverse, first_low, project_weight, first_gain,
         second_gain_part, own_output, lines, after=[inner_parts[0]],
     )
     at = 3 * local_cols // 2
     for i in range(len(turns) - 1):
         outer_parts, inner_parts = adds(
-            pairs_of(outer_parts, inner_parts, i),
-            [halves(outer_steps[i + 1]), halves(inner_steps[i + 1])],
-            after=[kept],
+            info, adds_at[i], pairs_of(outer_parts, inner_parts, i), 2, after=[kept]
         )
     more = touch([got_output], outer_parts, flops=BACK_FLOPS)
     got = swap(sent, "core", 1, "weight")
@@ -1162,29 +1124,16 @@
     input_grad = first_back(
         block_input, first_gain, hidden_grad, mine, theirs, after=[block_output]
     )
+    got_tail = swap(tail, "head", 1, "gains")
     (outer_own,), (inner_own,) = adds(
-        pairs_of(outer_parts, inner_parts, -1), [[0 * core]] * 2, after=[input_grad]
+        info, 0, pairs_of(outer_parts, inner_parts, -1), 1, after=[input_grad, got_tail]
     )
     outer_pieces = gather_pieces(outer_own, outer_steps, outer_steps[::-1], BACK_FLOPS)
     inner_pieces = gather_pieces(inner_own, inner_steps, inner_steps[::-1], 1)
-    arrived = total(arrived, tail, after=[outer_own, inner_own])
+    arrived = total(
+        arrived, tail, got_tail, after=[outer_own, inner_own]
+    )
     summed = lax.all_to_all(arrived, crowd, split_axis=0, concat_axis=0, tiled=True)
-
-    def chosen_pieces(own_core, other_core, is_outer):
-        half = 1 << (len(turns) - 1)
-
-        def placed(place, which):
-            if is_outer:
-                return which * 2 * half + place, 0 * place
-            return place % half, which * 2 + place // half
-
-        return [
-            (piece, placed(at, which))
-            for pieces, which in ((own_core, core), (other_core, 1 - core))
-            for at, piece in pieces
-        ]
-
-    early = len(turns) + 1
 
     def core_swaps(pieces):
         return [(at, swap(piece, "core", 1, "piece_core")) for at, piece in pieces]
@@ -1193,17 +1142,12 @@
     for pieces in (outer_pieces, inner_pieces):
         (held,) = touch([pieces[0][1]], [arrived])
         others.append(core_swaps([(pieces[0][0], held), *pieces[1:early]]))
+    shapes = [outer_weight.shape, inner_weight.shape]
     totals = []
-    for is_outer, own_core, other_core in zip(
-        (True, False), (outer_pieces, inner_pieces), others
-    ):
-        chosen = chosen_pieces(own_core[:early], other_core, is_outer)
+    for i, pieces in enumerate((outer_pieces, inner_pieces)):
+        chosen = [piece for _, piece in pieces[:early] + others[i]]
         totals += assemble(
-            [piece for piece, _ in chosen],
-            [place for _, place in chosen],
-            (outer_weight if is_outer else inner_weight).shape,
-            [],
-            after=[arrived] + totals[-1:],
+            info, piece_at[i], [chosen], shapes[i : i + 1], [], after=[arrived] + totals[-1:]
         )
     late = []
     for pieces in (outer_pieces, inner_pieces):
@@ -1212,20 +1156,12 @@
     late_others = [core_swaps(pieces) for pieces in late]
     (kept,) = touch([summed], [pieces[0][1] for pieces in late])
     got = swap(kept, "core", 1, "weight_back")
-    project_grad, output_weight_grad, gains = weight_outputs(
-        core, kept, got, local_cols
-    )
-    gains = gains + swap(gains, "head", 1, "gains")
-    outer_late, inner_late = [
-        chosen_pieces(own_core, other_core, is_outer)
-        for own_core, other_core, is_outer in zip(late, late_others, (True, False))
+    project_grad, output_weight_grad, gains = weight_outputs(core_at, kept, got, local_cols)
+    chosen = [
+        [piece for _, piece in own + other] for own, other in zip(late, late_others)
     ]
-    outer_total, inner_total = assemble_two(
-        [piece for piece, _ in outer_late],
-        [piece for piece, _ in inner_late],
-        [place for _, place in outer_late + inner_late],
-        totals,
-        after=[project_grad],
+    outer_total, inner_total = assemble(
+        info, piece_at[2], chosen, shapes, totals, after=[project_grad]
     )
     return (
         block_output,

time: 315 us -> 302 us (0.959)
  other arithmetic: 10.4 us -> 2.76 us
  Pallas kernels: 171 us -> 178 us
  starting transfers between devices: 54.9 us -> 49.6 us
  local copies, waits for them, and re-layouts: 15.2 us -> 11.4 us
    pallas_call x36 -> x38, Pallas kernels: 171 us -> 178 us  [call(): pl.pallas_call(body, input_output_aliases={first + i: i for i in range(le...]
    another operation x16 -> x2, other arithmetic: 7.44 us -> 1.41 us  [the longest x3 2.55 us: assemble_two(): table = jnp.stack([jnp.stack(place) for place in places]).astype(jnp.int32)]
    ppermute x37, starting transfers between devices: 36.6 us -> 31.2 us  [swap(): return lax.ppermute(values, axis, [(i, i ^ bit) for i in range(size)])]
  transfers between devices with their start and end apart: 41 -> 41, of which waited for: 14 -> 13; matrix products, arithmetic and copies ran while one was open for 8% -> 5% of each run, Pallas kernels for 53% -> 56%
where the time goes in v3:
time: 302 us; the launch traced here: 297 us
  Pallas kernels  178 us (59%)
  waiting for transfers between devices  54.2 us (18%)
  starting transfers between devices  49.6 us (16%)
  local copies, waits for them, and re-layouts  11.4 us (4%)
    pallas_call x38, Pallas kernels, call(): pl.pallas_call(body, input_output_aliases={first + i: i for i in range(le...  178 us
    ppermute x37, waiting for transfers between devices, swap(): return lax.ppermute(values, axis, [(i, i ^ bit) for i in range(size)])  50.7 us
    ppermute x37, starting transfers between devices, swap(): return lax.ppermute(values, axis, [(i, i ^ bit) for i in range(size)])  31.2 us
    all_to_all x2, starting transfers between devices, exchange_all(): lax.all_to_all(blocks, 'expert', split_axis=0, concat_axis=0, tiled=True)  9.71 us
  transfers between devices with their start and end apart: 41, of which 13 were waited for; matrix products, arithmetic and copies ran while one was open for 5% of the time, Pallas kernels for 56%

profile of v3, /device:TPU:0, one launch (start us, length us, event | category | flops | bytes accessed | tf_op | source)
XLA Modules:
  0.0 297.4 jit_solution(14346926725245495461)
XLA Ops:
  10.8 4.5 %project.2 = (bf16[2,512,768]{2,1,0:T(8,128)(2,1)}, bf16[3,2,512,384]{3,2,1,0:T(8,128)(2,1)}) custom-call(s32[1]{0:T(128)} %bitcast.refs_0_, bf16[512,768]{1,0:T(8,128)(2,1)} %refs_0_.7, f32[1,768]{1,0:T(1,128)} %reshape.86.refs_2_.refs_13_.refs_1_, bf16[3,768,384]{2,1,0:T(8,128)(2,1)} %refs_12_.1), custom_call_target="tpu_custom_call" | custom-call | flops 1 | bytes 1 | tf_op jit(solution)/shard_map/project/pallas_call | solution.py:86
  15.2 3.6 %sent_rows.1 = (bf16[4,256,768]{2,1,0:T(8,128)(2,1)}, bf16[384,768]{1,0:T(8,128)(2,1)}) custom-call(bf16[512,768]{1,0:T(8,128)(2,1)} %refs_0_.6, s32[1,512]{1,0:T(1,128)} %bitcast.70, bf16[384,768]{1,0:T(8,128)(2,1)} %refs_4_.1, bf16[2,512,768]{2,1,0:T(8,128)(2,1)} %get-tuple-element.76.refs_4_.refs_3_, s32[512]{0:T(512)} %collective-permute-done.1.refs_4_), custom_call_target="tpu_custom_call" | custom-call | flops 1 | bytes 1 | tf_op jit(solution)/shard_map/sent_rows/pallas_call | solution.py:86
  20.8 5.2 %all-to-all-start = ((bf16[4,256,768]{2,1,0:T(8,128)(2,1)}), bf16[4,256,768]{2,1,0:T(8,128)(2,1)}, u32[]{:S(2)}, u32[]{:S(2)}) async-start(bf16[4,256,768]{2,1,0:T(8,128)(2,1)} %get-tuple-element.87.refs_2_), calls=%async_computation | async-start | bytes 3145728 | tf_op jit(solution)/shard_map/all_to_all | solution.py:1022
  26.6 4.5 %project.3 = (bf16[2,512,768]{2,1,0:T(8,128)(2,1)}, bf16[3,2,512,384]{3,2,1,0:T(8,128)(2,1)}) custom-call(s32[1]{0:T(128)S(6)} %sub.107.refs_0_, bf16[512,768]{1,0:T(8,128)(2,1)} %collective-permute-done.refs_1_, f32[1,768]{1,0:T(1,128)} %reshape.86.refs_2_.refs_13_.refs_1_, ...), custom_call_target="tpu_custom_call", output_to_operand_aliasing={{0}: (4, {}), {1}: (5, {})} | custom-call | flops 1 | bytes 1 | tf_op jit(solution)/shard_map/project/pallas_call | solution.py:86
  31.0 8.5 %attend.2 = (bf16[2,6,512,512]{3,2,1,0:T(8,128)(2,1)}, bf16[2,6,512,512]{3,2,1,0:T(8,128)(2,1)}, f32[2,512,384]{2,1,0:T(8,128)}, bf16[512,384]{1,0:T(8,128)(2,1)}) custom-call(s32[1]{0:T(128)S(6)} %sub.107.refs_0_, bf16[3,2,512,384]{3,2,1,0:T(8,128)(2,1)} %get-tuple-element.78.refs_1_.refs_2_.refs_3_.refs_4_.refs_5_, ...), custom_call_target="tpu_custom_call" | custom-call | flops 1 | bytes 1 | tf_op jit(solution)/shard_map/attend/pallas_call | solution.py:86
  39.6 6.8 %attend.3 = (bf16[2,6,512,512]{3,2,1,0:T(8,128)(2,1)}, bf16[2,6,512,512]{3,2,1,0:T(8,128)(2,1)}, f32[2,512,384]{2,1,0:T(8,128)}, bf16[512,384]{1,0:T(8,128)(2,1)}) custom-call(s32[1]{0:T(128)} %bitcast.refs_0_, ...), custom_call_target="tpu_custom_call", output_to_operand_aliasing={{0}: (7, {}), {1}: (8, {}), {2}: (9, {})} | custom-call | flops 20000000000 | bytes 1 | tf_op jit(solution)/shard_map/attend/pallas_call | solution.py:86
  49.6 5.2 %hidden_rows.1 = (f32[512,768]{1,0:T(8,128)}, bf16[256,768]{1,0:T(8,128)(2,1)}, bf16[256,768]{1,0:T(8,128)(2,1)}, bf16[256,768]{1,0:T(8,128)(2,1)}, bf16[256,768]{1,0:T(8,128)(2,1)}) custom-call(bf16[512,768]{1,0:T(8,128)(2,1)} %refs_0_.7, bf16[512,384]{1,0:T(8,128)(2,1)} %get-tuple-element.83.refs_1_.refs_8_, ...), custom_call_target="tpu_custom_call" | custom-call | flops 1 | bytes 1 | tf_op jit(solution)/shard_map/hidden_rows/pallas_call | solution.py:86
  59.9 9.9 %expert.4 = (bf16[1024,3072]{1,0:T(8,128)(2,1)}, bf16[1024,3072]{1,0:T(8,128)(2,1)}, bf16[4,256,768]{2,1,0:T(8,128)(2,1)}, bf16[256,768]{1,0:T(8,128)(2,1)}) custom-call(s32[1]{0:T(128)} %bitcast.12.refs_0_, bf16[256,768]{1,0:T(8,128)(2,1)} %get-tuple-element.90.refs_1_.refs_2_, bf16[4,256,768]{2,1,0:T(8,128)(2,1)} %get-tuple-element.87.refs_2_, ...), custom_call_target="tpu_custom_call" | custom-call | flops 2000000000 | bytes 1 | tf_op jit(solution)/shard_map/expert/pallas_call | solution.py:86
  69.8 7.9 %collective-permute-done.6.refs_1_.refs_3_ = bf16[256,768]{1,0:T(8,128)(2,1)} collective-permute-done((bf16[256,768]{1,0:T(8,128)(2,1)}, bf16[256,768]{1,0:T(8,128)(2,1)}, u32[]{:S(2)}, u32[]{:S(2)}) %collective-permute-start.6) | collective-permute-done | bytes 393248 | tf_op jit(solution)/shard_map/dispatch1/ppermute | solution.py:19
  77.7 10.2 %expert.5 = (bf16[1024,3072]{1,0:T(8,128)(2,1)}, bf16[1024,3072]{1,0:T(8,128)(2,1)}, bf16[4,256,768]{2,1,0:T(8,128)(2,1)}, bf16[256,768]{1,0:T(8,128)(2,1)}) custom-call(s32[1]{0:T(128)} %bitcast.11.refs_0_, bf16[256,768]{1,0:T(8,128)(2,1)} %collective-permute-done.6.refs_1_.refs_3_, ...), custom_call_target="tpu_custom_call", output_to_operand_aliasing={{0}: (5, {}), {1}: (6, {}), {2}: (7, {})} | custom-call | flops 2000000000 | bytes 1 | tf_op jit(solution)/shard_map/expert/pallas_call | solution.py:86
  88.6 9.8 %expert.6 = (bf16[1024,3072]{1,0:T(8,128)(2,1)}, bf16[1024,3072]{1,0:T(8,128)(2,1)}, bf16[4,256,768]{2,1,0:T(8,128)(2,1)}, bf16[256,768]{1,0:T(8,128)(2,1)}) custom-call(s32[1]{0:T(128)} %bitcast.10.refs_0_, bf16[256,768]{1,0:T(8,128)(2,1)} %collective-permute-done.5.refs_1_.refs_4_, ...), custom_call_target="tpu_custom_call", output_to_operand_aliasing={{0}: (5, {}), {1}: (6, {}), {2}: (7, {})} | custom-call | flops 2000000000 | bytes 1 | tf_op jit(solution)/shard_map/expert/pallas_call | solution.py:86
  99.8 9.8 %expert.7 = (bf16[1024,3072]{1,0:T(8,128)(2,1)}, bf16[1024,3072]{1,0:T(8,128)(2,1)}, bf16[4,256,768]{2,1,0:T(8,128)(2,1)}, bf16[256,768]{1,0:T(8,128)(2,1)}) custom-call(s32[1]{0:T(128)} %bitcast.7.refs_0_, bf16[256,768]{1,0:T(8,128)(2,1)} %collective-permute-done.4.refs_1_.refs_5_, ...), custom_call_target="tpu_custom_call", output_to_operand_aliasing={{0}: (5, {}), {1}: (6, {}), {2}: (7, {})} | custom-call | flops 2000000000 | bytes 1 | tf_op jit(solution)/shard_map/expert/pallas_call | solution.py:86
  111.9 6.6 %weight_part.4.refs_6_ = bf16[1536,768]{1,0:T(8,128)(2,1)} custom-call(s32[47]{0:T(128)} %stack.119.refs_0_, bf16[1024,3072]{1,0:T(8,128)(2,1)} %get-tuple-element.106.refs_1_, bf16[4,256,768]{2,1,0:T(8,128)(2,1)} %all-to-all-done.refs_2_, bf16[256,768]{1,0:T(8,128)(2,1)} %get-tuple-element.104.refs_3_), custom_call_target="tpu_custom_call" | custom-call | flops 1 | bytes 1 | tf_op jit(solution)/shard_map/weight_part/pallas_call | solution.py:86
  118.6 6.6 %weight_part.5.refs_1_ = bf16[768,1536]{1,0:T(8,128)(2,1)} custom-call(s32[47]{0:T(128)} %stack.119.refs_0_, bf16[1024,3072]{1,0:T(8,128)(2,1)} %get-tuple-element.105.refs_1_, bf16[256,768]{1,0:T(8,128)(2,1)} %get-tuple-element.90.refs_1_.refs_2_, bf16[256,768]{1,0:T(8,128)(2,1)} %collective-permute-done.6.refs_1_.refs_3_, ...), custom_call_target="tpu_custom_call" | custom-call | flops 1 | bytes 1 | tf_op jit(solution)/shard_map/weight_part/pallas_call | solution.py:86
  126.3 7.3 %weight_part.6 = (bf16[768,768]{1,0:T(8,128)(2,1)}, bf16[768,768]{1,0:T(8,128)(2,1)}) custom-call(s32[47]{0:T(128)} %stack.119.refs_0_, bf16[1024,3072]{1,0:T(8,128)(2,1)} %get-tuple-element.106.refs_1_, bf16[4,256,768]{2,1,0:T(8,128)(2,1)} %all-to-all-done.refs_2_, bf16[1536,768]{1,0:T(8,128)(2,1)} %collective-permute-done.11.refs_3_, f32[8,128]{1,0:T(8,128)} %touch.10.refs_4_), custom_call_target="tpu_custom_call" | custom-call | flops 1 | bytes 1 | tf_op jit(solution)/shard_map/weight_part/pallas_call | solution.py:86
  133.6 7.3 %weight_part.7 = (bf16[768,768]{1,0:T(8,128)(2,1)}, bf16[768,768]{1,0:T(8,128)(2,1)}) custom-call(s32[47]{0:T(128)} %stack.119.refs_0_, bf16[1024,3072]{1,0:T(8,128)(2,1)} %get-tuple-element.105.refs_1_, bf16[256,768]{1,0:T(8,128)(2,1)} %get-tuple-element.90.refs_1_.refs_2_, bf16[256,768]{1,0:T(8,128)(2,1)} %collective-permute-done.6.refs_1_.refs_3_, ...), custom_call_target="tpu_custom_call" | custom-call | flops 1 | bytes 1 | tf_op jit(solution)/shard_map/weight_part/pallas_call | solution.py:86
  140.9 6.3 %second_back.1 = (f32[512,768]{1,0:T(8,128)}, bf16[512,768]{1,0:T(8,128)(2,1)}, f32[1,768]{1,0:T(1,128)}, bf16[512,384]{1,0:T(8,128)(2,1)}, bf16[512,384]{1,0:T(8,128)(2,1)}) custom-call(bf16[512,768]{1,0:T(8,128)(2,1)} %refs_0_.6, f32[512,768]{1,0:T(8,128)} %get-tuple-element.85.refs_1_.refs_0_, f32[1,768]{1,0:T(1,128)} %reshape.88.refs_5_.refs_2_, ...), custom_call_target="tpu_custom_call" | custom-call | flops 299999985664 | bytes 1 | tf_op jit(solution)/shard_map/second_back/pallas_call | solution.py:86
  156.4 4.5 %all-to-all-start.1 = ((bf16[4,256,768]{2,1,0:T(8,128)(2,1)}), bf16[4,256,768]{2,1,0:T(8,128)(2,1)}, u32[]{:S(2)}, u32[]{:S(2)}) async-start(bf16[4,256,768]{2,1,0:T(8,128)(2,1)} %touch.11), calls=%async_computation.1 | async-start | bytes 3145728 | tf_op jit(solution)/shard_map/all_to_all | solution.py:1022
  160.9 21.5 %attend_back.1 = (bf16[784,768]{1,0:T(8,128)(2,1)}, bf16[784,768]{1,0:T(8,128)(2,1)}, f32[512,768]{1,0:T(8,128)}, bf16[512,768]{1,0:T(8,128)(2,1)}) custom-call(s32[47]{0:T(128)} %stack.119.refs_0_, bf16[512,384]{1,0:T(8,128)(2,1)} %get-tuple-element.113.refs_1_, bf16[512,384]{1,0:T(8,128)(2,1)} %collective-permute-done.13.refs_2_, ...), custom_call_target="tpu_custom_call" | custom-call | flops 49999998976 | bytes 1 | tf_op jit(solution)/shard_map/attend_back/pallas_call | solution.py:86
  184.8 5.0 %adds.2 = (bf16[384,768]{1,0:T(8,128)(2,1)}, bf16[384,768]{1,0:T(8,128)(2,1)}, bf16[384,768]{1,0:T(8,128)(2,1)}, bf16[384,768]{1,0:T(8,128)(2,1)}) custom-call(s32[47]{0:T(128)} %stack.119.refs_0_, bf16[768,768]{1,0:T(8,128)(2,1)} %get-tuple-element.122.refs_1_, bf16[768,768]{1,0:T(8,128)(2,1)} %collective-permute-done.16.refs_2_, ...), custom_call_target="tpu_custom_call" | custom-call | flops 1 | bytes 1 | tf_op jit(solution)/shard_map/adds/pallas_call | solution.py:86
  198.1 4.3 %all-to-all-start.2 = ((bf16[8,96,768]{2,1,0:T(8,128)(2,1)}), bf16[8,96,768]{2,1,0:T(8,128)(2,1)}, u32[]{:S(2)}, u32[]{:S(2)}) async-start(bf16[8,96,768]{2,1,0:T(8,128)(2,1)} %bitcast.67), calls=%async_computation.2 | async-start | bytes 2359296 | tf_op jit(solution)/shard_map/all_to_all | solution.py:1121
  202.3 3.8 %output_rows.1.refs_5_ = bf16[512,768]{1,0:T(8,128)(2,1)} custom-call(f32[512,768]{1,0:T(8,128)} %get-tuple-element.85.refs_1_.refs_0_, s32[1,512]{1,0:T(1,128)} %bitcast.71, bf16[4,256,768]{2,1,0:T(8,128)(2,1)} %all-to-all-done.1.refs_2_, bf16[8,96,768]{2,1,0:T(8,128)(2,1)} %bitcast.68), custom_call_target="tpu_custom_call" | custom-call | flops 1 | bytes 1 | tf_op jit(solution)/shard_map/output_rows/pallas_call | solution.py:86
  207.9 4.6 %first_back.1.refs_5_ = f32[512,768]{1,0:T(8,128)} custom-call(bf16[512,768]{1,0:T(8,128)(2,1)} %refs_0_.7, f32[1,768]{1,0:T(1,128)} %reshape.86.refs_2_.refs_13_.refs_1_, f32[512,768]{1,0:T(8,128)} %get-tuple-element.127.refs_2_, f32[512,768]{1,0:T(8,128)} %get-tuple-element.128.refs_3_, bf16[512,768]{1,0:T(8,128)(2,1)} %collective-permute-done.18.refs_4_, ...), custom_call_target="tpu_custom_call" | custom-call | flops 299999985664 | bytes 1 | tf_op jit(solution)/shard_map/first_back/pallas_call | solution.py:86
  212.5 7.7 %collective-permute-done.19.refs_6_.refs_2_ = bf16[16,768]{1,0:T(8,128)(2,1)} collective-permute-done((bf16[16,768]{1,0:T(8,128)(2,1)}, bf16[16,768]{1,0:T(8,128)(2,1)}, u32[]{:S(2)}, u32[]{:S(2)}) %collective-permute-start.19) | collective-permute-done | bytes 24608 | tf_op jit(solution)/shard_map/gains/ppermute | solution.py:19
  234.0 4.5 %all-to-all-start.3 = ((bf16[8,112,768]{2,1,0:T(8,128)(2,1)}), bf16[8,112,768]{2,1,0:T(8,128)(2,1)}, u32[]{:S(2)}, u32[]{:S(2)}) async-start(bf16[8,112,768]{2,1,0:T(8,128)(2,1)} %total.1.refs_1_.refs_7_), calls=%async_computation.3 | async-start | bytes 2752512 | tf_op jit(solution)/shard_map/all_to_all | solution.py:1136
  240.2 4.7 %collective-permute-done.23.refs_1_ = bf16[384,768]{1,0:T(8,128)(2,1)} collective-permute-done((bf16[384,768]{1,0:T(8,128)(2,1)}, bf16[384,768]{1,0:T(8,128)(2,1)}, u32[]{:S(2)}, u32[]{:S(2)}) %collective-permute-start.23) | collective-permute-done | bytes 589856 | tf_op jit(solution)/shard_map/piece/ppermute | solution.py:19
  247.4 14.2 %collective-permute-done.28.refs_0_ = bf16[384,768]{1,0:T(8,128)(2,1)} collective-permute-done((bf16[384,768]{1,0:T(8,128)(2,1)}, bf16[384,768]{1,0:T(8,128)(2,1)}, u32[]{:S(2)}, u32[]{:S(2)}) %collective-permute-start.28) | collective-permute-done | bytes 589856 | tf_op jit(solution)/shard_map/piece/ppermute | solution.py:19
  264.4 6.4 %assemble.3.refs_8_.refs_1_.refs_5_ = f32[3072,768]{1,0:T(8,128)} custom-call(s32[47]{0:T(128)} %stack.119.refs_0_, bf16[384,768]{1,0:T(8,128)(2,1)} %get-tuple-element.133.refs_3_.refs_1_, bf16[384,768]{1,0:T(8,128)(2,1)} %get-tuple-element.135.refs_2_, bf16[384,768]{1,0:T(8,128)(2,1)} %get-tuple-element.136.refs_3_, ...), custom_call_target="tpu_custom_call" | custom-call | flops 1 | bytes 1 | tf_op jit(solution)/shard_map/assemble/pallas_call | solution.py:86
  270.8 6.4 %assemble.4.refs_2_.refs_6_ = f32[768,3072]{1,0:T(8,128)} custom-call(s32[47]{0:T(128)} %stack.119.refs_0_, bf16[384,768]{1,0:T(8,128)(2,1)} %get-tuple-element.134.refs_4_.refs_1_, bf16[384,768]{1,0:T(8,128)(2,1)} %get-tuple-element.137.refs_2_, bf16[384,768]{1,0:T(8,128)(2,1)} %get-tuple-element.138.refs_3_, ...), custom_call_target="tpu_custom_call" | custom-call | flops 1 | bytes 1 | tf_op jit(solution)/shard_map/assemble/pallas_call | solution.py:86
  277.2 4.9 %collective-permute-done.24.refs_0_ = bf16[384,768]{1,0:T(8,128)(2,1)} collective-permute-done((bf16[384,768]{1,0:T(8,128)(2,1)}, bf16[384,768]{1,0:T(8,128)(2,1)}, u32[]{:S(2)}, u32[]{:S(2)}) %collective-permute-start.24) | collective-permute-done | bytes 589856 | tf_op jit(solution)/shard_map/piece/ppermute | solution.py:19
  285.6 4.9 %weight_outputs.1 = (f32[3,768,384]{2,1,0:T(8,128)}, f32[384,768]{1,0:T(8,128)}, f32[2,768]{1,0:T(2,128)}) custom-call(s32[1]{0:T(128)} %bitcast.13.refs_0_, bf16[8,112,768]{2,1,0:T(8,128)(2,1)} %touch.19.refs_1_, bf16[8,112,768]{2,1,0:T(8,128)(2,1)} %collective-permute-done.34.refs_2_), custom_call_target="tpu_custom_call" | custom-call | flops 1 | bytes 1 | tf_op jit(solution)/shard_map/weight_outputs/pallas_call | solution.py:86
  291.9 5.3 %assemble.5 = (f32[3072,768]{1,0:T(8,128)}, f32[768,3072]{1,0:T(8,128)}) custom-call(s32[47]{0:T(128)} %stack.119.refs_0_, bf16[384,768]{1,0:T(8,128)(2,1)} %touch.17.refs_1_, bf16[384,768]{1,0:T(8,128)(2,1)} %collective-permute-done.35.refs_2_, bf16[384,768]{1,0:T(8,128)(2,1)} %touch.18.refs_2_.refs_3_, ...), custom_call_target="tpu_custom_call", output_to_operand_aliasing={{0}: (5, {}), {1}: (6, {})} | custom-call | flops 1 | bytes 1 | tf_op jit(solution)/shard_map/assemble/pallas_call | solution.py:86
  (112 shorter events, 74.0 us)
Async XLA Ops:
  0.7 14.6 %collective-permute-start.1 = (s32[512]{0:T(512)}, s32[512]{0:T(512)}, u32[]{:S(2)}, u32[]{:S(2)}) collective-permute-start(s32[512]{0:T(512)} %param.14), channel_id=1, source_target_pairs={{0,1},{1,0},{2,3},{3,2},{4,5},{5,4},{6,7},{7,6},{8,9},{9,8},{10,11... | collective-permute-start | bytes 6152 | tf_op jit(solution)/shard_map/positions/ppermute | solution.py:19
  3.7 22.9 %collective-permute-start = (bf16[512,768]{1,0:T(8,128)(2,1)}, bf16[512,768]{1,0:T(8,128)(2,1)}, u32[]{:S(2)}, u32[]{:S(2)}) collective-permute-start(bf16[512,768]{1,0:T(8,128)(2,1)} %refs_0_.7), channel_id=1, source_target_pairs={{0,1},{1,0},{2,3},{3,2},{4,5},{5,4},{6,7},{7,6},{8,9},{9,8},{10,11... | collective-permute-start | bytes 2359304 | tf_op jit(solution)/shard_map/rows/ppermute | solution.py:19
  18.8 20.7 %collective-permute-start.2 = (bf16[384,768]{1,0:T(8,128)(2,1)}, bf16[384,768]{1,0:T(8,128)(2,1)}, u32[]{:S(2)}, u32[]{:S(2)}) collective-permute-start(bf16[384,768]{1,0:T(8,128)(2,1)} %get-tuple-element.82), channel_id=1, source_target_pairs={{0,1},{1,0},{2,3},{3,2},{4,5},{5,4},{6,7},{7,6},{8,9},{9,8},{10,11... | collective-permute-start | bytes 1769480 | tf_op jit(solution)/shard_map/output_weight/ppermute | solution.py:19
  20.8 56.9 %all-to-all-start = ((bf16[4,256,768]{2,1,0:T(8,128)(2,1)}), bf16[4,256,768]{2,1,0:T(8,128)(2,1)}, u32[]{:S(2)}, u32[]{:S(2)}) async-start(bf16[4,256,768]{2,1,0:T(8,128)(2,1)} %get-tuple-element.87.refs_2_), calls=%async_computation | async-start | bytes 3145728 | tf_op jit(solution)/shard_map/all_to_all | solution.py:1022
  39.5 10.1 %collective-permute-start.3 = (bf16[512,384]{1,0:T(8,128)(2,1)}, bf16[512,384]{1,0:T(8,128)(2,1)}, u32[]{:S(2)}, u32[]{:S(2)}) collective-permute-start(bf16[512,384]{1,0:T(8,128)(2,1)} %get-tuple-element.84.refs_9_), channel_id=1, source_target_pairs={{0,1},{1,0},{2,3},{3,2},{4,5},{5,4},{6,7},{7,6},{8,9},{9,8},{10,11... | collective-permute-start | bytes 1179656 | tf_op jit(solution)/shard_map/context/ppermute | solution.py:19
  54.8 22.9 %collective-permute-start.6 = (bf16[256,768]{1,0:T(8,128)(2,1)}, bf16[256,768]{1,0:T(8,128)(2,1)}, u32[]{:S(2)}, u32[]{:S(2)}) collective-permute-start(bf16[256,768]{1,0:T(8,128)(2,1)} %get-tuple-element.89), channel_id=1, source_target_pairs={{0,2},{2,0},{4,6},{6,4},{1,3},{3,1},{5,7},{7,5},{8,10},{10,8},{12,... | collective-permute-start | bytes 1179656 | tf_op jit(solution)/shard_map/dispatch1/ppermute | solution.py:19
  56.6 32.0 %collective-permute-start.5 = (bf16[256,768]{1,0:T(8,128)(2,1)}, bf16[256,768]{1,0:T(8,128)(2,1)}, u32[]{:S(2)}, u32[]{:S(2)}) collective-permute-start(bf16[256,768]{1,0:T(8,128)(2,1)} %get-tuple-element.88), channel_id=1, source_target_pairs={{0,4},{2,6},{4,0},{6,2},{1,5},{3,7},{5,1},{7,3},{8,12},{10,14},{12... | collective-permute-start | bytes 1179656 | tf_op jit(solution)/shard_map/dispatch2/ppermute | solution.py:19
  59.7 40.2 %collective-permute-start.4 = (bf16[256,768]{1,0:T(8,128)(2,1)}, bf16[256,768]{1,0:T(8,128)(2,1)}, u32[]{:S(2)}, u32[]{:S(2)}) collective-permute-start(bf16[256,768]{1,0:T(8,128)(2,1)} %get-tuple-element.86), channel_id=1, source_target_pairs={{0,6},{2,4},{4,2},{6,0},{1,7},{3,5},{5,3},{7,1},{8,14},{10,12},{12... | collective-permute-start | bytes 1179656 | tf_op jit(solution)/shard_map/dispatch3/ppermute | solution.py:19
  87.9 53.0 %collective-permute-start.7 = (bf16[256,768]{1,0:T(8,128)(2,1)}, bf16[256,768]{1,0:T(8,128)(2,1)}, u32[]{:S(2)}, u32[]{:S(2)}) collective-permute-start(bf16[256,768]{1,0:T(8,128)(2,1)} %get-tuple-element.102), channel_id=1, source_target_pairs={{0,2},{2,0},{4,6},{6,4},{1,3},{3,1},{5,7},{7,5},{8,10},{10,8},{12,... | collective-permute-start | bytes 1179656 | tf_op jit(solution)/shard_map/return1/ppermute | solution.py:19
  98.3 42.5 %collective-permute-start.8 = (bf16[256,768]{1,0:T(8,128)(2,1)}, bf16[256,768]{1,0:T(8,128)(2,1)}, u32[]{:S(2)}, u32[]{:S(2)}) collective-permute-start(bf16[256,768]{1,0:T(8,128)(2,1)} %get-tuple-element.103), channel_id=1, source_target_pairs={{0,4},{2,6},{4,0},{6,2},{1,5},{3,7},{5,1},{7,3},{8,12},{10,14},{12... | collective-permute-start | bytes 1179656 | tf_op jit(solution)/shard_map/return2/ppermute | solution.py:19
  109.7 31.2 %collective-permute-start.9 = (bf16[256,768]{1,0:T(8,128)(2,1)}, bf16[256,768]{1,0:T(8,128)(2,1)}, u32[]{:S(2)}, u32[]{:S(2)}) collective-permute-start(bf16[256,768]{1,0:T(8,128)(2,1)} %get-tuple-element.104.refs_3_), channel_id=1, source_target_pairs={{0,6},{2,4},{4,2},{6,0},{1,7},{3,5},{5,3},{7,1},{8,14},{10,12},{12... | collective-permute-start | bytes 1179656 | tf_op jit(solution)/shard_map/return3/ppermute | solution.py:19
  147.2 13.7 %collective-permute-start.13 = (bf16[512,384]{1,0:T(8,128)(2,1)}, bf16[512,384]{1,0:T(8,128)(2,1)}, u32[]{:S(2)}, u32[]{:S(2)}) collective-permute-start(bf16[512,384]{1,0:T(8,128)(2,1)} %get-tuple-element.110.refs_4_), channel_id=1, source_target_pairs={{0,1},{1,0},{2,3},{3,2},{4,5},{5,4},{6,7},{7,6},{8,9},{9,8},{10,11... | collective-permute-start | bytes 1179656 | tf_op jit(solution)/shard_map/context_grad/ppermute | solution.py:19
  151.0 32.9 %collective-permute-start.16 = (bf16[768,768]{1,0:T(8,128)(2,1)}, bf16[768,768]{1,0:T(8,128)(2,1)}, u32[]{:S(2)}, u32[]{:S(2)}) collective-permute-start(bf16[768,768]{1,0:T(8,128)(2,1)} %get-tuple-element.107.refs_7_), channel_id=1, source_target_pairs={{0,16},{16,0},{1,17},{17,1},{2,18},{18,2},{3,19},{19,3},{4,20},{20... | collective-permute-start | bytes 3538952 | tf_op jit(solution)/shard_map/outer0/ppermute | solution.py:19
  152.5 32.2 %collective-permute-start.17 = (bf16[768,768]{1,0:T(8,128)(2,1)}, bf16[768,768]{1,0:T(8,128)(2,1)}, u32[]{:S(2)}, u32[]{:S(2)}) collective-permute-start(bf16[768,768]{1,0:T(8,128)(2,1)} %get-tuple-element.108.refs_10_.refs_16_), channel_id=1, source_target_pairs={{0,1},{1,0},{2,3},{3,2},{4,5},{5,4},{6,7},{7,6},{8,9},{9,8},{10,11... | collective-permute-start | bytes 3538952 | tf_op jit(solution)/shard_map/inner0/ppermute | solution.py:19
  155.7 36.4 %collective-permute-start.15 = (bf16[192,768]{1,0:T(8,128)(2,1)}, bf16[192,768]{1,0:T(8,128)(2,1)}, u32[]{:S(2)}, u32[]{:S(2)}) collective-permute-start(bf16[192,768]{1,0:T(8,128)(2,1)} %add.231.refs_1_), channel_id=1, source_target_pairs={{0,1},{1,0},{2,3},{3,2},{4,5},{5,4},{6,7},{7,6},{8,9},{9,8},{10,11... | collective-permute-start | bytes 884744 | tf_op jit(solution)/shard_map/output_grad/ppermute | solution.py:19
  156.4 41.7 %all-to-all-start.1 = ((bf16[4,256,768]{2,1,0:T(8,128)(2,1)}), bf16[4,256,768]{2,1,0:T(8,128)(2,1)}, u32[]{:S(2)}, u32[]{:S(2)}) async-start(bf16[4,256,768]{2,1,0:T(8,128)(2,1)} %touch.11), calls=%async_computation.1 | async-start | bytes 3145728 | tf_op jit(solution)/shard_map/all_to_all | solution.py:1022
  182.5 25.4 %collective-permute-start.18 = (bf16[512,768]{1,0:T(8,128)(2,1)}, bf16[512,768]{1,0:T(8,128)(2,1)}, u32[]{:S(2)}, u32[]{:S(2)}) collective-permute-start(bf16[512,768]{1,0:T(8,128)(2,1)} %get-tuple-element.129), channel_id=1, source_target_pairs={{0,1},{1,0},{2,3},{3,2},{4,5},{5,4},{6,7},{7,6},{8,9},{9,8},{10,11... | collective-permute-start | bytes 2359304 | tf_op jit(solution)/shard_map/theirs/ppermute | solution.py:19
  189.7 30.5 %collective-permute-start.20 = (bf16[384,768]{1,0:T(8,128)(2,1)}, bf16[384,768]{1,0:T(8,128)(2,1)}, u32[]{:S(2)}, u32[]{:S(2)}) collective-permute-start(bf16[384,768]{1,0:T(8,128)(2,1)} %get-tuple-element.124.refs_1_), channel_id=1, source_target_pairs={{0,1},{1,0},{2,3},{3,2},{4,5},{5,4},{6,7},{7,6},{8,9},{9,8},{10,11... | collective-permute-start | bytes 1769480 | tf_op jit(solution)/shard_map/outer-1/ppermute | solution.py:19
  190.5 29.7 %collective-permute-start.21 = (bf16[384,768]{1,0:T(8,128)(2,1)}, bf16[384,768]{1,0:T(8,128)(2,1)}, u32[]{:S(2)}, u32[]{:S(2)}) collective-permute-start(bf16[384,768]{1,0:T(8,128)(2,1)} %get-tuple-element.132), channel_id=1, source_target_pairs={{0,16},{16,0},{1,17},{17,1},{2,18},{18,2},{3,19},{19,3},{4,20},{20... | collective-permute-start | bytes 1769480 | tf_op jit(solution)/shard_map/inner-1/ppermute | solution.py:19
  195.1 25.1 %collective-permute-start.19 = (bf16[16,768]{1,0:T(8,128)(2,1)}, bf16[16,768]{1,0:T(8,128)(2,1)}, u32[]{:S(2)}, u32[]{:S(2)}) collective-permute-start(bf16[16,768]{1,0:T(8,128)(2,1)} %get-tuple-element.130.refs_1_), channel_id=1, source_target_pairs={{0,1},{1,0},{2,3},{3,2},{4,5},{5,4},{6,7},{7,6},{8,9},{9,8},{10,11... | collective-permute-start | bytes 73736 | tf_op jit(solution)/shard_map/gains/ppermute | solution.py:19
  198.1 33.4 %all-to-all-start.2 = ((bf16[8,96,768]{2,1,0:T(8,128)(2,1)}), bf16[8,96,768]{2,1,0:T(8,128)(2,1)}, u32[]{:S(2)}, u32[]{:S(2)}) async-start(bf16[8,96,768]{2,1,0:T(8,128)(2,1)} %bitcast.67), calls=%async_computation.2 | async-start | bytes 2359296 | tf_op jit(solution)/shard_map/all_to_all | solution.py:1121
  223.6 16.6 %collective-permute-start.22 = (bf16[384,768]{1,0:T(8,128)(2,1)}, bf16[384,768]{1,0:T(8,128)(2,1)}, u32[]{:S(2)}, u32[]{:S(2)}) collective-permute-start(bf16[384,768]{1,0:T(8,128)(2,1)} %get-tuple-element.133.refs_3_.refs_1_), channel_id=1, source_target_pairs={{0,1},{1,0},{2,3},{3,2},{4,5},{5,4},{6,7},{7,6},{8,9},{9,8},{10,11... | collective-permute-start | bytes 1769480 | tf_op jit(solution)/shard_map/piece/ppermute | solution.py:19
  224.4 20.6 %collective-permute-start.23 = (bf16[384,768]{1,0:T(8,128)(2,1)}, bf16[384,768]{1,0:T(8,128)(2,1)}, u32[]{:S(2)}, u32[]{:S(2)}) collective-permute-start(bf16[384,768]{1,0:T(8,128)(2,1)} %get-tuple-element.133.refs_3_.refs_1_), channel_id=1, source_target_pairs={{0,16},{16,0},{1,17},{17,1},{2,18},{18,2},{3,19},{19,3},{4,20},{20... | collective-permute-start | bytes 1769480 | tf_op jit(solution)/shard_map/piece/ppermute | solution.py:19
  227.8 33.8 %collective-permute-start.28 = (bf16[384,768]{1,0:T(8,128)(2,1)}, bf16[384,768]{1,0:T(8,128)(2,1)}, u32[]{:S(2)}, u32[]{:S(2)}) collective-permute-start(bf16[384,768]{1,0:T(8,128)(2,1)} %get-tuple-element.134.refs_4_.refs_1_), channel_id=1, source_target_pairs={{0,16},{16,0},{1,17},{17,1},{2,18},{18,2},{3,19},{19,3},{4,20},{20... | collective-permute-start | bytes 1769480 | tf_op jit(solution)/shard_map/piece/ppermute | solution.py:19
  228.3 33.2 %collective-permute-start.29 = (bf16[384,768]{1,0:T(8,128)(2,1)}, bf16[384,768]{1,0:T(8,128)(2,1)}, u32[]{:S(2)}, u32[]{:S(2)}) collective-permute-start(bf16[384,768]{1,0:T(8,128)(2,1)} %get-tuple-element.134.refs_4_.refs_1_), channel_id=1, source_target_pairs={{0,1},{1,0},{2,3},{3,2},{4,5},{5,4},{6,7},{7,6},{8,9},{9,8},{10,11... | collective-permute-start | bytes 1769480 | tf_op jit(solution)/shard_map/piece/ppermute | solution.py:19
  234.0 48.1 %all-to-all-start.3 = ((bf16[8,112,768]{2,1,0:T(8,128)(2,1)}), bf16[8,112,768]{2,1,0:T(8,128)(2,1)}, u32[]{:S(2)}, u32[]{:S(2)}) async-start(bf16[8,112,768]{2,1,0:T(8,128)(2,1)} %total.1.refs_1_.refs_7_), calls=%async_computation.3 | async-start | bytes 2752512 | tf_op jit(solution)/shard_map/all_to_all | solution.py:1136
  244.9 17.1 %collective-permute-start.26 = (bf16[384,768]{1,0:T(8,128)(2,1)}, bf16[384,768]{1,0:T(8,128)(2,1)}, u32[]{:S(2)}, u32[]{:S(2)}) collective-permute-start(bf16[384,768]{1,0:T(8,128)(2,1)} %get-tuple-element.135.refs_2_), channel_id=1, source_target_pairs={{0,8},{8,0},{1,9},{9,1},{2,10},{10,2},{3,11},{11,3},{4,12},{12,4},... | collective-permute-start | bytes 1769480 | tf_op jit(solution)/shard_map/piece_core/ppermute | solution.py:19
  244.9 17.2 %collective-permute-start.27 = (bf16[384,768]{1,0:T(8,128)(2,1)}, bf16[384,768]{1,0:T(8,128)(2,1)}, u32[]{:S(2)}, u32[]{:S(2)}) collective-permute-start(bf16[384,768]{1,0:T(8,128)(2,1)} %get-tuple-element.136.refs_3_), channel_id=1, source_target_pairs={{0,8},{8,0},{1,9},{9,1},{2,10},{10,2},{3,11},{11,3},{4,12},{12,4},... | collective-permute-start | bytes 1769480 | tf_op jit(solution)/shard_map/piece_core/ppermute | solution.py:19
  245.4 17.7 %collective-permute-start.25 = (bf16[384,768]{1,0:T(8,128)(2,1)}, bf16[384,768]{1,0:T(8,128)(2,1)}, u32[]{:S(2)}, u32[]{:S(2)}) collective-permute-start(bf16[384,768]{1,0:T(8,128)(2,1)} %touch.14), channel_id=1, source_target_pairs={{0,8},{8,0},{1,9},{9,1},{2,10},{10,2},{3,11},{11,3},{4,12},{12,4},... | collective-permute-start | bytes 1769480 | tf_op jit(solution)/shard_map/piece_core/ppermute | solution.py:19
  262.1 19.9 %collective-permute-start.24 = (bf16[384,768]{1,0:T(8,128)(2,1)}, bf16[384,768]{1,0:T(8,128)(2,1)}, u32[]{:S(2)}, u32[]{:S(2)}) collective-permute-start(bf16[384,768]{1,0:T(8,128)(2,1)} %get-tuple-element.135.refs_2_), channel_id=1, source_target_pairs={{0,16},{16,0},{1,17},{17,1},{2,18},{18,2},{3,19},{19,3},{4,20},{20... | collective-permute-start | bytes 1769480 | tf_op jit(solution)/shard_map/piece/ppermute | solution.py:19
  263.1 18.9 %collective-permute-start.33 = (bf16[384,768]{1,0:T(8,128)(2,1)}, bf16[384,768]{1,0:T(8,128)(2,1)}, u32[]{:S(2)}, u32[]{:S(2)}) collective-permute-start(bf16[384,768]{1,0:T(8,128)(2,1)} %get-tuple-element.137.refs_2_), channel_id=1, source_target_pairs={{0,1},{1,0},{2,3},{3,2},{4,5},{5,4},{6,7},{7,6},{8,9},{9,8},{10,11... | collective-permute-start | bytes 1769480 | tf_op jit(solution)/shard_map/piece/ppermute | solution.py:19
  282.1 9.8 %collective-permute-start.35 = (bf16[384,768]{1,0:T(8,128)(2,1)}, bf16[384,768]{1,0:T(8,128)(2,1)}, u32[]{:S(2)}, u32[]{:S(2)}) collective-permute-start(bf16[384,768]{1,0:T(8,128)(2,1)} %touch.17.refs_1_), channel_id=1, source_target_pairs={{0,8},{8,0},{1,9},{9,1},{2,10},{10,2},{3,11},{11,3},{4,12},{12,4},... | collective-permute-start | bytes 1769480 | tf_op jit(solution)/shard_map/piece_core/ppermute | solution.py:19
  (12 other events, 90.6 us)

commit v4 on v3

--- a/solution.py
+++ b/solution.py
@@ -312,6 +312,7 @@
         shaped(hidden.shape, BF),
         "output_rows",
         after,
+        flops=FIRST_FLOPS,
     )
 
 
@@ -394,7 +395,6 @@
         shaped(x.shape, F32),
         "first_back",
         after,
-        flops=FIRST_FLOPS,
     )
 
 
@@ -466,7 +466,7 @@
             ref[...] = grad_acc[i * size : (i + 1) * size].astype(BF)
 
 
-def expert(place, index, blocks, cot, inner, outer, earlier, after=(), tile=768, sub=256):
+def expert(place, index, blocks, cot, inner, outer, earlier, after=(), tile=1536, sub=256):
     count, width = blocks[0].shape
     size, units = len(blocks), inner.shape[1]
     total = count * cot.shape[0]
@@ -630,25 +630,27 @@
     return plain(gather_sum_kernel, [kept, got, more], out, "gather_sum", after)
 
 
-def adds_kernel(start, count, cuts, info_ref, *refs):
+def adds_kernel(start, count, cuts, whole_sum, info_ref, *refs):
     in_refs, out_refs = refs[: 2 * count], refs[2 * count :]
     for i in range(count):
         kept_ref, got_ref = in_refs[2 * i : 2 * i + 2]
         for j in range(cuts):
             ref = out_refs[cuts * i + j]
             rows = ref.shape[0]
-            at = info_ref[start + cuts * i + j] if cuts > 1 else 0
+            at = 0 if whole_sum else info_ref[start + cuts * i + j]
             cut = pl.ds(pl.multiple_of(at * rows, rows), rows)
             ref[...] = (kept_ref[cut, :].astype(F32) + got_ref[cut, :].astype(F32)).astype(BF)
 
 
-def adds(info, start, pairs, cuts, after=()):
+def adds(info, start, pairs, cuts, whole_sum=False, after=()):
     out = [
-        shaped((kept.shape[0] // cuts, kept.shape[1]), BF) for kept, _ in pairs for _ in range(cuts)
+        shaped((kept.shape[0] // (1 if whole_sum else cuts), kept.shape[1]), BF)
+        for kept, _ in pairs
+        for _ in range(cuts)
     ]
     operands = [x for pair in pairs for x in pair]
     parts = call(
-        functools.partial(adds_kernel, start, len(pairs), cuts),
+        functools.partial(adds_kernel, start, len(pairs), cuts, whole_sum),
         operands,
         after=after,
         prefetch=[info],
@@ -675,7 +677,7 @@
     return places
 
 
-def gather_pieces(own, steps, order, flops):
+def gather_pieces(own, steps, order, flops, after):
     pieces, newest = [own], [(0, own)]
     while newest:
         found = [
@@ -684,7 +686,7 @@
             for i in range(first, len(order))
         ]
         if len(pieces) == 1:
-            held = touch([piece for _, piece in found], [], flops=flops)
+            held = touch([piece for _, piece in found], after, flops=flops)
             found = [(first, piece) for (first, _), piece in zip(found, held)]
         pieces += [piece for _, piece in found]
         newest = found
@@ -1119,28 +1121,28 @@
     crowd = ("x", "expert")
     summed = summed.reshape(-1, end // lax.axis_size(crowd), model_width)
     arrived = lax.all_to_all(summed, crowd, split_axis=0, concat_axis=0, tiled=True)
-    theirs = swap(theirs, "head", 1, "theirs")
     block_output = output_rows(hidden, absolute[None, :], combined, after=[summed])
-    input_grad = first_back(
-        block_input, first_gain, hidden_grad, mine, theirs, after=[block_output]
-    )
     got_tail = swap(tail, "head", 1, "gains")
-    (outer_own,), (inner_own,) = adds(
-        info, 0, pairs_of(outer_parts, inner_parts, -1), 1, after=[input_grad, got_tail]
-    )
-    outer_pieces = gather_pieces(outer_own, outer_steps, outer_steps[::-1], BACK_FLOPS)
-    inner_pieces = gather_pieces(inner_own, inner_steps, inner_steps[::-1], 1)
+    theirs = swap(touch([theirs], [got_tail])[0], "head", 1, "theirs")
+    (outer_own, outer_copy), (inner_own, inner_copy) = adds(
+        info, 0, pairs_of(outer_parts, inner_parts, -1), 2, True, after=[block_output, got_tail]
+    )
     arrived = total(
         arrived, tail, got_tail, after=[outer_own, inner_own]
     )
+    input_grad = first_back(
+        block_input, first_gain, hidden_grad, mine, theirs, after=[arrived]
+    )
+    outer_pieces = gather_pieces(outer_own, outer_steps, outer_steps[::-1], BACK_FLOPS, [input_grad])
+    inner_pieces = gather_pieces(inner_own, inner_steps, inner_steps[::-1], 1, [input_grad])
     summed = lax.all_to_all(arrived, crowd, split_axis=0, concat_axis=0, tiled=True)
 
     def core_swaps(pieces):
         return [(at, swap(piece, "core", 1, "piece_core")) for at, piece in pieces]
 
     others = []
-    for pieces in (outer_pieces, inner_pieces):
-        (held,) = touch([pieces[0][1]], [arrived])
+    for pieces, own in ((outer_pieces, outer_copy), (inner_pieces, inner_copy)):
+        (held,) = touch([own], [arrived])
         others.append(core_swaps([(pieces[0][0], held), *pieces[1:early]]))
     shapes = [outer_weight.shape, inner_weight.shape]
     totals = []

time: 302 us -> 296 us (0.980)
  local copies, waits for them, and re-layouts: 11.4 us -> 7.54 us
    all_to_all x1, waiting for transfers between devices: 1.8 us -> 9.43 us  [on_device(): lax.all_to_all(summed, crowd, split_axis=0, concat_axis=0, tiled=True)]
    ppermute x37, waiting for transfers between devices: 50.7 us -> 43.4 us  [swap(): return lax.ppermute(values, axis, [(i, i ^ bit) for i in range(size)])]
    unnamed x8 -> x6, local copies, waits for them, and re-layouts: 3.88 us -> 0.01 us
    pallas_call x38 -> x39, Pallas kernels: 178 us -> 179 us  [call(): pl.pallas_call(body, input_output_aliases={first + i: i for i in range(le...]
  transfers between devices with their start and end apart: 41 -> 41, of which waited for: 13 -> 12; matrix products, arithmetic and copies ran while one was open for 5% -> 4% of each run, Pallas kernels for 56% -> 57%
where the time goes in v4:
time: 296 us; the launch traced here: 292 us
  Pallas kernels  179 us (60%)
  waiting for transfers between devices  52.8 us (18%)
  starting transfers between devices  49 us (17%)
  local copies, waits for them, and re-layouts  7.54 us (3%)
    pallas_call x39, Pallas kernels, call(): pl.pallas_call(body, input_output_aliases={first + i: i for i in range(le...  179 us
    ppermute x37, waiting for transfers between devices, swap(): return lax.ppermute(values, axis, [(i, i ^ bit) for i in range(size)])  43.4 us
    ppermute x37, starting transfers between devices, swap(): return lax.ppermute(values, axis, [(i, i ^ bit) for i in range(size)])  30.5 us
    all_to_all x2, starting transfers between devices, exchange_all(): lax.all_to_all(blocks, 'expert', split_axis=0, concat_axis=0, tiled=True)  9.74 us
    all_to_all x1, waiting for transfers between devices, on_device(): lax.all_to_all(summed, crowd, split_axis=0, concat_axis=0, tiled=True)  9.43 us
  transfers between devices with their start and end apart: 41, of which 12 were waited for; matrix products, arithmetic and copies ran while one was open for 4% of the time, Pallas kernels for 57%

profile of v4, /device:TPU:0, one launch (start us, length us, event | category | flops | bytes accessed | tf_op | source)
XLA Modules:
  0.0 291.8 jit_solution(22142454488820642)
XLA Ops:
  10.8 4.5 %project.2 = (bf16[2,512,768]{2,1,0:T(8,128)(2,1)}, bf16[3,2,512,384]{3,2,1,0:T(8,128)(2,1)}) custom-call(s32[1]{0:T(128)} %bitcast.refs_0_, bf16[512,768]{1,0:T(8,128)(2,1)} %refs_0_.7, f32[1,768]{1,0:T(1,128)} %reshape.86.refs_2_.refs_13_.refs_1_, bf16[3,768,384]{2,1,0:T(8,128)(2,1)} %refs_12_.1), custom_call_target="tpu_custom_call" | custom-call | flops 1 | bytes 1 | tf_op jit(solution)/shard_map/project/pallas_call | solution.py:86
  20.8 5.2 %all-to-all-start = ((bf16[4,256,768]{2,1,0:T(8,128)(2,1)}), bf16[4,256,768]{2,1,0:T(8,128)(2,1)}, u32[]{:S(2)}, u32[]{:S(2)}) async-start(bf16[4,256,768]{2,1,0:T(8,128)(2,1)} %get-tuple-element.89.refs_2_), calls=%async_computation | async-start | bytes 3145728 | tf_op jit(solution)/shard_map/all_to_all | solution.py:1024
  26.6 4.5 %project.3 = (bf16[2,512,768]{2,1,0:T(8,128)(2,1)}, bf16[3,2,512,384]{3,2,1,0:T(8,128)(2,1)}) custom-call(s32[1]{0:T(128)S(6)} %sub.107.refs_0_, bf16[512,768]{1,0:T(8,128)(2,1)} %collective-permute-done.refs_1_, f32[1,768]{1,0:T(1,128)} %reshape.86.refs_2_.refs_13_.refs_1_, ...), custom_call_target="tpu_custom_call", output_to_operand_aliasing={{0}: (4, {}), {1}: (5, {})} | custom-call | flops 1 | bytes 1 | tf_op jit(solution)/shard_map/project/pallas_call | solution.py:86
  31.1 8.5 %attend.2 = (bf16[2,6,512,512]{3,2,1,0:T(8,128)(2,1)}, bf16[2,6,512,512]{3,2,1,0:T(8,128)(2,1)}, f32[2,512,384]{2,1,0:T(8,128)}, bf16[512,384]{1,0:T(8,128)(2,1)}) custom-call(s32[1]{0:T(128)S(6)} %sub.107.refs_0_, bf16[3,2,512,384]{3,2,1,0:T(8,128)(2,1)} %get-tuple-element.80.refs_1_.refs_2_.refs_3_.refs_4_.refs_5_, ...), custom_call_target="tpu_custom_call" | custom-call | flops 1 | bytes 1 | tf_op jit(solution)/shard_map/attend/pallas_call | solution.py:86
  39.6 6.8 %attend.3 = (bf16[2,6,512,512]{3,2,1,0:T(8,128)(2,1)}, bf16[2,6,512,512]{3,2,1,0:T(8,128)(2,1)}, f32[2,512,384]{2,1,0:T(8,128)}, bf16[512,384]{1,0:T(8,128)(2,1)}) custom-call(s32[1]{0:T(128)} %bitcast.refs_0_, ...), custom_call_target="tpu_custom_call", output_to_operand_aliasing={{0}: (7, {}), {1}: (8, {}), {2}: (9, {})} | custom-call | flops 20000000000 | bytes 1 | tf_op jit(solution)/shard_map/attend/pallas_call | solution.py:86
  49.6 5.2 %hidden_rows.1 = (f32[512,768]{1,0:T(8,128)}, bf16[256,768]{1,0:T(8,128)(2,1)}, bf16[256,768]{1,0:T(8,128)(2,1)}, bf16[256,768]{1,0:T(8,128)(2,1)}, bf16[256,768]{1,0:T(8,128)(2,1)}) custom-call(bf16[512,768]{1,0:T(8,128)(2,1)} %refs_0_.7, bf16[512,384]{1,0:T(8,128)(2,1)} %get-tuple-element.85.refs_1_.refs_8_, ...), custom_call_target="tpu_custom_call" | custom-call | flops 1 | bytes 1 | tf_op jit(solution)/shard_map/hidden_rows/pallas_call | solution.py:86
  60.0 9.9 %expert.4 = (bf16[1024,3072]{1,0:T(8,128)(2,1)}, bf16[1024,3072]{1,0:T(8,128)(2,1)}, bf16[4,256,768]{2,1,0:T(8,128)(2,1)}, bf16[256,768]{1,0:T(8,128)(2,1)}) custom-call(s32[1]{0:T(128)} %bitcast.12.refs_0_, bf16[256,768]{1,0:T(8,128)(2,1)} %get-tuple-element.92.refs_1_.refs_2_, bf16[4,256,768]{2,1,0:T(8,128)(2,1)} %get-tuple-element.89.refs_2_, ...), custom_call_target="tpu_custom_call" | custom-call | flops 2000000000 | bytes 1 | tf_op jit(solution)/shard_map/expert/pallas_call | solution.py:86
  69.9 7.8 %collective-permute-done.6.refs_1_.refs_3_ = bf16[256,768]{1,0:T(8,128)(2,1)} collective-permute-done((bf16[256,768]{1,0:T(8,128)(2,1)}, bf16[256,768]{1,0:T(8,128)(2,1)}, u32[]{:S(2)}, u32[]{:S(2)}) %collective-permute-start.6) | collective-permute-done | bytes 393248 | tf_op jit(solution)/shard_map/dispatch1/ppermute | solution.py:19
  77.7 9.6 %expert.5 = (bf16[1024,3072]{1,0:T(8,128)(2,1)}, bf16[1024,3072]{1,0:T(8,128)(2,1)}, bf16[4,256,768]{2,1,0:T(8,128)(2,1)}, bf16[256,768]{1,0:T(8,128)(2,1)}) custom-call(s32[1]{0:T(128)} %bitcast.11.refs_0_, bf16[256,768]{1,0:T(8,128)(2,1)} %collective-permute-done.6.refs_1_.refs_3_, ...), custom_call_target="tpu_custom_call", output_to_operand_aliasing={{0}: (5, {}), {1}: (6, {}), {2}: (7, {})} | custom-call | flops 2000000000 | bytes 1 | tf_op jit(solution)/shard_map/expert/pallas_call | solution.py:86
  88.6 9.7 %expert.6 = (bf16[1024,3072]{1,0:T(8,128)(2,1)}, bf16[1024,3072]{1,0:T(8,128)(2,1)}, bf16[4,256,768]{2,1,0:T(8,128)(2,1)}, bf16[256,768]{1,0:T(8,128)(2,1)}) custom-call(s32[1]{0:T(128)} %bitcast.10.refs_0_, bf16[256,768]{1,0:T(8,128)(2,1)} %collective-permute-done.5.refs_1_.refs_4_, ...), custom_call_target="tpu_custom_call", output_to_operand_aliasing={{0}: (5, {}), {1}: (6, {}), {2}: (7, {})} | custom-call | flops 2000000000 | bytes 1 | tf_op jit(solution)/shard_map/expert/pallas_call | solution.py:86
  99.4 9.7 %expert.7 = (bf16[1024,3072]{1,0:T(8,128)(2,1)}, bf16[1024,3072]{1,0:T(8,128)(2,1)}, bf16[4,256,768]{2,1,0:T(8,128)(2,1)}, bf16[256,768]{1,0:T(8,128)(2,1)}) custom-call(s32[1]{0:T(128)} %bitcast.7.refs_0_, bf16[256,768]{1,0:T(8,128)(2,1)} %collective-permute-done.4.refs_1_.refs_5_, ...), custom_call_target="tpu_custom_call", output_to_operand_aliasing={{0}: (5, {}), {1}: (6, {}), {2}: (7, {})} | custom-call | flops 2000000000 | bytes 1 | tf_op jit(solution)/shard_map/expert/pallas_call | solution.py:86
  111.3 7.1 %weight_part.4.refs_6_ = bf16[1536,768]{1,0:T(8,128)(2,1)} custom-call(s32[47]{0:T(128)} %stack.119.refs_0_, bf16[1024,3072]{1,0:T(8,128)(2,1)} %get-tuple-element.108.refs_1_, bf16[4,256,768]{2,1,0:T(8,128)(2,1)} %all-to-all-done.refs_2_, bf16[256,768]{1,0:T(8,128)(2,1)} %get-tuple-element.106.refs_3_), custom_call_target="tpu_custom_call" | custom-call | flops 1 | bytes 1 | tf_op jit(solution)/shard_map/weight_part/pallas_call | solution.py:86
  118.4 6.6 %weight_part.5.refs_1_ = bf16[768,1536]{1,0:T(8,128)(2,1)} custom-call(s32[47]{0:T(128)} %stack.119.refs_0_, bf16[1024,3072]{1,0:T(8,128)(2,1)} %get-tuple-element.107.refs_1_, bf16[256,768]{1,0:T(8,128)(2,1)} %get-tuple-element.92.refs_1_.refs_2_, bf16[256,768]{1,0:T(8,128)(2,1)} %collective-permute-done.6.refs_1_.refs_3_, ...), custom_call_target="tpu_custom_call" | custom-call | flops 1 | bytes 1 | tf_op jit(solution)/shard_map/weight_part/pallas_call | solution.py:86
  126.2 7.3 %weight_part.6 = (bf16[768,768]{1,0:T(8,128)(2,1)}, bf16[768,768]{1,0:T(8,128)(2,1)}) custom-call(s32[47]{0:T(128)} %stack.119.refs_0_, bf16[1024,3072]{1,0:T(8,128)(2,1)} %get-tuple-element.108.refs_1_, bf16[4,256,768]{2,1,0:T(8,128)(2,1)} %all-to-all-done.refs_2_, bf16[1536,768]{1,0:T(8,128)(2,1)} %collective-permute-done.11.refs_3_, f32[8,128]{1,0:T(8,128)} %touch.11.refs_4_), custom_call_target="tpu_custom_call" | custom-call | flops 1 | bytes 1 | tf_op jit(solution)/shard_map/weight_part/pallas_call | solution.py:86
  133.5 7.3 %weight_part.7 = (bf16[768,768]{1,0:T(8,128)(2,1)}, bf16[768,768]{1,0:T(8,128)(2,1)}) custom-call(s32[47]{0:T(128)} %stack.119.refs_0_, bf16[1024,3072]{1,0:T(8,128)(2,1)} %get-tuple-element.107.refs_1_, bf16[256,768]{1,0:T(8,128)(2,1)} %get-tuple-element.92.refs_1_.refs_2_, bf16[256,768]{1,0:T(8,128)(2,1)} %collective-permute-done.6.refs_1_.refs_3_, ...), custom_call_target="tpu_custom_call" | custom-call | flops 1 | bytes 1 | tf_op jit(solution)/shard_map/weight_part/pallas_call | solution.py:86
  140.7 6.3 %second_back.1 = (f32[512,768]{1,0:T(8,128)}, bf16[512,768]{1,0:T(8,128)(2,1)}, f32[1,768]{1,0:T(1,128)}, bf16[512,384]{1,0:T(8,128)(2,1)}, bf16[512,384]{1,0:T(8,128)(2,1)}) custom-call(bf16[512,768]{1,0:T(8,128)(2,1)} %refs_0_.6, f32[512,768]{1,0:T(8,128)} %get-tuple-element.87.refs_1_.refs_0_, f32[1,768]{1,0:T(1,128)} %reshape.88.refs_5_.refs_2_, ...), custom_call_target="tpu_custom_call" | custom-call | flops 299999985664 | bytes 1 | tf_op jit(solution)/shard_map/second_back/pallas_call | solution.py:86
  156.3 4.5 %all-to-all-start.1 = ((bf16[4,256,768]{2,1,0:T(8,128)(2,1)}), bf16[4,256,768]{2,1,0:T(8,128)(2,1)}, u32[]{:S(2)}, u32[]{:S(2)}) async-start(bf16[4,256,768]{2,1,0:T(8,128)(2,1)} %touch.12), calls=%async_computation.1 | async-start | bytes 3145728 | tf_op jit(solution)/shard_map/all_to_all | solution.py:1024
  160.8 21.5 %attend_back.1 = (bf16[784,768]{1,0:T(8,128)(2,1)}, bf16[784,768]{1,0:T(8,128)(2,1)}, f32[512,768]{1,0:T(8,128)}, bf16[512,768]{1,0:T(8,128)(2,1)}) custom-call(s32[47]{0:T(128)} %stack.119.refs_0_, bf16[512,384]{1,0:T(8,128)(2,1)} %get-tuple-element.115.refs_1_, bf16[512,384]{1,0:T(8,128)(2,1)} %collective-permute-done.13.refs_2_, ...), custom_call_target="tpu_custom_call" | custom-call | flops 49999998976 | bytes 1 | tf_op jit(solution)/shard_map/attend_back/pallas_call | solution.py:86
  184.6 4.9 %adds.2 = (bf16[384,768]{1,0:T(8,128)(2,1)}, bf16[384,768]{1,0:T(8,128)(2,1)}, bf16[384,768]{1,0:T(8,128)(2,1)}, bf16[384,768]{1,0:T(8,128)(2,1)}) custom-call(s32[47]{0:T(128)} %stack.119.refs_0_, bf16[768,768]{1,0:T(8,128)(2,1)} %get-tuple-element.124.refs_1_, bf16[768,768]{1,0:T(8,128)(2,1)} %collective-permute-done.16.refs_2_, ...), custom_call_target="tpu_custom_call" | custom-call | flops 1 | bytes 1 | tf_op jit(solution)/shard_map/adds/pallas_call | solution.py:86
  198.2 4.3 %all-to-all-start.2 = ((bf16[8,96,768]{2,1,0:T(8,128)(2,1)}), bf16[8,96,768]{2,1,0:T(8,128)(2,1)}, u32[]{:S(2)}, u32[]{:S(2)}) async-start(bf16[8,96,768]{2,1,0:T(8,128)(2,1)} %bitcast.67), calls=%async_computation.2 | async-start | bytes 2359296 | tf_op jit(solution)/shard_map/all_to_all | solution.py:1123
  202.5 3.8 %output_rows.1.refs_5_ = bf16[512,768]{1,0:T(8,128)(2,1)} custom-call(f32[512,768]{1,0:T(8,128)} %get-tuple-element.87.refs_1_.refs_0_, s32[1,512]{1,0:T(1,128)} %bitcast.74, bf16[4,256,768]{2,1,0:T(8,128)(2,1)} %all-to-all-done.1.refs_2_, bf16[8,96,768]{2,1,0:T(8,128)(2,1)} %bitcast.68), custom_call_target="tpu_custom_call" | custom-call | flops 299999985664 | bytes 1 | tf_op jit(solution)/shard_map/output_rows/pallas_call | solution.py:86
  206.3 4.1 %collective-permute-done.20.refs_2_ = bf16[384,768]{1,0:T(8,128)(2,1)} collective-permute-done((bf16[384,768]{1,0:T(8,128)(2,1)}, bf16[384,768]{1,0:T(8,128)(2,1)}, u32[]{:S(2)}, u32[]{:S(2)}) %collective-permute-start.20) | collective-permute-done | bytes 589856 | tf_op jit(solution)/shard_map/outer-1/ppermute | solution.py:19
  214.0 3.8 %adds.3 = (bf16[384,768]{1,0:T(8,128)(2,1)}, bf16[384,768]{1,0:T(8,128)(2,1)}, bf16[384,768]{1,0:T(8,128)(2,1)}, bf16[384,768]{1,0:T(8,128)(2,1)}) custom-call(s32[47]{0:T(128)} %stack.119.refs_0_, bf16[384,768]{1,0:T(8,128)(2,1)} %get-tuple-element.127.refs_2_.refs_1_, bf16[384,768]{1,0:T(8,128)(2,1)} %collective-permute-done.20.refs_2_, ...), custom_call_target="tpu_custom_call" | custom-call | flops 1 | bytes 1 | tf_op jit(solution)/shard_map/adds/pallas_call | solution.py:86
  221.9 9.4 %all-to-all-done.2.refs_0_ = bf16[8,96,768]{2,1,0:T(8,128)(2,1)} async-done(((bf16[8,96,768]{2,1,0:T(8,128)(2,1)}), bf16[8,96,768]{2,1,0:T(8,128)(2,1)}, u32[]{:S(2)}, u32[]{:S(2)}) %all-to-all-start.2) | async-done | bytes 1179680 | tf_op jit(solution)/shard_map/all_to_all | solution.py:1123
  233.8 4.5 %all-to-all-start.3 = ((bf16[8,112,768]{2,1,0:T(8,128)(2,1)}), bf16[8,112,768]{2,1,0:T(8,128)(2,1)}, u32[]{:S(2)}, u32[]{:S(2)}) async-start(bf16[8,112,768]{2,1,0:T(8,128)(2,1)} %total.1.refs_5_.refs_1_.refs_7_), calls=%async_computation.3 | async-start | bytes 2752512 | tf_op jit(solution)/shard_map/all_to_all | solution.py:1138
  238.4 4.5 %first_back.1.refs_2_ = f32[512,768]{1,0:T(8,128)} custom-call(bf16[512,768]{1,0:T(8,128)(2,1)} %refs_0_.7, f32[1,768]{1,0:T(1,128)} %reshape.86.refs_2_.refs_13_.refs_1_, f32[512,768]{1,0:T(8,128)} %get-tuple-element.129.refs_2_, f32[512,768]{1,0:T(8,128)} %get-tuple-element.130.refs_3_, bf16[512,768]{1,0:T(8,128)(2,1)} %collective-permute-done.19.refs_4_, ...), custom_call_target="tpu_custom_call" | custom-call | flops 1 | bytes 1 | tf_op jit(solution)/shard_map/first_back/pallas_call | solution.py:86
  243.6 9.5 %collective-permute-done.28.refs_0_ = bf16[384,768]{1,0:T(8,128)(2,1)} collective-permute-done((bf16[384,768]{1,0:T(8,128)(2,1)}, bf16[384,768]{1,0:T(8,128)(2,1)}, u32[]{:S(2)}, u32[]{:S(2)}) %collective-permute-start.28) | collective-permute-done | bytes 589856 | tf_op jit(solution)/shard_map/piece/ppermute | solution.py:19
  256.3 6.4 %assemble.3.refs_8_.refs_1_.refs_5_ = f32[3072,768]{1,0:T(8,128)} custom-call(s32[47]{0:T(128)} %stack.119.refs_0_, bf16[384,768]{1,0:T(8,128)(2,1)} %get-tuple-element.135.refs_3_.refs_1_, bf16[384,768]{1,0:T(8,128)(2,1)} %get-tuple-element.137.refs_2_, bf16[384,768]{1,0:T(8,128)(2,1)} %get-tuple-element.138.refs_3_, ...), custom_call_target="tpu_custom_call" | custom-call | flops 1 | bytes 1 | tf_op jit(solution)/shard_map/assemble/pallas_call | solution.py:86
  262.7 6.4 %assemble.4.refs_2_.refs_6_ = f32[768,3072]{1,0:T(8,128)} custom-call(s32[47]{0:T(128)} %stack.119.refs_0_, bf16[384,768]{1,0:T(8,128)(2,1)} %get-tuple-element.136.refs_4_.refs_1_, bf16[384,768]{1,0:T(8,128)(2,1)} %get-tuple-element.140.refs_2_, bf16[384,768]{1,0:T(8,128)(2,1)} %get-tuple-element.141.refs_3_, ...), custom_call_target="tpu_custom_call" | custom-call | flops 1 | bytes 1 | tf_op jit(solution)/shard_map/assemble/pallas_call | solution.py:86
  269.1 7.2 %collective-permute-done.24.refs_0_ = bf16[384,768]{1,0:T(8,128)(2,1)} collective-permute-done((bf16[384,768]{1,0:T(8,128)(2,1)}, bf16[384,768]{1,0:T(8,128)(2,1)}, u32[]{:S(2)}, u32[]{:S(2)}) %collective-permute-start.24) | collective-permute-done | bytes 589856 | tf_op jit(solution)/shard_map/piece/ppermute | solution.py:19
  279.9 4.9 %weight_outputs.1 = (f32[3,768,384]{2,1,0:T(8,128)}, f32[384,768]{1,0:T(8,128)}, f32[2,768]{1,0:T(2,128)}) custom-call(s32[1]{0:T(128)} %bitcast.13.refs_0_, bf16[8,112,768]{2,1,0:T(8,128)(2,1)} %touch.21.refs_1_, bf16[8,112,768]{2,1,0:T(8,128)(2,1)} %collective-permute-done.34.refs_2_), custom_call_target="tpu_custom_call" | custom-call | flops 1 | bytes 1 | tf_op jit(solution)/shard_map/weight_outputs/pallas_call | solution.py:86
  286.2 5.3 %assemble.5 = (f32[3072,768]{1,0:T(8,128)}, f32[768,3072]{1,0:T(8,128)}) custom-call(s32[47]{0:T(128)} %stack.119.refs_0_, bf16[384,768]{1,0:T(8,128)(2,1)} %touch.19.refs_1_, bf16[384,768]{1,0:T(8,128)(2,1)} %collective-permute-done.35.refs_2_, bf16[384,768]{1,0:T(8,128)(2,1)} %touch.20.refs_2_.refs_3_, ...), custom_call_target="tpu_custom_call", output_to_operand_aliasing={{0}: (5, {}), {1}: (6, {})} | custom-call | flops 1 | bytes 1 | tf_op jit(solution)/shard_map/assemble/pallas_call | solution.py:86
  (111 shorter events, 69.5 us)
Async XLA Ops:
  0.7 14.6 %collective-permute-start.1 = (s32[512]{0:T(512)}, s32[512]{0:T(512)}, u32[]{:S(2)}, u32[]{:S(2)}) collective-permute-start(s32[512]{0:T(512)} %param.14), channel_id=1, source_target_pairs={{0,1},{1,0},{2,3},{3,2},{4,5},{5,4},{6,7},{7,6},{8,9},{9,8},{10,11... | collective-permute-start | bytes 6152 | tf_op jit(solution)/shard_map/positions/ppermute | solution.py:19
  3.7 22.9 %collective-permute-start = (bf16[512,768]{1,0:T(8,128)(2,1)}, bf16[512,768]{1,0:T(8,128)(2,1)}, u32[]{:S(2)}, u32[]{:S(2)}) collective-permute-start(bf16[512,768]{1,0:T(8,128)(2,1)} %refs_0_.7), channel_id=1, source_target_pairs={{0,1},{1,0},{2,3},{3,2},{4,5},{5,4},{6,7},{7,6},{8,9},{9,8},{10,11... | collective-permute-start | bytes 2359304 | tf_op jit(solution)/shard_map/rows/ppermute | solution.py:19
  18.8 20.8 %collective-permute-start.2 = (bf16[384,768]{1,0:T(8,128)(2,1)}, bf16[384,768]{1,0:T(8,128)(2,1)}, u32[]{:S(2)}, u32[]{:S(2)}) collective-permute-start(bf16[384,768]{1,0:T(8,128)(2,1)} %get-tuple-element.84), channel_id=1, source_target_pairs={{0,1},{1,0},{2,3},{3,2},{4,5},{5,4},{6,7},{7,6},{8,9},{9,8},{10,11... | collective-permute-start | bytes 1769480 | tf_op jit(solution)/shard_map/output_weight/ppermute | solution.py:19
  20.8 57.0 %all-to-all-start = ((bf16[4,256,768]{2,1,0:T(8,128)(2,1)}), bf16[4,256,768]{2,1,0:T(8,128)(2,1)}, u32[]{:S(2)}, u32[]{:S(2)}) async-start(bf16[4,256,768]{2,1,0:T(8,128)(2,1)} %get-tuple-element.89.refs_2_), calls=%async_computation | async-start | bytes 3145728 | tf_op jit(solution)/shard_map/all_to_all | solution.py:1024
  39.5 10.1 %collective-permute-start.3 = (bf16[512,384]{1,0:T(8,128)(2,1)}, bf16[512,384]{1,0:T(8,128)(2,1)}, u32[]{:S(2)}, u32[]{:S(2)}) collective-permute-start(bf16[512,384]{1,0:T(8,128)(2,1)} %get-tuple-element.86.refs_9_), channel_id=1, source_target_pairs={{0,1},{1,0},{2,3},{3,2},{4,5},{5,4},{6,7},{7,6},{8,9},{9,8},{10,11... | collective-permute-start | bytes 1179656 | tf_op jit(solution)/shard_map/context/ppermute | solution.py:19
  54.9 22.9 %collective-permute-start.6 = (bf16[256,768]{1,0:T(8,128)(2,1)}, bf16[256,768]{1,0:T(8,128)(2,1)}, u32[]{:S(2)}, u32[]{:S(2)}) collective-permute-start(bf16[256,768]{1,0:T(8,128)(2,1)} %get-tuple-element.91), channel_id=1, source_target_pairs={{0,2},{2,0},{4,6},{6,4},{1,3},{3,1},{5,7},{7,5},{8,10},{10,8},{12,... | collective-permute-start | bytes 1179656 | tf_op jit(solution)/shard_map/dispatch1/ppermute | solution.py:19
  56.6 32.0 %collective-permute-start.5 = (bf16[256,768]{1,0:T(8,128)(2,1)}, bf16[256,768]{1,0:T(8,128)(2,1)}, u32[]{:S(2)}, u32[]{:S(2)}) collective-permute-start(bf16[256,768]{1,0:T(8,128)(2,1)} %get-tuple-element.90), channel_id=1, source_target_pairs={{0,4},{2,6},{4,0},{6,2},{1,5},{3,7},{5,1},{7,3},{8,12},{10,14},{12... | collective-permute-start | bytes 1179656 | tf_op jit(solution)/shard_map/dispatch2/ppermute | solution.py:19
  59.7 39.7 %collective-permute-start.4 = (bf16[256,768]{1,0:T(8,128)(2,1)}, bf16[256,768]{1,0:T(8,128)(2,1)}, u32[]{:S(2)}, u32[]{:S(2)}) collective-permute-start(bf16[256,768]{1,0:T(8,128)(2,1)} %get-tuple-element.88), channel_id=1, source_target_pairs={{0,6},{2,4},{4,2},{6,0},{1,7},{3,5},{5,3},{7,1},{8,14},{10,12},{12... | collective-permute-start | bytes 1179656 | tf_op jit(solution)/shard_map/dispatch3/ppermute | solution.py:19
  87.4 53.3 %collective-permute-start.7 = (bf16[256,768]{1,0:T(8,128)(2,1)}, bf16[256,768]{1,0:T(8,128)(2,1)}, u32[]{:S(2)}, u32[]{:S(2)}) collective-permute-start(bf16[256,768]{1,0:T(8,128)(2,1)} %get-tuple-element.104), channel_id=1, source_target_pairs={{0,2},{2,0},{4,6},{6,4},{1,3},{3,1},{5,7},{7,5},{8,10},{10,8},{12,... | collective-permute-start | bytes 1179656 | tf_op jit(solution)/shard_map/return1/ppermute | solution.py:19
  98.3 42.4 %collective-permute-start.8 = (bf16[256,768]{1,0:T(8,128)(2,1)}, bf16[256,768]{1,0:T(8,128)(2,1)}, u32[]{:S(2)}, u32[]{:S(2)}) collective-permute-start(bf16[256,768]{1,0:T(8,128)(2,1)} %get-tuple-element.105), channel_id=1, source_target_pairs={{0,4},{2,6},{4,0},{6,2},{1,5},{3,7},{5,1},{7,3},{8,12},{10,14},{12... | collective-permute-start | bytes 1179656 | tf_op jit(solution)/shard_map/return2/ppermute | solution.py:19
  109.1 31.6 %collective-permute-start.9 = (bf16[256,768]{1,0:T(8,128)(2,1)}, bf16[256,768]{1,0:T(8,128)(2,1)}, u32[]{:S(2)}, u32[]{:S(2)}) collective-permute-start(bf16[256,768]{1,0:T(8,128)(2,1)} %get-tuple-element.106.refs_3_), channel_id=1, source_target_pairs={{0,6},{2,4},{4,2},{6,0},{1,7},{3,5},{5,3},{7,1},{8,14},{10,12},{12... | collective-permute-start | bytes 1179656 | tf_op jit(solution)/shard_map/return3/ppermute | solution.py:19
  147.1 13.7 %collective-permute-start.13 = (bf16[512,384]{1,0:T(8,128)(2,1)}, bf16[512,384]{1,0:T(8,128)(2,1)}, u32[]{:S(2)}, u32[]{:S(2)}) collective-permute-start(bf16[512,384]{1,0:T(8,128)(2,1)} %get-tuple-element.112.refs_4_), channel_id=1, source_target_pairs={{0,1},{1,0},{2,3},{3,2},{4,5},{5,4},{6,7},{7,6},{8,9},{9,8},{10,11... | collective-permute-start | bytes 1179656 | tf_op jit(solution)/shard_map/context_grad/ppermute | solution.py:19
  150.9 31.6 %collective-permute-start.16 = (bf16[768,768]{1,0:T(8,128)(2,1)}, bf16[768,768]{1,0:T(8,128)(2,1)}, u32[]{:S(2)}, u32[]{:S(2)}) collective-permute-start(bf16[768,768]{1,0:T(8,128)(2,1)} %get-tuple-element.109.refs_7_), channel_id=1, source_target_pairs={{0,16},{16,0},{1,17},{17,1},{2,18},{18,2},{3,19},{19,3},{4,20},{20... | collective-permute-start | bytes 3538952 | tf_op jit(solution)/shard_map/outer0/ppermute | solution.py:19
  152.4 32.2 %collective-permute-start.17 = (bf16[768,768]{1,0:T(8,128)(2,1)}, bf16[768,768]{1,0:T(8,128)(2,1)}, u32[]{:S(2)}, u32[]{:S(2)}) collective-permute-start(bf16[768,768]{1,0:T(8,128)(2,1)} %get-tuple-element.110.refs_10_.refs_16_), channel_id=1, source_target_pairs={{0,1},{1,0},{2,3},{3,2},{4,5},{5,4},{6,7},{7,6},{8,9},{9,8},{10,11... | collective-permute-start | bytes 3538952 | tf_op jit(solution)/shard_map/inner0/ppermute | solution.py:19
  155.5 34.5 %collective-permute-start.15 = (bf16[192,768]{1,0:T(8,128)(2,1)}, bf16[192,768]{1,0:T(8,128)(2,1)}, u32[]{:S(2)}, u32[]{:S(2)}) collective-permute-start(bf16[192,768]{1,0:T(8,128)(2,1)} %add.231.refs_1_), channel_id=1, source_target_pairs={{0,1},{1,0},{2,3},{3,2},{4,5},{5,4},{6,7},{7,6},{8,9},{9,8},{10,11... | collective-permute-start | bytes 884744 | tf_op jit(solution)/shard_map/output_grad/ppermute | solution.py:19
  156.3 41.9 %all-to-all-start.1 = ((bf16[4,256,768]{2,1,0:T(8,128)(2,1)}), bf16[4,256,768]{2,1,0:T(8,128)(2,1)}, u32[]{:S(2)}, u32[]{:S(2)}) async-start(bf16[4,256,768]{2,1,0:T(8,128)(2,1)} %touch.12), calls=%async_computation.1 | async-start | bytes 3145728 | tf_op jit(solution)/shard_map/all_to_all | solution.py:1024
  193.8 16.6 %collective-permute-start.20 = (bf16[384,768]{1,0:T(8,128)(2,1)}, bf16[384,768]{1,0:T(8,128)(2,1)}, u32[]{:S(2)}, u32[]{:S(2)}) collective-permute-start(bf16[384,768]{1,0:T(8,128)(2,1)} %get-tuple-element.126.refs_1_), channel_id=1, source_target_pairs={{0,1},{1,0},{2,3},{3,2},{4,5},{5,4},{6,7},{7,6},{8,9},{9,8},{10,11... | collective-permute-start | bytes 1769480 | tf_op jit(solution)/shard_map/outer-1/ppermute | solution.py:19
  195.1 18.9 %collective-permute-start.21 = (bf16[384,768]{1,0:T(8,128)(2,1)}, bf16[384,768]{1,0:T(8,128)(2,1)}, u32[]{:S(2)}, u32[]{:S(2)}) collective-permute-start(bf16[384,768]{1,0:T(8,128)(2,1)} %get-tuple-element.134), channel_id=1, source_target_pairs={{0,16},{16,0},{1,17},{17,1},{2,18},{18,2},{3,19},{19,3},{4,20},{20... | collective-permute-start | bytes 1769480 | tf_op jit(solution)/shard_map/inner-1/ppermute | solution.py:19
  197.5 40.8 %collective-permute-start.19 = (bf16[512,768]{1,0:T(8,128)(2,1)}, bf16[512,768]{1,0:T(8,128)(2,1)}, u32[]{:S(2)}, u32[]{:S(2)}) collective-permute-start(bf16[512,768]{1,0:T(8,128)(2,1)} %touch.14), channel_id=1, source_target_pairs={{0,1},{1,0},{2,3},{3,2},{4,5},{5,4},{6,7},{7,6},{8,9},{9,8},{10,11... | collective-permute-start | bytes 2359304 | tf_op jit(solution)/shard_map/theirs/ppermute | solution.py:19
  198.2 33.1 %all-to-all-start.2 = ((bf16[8,96,768]{2,1,0:T(8,128)(2,1)}), bf16[8,96,768]{2,1,0:T(8,128)(2,1)}, u32[]{:S(2)}, u32[]{:S(2)}) async-start(bf16[8,96,768]{2,1,0:T(8,128)(2,1)} %bitcast.67), calls=%async_computation.2 | async-start | bytes 2359296 | tf_op jit(solution)/shard_map/all_to_all | solution.py:1123
  217.8 25.2 %collective-permute-start.22 = (bf16[384,768]{1,0:T(8,128)(2,1)}, bf16[384,768]{1,0:T(8,128)(2,1)}, u32[]{:S(2)}, u32[]{:S(2)}) collective-permute-start(bf16[384,768]{1,0:T(8,128)(2,1)} %get-tuple-element.135.refs_3_.refs_1_), channel_id=1, source_target_pairs={{0,1},{1,0},{2,3},{3,2},{4,5},{5,4},{6,7},{7,6},{8,9},{9,8},{10,11... | collective-permute-start | bytes 1769480 | tf_op jit(solution)/shard_map/piece/ppermute | solution.py:19
  218.6 24.4 %collective-permute-start.23 = (bf16[384,768]{1,0:T(8,128)(2,1)}, bf16[384,768]{1,0:T(8,128)(2,1)}, u32[]{:S(2)}, u32[]{:S(2)}) collective-permute-start(bf16[384,768]{1,0:T(8,128)(2,1)} %get-tuple-element.135.refs_3_.refs_1_), channel_id=1, source_target_pairs={{0,16},{16,0},{1,17},{17,1},{2,18},{18,2},{3,19},{19,3},{4,20},{20... | collective-permute-start | bytes 1769480 | tf_op jit(solution)/shard_map/piece/ppermute | solution.py:19
  219.9 33.2 %collective-permute-start.28 = (bf16[384,768]{1,0:T(8,128)(2,1)}, bf16[384,768]{1,0:T(8,128)(2,1)}, u32[]{:S(2)}, u32[]{:S(2)}) collective-permute-start(bf16[384,768]{1,0:T(8,128)(2,1)} %get-tuple-element.136.refs_4_.refs_1_), channel_id=1, source_target_pairs={{0,16},{16,0},{1,17},{17,1},{2,18},{18,2},{3,19},{19,3},{4,20},{20... | collective-permute-start | bytes 1769480 | tf_op jit(solution)/shard_map/piece/ppermute | solution.py:19
  220.6 32.5 %collective-permute-start.29 = (bf16[384,768]{1,0:T(8,128)(2,1)}, bf16[384,768]{1,0:T(8,128)(2,1)}, u32[]{:S(2)}, u32[]{:S(2)}) collective-permute-start(bf16[384,768]{1,0:T(8,128)(2,1)} %get-tuple-element.136.refs_4_.refs_1_), channel_id=1, source_target_pairs={{0,1},{1,0},{2,3},{3,2},{4,5},{5,4},{6,7},{7,6},{8,9},{9,8},{10,11... | collective-permute-start | bytes 1769480 | tf_op jit(solution)/shard_map/piece/ppermute | solution.py:19
  233.8 42.5 %all-to-all-start.3 = ((bf16[8,112,768]{2,1,0:T(8,128)(2,1)}), bf16[8,112,768]{2,1,0:T(8,128)(2,1)}, u32[]{:S(2)}, u32[]{:S(2)}) async-start(bf16[8,112,768]{2,1,0:T(8,128)(2,1)} %total.1.refs_5_.refs_1_.refs_7_), calls=%async_computation.3 | async-start | bytes 2752512 | tf_op jit(solution)/shard_map/all_to_all | solution.py:1138
  238.4 15.3 %collective-permute-start.25 = (bf16[384,768]{1,0:T(8,128)(2,1)}, bf16[384,768]{1,0:T(8,128)(2,1)}, u32[]{:S(2)}, u32[]{:S(2)}) collective-permute-start(bf16[384,768]{1,0:T(8,128)(2,1)} %touch.16), channel_id=1, source_target_pairs={{0,8},{8,0},{1,9},{9,1},{2,10},{10,2},{3,11},{11,3},{4,12},{12,4},... | collective-permute-start | bytes 1769480 | tf_op jit(solution)/shard_map/piece_core/ppermute | solution.py:19
  243.0 10.7 %collective-permute-start.26 = (bf16[384,768]{1,0:T(8,128)(2,1)}, bf16[384,768]{1,0:T(8,128)(2,1)}, u32[]{:S(2)}, u32[]{:S(2)}) collective-permute-start(bf16[384,768]{1,0:T(8,128)(2,1)} %get-tuple-element.137.refs_2_), channel_id=1, source_target_pairs={{0,8},{8,0},{1,9},{9,1},{2,10},{10,2},{3,11},{11,3},{4,12},{12,4},... | collective-permute-start | bytes 1769480 | tf_op jit(solution)/shard_map/piece_core/ppermute | solution.py:19
  243.6 11.5 %collective-permute-start.27 = (bf16[384,768]{1,0:T(8,128)(2,1)}, bf16[384,768]{1,0:T(8,128)(2,1)}, u32[]{:S(2)}, u32[]{:S(2)}) collective-permute-start(bf16[384,768]{1,0:T(8,128)(2,1)} %get-tuple-element.138.refs_3_), channel_id=1, source_target_pairs={{0,8},{8,0},{1,9},{9,1},{2,10},{10,2},{3,11},{11,3},{4,12},{12,4},... | collective-permute-start | bytes 1769480 | tf_op jit(solution)/shard_map/piece_core/ppermute | solution.py:19
  253.1 9.6 %collective-permute-start.30 = (bf16[384,768]{1,0:T(8,128)(2,1)}, bf16[384,768]{1,0:T(8,128)(2,1)}, u32[]{:S(2)}, u32[]{:S(2)}) collective-permute-start(bf16[384,768]{1,0:T(8,128)(2,1)} %touch.18), channel_id=1, source_target_pairs={{0,8},{8,0},{1,9},{9,1},{2,10},{10,2},{3,11},{11,3},{4,12},{12,4},... | collective-permute-start | bytes 1769480 | tf_op jit(solution)/shard_map/piece_core/ppermute | solution.py:19
  253.7 22.6 %collective-permute-start.24 = (bf16[384,768]{1,0:T(8,128)(2,1)}, bf16[384,768]{1,0:T(8,128)(2,1)}, u32[]{:S(2)}, u32[]{:S(2)}) collective-permute-start(bf16[384,768]{1,0:T(8,128)(2,1)} %get-tuple-element.137.refs_2_), channel_id=1, source_target_pairs={{0,16},{16,0},{1,17},{17,1},{2,18},{18,2},{3,19},{19,3},{4,20},{20... | collective-permute-start | bytes 1769480 | tf_op jit(solution)/shard_map/piece/ppermute | solution.py:19
  255.1 21.3 %collective-permute-start.33 = (bf16[384,768]{1,0:T(8,128)(2,1)}, bf16[384,768]{1,0:T(8,128)(2,1)}, u32[]{:S(2)}, u32[]{:S(2)}) collective-permute-start(bf16[384,768]{1,0:T(8,128)(2,1)} %get-tuple-element.140.refs_2_), channel_id=1, source_target_pairs={{0,1},{1,0},{2,3},{3,2},{4,5},{5,4},{6,7},{7,6},{8,9},{9,8},{10,11... | collective-permute-start | bytes 1769480 | tf_op jit(solution)/shard_map/piece/ppermute | solution.py:19
  276.4 9.8 %collective-permute-start.35 = (bf16[384,768]{1,0:T(8,128)(2,1)}, bf16[384,768]{1,0:T(8,128)(2,1)}, u32[]{:S(2)}, u32[]{:S(2)}) collective-permute-start(bf16[384,768]{1,0:T(8,128)(2,1)} %touch.19.refs_1_), channel_id=1, source_target_pairs={{0,8},{8,0},{1,9},{9,1},{2,10},{10,2},{3,11},{11,3},{4,12},{12,4},... | collective-permute-start | bytes 1769480 | tf_op jit(solution)/shard_map/piece_core/ppermute | solution.py:19
  (12 other events, 84.6 us)

commit v5 on v4

--- a/solution.py
+++ b/solution.py
@@ -49,6 +49,10 @@
 
 def dot_nt(left, right):
     return lax.dot_general(left, right, (((1,), (1,)), ((), ())), preferred_element_type=F32)
+
+
+def row_of(ref):
+    return ref[...].reshape(1, ref.shape[0])
 
 
 def norm_parts(values):
@@ -113,7 +117,7 @@
 
 def project_kernel(which_ref, x_ref, gain_ref, weight_ref, first_ref, out_ref):
     normed, _ = norm_parts(x_ref[...].astype(F32))
-    first = (normed * gain_ref[...]).astype(BF)
+    first = (normed * row_of(gain_ref)).astype(BF)
     first_ref[0] = first
     for c in range(3):
         out_ref[c, 0] = dot(first, weight_ref[c]).astype(BF)
@@ -132,7 +136,7 @@
         grid=(tiles,),
         in_specs=[
             pl.BlockSpec((size, width), lambda i, w: (i, 0)),
-            whole((1, width)),
+            whole((width,)),
             whole((3, width, cols)),
         ],
         out_specs=[
@@ -253,7 +257,7 @@
     hidden = x_ref[...].astype(F32) + attended
     hidden_ref[...] = hidden
     normed, _ = norm_parts(hidden)
-    second = (normed * gain_ref[...]).astype(BF)
+    second = (normed * row_of(gain_ref)).astype(BF)
     send_rows(second, slot_ref, out_refs)
 
 
@@ -321,7 +325,7 @@
     second_grad = taken_rows(slot_ref, refs[:-5])
     normed, scale = norm_parts(hidden_ref[...])
     gain_grad_ref[...] = jnp.sum(second_grad * normed, axis=0, keepdims=True)
-    grad = cot_ref[...].astype(F32) + norm_back(second_grad * gain_ref[...], normed, scale)
+    grad = cot_ref[...].astype(F32) + norm_back(second_grad * row_of(gain_ref), normed, scale)
     grad_ref[...] = grad
     low = grad.astype(BF)
     low_ref[...] = low
@@ -383,7 +387,7 @@
 
 
 def first_kernel(x_ref, gain_ref, hidden_grad_ref, own_ref, theirs_ref, out_ref):
-    grad = (own_ref[...] + theirs_ref[...].astype(F32)) * gain_ref[...]
+    grad = (own_ref[...] + theirs_ref[...].astype(F32)) * row_of(gain_ref)
     normed, scale = norm_parts(x_ref[...].astype(F32))
     out_ref[...] = hidden_grad_ref[...] + norm_back(grad, normed, scale)
 
@@ -829,7 +833,7 @@
         gain = 0.0
         for h in (0, 1):
             gain = gain + jnp.sum(acc[h] * first_ref[h].astype(F32), axis=0, keepdims=True)
-        gain = gain / gain_ref[...]
+        gain = gain / row_of(gain_ref)
         part = own_output_ref.shape[0] // 2
         at = groups * size
         end = at + part
@@ -880,7 +884,7 @@
             pl.BlockSpec((2, count, PAIR), lambda g, w: (0, 0, g)),
             whole((2, count, width)),
             pl.BlockSpec((3, width, PAIR), lambda g, w: (0, 0, g)),
-            whole((1, width)),
+            whole((width,)),
             whole((1, width)),
             whole((cols, width)),
         ],
@@ -900,7 +904,7 @@
     )
 
 
-def weight_outputs_kernel(rows, core_ref, kept_ref, got_ref, project_ref, output_ref, gains_ref):
+def weight_outputs_kernel(rows, core_ref, kept_ref, got_ref, project_ref, output_ref, *gain_refs):
     group, groups = pl.program_id(0), pl.num_programs(0)
     size = 3 * PAIR // 2
 
@@ -925,9 +929,9 @@
         output_ref[:part], output_ref[part:] = halves_of(body, range(first, count))
         tails = halves_of(slice(rows, rows + 16), range(count))
         for i, tail in enumerate(tails):
-            gains_ref[i : i + 1] = sum(
+            gain_refs[i][...] = sum(
                 tail[16 * b : 16 * b + 1] + tail[16 * b + 1 : 16 * b + 2] for b in range(count)
-            )
+            )[0]
 
 
 def weight_outputs(core, kept, got, cols, after=()):
@@ -942,9 +946,11 @@
         out_specs=[
             pl.BlockSpec((3, width, PAIR), lambda g, w: (0, 0, g)),
             whole((cols, width)),
-            whole((2, width)),
+            whole((width,)),
+            whole((width,)),
         ],
-        out_shape=[shaped((3, width, cols), F32), shaped((cols, width), F32), shaped((2, width), F32)],
+        out_shape=[shaped((3, width, cols), F32), shaped((cols, width), F32)]
+        + [shaped((width,), F32)] * 2,
         name="weight_outputs",
     )
 
@@ -1000,8 +1006,6 @@
     info = jnp.stack(entries).astype(jnp.int32)
     own_at, core_at = my_head.reshape(1).astype(jnp.int32), core.reshape(1).astype(jnp.int32)
     other_at = 1 - own_at
-    first_gain = first_gain.reshape(1, model_width)
-    second_gain = second_gain.reshape(1, model_width)
 
     other_input = swap(block_input, "head", 1, "rows")
     other_pos = swap(positions, "head", 1, "positions")
@@ -1158,7 +1162,7 @@
     late_others = [core_swaps(pieces) for pieces in late]
     (kept,) = touch([summed], [pieces[0][1] for pieces in late])
     got = swap(kept, "core", 1, "weight_back")
-    project_grad, output_weight_grad, gains = weight_outputs(core_at, kept, got, local_cols)
+    project_grad, output_weight_grad, first_total, second_total = weight_outputs(core_at, kept, got, local_cols)
     chosen = [
         [piece for _, piece in own + other] for own, other in zip(late, late_others)
     ]
@@ -1168,8 +1172,8 @@
     return (
         block_output,
         input_grad,
-        gains[0],
-        gains[1],
+        first_total,
+        second_total,
         project_grad,
         output_weight_grad,
         inner_total[None],

time: 296 us -> 294 us (level)
  transfers between devices with their start and end apart: 41 -> 41, of which waited for: 12 -> 12; matrix products, arithmetic and copies ran while one was open for 4% -> 3% of each run, Pallas kernels for 57% -> 58%
where the time goes in v5:
time: 294 us; the launch traced here: 289 us
  Pallas kernels  178 us (61%)
  waiting for transfers between devices  53.8 us (18%)
  starting transfers between devices  48 us (16%)
  local copies, waits for them, and re-layouts  4.98 us (2%)
    pallas_call x39, Pallas kernels, call(): pl.pallas_call(body, input_output_aliases={first + i: i for i in range(le...  178 us
    ppermute x37, waiting for transfers between devices, swap(): return lax.ppermute(values, axis, [(i, i ^ bit) for i in range(size)])  44.3 us
    ppermute x37, starting transfers between devices, swap(): return lax.ppermute(values, axis, [(i, i ^ bit) for i in range(size)])  29.7 us
    all_to_all x2, starting transfers between devices, exchange_all(): lax.all_to_all(blocks, 'expert', split_axis=0, concat_axis=0, tiled=True)  9.6 us
    all_to_all x1, waiting for transfers between devices, on_device(): lax.all_to_all(summed, crowd, split_axis=0, concat_axis=0, tiled=True)  9.46 us
  transfers between devices with their start and end apart: 41, of which 12 were waited for; matrix products, arithmetic and copies ran while one was open for 3% of the time, Pallas kernels for 58%

profile of v5, /device:TPU:0, one launch (start us, length us, event | category | flops | bytes accessed | tf_op | source)
XLA Modules:
  0.0 289.2 jit_solution(16597463786597576860)
XLA Ops:
  10.2 4.5 %project.2 = (bf16[2,512,768]{2,1,0:T(8,128)(2,1)}, bf16[3,2,512,384]{3,2,1,0:T(8,128)(2,1)}) custom-call(s32[1]{0:T(128)} %bitcast.refs_0_, bf16[512,768]{1,0:T(8,128)(2,1)} %refs_0_.7, f32[768]{0:T(1024)} %refs_1_.3, bf16[3,768,384]{2,1,0:T(8,128)(2,1)} %refs_12_.1), custom_call_target="tpu_custom_call" | custom-call | flops 1 | bytes 1 | tf_op jit(solution)/shard_map/project/pallas_call | solution.py:90
  20.2 5.1 %all-to-all-start = ((bf16[4,256,768]{2,1,0:T(8,128)(2,1)}), bf16[4,256,768]{2,1,0:T(8,128)(2,1)}, u32[]{:S(2)}, u32[]{:S(2)}) async-start(bf16[4,256,768]{2,1,0:T(8,128)(2,1)} %get-tuple-element.90.refs_2_), calls=%async_computation | async-start | bytes 3145728 | tf_op jit(solution)/shard_map/all_to_all | solution.py:1028
  25.3 4.5 %project.3 = (bf16[2,512,768]{2,1,0:T(8,128)(2,1)}, bf16[3,2,512,384]{3,2,1,0:T(8,128)(2,1)}) custom-call(s32[1]{0:T(128)S(6)} %sub.107.refs_0_, bf16[512,768]{1,0:T(8,128)(2,1)} %collective-permute-done.refs_1_, f32[768]{0:T(1024)} %refs_1_.3, bf16[3,768,384]{2,1,0:T(8,128)(2,1)} %refs_12_.1, ...), custom_call_target="tpu_custom_call", output_to_operand_aliasing={{0}: (4, {}), {1}: (5, {})} | custom-call | flops 1 | bytes 1 | tf_op jit(solution)/shard_map/project/pallas_call | solution.py:90
  29.8 8.5 %attend.2 = (bf16[2,6,512,512]{3,2,1,0:T(8,128)(2,1)}, bf16[2,6,512,512]{3,2,1,0:T(8,128)(2,1)}, f32[2,512,384]{2,1,0:T(8,128)}, bf16[512,384]{1,0:T(8,128)(2,1)}) custom-call(s32[1]{0:T(128)S(6)} %sub.107.refs_0_, bf16[3,2,512,384]{3,2,1,0:T(8,128)(2,1)} %get-tuple-element.81.refs_1_.refs_2_.refs_3_.refs_4_.refs_5_, ...), custom_call_target="tpu_custom_call" | custom-call | flops 1 | bytes 1 | tf_op jit(solution)/shard_map/attend/pallas_call | solution.py:90
  38.3 6.8 %attend.3 = (bf16[2,6,512,512]{3,2,1,0:T(8,128)(2,1)}, bf16[2,6,512,512]{3,2,1,0:T(8,128)(2,1)}, f32[2,512,384]{2,1,0:T(8,128)}, bf16[512,384]{1,0:T(8,128)(2,1)}) custom-call(s32[1]{0:T(128)} %bitcast.refs_0_, ...), custom_call_target="tpu_custom_call", output_to_operand_aliasing={{0}: (7, {}), {1}: (8, {}), {2}: (9, {})} | custom-call | flops 20000000000 | bytes 1 | tf_op jit(solution)/shard_map/attend/pallas_call | solution.py:90
  48.4 5.2 %hidden_rows.1 = (f32[512,768]{1,0:T(8,128)}, bf16[256,768]{1,0:T(8,128)(2,1)}, bf16[256,768]{1,0:T(8,128)(2,1)}, bf16[256,768]{1,0:T(8,128)(2,1)}, bf16[256,768]{1,0:T(8,128)(2,1)}) custom-call(bf16[512,768]{1,0:T(8,128)(2,1)} %refs_0_.7, bf16[512,384]{1,0:T(8,128)(2,1)} %get-tuple-element.86.refs_1_.refs_8_, ...), custom_call_target="tpu_custom_call" | custom-call | flops 1 | bytes 1 | tf_op jit(solution)/shard_map/hidden_rows/pallas_call | solution.py:90
  58.7 9.9 %expert.4 = (bf16[1024,3072]{1,0:T(8,128)(2,1)}, bf16[1024,3072]{1,0:T(8,128)(2,1)}, bf16[4,256,768]{2,1,0:T(8,128)(2,1)}, bf16[256,768]{1,0:T(8,128)(2,1)}) custom-call(s32[1]{0:T(128)} %bitcast.12.refs_0_, bf16[256,768]{1,0:T(8,128)(2,1)} %get-tuple-element.93.refs_1_.refs_2_, bf16[4,256,768]{2,1,0:T(8,128)(2,1)} %get-tuple-element.90.refs_2_, ...), custom_call_target="tpu_custom_call" | custom-call | flops 2000000000 | bytes 1 | tf_op jit(solution)/shard_map/expert/pallas_call | solution.py:90
  68.6 7.9 %collective-permute-done.6.refs_1_.refs_3_ = bf16[256,768]{1,0:T(8,128)(2,1)} collective-permute-done((bf16[256,768]{1,0:T(8,128)(2,1)}, bf16[256,768]{1,0:T(8,128)(2,1)}, u32[]{:S(2)}, u32[]{:S(2)}) %collective-permute-start.6) | collective-permute-done | bytes 393248 | tf_op jit(solution)/shard_map/dispatch1/ppermute | solution.py:19
  76.5 9.6 %expert.5 = (bf16[1024,3072]{1,0:T(8,128)(2,1)}, bf16[1024,3072]{1,0:T(8,128)(2,1)}, bf16[4,256,768]{2,1,0:T(8,128)(2,1)}, bf16[256,768]{1,0:T(8,128)(2,1)}) custom-call(s32[1]{0:T(128)} %bitcast.11.refs_0_, bf16[256,768]{1,0:T(8,128)(2,1)} %collective-permute-done.6.refs_1_.refs_3_, ...), custom_call_target="tpu_custom_call", output_to_operand_aliasing={{0}: (5, {}), {1}: (6, {}), {2}: (7, {})} | custom-call | flops 2000000000 | bytes 1 | tf_op jit(solution)/shard_map/expert/pallas_call | solution.py:90
  87.9 9.7 %expert.6 = (bf16[1024,3072]{1,0:T(8,128)(2,1)}, bf16[1024,3072]{1,0:T(8,128)(2,1)}, bf16[4,256,768]{2,1,0:T(8,128)(2,1)}, bf16[256,768]{1,0:T(8,128)(2,1)}) custom-call(s32[1]{0:T(128)} %bitcast.10.refs_0_, bf16[256,768]{1,0:T(8,128)(2,1)} %collective-permute-done.5.refs_1_.refs_4_, ...), custom_call_target="tpu_custom_call", output_to_operand_aliasing={{0}: (5, {}), {1}: (6, {}), {2}: (7, {})} | custom-call | flops 2000000000 | bytes 1 | tf_op jit(solution)/shard_map/expert/pallas_call | solution.py:90
  98.0 9.7 %expert.7 = (bf16[1024,3072]{1,0:T(8,128)(2,1)}, bf16[1024,3072]{1,0:T(8,128)(2,1)}, bf16[4,256,768]{2,1,0:T(8,128)(2,1)}, bf16[256,768]{1,0:T(8,128)(2,1)}) custom-call(s32[1]{0:T(128)} %bitcast.7.refs_0_, bf16[256,768]{1,0:T(8,128)(2,1)} %collective-permute-done.4.refs_1_.refs_5_, ...), custom_call_target="tpu_custom_call", output_to_operand_aliasing={{0}: (5, {}), {1}: (6, {}), {2}: (7, {})} | custom-call | flops 2000000000 | bytes 1 | tf_op jit(solution)/shard_map/expert/pallas_call | solution.py:90
  110.1 7.1 %weight_part.4.refs_6_ = bf16[1536,768]{1,0:T(8,128)(2,1)} custom-call(s32[47]{0:T(128)} %stack.119.refs_0_, bf16[1024,3072]{1,0:T(8,128)(2,1)} %get-tuple-element.109.refs_1_, bf16[4,256,768]{2,1,0:T(8,128)(2,1)} %all-to-all-done.refs_2_, bf16[256,768]{1,0:T(8,128)(2,1)} %get-tuple-element.107.refs_3_), custom_call_target="tpu_custom_call" | custom-call | flops 1 | bytes 1 | tf_op jit(solution)/shard_map/weight_part/pallas_call | solution.py:90
  117.2 6.6 %weight_part.5.refs_1_ = bf16[768,1536]{1,0:T(8,128)(2,1)} custom-call(s32[47]{0:T(128)} %stack.119.refs_0_, bf16[1024,3072]{1,0:T(8,128)(2,1)} %get-tuple-element.108.refs_1_, bf16[256,768]{1,0:T(8,128)(2,1)} %get-tuple-element.93.refs_1_.refs_2_, bf16[256,768]{1,0:T(8,128)(2,1)} %collective-permute-done.6.refs_1_.refs_3_, ...), custom_call_target="tpu_custom_call" | custom-call | flops 1 | bytes 1 | tf_op jit(solution)/shard_map/weight_part/pallas_call | solution.py:90
  124.9 7.3 %weight_part.6 = (bf16[768,768]{1,0:T(8,128)(2,1)}, bf16[768,768]{1,0:T(8,128)(2,1)}) custom-call(s32[47]{0:T(128)} %stack.119.refs_0_, bf16[1024,3072]{1,0:T(8,128)(2,1)} %get-tuple-element.109.refs_1_, bf16[4,256,768]{2,1,0:T(8,128)(2,1)} %all-to-all-done.refs_2_, bf16[1536,768]{1,0:T(8,128)(2,1)} %collective-permute-done.11.refs_3_, f32[8,128]{1,0:T(8,128)} %touch.11.refs_4_), custom_call_target="tpu_custom_call" | custom-call | flops 1 | bytes 1 | tf_op jit(solution)/shard_map/weight_part/pallas_call | solution.py:90
  132.2 7.2 %weight_part.7 = (bf16[768,768]{1,0:T(8,128)(2,1)}, bf16[768,768]{1,0:T(8,128)(2,1)}) custom-call(s32[47]{0:T(128)} %stack.119.refs_0_, bf16[1024,3072]{1,0:T(8,128)(2,1)} %get-tuple-element.108.refs_1_, bf16[256,768]{1,0:T(8,128)(2,1)} %get-tuple-element.93.refs_1_.refs_2_, bf16[256,768]{1,0:T(8,128)(2,1)} %collective-permute-done.6.refs_1_.refs_3_, ...), custom_call_target="tpu_custom_call" | custom-call | flops 1 | bytes 1 | tf_op jit(solution)/shard_map/weight_part/pallas_call | solution.py:90
  139.4 6.4 %second_back.1 = (f32[512,768]{1,0:T(8,128)}, bf16[512,768]{1,0:T(8,128)(2,1)}, f32[1,768]{1,0:T(1,128)}, bf16[512,384]{1,0:T(8,128)(2,1)}, bf16[512,384]{1,0:T(8,128)(2,1)}) custom-call(bf16[512,768]{1,0:T(8,128)(2,1)} %refs_0_.6, f32[512,768]{1,0:T(8,128)} %get-tuple-element.88.refs_1_.refs_0_, f32[768]{0:T(1024)} %refs_2_.7, s32[1,512]{1,0:T(1,128)} %bitcast.71, ...), custom_call_target="tpu_custom_call" | custom-call | flops 299999985664 | bytes 1 | tf_op jit(solution)/shard_map/second_back/pallas_call | solution.py:90
  155.0 4.5 %all-to-all-start.1 = ((bf16[4,256,768]{2,1,0:T(8,128)(2,1)}), bf16[4,256,768]{2,1,0:T(8,128)(2,1)}, u32[]{:S(2)}, u32[]{:S(2)}) async-start(bf16[4,256,768]{2,1,0:T(8,128)(2,1)} %touch.12), calls=%async_computation.1 | async-start | bytes 3145728 | tf_op jit(solution)/shard_map/all_to_all | solution.py:1028
  159.5 21.5 %attend_back.1 = (bf16[784,768]{1,0:T(8,128)(2,1)}, bf16[784,768]{1,0:T(8,128)(2,1)}, f32[512,768]{1,0:T(8,128)}, bf16[512,768]{1,0:T(8,128)(2,1)}) custom-call(s32[47]{0:T(128)} %stack.119.refs_0_, bf16[512,384]{1,0:T(8,128)(2,1)} %get-tuple-element.116.refs_1_, bf16[512,384]{1,0:T(8,128)(2,1)} %collective-permute-done.13.refs_2_, ...), custom_call_target="tpu_custom_call" | custom-call | flops 49999998976 | bytes 1 | tf_op jit(solution)/shard_map/attend_back/pallas_call | solution.py:90
  183.4 4.9 %adds.2 = (bf16[384,768]{1,0:T(8,128)(2,1)}, bf16[384,768]{1,0:T(8,128)(2,1)}, bf16[384,768]{1,0:T(8,128)(2,1)}, bf16[384,768]{1,0:T(8,128)(2,1)}) custom-call(s32[47]{0:T(128)} %stack.119.refs_0_, bf16[768,768]{1,0:T(8,128)(2,1)} %get-tuple-element.125.refs_1_, bf16[768,768]{1,0:T(8,128)(2,1)} %collective-permute-done.16.refs_2_, ...), custom_call_target="tpu_custom_call" | custom-call | flops 1 | bytes 1 | tf_op jit(solution)/shard_map/adds/pallas_call | solution.py:90
  196.8 4.3 %all-to-all-start.2 = ((bf16[8,96,768]{2,1,0:T(8,128)(2,1)}), bf16[8,96,768]{2,1,0:T(8,128)(2,1)}, u32[]{:S(2)}, u32[]{:S(2)}) async-start(bf16[8,96,768]{2,1,0:T(8,128)(2,1)} %bitcast.67), calls=%async_computation.2 | async-start | bytes 2359296 | tf_op jit(solution)/shard_map/all_to_all | solution.py:1127
  201.0 3.8 %output_rows.1.refs_5_ = bf16[512,768]{1,0:T(8,128)(2,1)} custom-call(f32[512,768]{1,0:T(8,128)} %get-tuple-element.88.refs_1_.refs_0_, s32[1,512]{1,0:T(1,128)} %bitcast.74, bf16[4,256,768]{2,1,0:T(8,128)(2,1)} %all-to-all-done.1.refs_2_, bf16[8,96,768]{2,1,0:T(8,128)(2,1)} %bitcast.68), custom_call_target="tpu_custom_call" | custom-call | flops 299999985664 | bytes 1 | tf_op jit(solution)/shard_map/output_rows/pallas_call | solution.py:90
  204.9 4.1 %collective-permute-done.20.refs_2_ = bf16[384,768]{1,0:T(8,128)(2,1)} collective-permute-done((bf16[384,768]{1,0:T(8,128)(2,1)}, bf16[384,768]{1,0:T(8,128)(2,1)}, u32[]{:S(2)}, u32[]{:S(2)}) %collective-permute-start.20) | collective-permute-done | bytes 589856 | tf_op jit(solution)/shard_map/outer-1/ppermute | solution.py:19
  212.7 3.8 %adds.3 = (bf16[384,768]{1,0:T(8,128)(2,1)}, bf16[384,768]{1,0:T(8,128)(2,1)}, bf16[384,768]{1,0:T(8,128)(2,1)}, bf16[384,768]{1,0:T(8,128)(2,1)}) custom-call(s32[47]{0:T(128)} %stack.119.refs_0_, bf16[384,768]{1,0:T(8,128)(2,1)} %get-tuple-element.128.refs_2_.refs_1_, bf16[384,768]{1,0:T(8,128)(2,1)} %collective-permute-done.20.refs_2_, ...), custom_call_target="tpu_custom_call" | custom-call | flops 1 | bytes 1 | tf_op jit(solution)/shard_map/adds/pallas_call | solution.py:90
  220.5 9.5 %all-to-all-done.2.refs_0_ = bf16[8,96,768]{2,1,0:T(8,128)(2,1)} async-done(((bf16[8,96,768]{2,1,0:T(8,128)(2,1)}), bf16[8,96,768]{2,1,0:T(8,128)(2,1)}, u32[]{:S(2)}, u32[]{:S(2)}) %all-to-all-start.2) | async-done | bytes 1179680 | tf_op jit(solution)/shard_map/all_to_all | solution.py:1127
  232.5 4.5 %all-to-all-start.3 = ((bf16[8,112,768]{2,1,0:T(8,128)(2,1)}), bf16[8,112,768]{2,1,0:T(8,128)(2,1)}, u32[]{:S(2)}, u32[]{:S(2)}) async-start(bf16[8,112,768]{2,1,0:T(8,128)(2,1)} %total.1.refs_5_.refs_1_.refs_7_), calls=%async_computation.3 | async-start | bytes 2752512 | tf_op jit(solution)/shard_map/all_to_all | solution.py:1142
  237.1 4.5 %first_back.1.refs_2_ = f32[512,768]{1,0:T(8,128)} custom-call(bf16[512,768]{1,0:T(8,128)(2,1)} %refs_0_.7, f32[768]{0:T(1024)} %refs_1_.3, f32[512,768]{1,0:T(8,128)} %get-tuple-element.130.refs_2_, f32[512,768]{1,0:T(8,128)} %get-tuple-element.131.refs_3_, bf16[512,768]{1,0:T(8,128)(2,1)} %collective-permute-done.19.refs_4_, ...), custom_call_target="tpu_custom_call" | custom-call | flops 1 | bytes 1 | tf_op jit(solution)/shard_map/first_back/pallas_call | solution.py:90
  242.3 9.4 %collective-permute-done.28.refs_0_ = bf16[384,768]{1,0:T(8,128)(2,1)} collective-permute-done((bf16[384,768]{1,0:T(8,128)(2,1)}, bf16[384,768]{1,0:T(8,128)(2,1)}, u32[]{:S(2)}, u32[]{:S(2)}) %collective-permute-start.28) | collective-permute-done | bytes 589856 | tf_op jit(solution)/shard_map/piece/ppermute | solution.py:19
  254.9 6.4 %assemble.3.refs_8_.refs_1_.refs_5_ = f32[3072,768]{1,0:T(8,128)} custom-call(s32[47]{0:T(128)} %stack.119.refs_0_, bf16[384,768]{1,0:T(8,128)(2,1)} %get-tuple-element.136.refs_3_.refs_1_, bf16[384,768]{1,0:T(8,128)(2,1)} %get-tuple-element.138.refs_2_, bf16[384,768]{1,0:T(8,128)(2,1)} %get-tuple-element.139.refs_3_, ...), custom_call_target="tpu_custom_call" | custom-call | flops 1 | bytes 1 | tf_op jit(solution)/shard_map/assemble/pallas_call | solution.py:90
  261.2 6.4 %assemble.4.refs_2_.refs_6_ = f32[768,3072]{1,0:T(8,128)} custom-call(s32[47]{0:T(128)} %stack.119.refs_0_, bf16[384,768]{1,0:T(8,128)(2,1)} %get-tuple-element.137.refs_4_.refs_1_, bf16[384,768]{1,0:T(8,128)(2,1)} %get-tuple-element.141.refs_2_, bf16[384,768]{1,0:T(8,128)(2,1)} %get-tuple-element.142.refs_3_, ...), custom_call_target="tpu_custom_call" | custom-call | flops 1 | bytes 1 | tf_op jit(solution)/shard_map/assemble/pallas_call | solution.py:90
  267.6 7.5 %collective-permute-done.24.refs_0_ = bf16[384,768]{1,0:T(8,128)(2,1)} collective-permute-done((bf16[384,768]{1,0:T(8,128)(2,1)}, bf16[384,768]{1,0:T(8,128)(2,1)}, u32[]{:S(2)}, u32[]{:S(2)}) %collective-permute-start.24) | collective-permute-done | bytes 589856 | tf_op jit(solution)/shard_map/piece/ppermute | solution.py:19
  278.7 4.9 %weight_outputs.1 = (f32[3,768,384]{2,1,0:T(8,128)}, f32[384,768]{1,0:T(8,128)}, f32[768]{0:T(1024)}, f32[768]{0:T(1024)}) custom-call(s32[1]{0:T(128)} %bitcast.13.refs_0_, bf16[8,112,768]{2,1,0:T(8,128)(2,1)} %touch.21.refs_1_, bf16[8,112,768]{2,1,0:T(8,128)(2,1)} %collective-permute-done.34.refs_2_), custom_call_target="tpu_custom_call" | custom-call | flops 1 | bytes 1 | tf_op jit(solution)/shard_map/weight_outputs/pallas_call | solution.py:90
  283.6 5.3 %assemble.5 = (f32[3072,768]{1,0:T(8,128)}, f32[768,3072]{1,0:T(8,128)}) custom-call(s32[47]{0:T(128)} %stack.119.refs_0_, bf16[384,768]{1,0:T(8,128)(2,1)} %touch.19.refs_1_, bf16[384,768]{1,0:T(8,128)(2,1)} %collective-permute-done.35.refs_2_, bf16[384,768]{1,0:T(8,128)(2,1)} %touch.20.refs_2_.refs_3_, ...), custom_call_target="tpu_custom_call", output_to_operand_aliasing={{0}: (5, {}), {1}: (6, {})} | custom-call | flops 1 | bytes 1 | tf_op jit(solution)/shard_map/assemble/pallas_call | solution.py:90
  (104 shorter events, 66.9 us)
Async XLA Ops:
  0.6 14.1 %collective-permute-start.1 = (s32[512]{0:T(512)}, s32[512]{0:T(512)}, u32[]{:S(2)}, u32[]{:S(2)}) collective-permute-start(s32[512]{0:T(512)} %param.14), channel_id=1, source_target_pairs={{0,1},{1,0},{2,3},{3,2},{4,5},{5,4},{6,7},{7,6},{8,9},{9,8},{10,11... | collective-permute-start | bytes 6152 | tf_op jit(solution)/shard_map/positions/ppermute | solution.py:19
  3.7 21.7 %collective-permute-start = (bf16[512,768]{1,0:T(8,128)(2,1)}, bf16[512,768]{1,0:T(8,128)(2,1)}, u32[]{:S(2)}, u32[]{:S(2)}) collective-permute-start(bf16[512,768]{1,0:T(8,128)(2,1)} %refs_0_.7), channel_id=1, source_target_pairs={{0,1},{1,0},{2,3},{3,2},{4,5},{5,4},{6,7},{7,6},{8,9},{9,8},{10,11... | collective-permute-start | bytes 2359304 | tf_op jit(solution)/shard_map/rows/ppermute | solution.py:19
  18.3 20.0 %collective-permute-start.2 = (bf16[384,768]{1,0:T(8,128)(2,1)}, bf16[384,768]{1,0:T(8,128)(2,1)}, u32[]{:S(2)}, u32[]{:S(2)}) collective-permute-start(bf16[384,768]{1,0:T(8,128)(2,1)} %get-tuple-element.85), channel_id=1, source_target_pairs={{0,1},{1,0},{2,3},{3,2},{4,5},{5,4},{6,7},{7,6},{8,9},{9,8},{10,11... | collective-permute-start | bytes 1769480 | tf_op jit(solution)/shard_map/output_weight/ppermute | solution.py:19
  20.2 56.3 %all-to-all-start = ((bf16[4,256,768]{2,1,0:T(8,128)(2,1)}), bf16[4,256,768]{2,1,0:T(8,128)(2,1)}, u32[]{:S(2)}, u32[]{:S(2)}) async-start(bf16[4,256,768]{2,1,0:T(8,128)(2,1)} %get-tuple-element.90.refs_2_), calls=%async_computation | async-start | bytes 3145728 | tf_op jit(solution)/shard_map/all_to_all | solution.py:1028
  38.3 10.1 %collective-permute-start.3 = (bf16[512,384]{1,0:T(8,128)(2,1)}, bf16[512,384]{1,0:T(8,128)(2,1)}, u32[]{:S(2)}, u32[]{:S(2)}) collective-permute-start(bf16[512,384]{1,0:T(8,128)(2,1)} %get-tuple-element.87.refs_9_), channel_id=1, source_target_pairs={{0,1},{1,0},{2,3},{3,2},{4,5},{5,4},{6,7},{7,6},{8,9},{9,8},{10,11... | collective-permute-start | bytes 1179656 | tf_op jit(solution)/shard_map/context/ppermute | solution.py:19
  53.6 22.9 %collective-permute-start.6 = (bf16[256,768]{1,0:T(8,128)(2,1)}, bf16[256,768]{1,0:T(8,128)(2,1)}, u32[]{:S(2)}, u32[]{:S(2)}) collective-permute-start(bf16[256,768]{1,0:T(8,128)(2,1)} %get-tuple-element.92), channel_id=1, source_target_pairs={{0,2},{2,0},{4,6},{6,4},{1,3},{3,1},{5,7},{7,5},{8,10},{10,8},{12,... | collective-permute-start | bytes 1179656 | tf_op jit(solution)/shard_map/dispatch1/ppermute | solution.py:19
  55.4 32.6 %collective-permute-start.5 = (bf16[256,768]{1,0:T(8,128)(2,1)}, bf16[256,768]{1,0:T(8,128)(2,1)}, u32[]{:S(2)}, u32[]{:S(2)}) collective-permute-start(bf16[256,768]{1,0:T(8,128)(2,1)} %get-tuple-element.91), channel_id=1, source_target_pairs={{0,4},{2,6},{4,0},{6,2},{1,5},{3,7},{5,1},{7,3},{8,12},{10,14},{12... | collective-permute-start | bytes 1179656 | tf_op jit(solution)/shard_map/dispatch2/ppermute | solution.py:19
  58.5 39.6 %collective-permute-start.4 = (bf16[256,768]{1,0:T(8,128)(2,1)}, bf16[256,768]{1,0:T(8,128)(2,1)}, u32[]{:S(2)}, u32[]{:S(2)}) collective-permute-start(bf16[256,768]{1,0:T(8,128)(2,1)} %get-tuple-element.89), channel_id=1, source_target_pairs={{0,6},{2,4},{4,2},{6,0},{1,7},{3,5},{5,3},{7,1},{8,14},{10,12},{12... | collective-permute-start | bytes 1179656 | tf_op jit(solution)/shard_map/dispatch3/ppermute | solution.py:19
  86.1 53.3 %collective-permute-start.7 = (bf16[256,768]{1,0:T(8,128)(2,1)}, bf16[256,768]{1,0:T(8,128)(2,1)}, u32[]{:S(2)}, u32[]{:S(2)}) collective-permute-start(bf16[256,768]{1,0:T(8,128)(2,1)} %get-tuple-element.105), channel_id=1, source_target_pairs={{0,2},{2,0},{4,6},{6,4},{1,3},{3,1},{5,7},{7,5},{8,10},{10,8},{12,... | collective-permute-start | bytes 1179656 | tf_op jit(solution)/shard_map/return1/ppermute | solution.py:19
  97.6 41.8 %collective-permute-start.8 = (bf16[256,768]{1,0:T(8,128)(2,1)}, bf16[256,768]{1,0:T(8,128)(2,1)}, u32[]{:S(2)}, u32[]{:S(2)}) collective-permute-start(bf16[256,768]{1,0:T(8,128)(2,1)} %get-tuple-element.106), channel_id=1, source_target_pairs={{0,4},{2,6},{4,0},{6,2},{1,5},{3,7},{5,1},{7,3},{8,12},{10,14},{12... | collective-permute-start | bytes 1179656 | tf_op jit(solution)/shard_map/return2/ppermute | solution.py:19
  107.8 31.7 %collective-permute-start.9 = (bf16[256,768]{1,0:T(8,128)(2,1)}, bf16[256,768]{1,0:T(8,128)(2,1)}, u32[]{:S(2)}, u32[]{:S(2)}) collective-permute-start(bf16[256,768]{1,0:T(8,128)(2,1)} %get-tuple-element.107.refs_3_), channel_id=1, source_target_pairs={{0,6},{2,4},{4,2},{6,0},{1,7},{3,5},{5,3},{7,1},{8,14},{10,12},{12... | collective-permute-start | bytes 1179656 | tf_op jit(solution)/shard_map/return3/ppermute | solution.py:19
  145.8 13.7 %collective-permute-start.13 = (bf16[512,384]{1,0:T(8,128)(2,1)}, bf16[512,384]{1,0:T(8,128)(2,1)}, u32[]{:S(2)}, u32[]{:S(2)}) collective-permute-start(bf16[512,384]{1,0:T(8,128)(2,1)} %get-tuple-element.113.refs_4_), channel_id=1, source_target_pairs={{0,1},{1,0},{2,3},{3,2},{4,5},{5,4},{6,7},{7,6},{8,9},{9,8},{10,11... | collective-permute-start | bytes 1179656 | tf_op jit(solution)/shard_map/context_grad/ppermute | solution.py:19
  149.5 31.6 %collective-permute-start.16 = (bf16[768,768]{1,0:T(8,128)(2,1)}, bf16[768,768]{1,0:T(8,128)(2,1)}, u32[]{:S(2)}, u32[]{:S(2)}) collective-permute-start(bf16[768,768]{1,0:T(8,128)(2,1)} %get-tuple-element.110.refs_7_), channel_id=1, source_target_pairs={{0,16},{16,0},{1,17},{17,1},{2,18},{18,2},{3,19},{19,3},{4,20},{20... | collective-permute-start | bytes 3538952 | tf_op jit(solution)/shard_map/outer0/ppermute | solution.py:19
  151.1 32.3 %collective-permute-start.17 = (bf16[768,768]{1,0:T(8,128)(2,1)}, bf16[768,768]{1,0:T(8,128)(2,1)}, u32[]{:S(2)}, u32[]{:S(2)}) collective-permute-start(bf16[768,768]{1,0:T(8,128)(2,1)} %get-tuple-element.111.refs_10_.refs_16_), channel_id=1, source_target_pairs={{0,1},{1,0},{2,3},{3,2},{4,5},{5,4},{6,7},{7,6},{8,9},{9,8},{10,11... | collective-permute-start | bytes 3538952 | tf_op jit(solution)/shard_map/inner0/ppermute | solution.py:19
  154.3 34.4 %collective-permute-start.15 = (bf16[192,768]{1,0:T(8,128)(2,1)}, bf16[192,768]{1,0:T(8,128)(2,1)}, u32[]{:S(2)}, u32[]{:S(2)}) collective-permute-start(bf16[192,768]{1,0:T(8,128)(2,1)} %add.229.refs_1_), channel_id=1, source_target_pairs={{0,1},{1,0},{2,3},{3,2},{4,5},{5,4},{6,7},{7,6},{8,9},{9,8},{10,11... | collective-permute-start | bytes 884744 | tf_op jit(solution)/shard_map/output_grad/ppermute | solution.py:19
  155.0 41.8 %all-to-all-start.1 = ((bf16[4,256,768]{2,1,0:T(8,128)(2,1)}), bf16[4,256,768]{2,1,0:T(8,128)(2,1)}, u32[]{:S(2)}, u32[]{:S(2)}) async-start(bf16[4,256,768]{2,1,0:T(8,128)(2,1)} %touch.12), calls=%async_computation.1 | async-start | bytes 3145728 | tf_op jit(solution)/shard_map/all_to_all | solution.py:1028
  192.4 16.6 %collective-permute-start.20 = (bf16[384,768]{1,0:T(8,128)(2,1)}, bf16[384,768]{1,0:T(8,128)(2,1)}, u32[]{:S(2)}, u32[]{:S(2)}) collective-permute-start(bf16[384,768]{1,0:T(8,128)(2,1)} %get-tuple-element.127.refs_1_), channel_id=1, source_target_pairs={{0,1},{1,0},{2,3},{3,2},{4,5},{5,4},{6,7},{7,6},{8,9},{9,8},{10,11... | collective-permute-start | bytes 1769480 | tf_op jit(solution)/shard_map/outer-1/ppermute | solution.py:19
  193.8 18.9 %collective-permute-start.21 = (bf16[384,768]{1,0:T(8,128)(2,1)}, bf16[384,768]{1,0:T(8,128)(2,1)}, u32[]{:S(2)}, u32[]{:S(2)}) collective-permute-start(bf16[384,768]{1,0:T(8,128)(2,1)} %get-tuple-element.135), channel_id=1, source_target_pairs={{0,16},{16,0},{1,17},{17,1},{2,18},{18,2},{3,19},{19,3},{4,20},{20... | collective-permute-start | bytes 1769480 | tf_op jit(solution)/shard_map/inner-1/ppermute | solution.py:19
  196.2 40.8 %collective-permute-start.19 = (bf16[512,768]{1,0:T(8,128)(2,1)}, bf16[512,768]{1,0:T(8,128)(2,1)}, u32[]{:S(2)}, u32[]{:S(2)}) collective-permute-start(bf16[512,768]{1,0:T(8,128)(2,1)} %touch.14), channel_id=1, source_target_pairs={{0,1},{1,0},{2,3},{3,2},{4,5},{5,4},{6,7},{7,6},{8,9},{9,8},{10,11... | collective-permute-start | bytes 2359304 | tf_op jit(solution)/shard_map/theirs/ppermute | solution.py:19
  196.8 33.2 %all-to-all-start.2 = ((bf16[8,96,768]{2,1,0:T(8,128)(2,1)}), bf16[8,96,768]{2,1,0:T(8,128)(2,1)}, u32[]{:S(2)}, u32[]{:S(2)}) async-start(bf16[8,96,768]{2,1,0:T(8,128)(2,1)} %bitcast.67), calls=%async_computation.2 | async-start | bytes 2359296 | tf_op jit(solution)/shard_map/all_to_all | solution.py:1127
  216.4 25.2 %collective-permute-start.22 = (bf16[384,768]{1,0:T(8,128)(2,1)}, bf16[384,768]{1,0:T(8,128)(2,1)}, u32[]{:S(2)}, u32[]{:S(2)}) collective-permute-start(bf16[384,768]{1,0:T(8,128)(2,1)} %get-tuple-element.136.refs_3_.refs_1_), channel_id=1, source_target_pairs={{0,1},{1,0},{2,3},{3,2},{4,5},{5,4},{6,7},{7,6},{8,9},{9,8},{10,11... | collective-permute-start | bytes 1769480 | tf_op jit(solution)/shard_map/piece/ppermute | solution.py:19
  217.1 24.5 %collective-permute-start.23 = (bf16[384,768]{1,0:T(8,128)(2,1)}, bf16[384,768]{1,0:T(8,128)(2,1)}, u32[]{:S(2)}, u32[]{:S(2)}) collective-permute-start(bf16[384,768]{1,0:T(8,128)(2,1)} %get-tuple-element.136.refs_3_.refs_1_), channel_id=1, source_target_pairs={{0,16},{16,0},{1,17},{17,1},{2,18},{18,2},{3,19},{19,3},{4,20},{20... | collective-permute-start | bytes 1769480 | tf_op jit(solution)/shard_map/piece/ppermute | solution.py:19
  218.5 33.3 %collective-permute-start.28 = (bf16[384,768]{1,0:T(8,128)(2,1)}, bf16[384,768]{1,0:T(8,128)(2,1)}, u32[]{:S(2)}, u32[]{:S(2)}) collective-permute-start(bf16[384,768]{1,0:T(8,128)(2,1)} %get-tuple-element.137.refs_4_.refs_1_), channel_id=1, source_target_pairs={{0,16},{16,0},{1,17},{17,1},{2,18},{18,2},{3,19},{19,3},{4,20},{20... | collective-permute-start | bytes 1769480 | tf_op jit(solution)/shard_map/piece/ppermute | solution.py:19
  219.1 32.6 %collective-permute-start.29 = (bf16[384,768]{1,0:T(8,128)(2,1)}, bf16[384,768]{1,0:T(8,128)(2,1)}, u32[]{:S(2)}, u32[]{:S(2)}) collective-permute-start(bf16[384,768]{1,0:T(8,128)(2,1)} %get-tuple-element.137.refs_4_.refs_1_), channel_id=1, source_target_pairs={{0,1},{1,0},{2,3},{3,2},{4,5},{5,4},{6,7},{7,6},{8,9},{9,8},{10,11... | collective-permute-start | bytes 1769480 | tf_op jit(solution)/shard_map/piece/ppermute | solution.py:19
  232.5 42.6 %all-to-all-start.3 = ((bf16[8,112,768]{2,1,0:T(8,128)(2,1)}), bf16[8,112,768]{2,1,0:T(8,128)(2,1)}, u32[]{:S(2)}, u32[]{:S(2)}) async-start(bf16[8,112,768]{2,1,0:T(8,128)(2,1)} %total.1.refs_5_.refs_1_.refs_7_), calls=%async_computation.3 | async-start | bytes 2752512 | tf_op jit(solution)/shard_map/all_to_all | solution.py:1142
  237.0 15.2 %collective-permute-start.25 = (bf16[384,768]{1,0:T(8,128)(2,1)}, bf16[384,768]{1,0:T(8,128)(2,1)}, u32[]{:S(2)}, u32[]{:S(2)}) collective-permute-start(bf16[384,768]{1,0:T(8,128)(2,1)} %touch.16), channel_id=1, source_target_pairs={{0,8},{8,0},{1,9},{9,1},{2,10},{10,2},{3,11},{11,3},{4,12},{12,4},... | collective-permute-start | bytes 1769480 | tf_op jit(solution)/shard_map/piece_core/ppermute | solution.py:19
  241.6 10.7 %collective-permute-start.26 = (bf16[384,768]{1,0:T(8,128)(2,1)}, bf16[384,768]{1,0:T(8,128)(2,1)}, u32[]{:S(2)}, u32[]{:S(2)}) collective-permute-start(bf16[384,768]{1,0:T(8,128)(2,1)} %get-tuple-element.138.refs_2_), channel_id=1, source_target_pairs={{0,8},{8,0},{1,9},{9,1},{2,10},{10,2},{3,11},{11,3},{4,12},{12,4},... | collective-permute-start | bytes 1769480 | tf_op jit(solution)/shard_map/piece_core/ppermute | solution.py:19
  242.2 11.5 %collective-permute-start.27 = (bf16[384,768]{1,0:T(8,128)(2,1)}, bf16[384,768]{1,0:T(8,128)(2,1)}, u32[]{:S(2)}, u32[]{:S(2)}) collective-permute-start(bf16[384,768]{1,0:T(8,128)(2,1)} %get-tuple-element.139.refs_3_), channel_id=1, source_target_pairs={{0,8},{8,0},{1,9},{9,1},{2,10},{10,2},{3,11},{11,3},{4,12},{12,4},... | collective-permute-start | bytes 1769480 | tf_op jit(solution)/shard_map/piece_core/ppermute | solution.py:19
  251.7 9.5 %collective-permute-start.30 = (bf16[384,768]{1,0:T(8,128)(2,1)}, bf16[384,768]{1,0:T(8,128)(2,1)}, u32[]{:S(2)}, u32[]{:S(2)}) collective-permute-start(bf16[384,768]{1,0:T(8,128)(2,1)} %touch.18), channel_id=1, source_target_pairs={{0,8},{8,0},{1,9},{9,1},{2,10},{10,2},{3,11},{11,3},{4,12},{12,4},... | collective-permute-start | bytes 1769480 | tf_op jit(solution)/shard_map/piece_core/ppermute | solution.py:19
  251.7 9.5 %collective-permute-start.31 = (bf16[384,768]{1,0:T(8,128)(2,1)}, bf16[384,768]{1,0:T(8,128)(2,1)}, u32[]{:S(2)}, u32[]{:S(2)}) collective-permute-start(bf16[384,768]{1,0:T(8,128)(2,1)} %get-tuple-element.141.refs_2_), channel_id=1, source_target_pairs={{0,8},{8,0},{1,9},{9,1},{2,10},{10,2},{3,11},{11,3},{4,12},{12,4},... | collective-permute-start | bytes 1769480 | tf_op jit(solution)/shard_map/piece_core/ppermute | solution.py:19
  252.3 22.8 %collective-permute-start.24 = (bf16[384,768]{1,0:T(8,128)(2,1)}, bf16[384,768]{1,0:T(8,128)(2,1)}, u32[]{:S(2)}, u32[]{:S(2)}) collective-permute-start(bf16[384,768]{1,0:T(8,128)(2,1)} %get-tuple-element.138.refs_2_), channel_id=1, source_target_pairs={{0,16},{16,0},{1,17},{17,1},{2,18},{18,2},{3,19},{19,3},{4,20},{20... | collective-permute-start | bytes 1769480 | tf_op jit(solution)/shard_map/piece/ppermute | solution.py:19
  253.7 21.4 %collective-permute-start.33 = (bf16[384,768]{1,0:T(8,128)(2,1)}, bf16[384,768]{1,0:T(8,128)(2,1)}, u32[]{:S(2)}, u32[]{:S(2)}) collective-permute-start(bf16[384,768]{1,0:T(8,128)(2,1)} %get-tuple-element.141.refs_2_), channel_id=1, source_target_pairs={{0,1},{1,0},{2,3},{3,2},{4,5},{5,4},{6,7},{7,6},{8,9},{9,8},{10,11... | collective-permute-start | bytes 1769480 | tf_op jit(solution)/shard_map/piece/ppermute | solution.py:19
  (10 other events, 67.4 us)

commit v6 on v5

--- a/solution.py
+++ b/solution.py
@@ -1115,17 +1115,17 @@
         second_gain_part, own_output, lines, after=[inner_parts[0]],
     )
     at = 3 * local_cols // 2
-    for i in range(len(turns) - 1):
-        outer_parts, inner_parts = adds(
-            info, adds_at[i], pairs_of(outer_parts, inner_parts, i), 2, after=[kept]
-        )
-    more = touch([got_output], outer_parts, flops=BACK_FLOPS)
+    more = touch([got_output], [kept], flops=BACK_FLOPS)
     got = swap(sent, "core", 1, "weight")
     summed, tail = gather_sum(kept, got, more[0], end, after=more)
     crowd = ("x", "expert")
     summed = summed.reshape(-1, end // lax.axis_size(crowd), model_width)
     arrived = lax.all_to_all(summed, crowd, split_axis=0, concat_axis=0, tiled=True)
-    block_output = output_rows(hidden, absolute[None, :], combined, after=[summed])
+    for i in range(len(turns) - 1):
+        outer_parts, inner_parts = adds(
+            info, adds_at[i], pairs_of(outer_parts, inner_parts, i), 2, after=[summed]
+        )
+    block_output = output_rows(hidden, absolute[None, :], combined, after=outer_parts)
     got_tail = swap(tail, "head", 1, "gains")
     theirs = swap(touch([theirs], [got_tail])[0], "head", 1, "theirs")
     (outer_own, outer_copy), (inner_own, inner_copy) = adds(

time: 294 us -> 298 us (1.014)
    ppermute x37, waiting for transfers between devices: 44.3 us -> 48.8 us  [swap(): return lax.ppermute(values, axis, [(i, i ^ bit) for i in range(size)])]
  transfers between devices with their start and end apart: 41 -> 41, of which waited for: 12 -> 10; matrix products, arithmetic and copies ran while one was open for 3% -> 3% of each run, Pallas kernels for 58% -> 57%
where the time goes in v6:
time: 298 us; the launch traced here: 293 us
  Pallas kernels  178 us (60%)
  waiting for transfers between devices  56.1 us (19%)
  starting transfers between devices  49.7 us (17%)
  local copies, waits for them, and re-layouts  4.98 us (2%)
    pallas_call x39, Pallas kernels, call(): pl.pallas_call(body, input_output_aliases={first + i: i for i in range(le...  178 us
    ppermute x37, waiting for transfers between devices, swap(): return lax.ppermute(values, axis, [(i, i ^ bit) for i in range(size)])  48.8 us
    ppermute x37, starting transfers between devices, swap(): return lax.ppermute(values, axis, [(i, i ^ bit) for i in range(size)])  31.3 us
    all_to_all x2, starting transfers between devices, exchange_all(): lax.all_to_all(blocks, 'expert', split_axis=0, concat_axis=0, tiled=True)  9.6 us
    all_to_all x1, waiting for transfers between devices, on_device(): lax.all_to_all(summed, crowd, split_axis=0, concat_axis=0, tiled=True)  7.28 us
  transfers between devices with their start and end apart: 41, of which 10 were waited for; matrix products, arithmetic and copies ran while one was open for 3% of the time, Pallas kernels for 57%

profile of v6, /device:TPU:0, one launch (start us, length us, event | category | flops | bytes accessed | tf_op | source)
XLA Modules:
  0.0 293.1 jit_solution(3188281522849094026)
XLA Ops:
  10.2 4.5 %project.2 = (bf16[2,512,768]{2,1,0:T(8,128)(2,1)}, bf16[3,2,512,384]{3,2,1,0:T(8,128)(2,1)}) custom-call(s32[1]{0:T(128)} %bitcast.refs_0_, bf16[512,768]{1,0:T(8,128)(2,1)} %refs_0_.7, f32[768]{0:T(1024)} %refs_1_.3, bf16[3,768,384]{2,1,0:T(8,128)(2,1)} %refs_12_.1), custom_call_target="tpu_custom_call" | custom-call | flops 1 | bytes 1 | tf_op jit(solution)/shard_map/project/pallas_call | solution.py:90
  20.2 5.1 %all-to-all-start = ((bf16[4,256,768]{2,1,0:T(8,128)(2,1)}), bf16[4,256,768]{2,1,0:T(8,128)(2,1)}, u32[]{:S(2)}, u32[]{:S(2)}) async-start(bf16[4,256,768]{2,1,0:T(8,128)(2,1)} %get-tuple-element.90.refs_2_), calls=%async_computation | async-start | bytes 3145728 | tf_op jit(solution)/shard_map/all_to_all | solution.py:1028
  25.3 4.5 %project.3 = (bf16[2,512,768]{2,1,0:T(8,128)(2,1)}, bf16[3,2,512,384]{3,2,1,0:T(8,128)(2,1)}) custom-call(s32[1]{0:T(128)S(6)} %sub.107.refs_0_, bf16[512,768]{1,0:T(8,128)(2,1)} %collective-permute-done.refs_1_, f32[768]{0:T(1024)} %refs_1_.3, bf16[3,768,384]{2,1,0:T(8,128)(2,1)} %refs_12_.1, ...), custom_call_target="tpu_custom_call", output_to_operand_aliasing={{0}: (4, {}), {1}: (5, {})} | custom-call | flops 1 | bytes 1 | tf_op jit(solution)/shard_map/project/pallas_call | solution.py:90
  29.8 8.5 %attend.2 = (bf16[2,6,512,512]{3,2,1,0:T(8,128)(2,1)}, bf16[2,6,512,512]{3,2,1,0:T(8,128)(2,1)}, f32[2,512,384]{2,1,0:T(8,128)}, bf16[512,384]{1,0:T(8,128)(2,1)}) custom-call(s32[1]{0:T(128)S(6)} %sub.107.refs_0_, bf16[3,2,512,384]{3,2,1,0:T(8,128)(2,1)} %get-tuple-element.81.refs_1_.refs_2_.refs_3_.refs_4_.refs_5_, ...), custom_call_target="tpu_custom_call" | custom-call | flops 1 | bytes 1 | tf_op jit(solution)/shard_map/attend/pallas_call | solution.py:90
  38.3 6.8 %attend.3 = (bf16[2,6,512,512]{3,2,1,0:T(8,128)(2,1)}, bf16[2,6,512,512]{3,2,1,0:T(8,128)(2,1)}, f32[2,512,384]{2,1,0:T(8,128)}, bf16[512,384]{1,0:T(8,128)(2,1)}) custom-call(s32[1]{0:T(128)} %bitcast.refs_0_, ...), custom_call_target="tpu_custom_call", output_to_operand_aliasing={{0}: (7, {}), {1}: (8, {}), {2}: (9, {})} | custom-call | flops 20000000000 | bytes 1 | tf_op jit(solution)/shard_map/attend/pallas_call | solution.py:90
  48.4 5.2 %hidden_rows.1 = (f32[512,768]{1,0:T(8,128)}, bf16[256,768]{1,0:T(8,128)(2,1)}, bf16[256,768]{1,0:T(8,128)(2,1)}, bf16[256,768]{1,0:T(8,128)(2,1)}, bf16[256,768]{1,0:T(8,128)(2,1)}) custom-call(bf16[512,768]{1,0:T(8,128)(2,1)} %refs_0_.7, bf16[512,384]{1,0:T(8,128)(2,1)} %get-tuple-element.86.refs_1_.refs_8_, ...), custom_call_target="tpu_custom_call" | custom-call | flops 1 | bytes 1 | tf_op jit(solution)/shard_map/hidden_rows/pallas_call | solution.py:90
  58.7 9.9 %expert.4 = (bf16[1024,3072]{1,0:T(8,128)(2,1)}, bf16[1024,3072]{1,0:T(8,128)(2,1)}, bf16[4,256,768]{2,1,0:T(8,128)(2,1)}, bf16[256,768]{1,0:T(8,128)(2,1)}) custom-call(s32[1]{0:T(128)} %bitcast.12.refs_0_, bf16[256,768]{1,0:T(8,128)(2,1)} %get-tuple-element.93.refs_1_.refs_2_, bf16[4,256,768]{2,1,0:T(8,128)(2,1)} %get-tuple-element.90.refs_2_, ...), custom_call_target="tpu_custom_call" | custom-call | flops 2000000000 | bytes 1 | tf_op jit(solution)/shard_map/expert/pallas_call | solution.py:90
  68.6 7.9 %collective-permute-done.6.refs_1_.refs_3_ = bf16[256,768]{1,0:T(8,128)(2,1)} collective-permute-done((bf16[256,768]{1,0:T(8,128)(2,1)}, bf16[256,768]{1,0:T(8,128)(2,1)}, u32[]{:S(2)}, u32[]{:S(2)}) %collective-permute-start.6) | collective-permute-done | bytes 393248 | tf_op jit(solution)/shard_map/dispatch1/ppermute | solution.py:19
  76.5 9.6 %expert.5 = (bf16[1024,3072]{1,0:T(8,128)(2,1)}, bf16[1024,3072]{1,0:T(8,128)(2,1)}, bf16[4,256,768]{2,1,0:T(8,128)(2,1)}, bf16[256,768]{1,0:T(8,128)(2,1)}) custom-call(s32[1]{0:T(128)} %bitcast.11.refs_0_, bf16[256,768]{1,0:T(8,128)(2,1)} %collective-permute-done.6.refs_1_.refs_3_, ...), custom_call_target="tpu_custom_call", output_to_operand_aliasing={{0}: (5, {}), {1}: (6, {}), {2}: (7, {})} | custom-call | flops 2000000000 | bytes 1 | tf_op jit(solution)/shard_map/expert/pallas_call | solution.py:90
  87.9 9.7 %expert.6 = (bf16[1024,3072]{1,0:T(8,128)(2,1)}, bf16[1024,3072]{1,0:T(8,128)(2,1)}, bf16[4,256,768]{2,1,0:T(8,128)(2,1)}, bf16[256,768]{1,0:T(8,128)(2,1)}) custom-call(s32[1]{0:T(128)} %bitcast.10.refs_0_, bf16[256,768]{1,0:T(8,128)(2,1)} %collective-permute-done.5.refs_1_.refs_4_, ...), custom_call_target="tpu_custom_call", output_to_operand_aliasing={{0}: (5, {}), {1}: (6, {}), {2}: (7, {})} | custom-call | flops 2000000000 | bytes 1 | tf_op jit(solution)/shard_map/expert/pallas_call | solution.py:90
  98.0 9.7 %expert.7 = (bf16[1024,3072]{1,0:T(8,128)(2,1)}, bf16[1024,3072]{1,0:T(8,128)(2,1)}, bf16[4,256,768]{2,1,0:T(8,128)(2,1)}, bf16[256,768]{1,0:T(8,128)(2,1)}) custom-call(s32[1]{0:T(128)} %bitcast.7.refs_0_, bf16[256,768]{1,0:T(8,128)(2,1)} %collective-permute-done.4.refs_1_.refs_5_, ...), custom_call_target="tpu_custom_call", output_to_operand_aliasing={{0}: (5, {}), {1}: (6, {}), {2}: (7, {})} | custom-call | flops 2000000000 | bytes 1 | tf_op jit(solution)/shard_map/expert/pallas_call | solution.py:90
  110.1 7.1 %weight_part.4.refs_6_ = bf16[1536,768]{1,0:T(8,128)(2,1)} custom-call(s32[47]{0:T(128)} %stack.119.refs_0_, bf16[1024,3072]{1,0:T(8,128)(2,1)} %get-tuple-element.109.refs_1_, bf16[4,256,768]{2,1,0:T(8,128)(2,1)} %all-to-all-done.refs_2_, bf16[256,768]{1,0:T(8,128)(2,1)} %get-tuple-element.107.refs_3_), custom_call_target="tpu_custom_call" | custom-call | flops 1 | bytes 1 | tf_op jit(solution)/shard_map/weight_part/pallas_call | solution.py:90
  117.2 6.6 %weight_part.5.refs_1_ = bf16[768,1536]{1,0:T(8,128)(2,1)} custom-call(s32[47]{0:T(128)} %stack.119.refs_0_, bf16[1024,3072]{1,0:T(8,128)(2,1)} %get-tuple-element.108.refs_1_, bf16[256,768]{1,0:T(8,128)(2,1)} %get-tuple-element.93.refs_1_.refs_2_, bf16[256,768]{1,0:T(8,128)(2,1)} %collective-permute-done.6.refs_1_.refs_3_, ...), custom_call_target="tpu_custom_call" | custom-call | flops 1 | bytes 1 | tf_op jit(solution)/shard_map/weight_part/pallas_call | solution.py:90
  124.9 7.3 %weight_part.6 = (bf16[768,768]{1,0:T(8,128)(2,1)}, bf16[768,768]{1,0:T(8,128)(2,1)}) custom-call(s32[47]{0:T(128)} %stack.119.refs_0_, bf16[1024,3072]{1,0:T(8,128)(2,1)} %get-tuple-element.109.refs_1_, bf16[4,256,768]{2,1,0:T(8,128)(2,1)} %all-to-all-done.refs_2_, bf16[1536,768]{1,0:T(8,128)(2,1)} %collective-permute-done.11.refs_3_, f32[8,128]{1,0:T(8,128)} %touch.11.refs_4_), custom_call_target="tpu_custom_call" | custom-call | flops 1 | bytes 1 | tf_op jit(solution)/shard_map/weight_part/pallas_call | solution.py:90
  132.2 7.2 %weight_part.7 = (bf16[768,768]{1,0:T(8,128)(2,1)}, bf16[768,768]{1,0:T(8,128)(2,1)}) custom-call(s32[47]{0:T(128)} %stack.119.refs_0_, bf16[1024,3072]{1,0:T(8,128)(2,1)} %get-tuple-element.108.refs_1_, bf16[256,768]{1,0:T(8,128)(2,1)} %get-tuple-element.93.refs_1_.refs_2_, bf16[256,768]{1,0:T(8,128)(2,1)} %collective-permute-done.6.refs_1_.refs_3_, ...), custom_call_target="tpu_custom_call" | custom-call | flops 1 | bytes 1 | tf_op jit(solution)/shard_map/weight_part/pallas_call | solution.py:90
  139.4 6.4 %second_back.1 = (f32[512,768]{1,0:T(8,128)}, bf16[512,768]{1,0:T(8,128)(2,1)}, f32[1,768]{1,0:T(1,128)}, bf16[512,384]{1,0:T(8,128)(2,1)}, bf16[512,384]{1,0:T(8,128)(2,1)}) custom-call(bf16[512,768]{1,0:T(8,128)(2,1)} %refs_0_.6, f32[512,768]{1,0:T(8,128)} %get-tuple-element.88.refs_1_.refs_0_, f32[768]{0:T(1024)} %refs_2_.7, s32[1,512]{1,0:T(1,128)} %bitcast.71, ...), custom_call_target="tpu_custom_call" | custom-call | flops 299999985664 | bytes 1 | tf_op jit(solution)/shard_map/second_back/pallas_call | solution.py:90
  155.0 4.5 %all-to-all-start.1 = ((bf16[4,256,768]{2,1,0:T(8,128)(2,1)}), bf16[4,256,768]{2,1,0:T(8,128)(2,1)}, u32[]{:S(2)}, u32[]{:S(2)}) async-start(bf16[4,256,768]{2,1,0:T(8,128)(2,1)} %touch.12), calls=%async_computation.1 | async-start | bytes 3145728 | tf_op jit(solution)/shard_map/all_to_all | solution.py:1028
  159.5 21.5 %attend_back.1 = (bf16[784,768]{1,0:T(8,128)(2,1)}, bf16[784,768]{1,0:T(8,128)(2,1)}, f32[512,768]{1,0:T(8,128)}, bf16[512,768]{1,0:T(8,128)(2,1)}) custom-call(s32[47]{0:T(128)} %stack.119.refs_0_, bf16[512,384]{1,0:T(8,128)(2,1)} %get-tuple-element.118.refs_1_, bf16[512,384]{1,0:T(8,128)(2,1)} %collective-permute-done.15.refs_2_, ...), custom_call_target="tpu_custom_call" | custom-call | flops 49999998976 | bytes 1 | tf_op jit(solution)/shard_map/attend_back/pallas_call | solution.py:90
  181.1 7.7 %collective-permute-done.17.refs_0_ = bf16[192,768]{1,0:T(8,128)(2,1)} collective-permute-done((bf16[192,768]{1,0:T(8,128)(2,1)}, bf16[192,768]{1,0:T(8,128)(2,1)}, u32[]{:S(2)}, u32[]{:S(2)}) %collective-permute-start.17) | collective-permute-done | bytes 294944 | tf_op jit(solution)/shard_map/output_grad/ppermute | solution.py:19
  192.4 4.9 %adds.2 = (bf16[384,768]{1,0:T(8,128)(2,1)}, bf16[384,768]{1,0:T(8,128)(2,1)}, bf16[384,768]{1,0:T(8,128)(2,1)}, bf16[384,768]{1,0:T(8,128)(2,1)}) custom-call(s32[47]{0:T(128)} %stack.119.refs_0_, bf16[768,768]{1,0:T(8,128)(2,1)} %get-tuple-element.116.refs_1_, bf16[768,768]{1,0:T(8,128)(2,1)} %collective-permute-done.13.refs_2_, ...), custom_call_target="tpu_custom_call" | custom-call | flops 1 | bytes 1 | tf_op jit(solution)/shard_map/adds/pallas_call | solution.py:90
  200.8 4.3 %all-to-all-start.2 = ((bf16[8,96,768]{2,1,0:T(8,128)(2,1)}), bf16[8,96,768]{2,1,0:T(8,128)(2,1)}, u32[]{:S(2)}, u32[]{:S(2)}) async-start(bf16[8,96,768]{2,1,0:T(8,128)(2,1)} %bitcast.68), calls=%async_computation.2 | async-start | bytes 2359296 | tf_op jit(solution)/shard_map/all_to_all | solution.py:1123
  208.9 5.0 %collective-permute-done.20.refs_2_ = bf16[384,768]{1,0:T(8,128)(2,1)} collective-permute-done((bf16[384,768]{1,0:T(8,128)(2,1)}, bf16[384,768]{1,0:T(8,128)(2,1)}, u32[]{:S(2)}, u32[]{:S(2)}) %collective-permute-start.20) | collective-permute-done | bytes 589856 | tf_op jit(solution)/shard_map/outer-1/ppermute | solution.py:19
  213.8 4.1 %collective-permute-done.21.refs_4_ = bf16[384,768]{1,0:T(8,128)(2,1)} collective-permute-done((bf16[384,768]{1,0:T(8,128)(2,1)}, bf16[384,768]{1,0:T(8,128)(2,1)}, u32[]{:S(2)}, u32[]{:S(2)}) %collective-permute-start.21) | collective-permute-done | bytes 589856 | tf_op jit(solution)/shard_map/inner-1/ppermute | solution.py:19
  225.8 7.3 %all-to-all-done.2.refs_0_ = bf16[8,96,768]{2,1,0:T(8,128)(2,1)} async-done(((bf16[8,96,768]{2,1,0:T(8,128)(2,1)}), bf16[8,96,768]{2,1,0:T(8,128)(2,1)}, u32[]{:S(2)}, u32[]{:S(2)}) %all-to-all-start.2) | async-done | bytes 1179680 | tf_op jit(solution)/shard_map/all_to_all | solution.py:1123
  235.6 4.5 %all-to-all-start.3 = ((bf16[8,112,768]{2,1,0:T(8,128)(2,1)}), bf16[8,112,768]{2,1,0:T(8,128)(2,1)}, u32[]{:S(2)}, u32[]{:S(2)}) async-start(bf16[8,112,768]{2,1,0:T(8,128)(2,1)} %total.1.refs_5_.refs_1_.refs_7_), calls=%async_computation.3 | async-start | bytes 2752512 | tf_op jit(solution)/shard_map/all_to_all | solution.py:1142
  240.2 4.5 %first_back.1.refs_2_ = f32[512,768]{1,0:T(8,128)} custom-call(bf16[512,768]{1,0:T(8,128)(2,1)} %refs_0_.7, f32[768]{0:T(1024)} %refs_1_.3, f32[512,768]{1,0:T(8,128)} %get-tuple-element.130.refs_2_, f32[512,768]{1,0:T(8,128)} %get-tuple-element.131.refs_3_, bf16[512,768]{1,0:T(8,128)(2,1)} %collective-permute-done.19.refs_4_, ...), custom_call_target="tpu_custom_call" | custom-call | flops 1 | bytes 1 | tf_op jit(solution)/shard_map/first_back/pallas_call | solution.py:90
  245.4 11.6 %collective-permute-done.28.refs_0_ = bf16[384,768]{1,0:T(8,128)(2,1)} collective-permute-done((bf16[384,768]{1,0:T(8,128)(2,1)}, bf16[384,768]{1,0:T(8,128)(2,1)}, u32[]{:S(2)}, u32[]{:S(2)}) %collective-permute-start.28) | collective-permute-done | bytes 589856 | tf_op jit(solution)/shard_map/piece/ppermute | solution.py:19
  261.6 6.4 %assemble.3.refs_8_.refs_1_.refs_5_ = f32[3072,768]{1,0:T(8,128)} custom-call(s32[47]{0:T(128)} %stack.119.refs_0_, bf16[384,768]{1,0:T(8,128)(2,1)} %get-tuple-element.136.refs_3_.refs_1_, bf16[384,768]{1,0:T(8,128)(2,1)} %get-tuple-element.138.refs_2_, bf16[384,768]{1,0:T(8,128)(2,1)} %get-tuple-element.139.refs_3_, ...), custom_call_target="tpu_custom_call" | custom-call | flops 1 | bytes 1 | tf_op jit(solution)/shard_map/assemble/pallas_call | solution.py:90
  268.0 6.4 %assemble.4.refs_2_.refs_6_ = f32[768,3072]{1,0:T(8,128)} custom-call(s32[47]{0:T(128)} %stack.119.refs_0_, bf16[384,768]{1,0:T(8,128)(2,1)} %get-tuple-element.137.refs_4_.refs_1_, bf16[384,768]{1,0:T(8,128)(2,1)} %get-tuple-element.141.refs_2_, bf16[384,768]{1,0:T(8,128)(2,1)} %get-tuple-element.142.refs_3_, ...), custom_call_target="tpu_custom_call" | custom-call | flops 1 | bytes 1 | tf_op jit(solution)/shard_map/assemble/pallas_call | solution.py:90
  274.4 4.6 %collective-permute-done.24.refs_0_ = bf16[384,768]{1,0:T(8,128)(2,1)} collective-permute-done((bf16[384,768]{1,0:T(8,128)(2,1)}, bf16[384,768]{1,0:T(8,128)(2,1)}, u32[]{:S(2)}, u32[]{:S(2)}) %collective-permute-start.24) | collective-permute-done | bytes 589856 | tf_op jit(solution)/shard_map/piece/ppermute | solution.py:19
  282.6 4.9 %weight_outputs.1 = (f32[3,768,384]{2,1,0:T(8,128)}, f32[384,768]{1,0:T(8,128)}, f32[768]{0:T(1024)}, f32[768]{0:T(1024)}) custom-call(s32[1]{0:T(128)} %bitcast.13.refs_0_, bf16[8,112,768]{2,1,0:T(8,128)(2,1)} %touch.21.refs_1_, bf16[8,112,768]{2,1,0:T(8,128)(2,1)} %collective-permute-done.34.refs_2_), custom_call_target="tpu_custom_call" | custom-call | flops 1 | bytes 1 | tf_op jit(solution)/shard_map/weight_outputs/pallas_call | solution.py:90
  287.5 5.3 %assemble.5 = (f32[3072,768]{1,0:T(8,128)}, f32[768,3072]{1,0:T(8,128)}) custom-call(s32[47]{0:T(128)} %stack.119.refs_0_, bf16[384,768]{1,0:T(8,128)(2,1)} %touch.19.refs_1_, bf16[384,768]{1,0:T(8,128)(2,1)} %collective-permute-done.35.refs_2_, bf16[384,768]{1,0:T(8,128)(2,1)} %touch.20.refs_2_.refs_3_, ...), custom_call_target="tpu_custom_call", output_to_operand_aliasing={{0}: (5, {}), {1}: (6, {})} | custom-call | flops 1 | bytes 1 | tf_op jit(solution)/shard_map/assemble/pallas_call | solution.py:90
  (104 shorter events, 68.7 us)
Async XLA Ops:
  0.6 14.1 %collective-permute-start.1 = (s32[512]{0:T(512)}, s32[512]{0:T(512)}, u32[]{:S(2)}, u32[]{:S(2)}) collective-permute-start(s32[512]{0:T(512)} %param.14), channel_id=1, source_target_pairs={{0,1},{1,0},{2,3},{3,2},{4,5},{5,4},{6,7},{7,6},{8,9},{9,8},{10,11... | collective-permute-start | bytes 6152 | tf_op jit(solution)/shard_map/positions/ppermute | solution.py:19
  3.7 21.7 %collective-permute-start = (bf16[512,768]{1,0:T(8,128)(2,1)}, bf16[512,768]{1,0:T(8,128)(2,1)}, u32[]{:S(2)}, u32[]{:S(2)}) collective-permute-start(bf16[512,768]{1,0:T(8,128)(2,1)} %refs_0_.7), channel_id=1, source_target_pairs={{0,1},{1,0},{2,3},{3,2},{4,5},{5,4},{6,7},{7,6},{8,9},{9,8},{10,11... | collective-permute-start | bytes 2359304 | tf_op jit(solution)/shard_map/rows/ppermute | solution.py:19
  18.3 20.0 %collective-permute-start.2 = (bf16[384,768]{1,0:T(8,128)(2,1)}, bf16[384,768]{1,0:T(8,128)(2,1)}, u32[]{:S(2)}, u32[]{:S(2)}) collective-permute-start(bf16[384,768]{1,0:T(8,128)(2,1)} %get-tuple-element.85), channel_id=1, source_target_pairs={{0,1},{1,0},{2,3},{3,2},{4,5},{5,4},{6,7},{7,6},{8,9},{9,8},{10,11... | collective-permute-start | bytes 1769480 | tf_op jit(solution)/shard_map/output_weight/ppermute | solution.py:19
  20.2 56.3 %all-to-all-start = ((bf16[4,256,768]{2,1,0:T(8,128)(2,1)}), bf16[4,256,768]{2,1,0:T(8,128)(2,1)}, u32[]{:S(2)}, u32[]{:S(2)}) async-start(bf16[4,256,768]{2,1,0:T(8,128)(2,1)} %get-tuple-element.90.refs_2_), calls=%async_computation | async-start | bytes 3145728 | tf_op jit(solution)/shard_map/all_to_all | solution.py:1028
  53.6 22.9 %collective-permute-start.6 = (bf16[256,768]{1,0:T(8,128)(2,1)}, bf16[256,768]{1,0:T(8,128)(2,1)}, u32[]{:S(2)}, u32[]{:S(2)}) collective-permute-start(bf16[256,768]{1,0:T(8,128)(2,1)} %get-tuple-element.92), channel_id=1, source_target_pairs={{0,2},{2,0},{4,6},{6,4},{1,3},{3,1},{5,7},{7,5},{8,10},{10,8},{12,... | collective-permute-start | bytes 1179656 | tf_op jit(solution)/shard_map/dispatch1/ppermute | solution.py:19
  55.4 32.6 %collective-permute-start.5 = (bf16[256,768]{1,0:T(8,128)(2,1)}, bf16[256,768]{1,0:T(8,128)(2,1)}, u32[]{:S(2)}, u32[]{:S(2)}) collective-permute-start(bf16[256,768]{1,0:T(8,128)(2,1)} %get-tuple-element.91), channel_id=1, source_target_pairs={{0,4},{2,6},{4,0},{6,2},{1,5},{3,7},{5,1},{7,3},{8,12},{10,14},{12... | collective-permute-start | bytes 1179656 | tf_op jit(solution)/shard_map/dispatch2/ppermute | solution.py:19
  58.5 39.6 %collective-permute-start.4 = (bf16[256,768]{1,0:T(8,128)(2,1)}, bf16[256,768]{1,0:T(8,128)(2,1)}, u32[]{:S(2)}, u32[]{:S(2)}) collective-permute-start(bf16[256,768]{1,0:T(8,128)(2,1)} %get-tuple-element.89), channel_id=1, source_target_pairs={{0,6},{2,4},{4,2},{6,0},{1,7},{3,5},{5,3},{7,1},{8,14},{10,12},{12... | collective-permute-start | bytes 1179656 | tf_op jit(solution)/shard_map/dispatch3/ppermute | solution.py:19
  86.1 53.3 %collective-permute-start.7 = (bf16[256,768]{1,0:T(8,128)(2,1)}, bf16[256,768]{1,0:T(8,128)(2,1)}, u32[]{:S(2)}, u32[]{:S(2)}) collective-permute-start(bf16[256,768]{1,0:T(8,128)(2,1)} %get-tuple-element.105), channel_id=1, source_target_pairs={{0,2},{2,0},{4,6},{6,4},{1,3},{3,1},{5,7},{7,5},{8,10},{10,8},{12,... | collective-permute-start | bytes 1179656 | tf_op jit(solution)/shard_map/return1/ppermute | solution.py:19
  97.6 41.8 %collective-permute-start.8 = (bf16[256,768]{1,0:T(8,128)(2,1)}, bf16[256,768]{1,0:T(8,128)(2,1)}, u32[]{:S(2)}, u32[]{:S(2)}) collective-permute-start(bf16[256,768]{1,0:T(8,128)(2,1)} %get-tuple-element.106), channel_id=1, source_target_pairs={{0,4},{2,6},{4,0},{6,2},{1,5},{3,7},{5,1},{7,3},{8,12},{10,14},{12... | collective-permute-start | bytes 1179656 | tf_op jit(solution)/shard_map/return2/ppermute | solution.py:19
  107.8 31.7 %collective-permute-start.9 = (bf16[256,768]{1,0:T(8,128)(2,1)}, bf16[256,768]{1,0:T(8,128)(2,1)}, u32[]{:S(2)}, u32[]{:S(2)}) collective-permute-start(bf16[256,768]{1,0:T(8,128)(2,1)} %get-tuple-element.107.refs_3_), channel_id=1, source_target_pairs={{0,6},{2,4},{4,2},{6,0},{1,7},{3,5},{5,3},{7,1},{8,14},{10,12},{12... | collective-permute-start | bytes 1179656 | tf_op jit(solution)/shard_map/return3/ppermute | solution.py:19
  145.8 13.7 %collective-permute-start.15 = (bf16[512,384]{1,0:T(8,128)(2,1)}, bf16[512,384]{1,0:T(8,128)(2,1)}, u32[]{:S(2)}, u32[]{:S(2)}) collective-permute-start(bf16[512,384]{1,0:T(8,128)(2,1)} %get-tuple-element.113.refs_4_), channel_id=1, source_target_pairs={{0,1},{1,0},{2,3},{3,2},{4,5},{5,4},{6,7},{7,6},{8,9},{9,8},{10,11... | collective-permute-start | bytes 1179656 | tf_op jit(solution)/shard_map/context_grad/ppermute | solution.py:19
  149.5 42.9 %collective-permute-start.13 = (bf16[768,768]{1,0:T(8,128)(2,1)}, bf16[768,768]{1,0:T(8,128)(2,1)}, u32[]{:S(2)}, u32[]{:S(2)}) collective-permute-start(bf16[768,768]{1,0:T(8,128)(2,1)} %get-tuple-element.110.refs_7_), channel_id=1, source_target_pairs={{0,16},{16,0},{1,17},{17,1},{2,18},{18,2},{3,19},{19,3},{4,20},{20... | collective-permute-start | bytes 3538952 | tf_op jit(solution)/shard_map/outer0/ppermute | solution.py:19
  151.1 41.3 %collective-permute-start.14 = (bf16[768,768]{1,0:T(8,128)(2,1)}, bf16[768,768]{1,0:T(8,128)(2,1)}, u32[]{:S(2)}, u32[]{:S(2)}) collective-permute-start(bf16[768,768]{1,0:T(8,128)(2,1)} %get-tuple-element.111.refs_10_.refs_16_), channel_id=1, source_target_pairs={{0,1},{1,0},{2,3},{3,2},{4,5},{5,4},{6,7},{7,6},{8,9},{9,8},{10,11... | collective-permute-start | bytes 3538952 | tf_op jit(solution)/shard_map/inner0/ppermute | solution.py:19
  154.3 34.4 %collective-permute-start.17 = (bf16[192,768]{1,0:T(8,128)(2,1)}, bf16[192,768]{1,0:T(8,128)(2,1)}, u32[]{:S(2)}, u32[]{:S(2)}) collective-permute-start(bf16[192,768]{1,0:T(8,128)(2,1)} %add.229.refs_1_), channel_id=1, source_target_pairs={{0,1},{1,0},{2,3},{3,2},{4,5},{5,4},{6,7},{7,6},{8,9},{9,8},{10,11... | collective-permute-start | bytes 884744 | tf_op jit(solution)/shard_map/output_grad/ppermute | solution.py:19
  155.0 45.8 %all-to-all-start.1 = ((bf16[4,256,768]{2,1,0:T(8,128)(2,1)}), bf16[4,256,768]{2,1,0:T(8,128)(2,1)}, u32[]{:S(2)}, u32[]{:S(2)}) async-start(bf16[4,256,768]{2,1,0:T(8,128)(2,1)} %touch.12), calls=%async_computation.1 | async-start | bytes 3145728 | tf_op jit(solution)/shard_map/all_to_all | solution.py:1028
  197.3 16.6 %collective-permute-start.20 = (bf16[384,768]{1,0:T(8,128)(2,1)}, bf16[384,768]{1,0:T(8,128)(2,1)}, u32[]{:S(2)}, u32[]{:S(2)}) collective-permute-start(bf16[384,768]{1,0:T(8,128)(2,1)} %get-tuple-element.128.refs_3_), channel_id=1, source_target_pairs={{0,1},{1,0},{2,3},{3,2},{4,5},{5,4},{6,7},{7,6},{8,9},{9,8},{10,11... | collective-permute-start | bytes 1769480 | tf_op jit(solution)/shard_map/outer-1/ppermute | solution.py:19
  198.6 19.3 %collective-permute-start.21 = (bf16[384,768]{1,0:T(8,128)(2,1)}, bf16[384,768]{1,0:T(8,128)(2,1)}, u32[]{:S(2)}, u32[]{:S(2)}) collective-permute-start(bf16[384,768]{1,0:T(8,128)(2,1)} %get-tuple-element.135), channel_id=1, source_target_pairs={{0,16},{16,0},{1,17},{17,1},{2,18},{18,2},{3,19},{19,3},{4,20},{20... | collective-permute-start | bytes 1769480 | tf_op jit(solution)/shard_map/inner-1/ppermute | solution.py:19
  200.1 39.9 %collective-permute-start.19 = (bf16[512,768]{1,0:T(8,128)(2,1)}, bf16[512,768]{1,0:T(8,128)(2,1)}, u32[]{:S(2)}, u32[]{:S(2)}) collective-permute-start(bf16[512,768]{1,0:T(8,128)(2,1)} %touch.14), channel_id=1, source_target_pairs={{0,1},{1,0},{2,3},{3,2},{4,5},{5,4},{6,7},{7,6},{8,9},{9,8},{10,11... | collective-permute-start | bytes 2359304 | tf_op jit(solution)/shard_map/theirs/ppermute | solution.py:19
  200.8 32.2 %all-to-all-start.2 = ((bf16[8,96,768]{2,1,0:T(8,128)(2,1)}), bf16[8,96,768]{2,1,0:T(8,128)(2,1)}, u32[]{:S(2)}, u32[]{:S(2)}) async-start(bf16[8,96,768]{2,1,0:T(8,128)(2,1)} %bitcast.68), calls=%async_computation.2 | async-start | bytes 2359296 | tf_op jit(solution)/shard_map/all_to_all | solution.py:1123
  221.7 23.0 %collective-permute-start.22 = (bf16[384,768]{1,0:T(8,128)(2,1)}, bf16[384,768]{1,0:T(8,128)(2,1)}, u32[]{:S(2)}, u32[]{:S(2)}) collective-permute-start(bf16[384,768]{1,0:T(8,128)(2,1)} %get-tuple-element.136.refs_3_.refs_1_), channel_id=1, source_target_pairs={{0,1},{1,0},{2,3},{3,2},{4,5},{5,4},{6,7},{7,6},{8,9},{9,8},{10,11... | collective-permute-start | bytes 1769480 | tf_op jit(solution)/shard_map/piece/ppermute | solution.py:19
  222.1 22.6 %collective-permute-start.23 = (bf16[384,768]{1,0:T(8,128)(2,1)}, bf16[384,768]{1,0:T(8,128)(2,1)}, u32[]{:S(2)}, u32[]{:S(2)}) collective-permute-start(bf16[384,768]{1,0:T(8,128)(2,1)} %get-tuple-element.136.refs_3_.refs_1_), channel_id=1, source_target_pairs={{0,16},{16,0},{1,17},{17,1},{2,18},{18,2},{3,19},{19,3},{4,20},{20... | collective-permute-start | bytes 1769480 | tf_op jit(solution)/shard_map/piece/ppermute | solution.py:19
  223.8 33.2 %collective-permute-start.28 = (bf16[384,768]{1,0:T(8,128)(2,1)}, bf16[384,768]{1,0:T(8,128)(2,1)}, u32[]{:S(2)}, u32[]{:S(2)}) collective-permute-start(bf16[384,768]{1,0:T(8,128)(2,1)} %get-tuple-element.137.refs_4_.refs_1_), channel_id=1, source_target_pairs={{0,16},{16,0},{1,17},{17,1},{2,18},{18,2},{3,19},{19,3},{4,20},{20... | collective-permute-start | bytes 1769480 | tf_op jit(solution)/shard_map/piece/ppermute | solution.py:19
  224.1 32.8 %collective-permute-start.29 = (bf16[384,768]{1,0:T(8,128)(2,1)}, bf16[384,768]{1,0:T(8,128)(2,1)}, u32[]{:S(2)}, u32[]{:S(2)}) collective-permute-start(bf16[384,768]{1,0:T(8,128)(2,1)} %get-tuple-element.137.refs_4_.refs_1_), channel_id=1, source_target_pairs={{0,1},{1,0},{2,3},{3,2},{4,5},{5,4},{6,7},{7,6},{8,9},{9,8},{10,11... | collective-permute-start | bytes 1769480 | tf_op jit(solution)/shard_map/piece/ppermute | solution.py:19
  235.6 43.5 %all-to-all-start.3 = ((bf16[8,112,768]{2,1,0:T(8,128)(2,1)}), bf16[8,112,768]{2,1,0:T(8,128)(2,1)}, u32[]{:S(2)}, u32[]{:S(2)}) async-start(bf16[8,112,768]{2,1,0:T(8,128)(2,1)} %total.1.refs_5_.refs_1_.refs_7_), calls=%async_computation.3 | async-start | bytes 2752512 | tf_op jit(solution)/shard_map/all_to_all | solution.py:1142
  240.1 17.4 %collective-permute-start.25 = (bf16[384,768]{1,0:T(8,128)(2,1)}, bf16[384,768]{1,0:T(8,128)(2,1)}, u32[]{:S(2)}, u32[]{:S(2)}) collective-permute-start(bf16[384,768]{1,0:T(8,128)(2,1)} %touch.16), channel_id=1, source_target_pairs={{0,8},{8,0},{1,9},{9,1},{2,10},{10,2},{3,11},{11,3},{4,12},{12,4},... | collective-permute-start | bytes 1769480 | tf_op jit(solution)/shard_map/piece_core/ppermute | solution.py:19
  244.7 12.9 %collective-permute-start.26 = (bf16[384,768]{1,0:T(8,128)(2,1)}, bf16[384,768]{1,0:T(8,128)(2,1)}, u32[]{:S(2)}, u32[]{:S(2)}) collective-permute-start(bf16[384,768]{1,0:T(8,128)(2,1)} %get-tuple-element.138.refs_2_), channel_id=1, source_target_pairs={{0,8},{8,0},{1,9},{9,1},{2,10},{10,2},{3,11},{11,3},{4,12},{12,4},... | collective-permute-start | bytes 1769480 | tf_op jit(solution)/shard_map/piece_core/ppermute | solution.py:19
  245.3 14.3 %collective-permute-start.27 = (bf16[384,768]{1,0:T(8,128)(2,1)}, bf16[384,768]{1,0:T(8,128)(2,1)}, u32[]{:S(2)}, u32[]{:S(2)}) collective-permute-start(bf16[384,768]{1,0:T(8,128)(2,1)} %get-tuple-element.139.refs_3_), channel_id=1, source_target_pairs={{0,8},{8,0},{1,9},{9,1},{2,10},{10,2},{3,11},{11,3},{4,12},{12,4},... | collective-permute-start | bytes 1769480 | tf_op jit(solution)/shard_map/piece_core/ppermute | solution.py:19
  257.0 11.0 %collective-permute-start.30 = (bf16[384,768]{1,0:T(8,128)(2,1)}, bf16[384,768]{1,0:T(8,128)(2,1)}, u32[]{:S(2)}, u32[]{:S(2)}) collective-permute-start(bf16[384,768]{1,0:T(8,128)(2,1)} %touch.18), channel_id=1, source_target_pairs={{0,8},{8,0},{1,9},{9,1},{2,10},{10,2},{3,11},{11,3},{4,12},{12,4},... | collective-permute-start | bytes 1769480 | tf_op jit(solution)/shard_map/piece_core/ppermute | solution.py:19
  257.0 11.0 %collective-permute-start.31 = (bf16[384,768]{1,0:T(8,128)(2,1)}, bf16[384,768]{1,0:T(8,128)(2,1)}, u32[]{:S(2)}, u32[]{:S(2)}) collective-permute-start(bf16[384,768]{1,0:T(8,128)(2,1)} %get-tuple-element.141.refs_2_), channel_id=1, source_target_pairs={{0,8},{8,0},{1,9},{9,1},{2,10},{10,2},{3,11},{11,3},{4,12},{12,4},... | collective-permute-start | bytes 1769480 | tf_op jit(solution)/shard_map/piece_core/ppermute | solution.py:19
  257.5 10.5 %collective-permute-start.32 = (bf16[384,768]{1,0:T(8,128)(2,1)}, bf16[384,768]{1,0:T(8,128)(2,1)}, u32[]{:S(2)}, u32[]{:S(2)}) collective-permute-start(bf16[384,768]{1,0:T(8,128)(2,1)} %get-tuple-element.142.refs_3_), channel_id=1, source_target_pairs={{0,8},{8,0},{1,9},{9,1},{2,10},{10,2},{3,11},{11,3},{4,12},{12,4},... | collective-permute-start | bytes 1769480 | tf_op jit(solution)/shard_map/piece_core/ppermute | solution.py:19
  257.6 21.5 %collective-permute-start.24 = (bf16[384,768]{1,0:T(8,128)(2,1)}, bf16[384,768]{1,0:T(8,128)(2,1)}, u32[]{:S(2)}, u32[]{:S(2)}) collective-permute-start(bf16[384,768]{1,0:T(8,128)(2,1)} %get-tuple-element.138.refs_2_), channel_id=1, source_target_pairs={{0,16},{16,0},{1,17},{17,1},{2,18},{18,2},{3,19},{19,3},{4,20},{20... | collective-permute-start | bytes 1769480 | tf_op jit(solution)/shard_map/piece/ppermute | solution.py:19
  259.5 19.5 %collective-permute-start.33 = (bf16[384,768]{1,0:T(8,128)(2,1)}, bf16[384,768]{1,0:T(8,128)(2,1)}, u32[]{:S(2)}, u32[]{:S(2)}) collective-permute-start(bf16[384,768]{1,0:T(8,128)(2,1)} %get-tuple-element.141.refs_2_), channel_id=1, source_target_pairs={{0,1},{1,0},{2,3},{3,2},{4,5},{5,4},{6,7},{7,6},{8,9},{9,8},{10,11... | collective-permute-start | bytes 1769480 | tf_op jit(solution)/shard_map/piece/ppermute | solution.py:19
  (10 other events, 72.4 us)
